TPU v7x, 32 devices: a whole 2x2x4 slice. The times are simulated.
32 devices in a mesh: section: 2 (over y), dp: 16 (over z, x, core).
Axes of the slice: x: 2, y: 2, z: 4, core: 2. Of those that a mesh axis runs over, the one named last changes fastest.
Arguments:
- boundary: bfloat16 [2, 32, 1024, 768], P('section', 'dp'), may hold values from -6 to 6
- doc_lengths: int32 [32], P('dp'), may hold values from 256 to 1024, as said below
- horizontal: int32 [32, 1024], P('dp'), may hold values from 0 to 511
- vertical: int32 [32, 1024], P('dp'), may hold values from 0 to 511
- attention_in: bfloat16 [2, 768, 2304], P('section'), may hold values from -0.21875 to 0.21875
- attention_out: bfloat16 [2, 768, 768], P('section'), may hold values from -1.75 to 1.75
- expand_weight: bfloat16 [2, 768, 3072], P('section'), may hold values from -0.21875 to 0.21875
- contract_weight: bfloat16 [2, 768, 3072], P('section'), may hold values from -0.109375 to 0.109375
- norm_gains: bfloat16 [2, 2, 768], P('section'), may hold values from 0.5 to 1.5
- bias_rows: bfloat16 [2, 6, 768], P('section'), may hold values from -3 to 3
- expand_bias: bfloat16 [2, 3072], P('section'), may hold values from -3 to 3
- position_table: bfloat16 [2, 32, 12], P('section'), may hold values from -3 to 3
- horizontal_table: bfloat16 [2, 31, 12], P('section'), may hold values from -3 to 3
- vertical_table: bfloat16 [2, 31, 12], P('section'), may hold values from -3 to 3
Outputs:
- boundary_out: bfloat16 [2, 32, 1024, 768], P('section', 'dp')
- grad_attention_in: float32 [2, 768, 2304], P('section')
- grad_attention_out: float32 [2, 768, 768], P('section')
- grad_expand_weight: float32 [2, 768, 3072], P('section')
- grad_contract_weight: float32 [2, 768, 3072], P('section')
- grad_norm_gains: float32 [2, 2, 768], P('section')
- grad_bias_rows: float32 [2, 6, 768], P('section')
- grad_expand_bias: float32 [2, 3072], P('section')
- grad_position_table: float32 [2, 32, 12], P('section')
- grad_horizontal_table: float32 [2, 31, 12], P('section')
- grad_vertical_table: float32 [2, 31, 12], P('section')
Inputs may be any that keep to these rules, and one draw needn't show every extreme that they name: A window's tokens fill its first doc_lengths slots and the rest is padding; in every draw some window has 1024 tokens and some has 256.
All inputs are finite; a program needn't handle non-finite values.
Results may differ from a plain program's by a relative error of at most 0.03.
Values may be sent and summed in bfloat16 or wider, within the bound.
No kernel may reach another device: no remote copies, remote signals or barrier semaphores. Data moves between devices by JAX's collectives and lax.ppermute only.
A program may use at most 448 MiB of HBM per device.

v0:
```python
import math

import jax
import jax.numpy as jnp
from jax import lax
from jax.sharding import PartitionSpec as P

GRID = 16
SPAN = 32
BLK = 512


epsilon = 1e-05
masked_score = -1e30
score_scale = 0.125
small_width = 128


def passed_along(shard, axis, by):
    devices = lax.axis_size(axis)
    pairs = [(i, i + by) for i in range(devices) if 0 <= i + by < devices]
    return lax.ppermute(shard, axis, pairs)


def layer_norm(summed, norm_gain, offset):
    center = summed - jnp.mean(summed, axis=-1, keepdims=True)
    second = jnp.mean(center * center, axis=-1, keepdims=True)
    return center * lax.rsqrt(second + epsilon) * norm_gain + offset


def gelu_exact(values):
    return jax.nn.gelu(values, approximate=False)


def cell_hot(labels, total_cells):
    return (labels[:, None] == jnp.arange(total_cells, dtype=jnp.int32)[None, :]).astype(
        jnp.bfloat16
    )


def bucket_select(cell_count, bucket_count, offset):
    cell_ids = jnp.arange(cell_count, dtype=jnp.int32)
    bucket_ids = (
        jnp.clip(cell_ids[None, :] - cell_ids[:, None], -offset, bucket_count - 1 - offset) + offset
    )
    return (
        bucket_ids[:, :, None] == jnp.arange(bucket_count, dtype=jnp.int32)[None, None, :]
    ).astype(jnp.float32)


def window_layout(horizontal_row, vertical_row, tables):
    slot_count = horizontal_row.shape[0]
    position_cells = slot_count // SPAN
    slot_ids = jnp.arange(slot_count, dtype=jnp.int32)
    query_side = jnp.concatenate(
        [
            cell_hot(slot_ids // SPAN, position_cells),
            cell_hot(horizontal_row // SPAN, GRID),
            cell_hot(vertical_row // SPAN, GRID),
        ],
        axis=1,
    )
    groups = (
        (0, position_cells, tables[0].shape[0] // 2),
        (position_cells, GRID, GRID - 1),
        (position_cells + GRID, GRID, GRID - 1),
    )
    selects = []
    key_parts = []
    for table_rows, group_info in zip(tables, groups):
        group_begin, group_cells, offset = group_info
        select_map = bucket_select(group_cells, table_rows.shape[0], offset)
        cell_table = jnp.einsum(
            "xcb,bh->hxc",
            select_map,
            table_rows.astype(jnp.float32),
            precision=lax.Precision.HIGHEST,
        ).astype(jnp.bfloat16)
        key_parts.append(
            jnp.einsum(
                "kx,hxc->hkc",
                query_side[:, group_begin : group_begin + group_cells],
                cell_table,
                preferred_element_type=jnp.float32,
            ).astype(jnp.bfloat16)
        )
        selects.append(select_map)
    return (query_side, jnp.concatenate(key_parts, axis=2), tuple(selects), groups)


def split_heads(joined, head_count):
    slot_count = joined.shape[0]
    model_width = joined.shape[1] // 3
    shaped = joined.reshape(slot_count, 3, head_count, model_width // head_count)
    return (shaped[:, 0] * score_scale, shaped[:, 1], shaped[:, 2])


def block_scores(query_block, side_block, key_heads, key_side, key_valid):
    scores = jnp.einsum("qhd,khd->hqk", query_block, key_heads, preferred_element_type=jnp.float32)
    scores = scores + jnp.einsum(
        "qc,hkc->hqk", side_block, key_side, preferred_element_type=jnp.float32
    )
    return jnp.where(key_valid[None, None, :], scores, masked_score)


def attend(query_heads, key_heads, value_heads, query_side, key_side, key_valid):
    outputs = []
    log_sums = []
    for row_begin in range(0, query_heads.shape[0], BLK):
        scores = block_scores(
            query_heads[row_begin : row_begin + BLK],
            query_side[row_begin : row_begin + BLK],
            key_heads,
            key_side,
            key_valid,
        )
        row_peak = jnp.max(scores, axis=-1, keepdims=True)
        exp_terms = jnp.exp(scores - row_peak)
        row_total = jnp.sum(exp_terms, axis=-1, keepdims=True)
        weights_low = (exp_terms / row_total).astype(jnp.bfloat16)
        outputs.append(
            jnp.einsum("hqk,khd->qhd", weights_low, value_heads, preferred_element_type=jnp.float32)
        )
        log_sums.append((row_peak + jnp.log(row_total))[:, :, 0])
    return (jnp.concatenate(outputs, axis=0), jnp.concatenate(log_sums, axis=1))


def attend_back(
    query_heads, key_heads, value_heads, query_side, key_side, key_valid, log_sums, grad_attended
):
    grad_keys = jnp.zeros(key_heads.shape, jnp.float32)
    grad_values = jnp.zeros(value_heads.shape, jnp.float32)
    grad_side = jnp.zeros(key_side.shape, jnp.float32)
    grad_rows = []
    for row_begin in range(0, query_heads.shape[0], BLK):
        query_block = query_heads[row_begin : row_begin + BLK]
        side_block = query_side[row_begin : row_begin + BLK]
        grad_block = grad_attended[row_begin : row_begin + BLK]
        scores = block_scores(query_block, side_block, key_heads, key_side, key_valid)
        prob_block = jnp.exp(scores - log_sums[:, row_begin : row_begin + BLK, None])
        grad_probs = jnp.einsum(
            "qhd,khd->hqk", grad_block, value_heads, preferred_element_type=jnp.float32
        )
        row_inner = jnp.sum(prob_block * grad_probs, axis=-1, keepdims=True)
        grad_scores = (prob_block * (grad_probs - row_inner)).astype(jnp.bfloat16)
        grad_values = grad_values + jnp.einsum(
            "hqk,qhd->khd",
            prob_block.astype(jnp.bfloat16),
            grad_block,
            preferred_element_type=jnp.float32,
        )
        grad_rows.append(
            jnp.einsum("hqk,khd->qhd", grad_scores, key_heads, preferred_element_type=jnp.float32)
            * score_scale
        )
        grad_keys = grad_keys + jnp.einsum(
            "hqk,qhd->khd", grad_scores, query_block, preferred_element_type=jnp.float32
        )
        grad_side = grad_side + jnp.einsum(
            "hqk,qc->hkc", grad_scores, side_block, preferred_element_type=jnp.float32
        )
    return (jnp.concatenate(grad_rows, axis=0), grad_keys, grad_values, grad_side)


def table_grads(grad_side, query_side, selects, groups):
    results = []
    for select_map, group_info in zip(selects, groups):
        group_begin, group_cells, offset = group_info
        hot_cells = query_side[:, group_begin : group_begin + group_cells].astype(jnp.float32)
        cell_grad = jnp.einsum(
            "kx,hkc->hxc",
            hot_cells,
            grad_side[:, :, group_begin : group_begin + group_cells],
            precision=lax.Precision.HIGHEST,
        )
        results.append(
            jnp.einsum("xcb,hxc->bh", select_map, cell_grad, precision=lax.Precision.HIGHEST)
        )
    return results


def small_columns(vectors, model_width):
    flat_values = jnp.concatenate([vector_part.reshape(-1) for vector_part in vectors])
    flat_values = jnp.pad(flat_values, (0, small_width * model_width - flat_values.shape[0]))
    return flat_values.reshape(small_width, model_width).T


def layer_forward(layer_in, params, layout, key_valid):
    (
        attention_in,
        attention_out,
        expand_weight,
        contract_weight,
        gain_rows,
        bias_rows,
        expand_bias,
    ) = params
    query_side, key_side, selects, groups = layout
    slot_count, model_width = layer_in.shape
    contract_last = (((1,), (1,)), ((), ()))
    gain_vals = gain_rows.astype(jnp.float32)
    bias_vals = bias_rows.astype(jnp.float32)
    joined_bias = jnp.concatenate([bias_vals[0], jnp.zeros_like(bias_vals[0]), bias_vals[1]])
    joined = (
        jnp.dot(layer_in, attention_in, preferred_element_type=jnp.float32) + joined_bias
    ).astype(jnp.bfloat16)
    query_heads, key_heads, value_heads = split_heads(joined, key_side.shape[0])
    attended, log_sums = attend(
        query_heads, key_heads, value_heads, query_side, key_side, key_valid
    )
    attended_low = attended.reshape(slot_count, model_width).astype(jnp.bfloat16)
    summed_one = (
        jnp.dot(attended_low, attention_out, preferred_element_type=jnp.float32)
        + bias_vals[2]
        + layer_in.astype(jnp.float32)
    )
    hidden_one = layer_norm(summed_one, gain_vals[0], bias_vals[3])
    pre_gelu = jnp.dot(
        hidden_one.astype(jnp.bfloat16), expand_weight, preferred_element_type=jnp.float32
    ) + expand_bias.astype(jnp.float32)
    gelu_low = gelu_exact(pre_gelu).astype(jnp.bfloat16)
    summed_two = (
        lax.dot_general(
            gelu_low, contract_weight, contract_last, preferred_element_type=jnp.float32
        )
        + bias_vals[4]
        + hidden_one
    )
    result = layer_norm(summed_two, gain_vals[1], bias_vals[5]).astype(jnp.bfloat16)
    return (result, (layer_in, joined, log_sums, attended_low, summed_one, pre_gelu, summed_two))


def layer_backward(grad_out, kept_values, params, layout, key_valid):
    layer_in, joined, log_sums, attended_low, summed_one, pre_gelu, summed_two = kept_values
    (
        attention_in,
        attention_out,
        expand_weight,
        contract_weight,
        gain_rows,
        bias_rows,
        expand_bias,
    ) = params
    query_side, key_side, selects, groups = layout
    slot_count, model_width = layer_in.shape
    head_count = key_side.shape[0]
    contract_last = (((1,), (1,)), ((), ()))
    gain_vals = gain_rows.astype(jnp.float32)
    bias_vals = bias_rows.astype(jnp.float32)
    hidden_one, norm_one_back = jax.vjp(layer_norm, summed_one, gain_vals[0], bias_vals[3])
    normed_two, norm_two_back = jax.vjp(layer_norm, summed_two, gain_vals[1], bias_vals[5])
    grad_sum_two, grad_gain_two, grad_shift_two = norm_two_back(grad_out)
    grad_branch_two = grad_sum_two.astype(jnp.bfloat16)
    gelu_value, gelu_back = jax.vjp(gelu_exact, pre_gelu)
    gelu_low = gelu_value.astype(jnp.bfloat16)
    grad_gelu = jnp.dot(grad_branch_two, contract_weight, preferred_element_type=jnp.float32)
    grad_pre = gelu_back(grad_gelu)[0].astype(jnp.bfloat16)
    grad_hidden = grad_sum_two + lax.dot_general(
        grad_pre, expand_weight, contract_last, preferred_element_type=jnp.float32
    )
    grad_sum_one, grad_gain_one, grad_shift_one = norm_one_back(grad_hidden)
    grad_branch_one = grad_sum_one.astype(jnp.bfloat16)
    grad_attended = lax.dot_general(
        grad_branch_one, attention_out, contract_last, preferred_element_type=jnp.float32
    ).astype(jnp.bfloat16)
    grad_attended = grad_attended.reshape(slot_count, head_count, model_width // head_count)
    query_heads, key_heads, value_heads = split_heads(joined, head_count)
    grad_queries, grad_keys, grad_values, grad_side = attend_back(
        query_heads,
        key_heads,
        value_heads,
        query_side,
        key_side,
        key_valid,
        log_sums,
        grad_attended,
    )
    grad_joined = jnp.concatenate(
        [
            grad_queries.reshape(slot_count, model_width),
            grad_keys.reshape(slot_count, model_width),
            grad_values.reshape(slot_count, model_width),
        ],
        axis=1,
    ).astype(jnp.bfloat16)
    grad_in = (
        lax.dot_general(
            grad_joined, attention_in, contract_last, preferred_element_type=jnp.float32
        )
        + grad_sum_one
    )
    joined_sums = jnp.sum(grad_joined, axis=0, dtype=jnp.float32)
    vectors = [
        joined_sums[:model_width],
        joined_sums[2 * model_width :],
        jnp.sum(grad_branch_one, axis=0, dtype=jnp.float32),
        grad_shift_one,
        jnp.sum(grad_branch_two, axis=0, dtype=jnp.float32),
        grad_shift_two,
        grad_gain_one,
        grad_gain_two,
        jnp.sum(grad_pre, axis=0, dtype=jnp.float32),
    ]
    vectors = vectors + table_grads(grad_side, query_side, selects, groups)
    small = small_columns(vectors, model_width)
    products = (
        layer_in,
        grad_joined,
        attended_low,
        grad_branch_one,
        hidden_one.astype(jnp.bfloat16),
        grad_pre,
        grad_branch_two,
        gelu_low,
    )
    return (grad_in.astype(jnp.bfloat16), products, small)


def weight_terms(products, small):
    (
        layer_in,
        grad_joined,
        attended_low,
        grad_branch_one,
        hidden_low,
        grad_pre,
        grad_branch_two,
        gelu_low,
    ) = products
    contract_first = (((0,), (0,)), ((), ()))
    return jnp.concatenate(
        [
            lax.dot_general(
                layer_in, grad_joined, contract_first, preferred_element_type=jnp.float32
            ),
            lax.dot_general(
                attended_low, grad_branch_one, contract_first, preferred_element_type=jnp.float32
            ),
            lax.dot_general(
                hidden_low, grad_pre, contract_first, preferred_element_type=jnp.float32
            ),
            lax.dot_general(
                grad_branch_two, gelu_low, contract_first, preferred_element_type=jnp.float32
            ),
            small,
        ],
        axis=1,
    )


def unpack_grads(whole_grads, matrices, vector_args):
    outputs = []
    column = 0
    for template in matrices:
        span_cols = template.shape[2]
        outputs.append(whole_grads[:, column : column + span_cols][None])
        column += span_cols
    flat_values = whole_grads[:, column:].T.reshape(-1)
    pieces = []
    begin_at = 0
    for template in vector_args:
        count_now = math.prod(template.shape)
        pieces.append(flat_values[begin_at : begin_at + count_now].reshape(template.shape))
        begin_at += count_now
    return tuple(outputs) + (pieces[1], pieces[0]) + tuple(pieces[2:])


def on_device(
    boundary,
    doc_lengths,
    horizontal,
    vertical,
    attention_in,
    attention_out,
    expand_weight,
    contract_weight,
    norm_gains,
    bias_rows,
    expand_bias,
    position_table,
    horizontal_table,
    vertical_table,
):
    section_index = lax.axis_index("section")
    section_count = lax.axis_size("section")
    last_section = section_count - 1
    own_data = boundary[0]
    micro_count, slot_count, model_width = own_data.shape
    hidden_units = expand_weight.shape[2]
    head_count = position_table.shape[2]
    params = (
        attention_in[0],
        attention_out[0],
        expand_weight[0],
        contract_weight[0],
        norm_gains[0],
        bias_rows[0],
        expand_bias[0],
    )
    tables = (position_table[0], horizontal_table[0], vertical_table[0])
    tick_ids = jnp.arange(micro_count + section_count - 1, dtype=jnp.int32)
    slab_width = 4 * model_width + 2 * hidden_units + small_width

    def slot_setup(slot_index):
        horizontal_row = lax.dynamic_index_in_dim(horizontal, slot_index, 0, keepdims=False)
        vertical_row = lax.dynamic_index_in_dim(vertical, slot_index, 0, keepdims=False)
        length = lax.dynamic_index_in_dim(doc_lengths, slot_index, 0, keepdims=False)
        key_valid = jnp.arange(slot_count, dtype=jnp.int32) < length
        return (window_layout(horizontal_row, vertical_row, tables), key_valid)

    kept_start = (
        jnp.zeros((micro_count, slot_count, model_width), jnp.bfloat16),
        jnp.zeros((micro_count, slot_count, 3 * model_width), jnp.bfloat16),
        jnp.zeros((micro_count, head_count, slot_count), jnp.float32),
        jnp.zeros((micro_count, slot_count, model_width), jnp.bfloat16),
        jnp.zeros((micro_count, slot_count, model_width), jnp.float32),
        jnp.zeros((micro_count, slot_count, hidden_units), jnp.float32),
        jnp.zeros((micro_count, slot_count, model_width), jnp.float32),
    )

    def forward_tick(state_in, tick_index):
        received, kept_all, finals = state_in
        micro_index = tick_index - section_index
        active = (micro_index >= 0) & (micro_index < micro_count)
        slot_index = jnp.clip(micro_index, 0, micro_count - 1)
        own_block = lax.dynamic_index_in_dim(own_data, slot_index, 0, keepdims=False)
        layer_in = jnp.where(section_index == 0, own_block, received)

        def forward_run_slot(buffers):
            layout, key_valid = slot_setup(slot_index)
            result, kept_values = layer_forward(layer_in, params, layout, key_valid)
            kept_new = tuple(
                (
                    lax.dynamic_update_index_in_dim(buffer, value_new, slot_index, 0)
                    for buffer, value_new in zip(buffers[0], kept_values)
                )
            )
            return (
                result,
                kept_new,
                lax.dynamic_update_index_in_dim(buffers[1], result, slot_index, 0),
            )

        def forward_skip_slot(buffers):
            return (jnp.zeros_like(received), buffers[0], buffers[1])

        result, kept_all, finals = lax.cond(
            active, forward_run_slot, forward_skip_slot, (kept_all, finals)
        )
        received = passed_along(result, "section", 1)
        return ((received, kept_all, finals), None)

    forward_start = (
        jnp.zeros((slot_count, model_width), jnp.bfloat16),
        kept_start,
        jnp.zeros_like(own_data),
    )
    forward_end, ignored_ys = lax.scan(forward_tick, forward_start, tick_ids)
    kept_all = forward_end[1]
    finals = forward_end[2]
    totals_start = jnp.zeros((model_width, slab_width), jnp.float32)
    stored_start = ()

    def backward_tick(state_in, tick_index):
        received, totals, grad_inputs, stored = state_in
        micro_index = tick_index - (last_section - section_index)
        active = (micro_index >= 0) & (micro_index < micro_count)
        slot_index = jnp.clip(micro_index, 0, micro_count - 1)
        own_block = lax.dynamic_index_in_dim(own_data, slot_index, 0, keepdims=False)
        grad_out = jnp.where(section_index == last_section, own_block, received).astype(jnp.float32)

        def backward_run_slot(buffers):
            totals_in, grad_buffer, stored_in = buffers
            layout, key_valid = slot_setup(slot_index)
            kept_values = tuple(
                (
                    lax.dynamic_index_in_dim(buffer, slot_index, 0, keepdims=False)
                    for buffer in kept_all
                )
            )
            grad_in, products, small = layer_backward(
                grad_out, kept_values, params, layout, key_valid
            )
            grad_buffer = lax.dynamic_update_index_in_dim(grad_buffer, grad_in, slot_index, 0)
            totals_in = totals_in + weight_terms(products, small)
            return (grad_in, totals_in, grad_buffer, stored_in)

        def backward_skip_slot(buffers):
            return (jnp.zeros_like(received), buffers[0], buffers[1], buffers[2])

        grad_in, totals, grad_inputs, stored = lax.cond(
            active, backward_run_slot, backward_skip_slot, (totals, grad_inputs, stored)
        )
        received = passed_along(grad_in, "section", -1)
        return ((received, totals, grad_inputs, stored), None)

    backward_start = (
        jnp.zeros((slot_count, model_width), jnp.bfloat16),
        totals_start,
        jnp.zeros_like(own_data),
        stored_start,
    )
    backward_end, ignored_back = lax.scan(backward_tick, backward_start, tick_ids)
    totals = backward_end[1]
    grad_inputs = backward_end[2]
    stored = backward_end[3]
    grad_part = lax.psum_scatter(totals, "dp", scatter_dimension=0, tiled=True)
    whole_grads = lax.all_gather(grad_part.astype(jnp.bfloat16), "dp", axis=0, tiled=True).astype(
        grad_part.dtype
    )
    boundary_out = jnp.where(section_index == 0, grad_inputs, finals)[None]
    return (boundary_out,) + unpack_grads(
        whole_grads,
        (attention_in, attention_out, expand_weight, contract_weight),
        (bias_rows, norm_gains, expand_bias, position_table, horizontal_table, vertical_table),
    )


def solution(mesh):
    placed = (
        P("section", "dp", None, None),
        P("dp"),
        P("dp", None),
        P("dp", None),
        P("section", None, None),
        P("section", None, None),
        P("section", None, None),
        P("section", None, None),
        P("section", None, None),
        P("section", None, None),
        P("section", None),
        P("section", None, None),
        P("section", None, None),
        P("section", None, None),
    )
    return jax.shard_map(
        on_device,
        mesh=mesh,
        in_specs=placed,
        out_specs=(
            P("section", "dp", None, None),
            P("section", None, None),
            P("section", None, None),
            P("section", None, None),
            P("section", None, None),
            P("section", None, None),
            P("section", None, None),
            P("section", None),
            P("section", None, None),
            P("section", None, None),
            P("section", None, None),
        ),
        check_vma=False,
    )
```

profile of v0, /device:TPU:0, one launch (start us, length us, event | category | flops | bytes accessed | tf_op | source)
XLA Modules:
  0.0 2499.8 jit_solution(10376810766381882752)
XLA Ops:
  43.0 708.5 %while.43 = (s32[]{:T(128)}, bf16[1024,768]{0,1:T(8,128)(2,1)S(1)}, bf16[2,1024,768]{1,2,0:T(8,128)(2,1)}, bf16[2,1024,2304]{2,1,0:T(8,128)(2,1)}, f32[2,12,1024...) while((s32[]{:T(128)}, bf16[1024,768]{0,1:T(8,128)(2,1)S(1)}, ...), condition=%wide.region_11.12_spmd, body=%wide.region_0.11_spmd.sunk | while | flops 19718981632 | bytes 564338560 | solution.py:458
  67.1 188.4 %conditional.4 = (bf16[1024,768]{0,1:T(8,128)(2,1)}, bf16[2,1024,768]{1,2,0:T(8,128)(2,1)}, bf16[2,1024,2304]{2,1,0:T(8,128)(2,1)}, f32[2,12,1024]{2,1,0:T(8,128...) conditional(s32[]{:T(128)} %convert_element_type.341, ...), branch_computations={%region_1.1_spmd, %region_2.10_spmd} | conditional | flops 19718981632 | bytes 558046528 | solution.py:447
  212.1 34.2 %fusion.203 = (f32[1024]{0:T(1024)S(1)}, f32[1024,768]{0,1:T(8,128)S(1)}) fusion(f32[768]{0:T(1024)S(1)} %get-tuple-element.1054, f32[768]{0:T(1024)S(1)} %get-tuple-element.1059, f32[1024]{0:T(1024)S(1)} %add_rsqrt_fusion.1, f32[1024,768]{0,1:T(8,128)S(1)} %get-tuple-element.1193, f32[1024]{0:T(1024)S(1)} %broadcast_multiply_fusion.1, ...), kind=kOutput, calls=%fused_computation.392 | convolution fusion | flops 5044960256 | bytes 23626752 | tf_op jit(solution)/shard_map/while/body/eval_jaxpr/cond/branch_1_fun/dot_general | solution.py:223
  256.9 34.7 %collective-permute-done = bf16[1024,768]{0,1:T(8,128)(2,1)S(1)} collective-permute-done((bf16[1024,768]{0,1:T(8,128)(2,1)}, bf16[1024,768]{0,1:T(8,128)(2,1)S(1)}, u32[]{:S(2)}, u32[]{:S(2)}) %collective-permute-start) | collective-permute-done | bytes 1572896 | tf_op jit(solution)/shard_map/while/body/eval_jaxpr/ppermute | solution.py:22
  293.5 188.5 %conditional.4 = (bf16[1024,768]{0,1:T(8,128)(2,1)}, bf16[2,1024,768]{1,2,0:T(8,128)(2,1)}, bf16[2,1024,2304]{2,1,0:T(8,128)(2,1)}, f32[2,12,1024]{2,1,0:T(8,128...) conditional(s32[]{:T(128)} %convert_element_type.341, ...), branch_computations={%region_1.1_spmd, %region_2.10_spmd} | conditional | flops 19718981632 | bytes 558046528 | solution.py:447
  383.7 16.0 fusion.201
  438.6 34.2 %fusion.203 = (f32[1024]{0:T(1024)S(1)}, f32[1024,768]{0,1:T(8,128)S(1)}) fusion(f32[768]{0:T(1024)S(1)} %get-tuple-element.1054, f32[768]{0:T(1024)S(1)} %get-tuple-element.1059, f32[1024]{0:T(1024)S(1)} %add_rsqrt_fusion.1, f32[1024,768]{0,1:T(8,128)S(1)} %get-tuple-element.1193, f32[1024]{0:T(1024)S(1)} %broadcast_multiply_fusion.1, ...), kind=kOutput, calls=%fused_computation.392 | convolution fusion | flops 5044960256 | bytes 23626752 | tf_op jit(solution)/shard_map/while/body/eval_jaxpr/cond/branch_1_fun/dot_general | solution.py:223
  486.4 33.9 %collective-permute-done = bf16[1024,768]{0,1:T(8,128)(2,1)S(1)} collective-permute-done((bf16[1024,768]{0,1:T(8,128)(2,1)}, bf16[1024,768]{0,1:T(8,128)(2,1)S(1)}, u32[]{:S(2)}, u32[]{:S(2)}) %collective-permute-start) | collective-permute-done | bytes 1572896 | tf_op jit(solution)/shard_map/while/body/eval_jaxpr/ppermute | solution.py:22
  523.5 191.5 %collective-permute-start = (bf16[1024,768]{0,1:T(8,128)(2,1)}, bf16[1024,768]{0,1:T(8,128)(2,1)S(1)}, u32[]{:S(2)}, u32[]{:S(2)}) collective-permute-start(bf16[1024,768]{0,1:T(8,128)(2,1)} %get-tuple-element.1540), channel_id=1, source_target_pairs={{0,16},{1,17},{2,18},{3,19},{4,20},{5,21},{6,22},{7,23},{8,24},{9,... | collective-permute-start | bytes 4718600 | tf_op jit(solution)/shard_map/while/body/eval_jaxpr/ppermute | solution.py:22
  715.0 33.0 %collective-permute-done = bf16[1024,768]{0,1:T(8,128)(2,1)S(1)} collective-permute-done((bf16[1024,768]{0,1:T(8,128)(2,1)}, bf16[1024,768]{0,1:T(8,128)(2,1)S(1)}, u32[]{:S(2)}, u32[]{:S(2)}) %collective-permute-start) | collective-permute-done | bytes 1572896 | tf_op jit(solution)/shard_map/while/body/eval_jaxpr/ppermute | solution.py:22
  800.1 1257.3 %while.44 = (s32[]{:T(128)}, bf16[1024,768]{1,0:T(8,128)(2,1)}, f32[768,9344]{1,0:T(8,128)}, bf16[2,1024,768]{2,1,0:T(8,128)(2,1)}, s32[3]{0:T(128)}, /*index=5*...) while((s32[]{:T(128)}, bf16[1024,768]{1,0:T(8,128)(2,1)}, ...), condition=%wide.region_33.34_spmd, body=%wide.region_12.33_spmd.sunk | while | flops 41024372736 | bytes 1279895680 | solution.py:503
  809.4 407.7 %collective-permute-done.1 = bf16[1024,768]{1,0:T(8,128)(2,1)S(1)} collective-permute-done((bf16[1024,768]{1,0:T(8,128)(2,1)}, bf16[1024,768]{1,0:T(8,128)(2,1)S(1)}, u32[]{:S(2)}, u32[]{:S(2)}) %collective-permute-start.1) | collective-permute-done | bytes 1572896 | tf_op jit(solution)/shard_map/while/body/eval_jaxpr/ppermute | solution.py:22
  1222.3 376.8 %conditional.5 = (bf16[1024,768]{1,0:T(8,128)(2,1)}, f32[768,9344]{1,0:T(8,128)}, bf16[2,1024,768]{2,1,0:T(8,128)(2,1)}) conditional(s32[]{:T(128)} %convert_element_type.343, (f32[768,9344]{1,0:T(8,128)}, bf16[2,1024,768]{2,1,0:T(8,128)(2,1)}) %tuple.119, (s32[]{:T(128)}, bf16[2,1024,2304]{1,2,0:T(8,128)(2,1)}, s32[2]{0:T(128)}, ...), branch_computations={%region_13.13_spmd, %region_14.32_spmd} | conditional | flops 41022799872 | bytes 1261020800 | solution.py:491
  1250.1 28.6 %fusion.93 = f32[1024,3072]{1,0:T(8,128)} fusion(f32[2,1024,3072]{2,1,0:T(8,128)} %get-tuple-element.795, s32[]{:T(128)S(6)} %select_n.137), kind=kLoop, calls=%fused_computation.182 | loop fusion | flops 195035136 | bytes 25165828 | tf_op jit(solution)/shard_map/while/body/eval_jaxpr/cond/branch_1_fun/jvp()/erfc | solution.py:32
  1278.7 17.3 convert_reduce_fusion
  1343.3 25.7 %multiply_reduce_fusion.2 = (f32[12,512]{1,0:T(8,128)S(1)}, f32[12,512,1024]{2,1,0:T(8,128)}) fusion(f32[12,512,1024]{2,1,0:T(8,128)} %fusion.132, f32[12,512]{1,0:T(8,128)S(1)} %get-tuple-element.1208, f32[12,512,1024]{2,1,0:T(8,128)} %fusion.145, pred[1024,64]{0,1:T(32,128)(4,1)S(1)} %pad_add_fusion.1, bf16[12,1024,16]{1,2,0:T(8,128)(2,1)} %fusion.138, ...), kind=kOutput, calls=%fused_computation.178 | convolution fusion | flops 841476096 | bytes 77161472 | tf_op jit(solution)/shard_map/while/body/eval_jaxpr/cond/branch_1_fun/qc,hkc->hqk/dot_general | solution.py:100
  1368.9 21.5 multiply_convert_fusion
  1421.9 25.6 %multiply_reduce_fusion.3 = (f32[12,512]{1,0:T(8,128)S(1)}, f32[12,512,1024]{2,1,0:T(8,128)}) fusion(f32[12,512,1024]{2,1,0:T(8,128)} %fusion.133, f32[12,512]{1,0:T(8,128)S(1)} %copy-done.29, f32[12,512,1024]{2,1,0:T(8,128)} %fusion.146, pred[1024,64]{0,1:T(32,128)(4,1)S(1)} %pad_add_fusion.1, bf16[12,1024,16]{1,2,0:T(8,128)(2,1)} %fusion.138, ...), kind=kOutput, calls=%fused_computation.180 | convolution fusion | flops 841476096 | bytes 77161472 | tf_op jit(solution)/shard_map/while/body/eval_jaxpr/cond/branch_1_fun/qc,hkc->hqk/dot_general | solution.py:100
  1460.1 21.3 multiply_convert_fusion.1
  1570.5 28.4 %add.340 = f32[768,9344]{1,0:T(8,128)} add(f32[768,9344]{1,0:T(8,128)} %get-tuple-element.801, f32[768,9344]{1,0:T(8,128)} %bitcast_dynamic-update-slice_fusion.7) | non-fusion elementwise | flops 7176192 | bytes 86114304 | tf_op jit(solution)/shard_map/while/body/eval_jaxpr/cond/branch_1_fun/add | solution.py:485
  1600.4 34.5 %collective-permute-done.1 = bf16[1024,768]{1,0:T(8,128)(2,1)S(1)} collective-permute-done((bf16[1024,768]{1,0:T(8,128)(2,1)}, bf16[1024,768]{1,0:T(8,128)(2,1)S(1)}, u32[]{:S(2)}, u32[]{:S(2)}) %collective-permute-start.1) | collective-permute-done | bytes 1572896 | tf_op jit(solution)/shard_map/while/body/eval_jaxpr/ppermute | solution.py:22
  1640.4 376.9 %conditional.5 = (bf16[1024,768]{1,0:T(8,128)(2,1)}, f32[768,9344]{1,0:T(8,128)}, bf16[2,1024,768]{2,1,0:T(8,128)(2,1)}) conditional(s32[]{:T(128)} %convert_element_type.343, (f32[768,9344]{1,0:T(8,128)}, bf16[2,1024,768]{2,1,0:T(8,128)(2,1)}) %tuple.119, (s32[]{:T(128)}, bf16[2,1024,2304]{1,2,0:T(8,128)(2,1)}, s32[2]{0:T(128)}, ...), branch_computations={%region_13.13_spmd, %region_14.32_spmd} | conditional | flops 41022799872 | bytes 1261020800 | solution.py:491
  1668.1 28.6 %fusion.93 = f32[1024,3072]{1,0:T(8,128)} fusion(f32[2,1024,3072]{2,1,0:T(8,128)} %get-tuple-element.795, s32[]{:T(128)S(6)} %select_n.137), kind=kLoop, calls=%fused_computation.182 | loop fusion | flops 195035136 | bytes 25165828 | tf_op jit(solution)/shard_map/while/body/eval_jaxpr/cond/branch_1_fun/jvp()/erfc | solution.py:32
  1696.7 17.3 convert_reduce_fusion
  1761.4 25.7 %multiply_reduce_fusion.2 = (f32[12,512]{1,0:T(8,128)S(1)}, f32[12,512,1024]{2,1,0:T(8,128)}) fusion(f32[12,512,1024]{2,1,0:T(8,128)} %fusion.132, f32[12,512]{1,0:T(8,128)S(1)} %get-tuple-element.1208, f32[12,512,1024]{2,1,0:T(8,128)} %fusion.145, pred[1024,64]{0,1:T(32,128)(4,1)S(1)} %pad_add_fusion.1, bf16[12,1024,16]{1,2,0:T(8,128)(2,1)} %fusion.138, ...), kind=kOutput, calls=%fused_computation.178 | convolution fusion | flops 841476096 | bytes 77161472 | tf_op jit(solution)/shard_map/while/body/eval_jaxpr/cond/branch_1_fun/qc,hkc->hqk/dot_general | solution.py:100
  1787.0 21.5 multiply_convert_fusion
  1840.0 25.6 %multiply_reduce_fusion.3 = (f32[12,512]{1,0:T(8,128)S(1)}, f32[12,512,1024]{2,1,0:T(8,128)}) fusion(f32[12,512,1024]{2,1,0:T(8,128)} %fusion.133, f32[12,512]{1,0:T(8,128)S(1)} %copy-done.29, f32[12,512,1024]{2,1,0:T(8,128)} %fusion.146, pred[1024,64]{0,1:T(32,128)(4,1)S(1)} %pad_add_fusion.1, bf16[12,1024,16]{1,2,0:T(8,128)(2,1)} %fusion.138, ...), kind=kOutput, calls=%fused_computation.180 | convolution fusion | flops 841476096 | bytes 77161472 | tf_op jit(solution)/shard_map/while/body/eval_jaxpr/cond/branch_1_fun/qc,hkc->hqk/dot_general | solution.py:100
  1878.2 21.3 multiply_convert_fusion.1
  1988.6 28.4 %add.340 = f32[768,9344]{1,0:T(8,128)} add(f32[768,9344]{1,0:T(8,128)} %get-tuple-element.801, f32[768,9344]{1,0:T(8,128)} %bitcast_dynamic-update-slice_fusion.7) | non-fusion elementwise | flops 7176192 | bytes 86114304 | tf_op jit(solution)/shard_map/while/body/eval_jaxpr/cond/branch_1_fun/add | solution.py:485
  2018.5 33.6 %collective-permute-done.1 = bf16[1024,768]{1,0:T(8,128)(2,1)S(1)} collective-permute-done((bf16[1024,768]{1,0:T(8,128)(2,1)}, bf16[1024,768]{1,0:T(8,128)(2,1)S(1)}, u32[]{:S(2)}, u32[]{:S(2)}) %collective-permute-start.1) | collective-permute-done | bytes 1572896 | tf_op jit(solution)/shard_map/while/body/eval_jaxpr/ppermute | solution.py:22
  2057.4 271.0 %reduce-scatter.2.cloned.1.call-done = f32[48,9344]{1,0:T(8,128)} async-done(((f32[768,9344]{1,0:T(8,128)}), f32[48,9344]{1,0:T(8,128)}) %reduce-scatter.2.cloned.1.call-update) | async-done | bytes 1794064 | tf_op jit(solution)/shard_map/reduce_scatter | solution.py:507
  2337.6 104.5 %all-gather.2.cloned.1.call-done = bf16[768,9344]{1,0:T(8,128)(2,1)} async-done(((bf16[48,9344]{1,0:T(8,128)(2,1)}), bf16[768,9344]{1,0:T(8,128)(2,1)}) %all-gather.2.cloned.1.call-update) | async-done | bytes 14352400 | tf_op jit(solution)/shard_map/all_gather | solution.py:508
  (698 shorter events, 885.1 us)
Async XLA Ops:
  7.2 2321.2 %reduce-scatter.2.cloned.1.call-start = ((), (), s32[]{:S(2)}) async-start(), calls=%async_computation.1 | async-start | bytes 30498816 | tf_op jit(solution)/shard_map/reduce_scatter | solution.py:507
  198.3 50.8 %slice-start.19 = ((s8[6291456]{0:T(1024)(128)(4,1)}), s8[4194304]{0:T(1024)(128)(4,1)S(1)}, s32[]{:S(2)}) async-start(s8[6291456]{0:T(1024)(128)(4,1)} %bitcast.428), calls=%async_computation.22 | async-start | bytes 8388608 | tf_op jit(solution)/shard_map/while/body/eval_jaxpr/cond
  198.3 50.8 %slice-start.21 = ((s8[6291456]{0:T(1024)(128)(4,1)}), s8[4194304]{0:T(1024)(128)(4,1)S(1)}, s32[]{:S(2)}) async-start(s8[6291456]{0:T(1024)(128)(4,1)} %bitcast.430), calls=%async_computation.24 | async-start | bytes 8388608 | tf_op jit(solution)/shard_map/while/body/eval_jaxpr/cond
  212.0 34.6 %copy-start.44 = (f32[768]{0:T(1024)S(1)}, f32[768]{0:T(1024)}, u32[]{:S(2)}) copy-start(f32[768]{0:T(1024)} %get-tuple-element.1058) | copy-start | bytes 9220 | tf_op jit(solution)/shard_map/while/body/eval_jaxpr/cond
  212.0 34.6 %copy-start.53 = (f32[768]{0:T(1024)S(1)}, f32[768]{0:T(1024)}, u32[]{:S(2)}) copy-start(f32[768]{0:T(1024)} %get-tuple-element.1052) | copy-start | bytes 9220 | tf_op jit(solution)/shard_map/while/body/eval_jaxpr/cond
  212.1 37.0 %slice-start.20 = ((s8[6291456]{0:T(1024)(128)(4,1)}), s8[2097152]{0:T(1024)(128)(4,1)S(1)}, s32[]{:S(2)}) async-start(s8[6291456]{0:T(1024)(128)(4,1)} %bitcast.428), calls=%async_computation.23 | async-start | bytes 4194304 | tf_op jit(solution)/shard_map/while/body/eval_jaxpr/cond
  212.1 37.0 %slice-start.22 = ((s8[6291456]{0:T(1024)(128)(4,1)}), s8[2097152]{0:T(1024)(128)(4,1)S(1)}, s32[]{:S(2)}) async-start(s8[6291456]{0:T(1024)(128)(4,1)} %bitcast.430), calls=%async_computation.25 | async-start | bytes 4194304 | tf_op jit(solution)/shard_map/while/body/eval_jaxpr/cond
  255.5 36.1 %collective-permute-start = (bf16[1024,768]{0,1:T(8,128)(2,1)}, bf16[1024,768]{0,1:T(8,128)(2,1)S(1)}, u32[]{:S(2)}, u32[]{:S(2)}) collective-permute-start(bf16[1024,768]{0,1:T(8,128)(2,1)} %get-tuple-element.1540), channel_id=1, source_target_pairs={{0,16},{1,17},{2,18},{3,19},{4,20},{5,21},{6,22},{7,23},{8,24},{9,... | collective-permute-start | bytes 4718600 | tf_op jit(solution)/shard_map/while/body/eval_jaxpr/ppermute | solution.py:22
  424.8 50.8 %slice-start.19 = ((s8[6291456]{0:T(1024)(128)(4,1)}), s8[4194304]{0:T(1024)(128)(4,1)S(1)}, s32[]{:S(2)}) async-start(s8[6291456]{0:T(1024)(128)(4,1)} %bitcast.428), calls=%async_computation.22 | async-start | bytes 8388608 | tf_op jit(solution)/shard_map/while/body/eval_jaxpr/cond
  424.8 50.8 %slice-start.21 = ((s8[6291456]{0:T(1024)(128)(4,1)}), s8[4194304]{0:T(1024)(128)(4,1)S(1)}, s32[]{:S(2)}) async-start(s8[6291456]{0:T(1024)(128)(4,1)} %bitcast.430), calls=%async_computation.24 | async-start | bytes 8388608 | tf_op jit(solution)/shard_map/while/body/eval_jaxpr/cond
  438.6 34.6 %copy-start.25 = (bf16[2,1024,768]{1,2,0:T(8,128)(2,1)S(1)}, bf16[2,1024,768]{1,2,0:T(8,128)(2,1)}, u32[]{:S(2)}) copy-start(bf16[2,1024,768]{1,2,0:T(8,128)(2,1)} %get-tuple-element.743) | copy-start | bytes 9437188 | tf_op jit(solution)/shard_map/while/body/eval_jaxpr/cond
  438.6 34.6 %copy-start.44 = (f32[768]{0:T(1024)S(1)}, f32[768]{0:T(1024)}, u32[]{:S(2)}) copy-start(f32[768]{0:T(1024)} %get-tuple-element.1058) | copy-start | bytes 9220 | tf_op jit(solution)/shard_map/while/body/eval_jaxpr/cond
  438.6 34.6 %copy-start.53 = (f32[768]{0:T(1024)S(1)}, f32[768]{0:T(1024)}, u32[]{:S(2)}) copy-start(f32[768]{0:T(1024)} %get-tuple-element.1052) | copy-start | bytes 9220 | tf_op jit(solution)/shard_map/while/body/eval_jaxpr/cond
  438.6 37.0 %slice-start.20 = ((s8[6291456]{0:T(1024)(128)(4,1)}), s8[2097152]{0:T(1024)(128)(4,1)S(1)}, s32[]{:S(2)}) async-start(s8[6291456]{0:T(1024)(128)(4,1)} %bitcast.428), calls=%async_computation.23 | async-start | bytes 4194304 | tf_op jit(solution)/shard_map/while/body/eval_jaxpr/cond
  438.6 37.0 %slice-start.22 = ((s8[6291456]{0:T(1024)(128)(4,1)}), s8[2097152]{0:T(1024)(128)(4,1)S(1)}, s32[]{:S(2)}) async-start(s8[6291456]{0:T(1024)(128)(4,1)} %bitcast.430), calls=%async_computation.25 | async-start | bytes 4194304 | tf_op jit(solution)/shard_map/while/body/eval_jaxpr/cond
  482.0 38.2 %collective-permute-start = (bf16[1024,768]{0,1:T(8,128)(2,1)}, bf16[1024,768]{0,1:T(8,128)(2,1)S(1)}, u32[]{:S(2)}, u32[]{:S(2)}) collective-permute-start(bf16[1024,768]{0,1:T(8,128)(2,1)} %get-tuple-element.1540), channel_id=1, source_target_pairs={{0,16},{1,17},{2,18},{3,19},{4,20},{5,21},{6,22},{7,23},{8,24},{9,... | collective-permute-start | bytes 4718600 | tf_op jit(solution)/shard_map/while/body/eval_jaxpr/ppermute | solution.py:22
  523.5 224.6 %collective-permute-start = (bf16[1024,768]{0,1:T(8,128)(2,1)}, bf16[1024,768]{0,1:T(8,128)(2,1)S(1)}, u32[]{:S(2)}, u32[]{:S(2)}) collective-permute-start(bf16[1024,768]{0,1:T(8,128)(2,1)} %get-tuple-element.1540), channel_id=1, source_target_pairs={{0,16},{1,17},{2,18},{3,19},{4,20},{5,21},{6,22},{7,23},{8,24},{9,... | collective-permute-start | bytes 4718600 | tf_op jit(solution)/shard_map/while/body/eval_jaxpr/ppermute | solution.py:22
  808.1 409.0 %collective-permute-start.1 = (bf16[1024,768]{1,0:T(8,128)(2,1)}, bf16[1024,768]{1,0:T(8,128)(2,1)S(1)}, u32[]{:S(2)}, u32[]{:S(2)}) collective-permute-start(bf16[1024,768]{1,0:T(8,128)(2,1)} %get-tuple-element.1576), channel_id=1, source_target_pairs={{16,0},{17,1},{18,2},{19,3},{20,4},{21,5},{22,6},{23,7},{24,8},{25... | collective-permute-start | bytes 4718600 | tf_op jit(solution)/shard_map/while/body/eval_jaxpr/ppermute | solution.py:22
  1231.5 75.1 %copy-start.40 = (f32[1024]{0:T(1024)}, f32[1024]{0:T(1024)S(1)}, u32[]{:S(2)}) copy-start(f32[1024]{0:T(1024)S(1)} %broadcast_multiply_fusion.2) | copy-start | bytes 12292 | tf_op jit(solution)/shard_map/while/body/eval_jaxpr/cond
  1233.6 73.1 %copy-start.51 = (f32[768]{0:T(1024)}, f32[768]{0:T(1024)S(1)}, u32[]{:S(2)}) copy-start(f32[768]{0:T(1024)S(1)} %get-tuple-element.1066) | copy-start | bytes 9220 | tf_op jit(solution)/shard_map/while/body/eval_jaxpr/cond
  1234.5 72.2 %copy-start.47 = (f32[1024]{0:T(1024)}, f32[1024]{0:T(1024)S(1)}, u32[]{:S(2)}) copy-start(f32[1024]{0:T(1024)S(1)} %fusion.189) | copy-start | bytes 12292 | tf_op jit(solution)/shard_map/while/body/eval_jaxpr/cond
  1250.1 46.0 %slice-start.15 = ((s8[6291456]{0:T(1024)(128)(4,1)}), s8[4194304]{0:T(1024)(128)(4,1)S(1)}, s32[]{:S(2)}) async-start(s8[6291456]{0:T(1024)(128)(4,1)} %bitcast.407), calls=%async_computation.18 | async-start | bytes 8388608 | tf_op jit(solution)/shard_map/while/body/eval_jaxpr/cond
  1343.3 59.2 %slice-start.8 = ((s8[4718592]{0:T(1024)(128)(4,1)}), s8[524288]{0:T(1024)(128)(4,1)S(1)}, s32[]{:S(2)}) async-start(s8[4718592]{0:T(1024)(128)(4,1)} %bitcast.394), calls=%async_computation.11 | async-start | bytes 1048576 | tf_op jit(solution)/shard_map/while/body/eval_jaxpr/cond
  1599.1 35.8 %collective-permute-start.1 = (bf16[1024,768]{1,0:T(8,128)(2,1)}, bf16[1024,768]{1,0:T(8,128)(2,1)S(1)}, u32[]{:S(2)}, u32[]{:S(2)}) collective-permute-start(bf16[1024,768]{1,0:T(8,128)(2,1)} %get-tuple-element.1576), channel_id=1, source_target_pairs={{16,0},{17,1},{18,2},{19,3},{20,4},{21,5},{22,6},{23,7},{24,8},{25... | collective-permute-start | bytes 4718600 | tf_op jit(solution)/shard_map/while/body/eval_jaxpr/ppermute | solution.py:22
  1649.6 75.1 %copy-start.40 = (f32[1024]{0:T(1024)}, f32[1024]{0:T(1024)S(1)}, u32[]{:S(2)}) copy-start(f32[1024]{0:T(1024)S(1)} %broadcast_multiply_fusion.2) | copy-start | bytes 12292 | tf_op jit(solution)/shard_map/while/body/eval_jaxpr/cond
  1651.6 73.1 %copy-start.51 = (f32[768]{0:T(1024)}, f32[768]{0:T(1024)S(1)}, u32[]{:S(2)}) copy-start(f32[768]{0:T(1024)S(1)} %get-tuple-element.1066) | copy-start | bytes 9220 | tf_op jit(solution)/shard_map/while/body/eval_jaxpr/cond
  1652.5 72.2 %copy-start.47 = (f32[1024]{0:T(1024)}, f32[1024]{0:T(1024)S(1)}, u32[]{:S(2)}) copy-start(f32[1024]{0:T(1024)S(1)} %fusion.189) | copy-start | bytes 12292 | tf_op jit(solution)/shard_map/while/body/eval_jaxpr/cond
  1668.1 46.0 %slice-start.15 = ((s8[6291456]{0:T(1024)(128)(4,1)}), s8[4194304]{0:T(1024)(128)(4,1)S(1)}, s32[]{:S(2)}) async-start(s8[6291456]{0:T(1024)(128)(4,1)} %bitcast.407), calls=%async_computation.18 | async-start | bytes 8388608 | tf_op jit(solution)/shard_map/while/body/eval_jaxpr/cond
  1761.4 59.2 %slice-start.8 = ((s8[4718592]{0:T(1024)(128)(4,1)}), s8[524288]{0:T(1024)(128)(4,1)S(1)}, s32[]{:S(2)}) async-start(s8[4718592]{0:T(1024)(128)(4,1)} %bitcast.394), calls=%async_computation.11 | async-start | bytes 1048576 | tf_op jit(solution)/shard_map/while/body/eval_jaxpr/cond
  2017.2 34.9 %collective-permute-start.1 = (bf16[1024,768]{1,0:T(8,128)(2,1)}, bf16[1024,768]{1,0:T(8,128)(2,1)S(1)}, u32[]{:S(2)}, u32[]{:S(2)}) collective-permute-start(bf16[1024,768]{1,0:T(8,128)(2,1)} %get-tuple-element.1576), channel_id=1, source_target_pairs={{16,0},{17,1},{18,2},{19,3},{20,4},{21,5},{22,6},{23,7},{24,8},{25... | collective-permute-start | bytes 4718600 | tf_op jit(solution)/shard_map/while/body/eval_jaxpr/ppermute | solution.py:22
  2057.4 273.5 %copy-start.27 = (bf16[2,1024,768]{1,2,0:T(8,128)(2,1)S(1)}, bf16[2,1024,768]{1,2,0:T(8,128)(2,1)}, u32[]{:S(2)}) copy-start(bf16[2,1024,768]{1,2,0:T(8,128)(2,1)} %get-tuple-element.866) | copy-start | bytes 9437188
  2057.4 384.7 %all-gather.2.cloned.1.call-start = ((), (), s32[]{:S(2)}) async-start(), calls=%async_computation.2 | async-start | bytes 15249408 | tf_op jit(solution)/shard_map/all_gather | solution.py:508
  (150 other events, 1345.0 us)
Sparse Core Ops, SparseCore 0:
  2057.5 270.8 reduce-scatter.1
  2331.1 110.9 all-gather.1
where the time goes:
time: 2510 us; the launch traced here: 2500 us
  waiting for transfers between devices  953 us (38%)
  matrix products  762 us (30%)
  other arithmetic  324 us (13%)
  local copies, waits for them, and re-layouts  205 us (8%)
  starting transfers between devices  201 us (8%)
  loops' own time  39.7 us (2%)
    ppermute x6, waiting for transfers between devices, passed_along(): return lax.ppermute(shard, axis, pairs)  578 us
    reduce_scatter x1, waiting for transfers between devices, on_device(): grad_part = lax.psum_scatter(totals, 'dp', scatter_dimension=0, tiled=True)  271 us
    ppermute x6, starting transfers between devices, passed_along(): return lax.ppermute(shard, axis, pairs)  201 us
    dot_general x8, matrix products, block_scores(): jnp.einsum('qc,hkc->hqk', side_block, key_side, preferred_element_type=jn...  166 us
    all_gather x1, waiting for transfers between devices, on_device(): lax.all_gather(grad_part.astype(jnp.bfloat16), 'dp', axis=0, tiled=True)  105 us
    convert_element_type x4, other arithmetic, attend_back(): grad_scores = (prob_block * (grad_probs - row_inner)).astype(jnp.bfloat16)  85.6 us
    dot_general x8, matrix products, block_scores(): jnp.einsum('qhd,khd->hqk', query_block, key_heads, preferred_element_type...  83.8 us
    dot_general x2, matrix products, layer_forward(): lax.dot_general(gelu_low, contract_weight, contract_last, preferred_eleme...  68.3 us
  transfers between devices with their start and end apart: 8, of which 8 were waited for; matrix products, arithmetic and copies ran while one was open for 0% of the time, Pallas kernels for 0%

commit v1 on v0

v1 whole, which is shorter than its diff:
```python
import functools
import math

import jax
import jax.numpy as jnp
from jax import lax
from jax.experimental import pallas as pl
from jax.experimental.pallas import tpu as pltpu
from jax.sharding import PartitionSpec as P

GRID = 16
SPAN = 32
KEY_BLOCK = 256
ROW_BLOCK = 256
FF_BLOCK = 768
HALF = 64
PAIR = 128

epsilon = 1e-05
masked = -1e30
score_scale = 0.125
VMEM_LIMIT = 58 * 1024 * 1024

f32 = jnp.float32
bf16 = jnp.bfloat16

dot_nn = lambda a, b: lax.dot_general(a, b, (((1,), (0,)), ((), ())), preferred_element_type=f32)
dot_nt = lambda a, b: lax.dot_general(a, b, (((1,), (1,)), ((), ())), preferred_element_type=f32)
dot_tn = lambda a, b: lax.dot_general(a, b, (((0,), (0,)), ((), ())), preferred_element_type=f32)


def params_for(axes):
    return pltpu.CompilerParams(
        dimension_semantics=("arbitrary",) * axes, vmem_limit_bytes=VMEM_LIMIT
    )


ANY = pl.BlockSpec(memory_space=pl.ANY)


def like(a):
    return jax.ShapeDtypeStruct(a.shape, a.dtype)


def fixed(shape):
    return pl.BlockSpec(shape, lambda i, sp: (0,) * len(shape), pipeline_mode=pl.Buffered(1))


def stacked(rows, cols):
    return pl.BlockSpec((1, rows, cols), lambda i, sp: (sp[0], i, 0))


def plain(rows, cols):
    return pl.BlockSpec((rows, cols), lambda i, sp: (i, 0))


def call(body, sp, grid, ins, outs, aliased, scratch=(), us=10):
    operands = [a for a, _ in ins] + [a for a, _ in aliased]
    in_specs = [s for _, s in ins] + [ANY] * len(aliased)
    out_shape = [like(a) for a, _ in aliased] + [s for s, _ in outs]
    out_specs = [s for _, s in aliased] + [s for _, s in outs]
    kept = len(aliased)
    first = len(ins)

    def run(sp_ref, *refs):
        body(sp_ref, *refs[:first], *refs[first + kept :])

    return pl.pallas_call(
        run,
        grid_spec=pltpu.PrefetchScalarGridSpec(
            num_scalar_prefetch=1,
            grid=grid,
            in_specs=in_specs,
            out_specs=out_specs,
            scratch_shapes=list(scratch),
        ),
        out_shape=out_shape,
        input_output_aliases={1 + first + j: j for j in range(kept)},
        compiler_params=params_for(len(grid)),
        cost_estimate=pl.CostEstimate(
            flops=us * 1_000_000_000, bytes_accessed=us * 1_000_000, transcendentals=0
        ),
    )(sp, *operands)


def unwritten(shapes):
    return pl.pallas_call(
        lambda *refs: None, out_shape=shapes, out_specs=[ANY] * len(shapes)
    )()


def qkv_body(sp, x_ref, w_ref, b_ref, q_ref, kv_ref, fresh_ref):
    width = x_ref.shape[2]
    x = x_ref[0]
    q = dot_nn(x, w_ref[:, :width]) + b_ref[:, :width]
    q_ref[0] = (q.astype(bf16) * score_scale).astype(bf16)
    kv = (dot_nn(x, w_ref[:, width:]) + b_ref[:, width:]).astype(bf16)
    for begin in range(0, width, PAIR):
        for part, at in ((kv[:, begin : begin + PAIR], 0), (kv[:, width + begin : width + begin + PAIR], PAIR)):
            cols = slice(2 * begin + at, 2 * begin + at + PAIR)
            kv_ref[0, :, cols] = part
            fresh_ref[:, cols] = part


def qkv_call(sp, x_all, weight, bias, q_all, kv_all):
    rows, width = x_all.shape[1], x_all.shape[2]
    return call(
        qkv_body,
        sp,
        (rows // ROW_BLOCK,),
        [
            (x_all, stacked(ROW_BLOCK, width)),
            (weight, fixed(weight.shape)),
            (bias, fixed(bias.shape)),
        ],
        [(jax.ShapeDtypeStruct((rows, 2 * width), bf16), plain(ROW_BLOCK, 2 * width))],
        [(q_all, stacked(ROW_BLOCK, width)), (kv_all, stacked(ROW_BLOCK, 2 * width))],
        us=5,
    )


def low_half(shape):
    return lax.broadcasted_iota(jnp.int32, shape, 1) < HALF


def split_three(value, lane):
    high = value.astype(bf16).astype(f32)
    rest = value - high
    mid = rest.astype(bf16).astype(f32)
    last = rest - mid
    place = lane % HALF
    out = jnp.where(place == 0, high, jnp.where(place == 1, mid, jnp.where(place == 2, last, 0.0)))
    return out.astype(bf16)


def key_side(hot_ref, m_ref, begin, rows, length):
    ks = dot_nn(hot_ref[0, pl.ds(begin, rows), :], m_ref[...])
    lane = lax.broadcasted_iota(jnp.int32, ks.shape, 1)
    slot = lax.broadcasted_iota(jnp.int32, ks.shape, 0) + begin
    position_cells = 2 * rows // SPAN
    dead = (slot >= length) & (lane % HALF < position_cells)
    return jnp.where(dead, masked, ks).astype(bf16)


def attend_body(
    sp, q_ref, own_ref, peer_ref, hot_ref, m_ref, a_ref, rest_ref, lse_ref, kept_ref, kc, vc,
):
    rows = q_ref.shape[1]
    own = pl.multiple_of(sp[2] * rows, rows)
    peer = pl.multiple_of(rows - sp[2] * rows, rows)
    low = low_half((rows, PAIR))
    one = jnp.ones((rows, PAIR), bf16)
    for begin, kv_ref in ((own, own_ref), (peer, peer_ref)):
        k = kv_ref[:, :PAIR]
        v = kv_ref[:, PAIR:]
        ks = key_side(hot_ref, m_ref, begin, rows, sp[3])
        kc[0, pl.ds(begin, rows), :] = jnp.where(low, k, ks)
        kc[1, pl.ds(begin, rows), :] = jnp.where(low, ks, k)
        vc[0, pl.ds(begin, rows), :] = jnp.where(low, v, one)
        vc[1, pl.ds(begin, rows), :] = jnp.where(low, one, v)
    kept_ref[0] = peer_ref[...]

    def variant(keys):
        block_low = low_half((ROW_BLOCK, PAIR))
        lane = lax.broadcasted_iota(jnp.int32, (ROW_BLOCK, PAIR), 1)
        for r in range(0, rows, ROW_BLOCK):
            q = q_ref[0, r : r + ROW_BLOCK, :]
            side = hot_ref[0, pl.ds(own + r, ROW_BLOCK), :]
            outs = []
            peaks = []
            for head in (0, 1):
                cat = jnp.where(block_low, q, side) if head == 0 else jnp.where(block_low, side, q)
                s = dot_nt(cat, kc[head, :keys, :])
                peak = jnp.max(s, axis=1, keepdims=True)
                e = jnp.exp(s - peak).astype(bf16)
                outs.append(dot_nn(e, vc[head, :keys, :]))
                peaks.append(peak)
            top = jnp.where(block_low, outs[0], outs[1])
            total = pltpu.roll(jnp.where(block_low, outs[1], outs[0]), HALF, 1)
            mixed = top / total
            mixed_low = mixed.astype(bf16)
            a_ref[0, r : r + ROW_BLOCK, :] = mixed_low
            rest_ref[0, r : r + ROW_BLOCK, :] = (mixed - mixed_low.astype(f32)).astype(bf16)
            lse = jnp.where(block_low, peaks[0], peaks[1]) + jnp.log(total)
            lse_ref[0, r : r + ROW_BLOCK, :] = split_three(-lse, lane)

    for blocks in range(1, 2 * rows // KEY_BLOCK + 1):
        pl.when(sp[1] == blocks)(functools.partial(variant, blocks * KEY_BLOCK))


def attend_call(sp, q_all, kv_own, kv_peer, hot2_all, matrix, bufs):
    rows, width = q_all.shape[1], q_all.shape[2]
    pairs = width // PAIR
    by_pair = pl.BlockSpec((1, rows, PAIR), lambda p, sp: (sp[0], 0, p))
    kv_spec = pl.BlockSpec((rows, 2 * PAIR), lambda p, sp: (0, p))
    kept_spec = pl.BlockSpec((1, rows, 2 * PAIR), lambda p, sp: (sp[0], 0, p))
    return call(
        attend_body,
        sp,
        (pairs,),
        [
            (q_all, by_pair),
            (kv_own, kv_spec),
            (kv_peer, kv_spec),
            (hot2_all, pl.BlockSpec((1, 2 * rows, PAIR), lambda p, sp: (sp[0], 0, 0))),
            (matrix, pl.BlockSpec((PAIR, PAIR), lambda p, sp: (0, p))),
        ],
        [],
        [(b, by_pair) for b in bufs[:-1]] + [(bufs[-1], kept_spec)],
        [pltpu.VMEM((2, 2 * rows, PAIR), bf16), pltpu.VMEM((2, 2 * rows, PAIR), bf16)],
        us=17,
    )


def gelu_both(x):
    mag = jnp.abs(x)
    t = 1.0 / (1.0 + (0.3275911 / math.sqrt(2.0)) * mag)
    bell = jnp.exp(x * x * -0.5)
    poly = t * (
        0.5 * 0.254829592
        + t * (
            0.5 * -0.284496736
            + t * (0.5 * 1.421413741 + t * (0.5 * -1.453152027 + t * (0.5 * 1.061405429)))
        )
    )
    tail = poly * bell
    cdf = jnp.where(x >= 0.0, 1.0 - tail, tail)
    return x * cdf, cdf + x * bell * (1.0 / math.sqrt(2.0 * math.pi))


def centered(u):
    c = u - jnp.mean(u, axis=1, keepdims=True)
    r = lax.rsqrt(jnp.mean(c * c, axis=1, keepdims=True) + epsilon)
    return c * r, r


def dense_body(
    sp, a_ref, x_ref, wo_ref, w1_ref, w2_ref, gain_ref, bias_ref, eb_ref,
    n1_ref, h1_ref, g_ref, d_ref, n2_ref, r_ref, y_ref, fresh_ref,
):
    u1 = dot_nn(a_ref[0], wo_ref[...]) + bias_ref[2:3, :] + x_ref[0].astype(f32)
    n1, r1 = centered(u1)
    h1 = n1 * gain_ref[0:1, :] + bias_ref[3:4, :]
    h1_low = h1.astype(bf16)
    n1_ref[0] = n1.astype(bf16)
    h1_ref[0] = h1_low
    u2 = h1 + bias_ref[4:5, :]
    for c in range(0, w1_ref.shape[1], FF_BLOCK):
        f = dot_nn(h1_low, w1_ref[:, c : c + FF_BLOCK]) + eb_ref[:, c : c + FF_BLOCK]
        g, d = gelu_both(f)
        g = g.astype(bf16)
        g_ref[0, :, c : c + FF_BLOCK] = g
        d_ref[0, :, c : c + FF_BLOCK] = d.astype(bf16)
        u2 = u2 + dot_nt(g, w2_ref[:, c : c + FF_BLOCK])
    n2, r2 = centered(u2)
    n2_ref[0] = n2.astype(bf16)
    y = (n2 * gain_ref[1:2, :] + bias_ref[5:6, :]).astype(bf16)
    y_ref[0] = y
    fresh_ref[...] = y
    r_ref[0] = jnp.where(low_half(r_ref.shape[1:]), r1, r2)


def dense_call(sp, a_all, x_all, wo, w1, w2, gains, biases, eb, bufs):
    rows, width = a_all.shape[1], a_all.shape[2]
    hidden = w1.shape[1]
    row = stacked(ROW_BLOCK, width)
    wide = stacked(ROW_BLOCK, hidden)
    n1_all, h1_all, g_all, d_all, n2_all, r_all, y_all = bufs
    return call(
        dense_body,
        sp,
        (rows // ROW_BLOCK,),
        [(a_all, row), (x_all, row)]
        + [(w, fixed(w.shape)) for w in (wo, w1, w2, gains, biases, eb)],
        [(jax.ShapeDtypeStruct((rows, width), bf16), plain(ROW_BLOCK, width))],
        [
            (n1_all, row), (h1_all, row), (g_all, wide), (d_all, wide), (n2_all, row),
            (r_all, stacked(ROW_BLOCK, PAIR)), (y_all, row),
        ],
        us=16,
    )


def column_sum(v):
    return jnp.sum(v, axis=0, keepdims=True)


def norm_back(dy, n, r, gain):
    dn = dy * gain
    return r * (dn - jnp.mean(dn, axis=1, keepdims=True) - n * jnp.mean(dn * n, axis=1, keepdims=True))


def dense_back_body(
    sp, dy_ref, n2_ref, r_ref, d_ref, n1_ref, a_ref, rest_ref, wo_ref, w1_ref, w2_ref, gain_ref, sel_ref,
    db2_ref, df_ref, db1_ref, st_ref, se_ref, do_ref, dd_ref,
):
    width = dy_ref.shape[2]
    dy = dy_ref[0].astype(f32)
    n2 = n2_ref[0].astype(f32)
    r = r_ref[0]
    r1, r2 = r[:, 0:1], r[:, HALF : HALF + 1]
    du2 = norm_back(dy, n2, r2, gain_ref[1:2, :])
    db2 = du2.astype(bf16)
    db2_ref[0] = db2
    dh1 = du2
    sums = []
    for c in range(0, w1_ref.shape[1], FF_BLOCK):
        df = dot_nn(db2, w2_ref[:, c : c + FF_BLOCK]) * d_ref[0, :, c : c + FF_BLOCK].astype(f32)
        sums.append(column_sum(df))
        df = df.astype(bf16)
        df_ref[0, :, c : c + FF_BLOCK] = df
        dh1 = dh1 + dot_nt(df, w1_ref[:, c : c + FF_BLOCK])
    n1 = n1_ref[0].astype(f32)
    du1 = norm_back(dh1, n1, r1, gain_ref[0:1, :])
    db1 = du1.astype(bf16)
    db1_ref[0] = db1
    do = dot_nt(db1, wo_ref[...]).astype(bf16)
    do_ref[...] = do
    mixed = do.astype(f32) * (a_ref[0].astype(f32) + rest_ref[0].astype(f32))
    mixed_low = mixed.astype(bf16)
    inner = dot_nn(mixed_low, sel_ref[...])
    inner = inner + dot_nn((mixed - mixed_low.astype(f32)).astype(bf16), sel_ref[...])
    lane = lax.broadcasted_iota(jnp.int32, inner.shape, 1)
    dd_ref[...] = split_three(-inner, lane)
    rows = [
        column_sum(du1), column_sum(dh1), column_sum(du2), column_sum(dy),
        column_sum(dh1 * n1), column_sum(dy * n2), jnp.zeros((2, width), f32),
    ]
    stats = jnp.concatenate(rows, axis=0)
    wide = jnp.concatenate(sums, axis=1)

    @pl.when(pl.program_id(0) == 0)
    def _():
        st_ref[0] = stats
        se_ref[0] = wide

    @pl.when(pl.program_id(0) != 0)
    def _():
        st_ref[0] += stats
        se_ref[0] += wide


def dense_back_call(sp, dy_all, n2_all, r_all, d_all, n1_all, a_all, rest_all, wo, w1, w2, gains, sel, bufs):
    rows, width = dy_all.shape[1], dy_all.shape[2]
    hidden = w1.shape[1]
    row = stacked(ROW_BLOCK, width)
    wide = stacked(ROW_BLOCK, hidden)
    db2_all, df_all, db1_all, st_all, se_all = bufs
    once = lambda a: pl.BlockSpec((1,) + a.shape[1:], lambda i, sp: (sp[0], 0, 0))
    return call(
        dense_back_body,
        sp,
        (rows // ROW_BLOCK,),
        [
            (dy_all, row), (n2_all, row), (r_all, stacked(ROW_BLOCK, PAIR)), (d_all, wide),
            (n1_all, row), (a_all, row), (rest_all, row),
        ]
        + [(w, fixed(w.shape)) for w in (wo, w1, w2, gains, sel)],
        [(jax.ShapeDtypeStruct((rows, width), bf16), plain(ROW_BLOCK, width))] * 2,
        [(db2_all, row), (df_all, wide), (db1_all, row), (st_all, once(st_all)), (se_all, once(se_all))],
        us=16,
    )


def attend_back_body(
    sp, q_ref, own_ref, peer_ref, hot2_ref, m_ref, lse_ref, do_ref, dd_ref, hot_ref,
    cell_ref, dq_ref, keep_ref, send_ref, kc, kt, vc, qc, dc, dk, dv,
):
    rows = q_ref.shape[1]
    total = 2 * rows
    own = pl.multiple_of(sp[2] * rows, rows)
    peer = pl.multiple_of(rows - sp[2] * rows, rows)
    low = low_half((rows, PAIR))
    place = lax.broadcasted_iota(jnp.int32, (rows, PAIR), 1)
    first = place < 3
    second = (place >= HALF) & (place < HALF + 3)
    ones = jnp.where((place % HALF) < 3, 1.0, 0.0).astype(bf16)
    only_low = jnp.where(first, 1.0, 0.0).astype(bf16)
    only_high = jnp.where(second, 1.0, 0.0).astype(bf16)
    for begin, kv_ref in ((own, own_ref), (peer, peer_ref)):
        k = kv_ref[0, :, :PAIR]
        v = kv_ref[0, :, PAIR:]
        ks = key_side(hot2_ref, m_ref, begin, rows, sp[3])
        kc[0, pl.ds(begin, rows), :PAIR] = jnp.where(low, k, ks)
        kc[1, pl.ds(begin, rows), :PAIR] = jnp.where(low, ks, k)
        kc[0, pl.ds(begin, rows), PAIR:] = only_low
        kc[1, pl.ds(begin, rows), PAIR:] = only_high
        vc[0, pl.ds(begin, rows), :] = jnp.where(low, v, ones)
        vc[1, pl.ds(begin, rows), :] = jnp.where(low, ones, v)
        kt[:, pl.ds(begin, rows)] = k.T
    q = q_ref[0]
    side = hot2_ref[0, pl.ds(own, rows), :]
    do = do_ref[...]
    dd = dd_ref[...]
    qc[0, :, :PAIR] = jnp.where(low, q, side)
    qc[1, :, :PAIR] = jnp.where(low, side, q)
    qc[0, :, PAIR:] = lse_ref[0]
    qc[1, :, PAIR:] = lse_ref[0]
    dc[0] = jnp.where(low, do, dd)
    dc[1] = jnp.where(low, dd, do)

    def variant(blocks):
        block_low = low_half((KEY_BLOCK, PAIR))
        dq = [None, None]
        for b in range(blocks):
            at = slice(b * KEY_BLOCK, (b + 1) * KEY_BLOCK)
            dvs = []
            dks = []
            for head in (0, 1):
                p = jnp.exp(dot_nt(kc[head, at, :], qc[head]))
                dp = dot_nt(vc[head, at, :], dc[head])
                ds = (p * dp).astype(bf16)
                dvs.append(dot_nn(p.astype(bf16), do_ref[...]))
                dks.append(dot_nn(ds, qc[head, :, :PAIR]))
                part = dot_nn(kt[head * HALF : (head + 1) * HALF, at], ds)
                dq[head] = part if dq[head] is None else dq[head] + part
            dv[at, :] = jnp.where(block_low, dvs[0], dvs[1]).astype(bf16)
            dk[0, at, :] = jnp.where(block_low, dks[0], dks[1]).astype(bf16)
            dk[1, at, :] = jnp.where(block_low, dks[1], dks[0]).astype(bf16)
        left = slice(blocks * KEY_BLOCK, total)
        if blocks * KEY_BLOCK < total:
            zero = jnp.zeros((total - blocks * KEY_BLOCK, PAIR), bf16)
            dv[left, :] = zero
            dk[0, left, :] = zero
            dk[1, left, :] = zero
        both = jnp.concatenate(dq, axis=0)
        dq_ref[...] = (both.T * score_scale).astype(bf16)

    for blocks in range(1, total // KEY_BLOCK + 1):
        pl.when(sp[1] == blocks)(functools.partial(variant, blocks))
    cell_ref[0] = dot_nn(hot_ref[0], dk[1])
    for begin, out_ref in ((own, keep_ref), (peer, send_ref)):
        out_ref[:, :PAIR] = dk[0, pl.ds(begin, rows), :]
        out_ref[:, PAIR:] = dv[pl.ds(begin, rows), :]


def attend_back_call(
    sp, q_all, kv_all, peer_all, hot2_all, matrix, lse_all, do, dd, hot_all, cell_all
):
    rows, width = q_all.shape[1], q_all.shape[2]
    pairs = width // PAIR
    by_pair = pl.BlockSpec((1, rows, PAIR), lambda p, sp: (sp[0], 0, p))
    flat = pl.BlockSpec((rows, PAIR), lambda p, sp: (0, p))
    kv_spec = pl.BlockSpec((1, rows, 2 * PAIR), lambda p, sp: (sp[0], 0, p))
    flat_kv = pl.BlockSpec((rows, 2 * PAIR), lambda p, sp: (0, p))
    total = 2 * rows
    out_kv = jax.ShapeDtypeStruct((rows, 2 * width), bf16)
    out = jax.ShapeDtypeStruct((rows, width), bf16)
    return call(
        attend_back_body,
        sp,
        (pairs,),
        [
            (q_all, by_pair),
            (kv_all, kv_spec),
            (peer_all, kv_spec),
            (hot2_all, pl.BlockSpec((1, total, PAIR), lambda p, sp: (sp[0], 0, 0))),
            (matrix, pl.BlockSpec((PAIR, PAIR), lambda p, sp: (0, p))),
            (lse_all, by_pair),
            (do, flat),
            (dd, flat),
            (hot_all, pl.BlockSpec((1, HALF, total), lambda p, sp: (sp[0], 0, 0))),
        ],
        [(out, flat), (out_kv, flat_kv), (out_kv, flat_kv)],
        [(cell_all, pl.BlockSpec((1, HALF, PAIR), lambda p, sp: (sp[0], 0, p)))],
        [
            pltpu.VMEM((2, total, 2 * PAIR), bf16),
            pltpu.VMEM((PAIR, total), bf16),
            pltpu.VMEM((2, total, PAIR), bf16),
            pltpu.VMEM((2, rows, 2 * PAIR), bf16),
            pltpu.VMEM((2, rows, PAIR), bf16),
            pltpu.VMEM((2, total, PAIR), bf16),
            pltpu.VMEM((total, PAIR), bf16),
        ],
        us=25,
    )


def input_back_body(
    sp, dq_ref, own_ref, got_ref, db1_ref, w_ref, dj_ref, sj_ref, dx_ref, fresh_ref
):
    width = dq_ref.shape[1]
    dq = dq_ref[...]
    both = own_ref[...].astype(f32) + got_ref[...].astype(f32)
    part = lambda at: jnp.concatenate(
        [both[:, p + at : p + at + PAIR] for p in range(0, 2 * width, 2 * PAIR)], axis=1
    )
    dk = part(0).astype(bf16)
    dv32 = part(PAIR)
    dv = dv32.astype(bf16)
    dj_ref[0, :, :width] = dq
    dj_ref[0, :, width : 2 * width] = dk
    dj_ref[0, :, 2 * width :] = dv
    dx = db1_ref[0].astype(f32)
    dx = dx + dot_nt(dq, w_ref[:, :width])
    dx = dx + dot_nt(dk, w_ref[:, width : 2 * width])
    dx = dx + dot_nt(dv, w_ref[:, 2 * width :])
    dx = dx.astype(bf16)
    dx_ref[0] = dx
    fresh_ref[...] = dx
    stats = jnp.concatenate(
        [column_sum(dq.astype(f32)), column_sum(dv32), jnp.zeros((6, width), f32)], axis=0
    )

    @pl.when(pl.program_id(0) == 0)
    def _():
        sj_ref[0] = stats

    @pl.when(pl.program_id(0) != 0)
    def _():
        sj_ref[0] += stats


def input_back_call(sp, dq, own, got, db1_all, weight, dj_all, sj_all, dx_all):
    rows, width = dq.shape
    row = stacked(ROW_BLOCK, width)
    flat = plain(ROW_BLOCK, width)
    flat_kv = plain(ROW_BLOCK, 2 * width)
    return call(
        input_back_body,
        sp,
        (rows // ROW_BLOCK,),
        [(dq, flat), (own, flat_kv), (got, flat_kv), (db1_all, row), (weight, fixed(weight.shape))],
        [(jax.ShapeDtypeStruct((rows, width), bf16), flat)],
        [
            (dj_all, stacked(ROW_BLOCK, 3 * width)),
            (sj_all, pl.BlockSpec((1,) + sj_all.shape[1:], lambda i, sp: (sp[0], 0, 0))),
            (dx_all, row),
        ],
        us=6,
    )


def bucket_maps(position_cells, counts):
    key = jnp.arange(HALF, dtype=jnp.int32)[:, None]
    query = jnp.arange(HALF, dtype=jnp.int32)[None, :]
    begins = (0, position_cells, position_cells + GRID, HALF)
    bucket = jnp.full((HALF, HALF), -1, jnp.int32)
    base = 0
    for j, offset in enumerate((counts[0] // 2, GRID - 1, GRID - 1)):
        inside = (key >= begins[j]) & (key < begins[j + 1]) & (query >= begins[j]) & (query < begins[j + 1])
        ids = jnp.clip(query - key, -offset, counts[j] - 1 - offset) + offset + base
        bucket = jnp.where(inside, ids, bucket)
        base += counts[j]
    return bucket[:, :, None] == jnp.arange(base, dtype=jnp.int32)


def cell_matrix(tables, maps):
    whole = jnp.concatenate(tables, axis=0)
    heads = whole.shape[1]
    whole = whole.reshape(-1, heads // 2, 2)[:, :, ::-1].reshape(-1, heads)
    m = jnp.einsum("bh,xcb->xhc", whole, maps.astype(bf16), preferred_element_type=f32)
    m = m.reshape(HALF, heads * HALF).astype(bf16)
    return jnp.concatenate([m, jnp.zeros_like(m)], axis=0)


def table_grads(cells, maps, counts):
    heads = cells.shape[1] // HALF
    whole = jnp.einsum(
        "xcb,xhc->bh", maps.astype(f32), cells.reshape(HALF, heads, HALF), precision=lax.Precision.HIGHEST
    )
    whole = whole.reshape(-1, heads // 2, 2)[:, :, ::-1].reshape(-1, heads)
    a, b = counts[0], counts[0] + counts[1]
    return [whole[:a], whole[a:b], whole[b:]]


class Ring:
    def __init__(self, count):
        self.count = count
        self.index = lax.axis_index("dp")
        bits = list(range(1, count.bit_length() - 1))
        turned = bits[:2][::-1] + bits[2:]
        self.steps = list(zip(bits, turned))

    def bit(self, step):
        even, odd = step
        return jnp.where(self.index % 2 == 0, (self.index >> even) & 1, (self.index >> odd) & 1)

    def send(self, a, step):
        even, odd = step
        pairs = [(i, i ^ (1 << (even if i % 2 == 0 else odd))) for i in range(self.count)]
        return lax.ppermute(a, "dp", pairs)

    def swap(self, a):
        return lax.ppermute(a, "dp", [(i, i ^ 1) for i in range(self.count)])

    def reduce(self, part):
        for step in self.steps:
            half = part.shape[0] // 2
            bit = self.bit(step)
            keep = lax.dynamic_slice_in_dim(part, bit * half, half, 0)
            give = lax.dynamic_slice_in_dim(part, (1 - bit) * half, half, 0)
            part = keep + self.send(give, step)
        return part

    def gather(self, part):
        for step in self.steps[::-1]:
            first = self.bit(step) == 0
            got = self.send(part, step)
            part = jnp.concatenate(
                [jnp.where(first, part, got), jnp.where(first, got, part)], axis=0
            )
        return part

    def whole(self, part):
        got = self.swap(part).astype(f32)
        part = part.astype(f32)
        first = self.index % 2 == 0
        return jnp.concatenate([jnp.where(first, part, got), jnp.where(first, got, part)], axis=0)

    def total(self, part):
        for bit in range(self.count.bit_length() - 1):
            part = part + lax.ppermute(part, "dp", [(i, i ^ (1 << bit)) for i in range(self.count)])
        return part


SLOTS = (
    (("F", 0), None),
    (("F", 1), ("F", 0)),
    (("F", 2), ("B", 0)),
    (("F", 3), ("F", 1)),
    (("B", 0), ("B", 1)),
    (None, ("F", 2)),
    (("B", 1), ("B", 2)),
    (None, ("F", 3)),
    (("B", 2), ("B", 3)),
    (("B", 3), None),
)


def on_device(
    boundary, doc_lengths, horizontal, vertical, attention_in, attention_out, expand_weight,
    contract_weight, norm_gains, bias_rows, expand_bias, position_table, horizontal_table,
    vertical_table,
):
    section = lax.axis_index("section")
    dp_count = lax.axis_size("dp")
    core = lax.axis_index("dp") % 2
    swap = [(i, i ^ 1) for i in range(dp_count)]
    exchange = lambda a: lax.ppermute(a, "dp", swap)

    own = boundary[0]
    micro, slots, width = own.shape
    rows = slots // 2
    windows = 2 * micro
    hidden = expand_weight.shape[2]
    heads = position_table.shape[2]
    pairs = heads // 2
    w_in, w_out, w1, w2 = attention_in[0], attention_out[0], expand_weight[0], contract_weight[0]
    gains = norm_gains[0].astype(f32)
    biases = bias_rows[0].astype(f32)
    eb = expand_bias.astype(f32)
    in_bias = jnp.concatenate([biases[0], jnp.zeros_like(biases[0]), biases[1]])[None]
    tables = (position_table[0], horizontal_table[0], vertical_table[0])
    counts = tuple(t.shape[0] for t in tables)
    position_cells = slots // SPAN
    maps = bucket_maps(position_cells, counts)
    ring = Ring(dp_count)

    def both(mine, theirs):
        return jnp.concatenate(
            [jnp.where(core == 0, mine, theirs), jnp.where(core == 0, theirs, mine)], axis=0
        )

    halves = own.reshape(micro, 2, rows, width)
    own_half = jnp.where(core == 0, halves[:, 0], halves[:, 1])
    other_half = jnp.where(core == 0, halves[:, 1], halves[:, 0])
    own_all = both(own_half, exchange(other_half))
    places = jnp.concatenate(
        [horizontal, vertical, jnp.broadcast_to(doc_lengths[:, None], (micro, PAIR))], axis=1
    )
    places = both(places, exchange(places))
    across_cell = places[:, :slots] // SPAN
    down_cell = places[:, slots : 2 * slots] // SPAN
    lengths = places[:, 2 * slots]
    ids = jnp.arange(slots, dtype=jnp.int32)
    cell_ids = jnp.arange(HALF, dtype=jnp.int32)
    position_cell = jnp.broadcast_to((ids // SPAN)[None], (windows, slots))

    def hot_of(cells, axis):
        p, a, d = (jnp.expand_dims(c, axis) for c in cells)
        lanes = cell_ids[None, :, None] if axis == 1 else cell_ids[None, None, :]
        return (
            (lanes == p) | (lanes == a + position_cells) | (lanes == d + position_cells + GRID)
        ).astype(bf16)

    cells = (position_cell, across_cell, down_cell)
    hot_all = hot_of(cells, 1)
    hot2_all = hot_of(cells, 2)
    hot2_all = jnp.concatenate([hot2_all, hot2_all], axis=2)
    matrix = cell_matrix(tables, maps)

    lane_ids = jnp.arange(width, dtype=jnp.int32)
    sel = (lane_ids[:, None] // HALF == (lane_ids[None, :] // HALF) ^ 1).astype(bf16)

    blocks_of = (lengths + KEY_BLOCK - 1) // KEY_BLOCK
    infos = []
    for zero, one in SLOTS:
        w = jnp.where(section == 0, zero[1] if zero else 0, one[1] if one else 0).astype(jnp.int32)
        infos.append(jnp.stack([w, blocks_of[w], core.astype(jnp.int32), lengths[w]]))

    widths = dict(
        q=width, kv=2 * width, a=width, rest=width, lse=width, peer=2 * width, n1=width, h1=width,
        g=hidden, d=hidden, n2=width, y=width, db2=width, df=hidden, db1=width, dj=3 * width, dx=width,
    )
    shapes = {n: jax.ShapeDtypeStruct((windows, rows, c), bf16) for n, c in widths.items()}
    shapes["r"] = jax.ShapeDtypeStruct((windows, rows, PAIR), f32)
    shapes["st"] = shapes["sj"] = jax.ShapeDtypeStruct((windows, 8, width), f32)
    shapes["se"] = jax.ShapeDtypeStruct((windows, 1, hidden), f32)
    shapes["cell"] = jax.ShapeDtypeStruct((windows, HALF, width), f32)
    st = dict(zip(shapes, unwritten(list(shapes.values()))))
    st.update(x=own_all, dy=own_all)

    def forward_pre(sp, s):
        q, kv, fresh = qkv_call(sp, s["x"], w_in, in_bias, s["q"], s["kv"])
        return dict(s, q=q, kv=kv), fresh

    def forward_post(sp, s, kv_own, kv_peer):
        mixed = ("a", "rest", "lse", "peer")
        s = dict(s)
        s.update(
            zip(mixed, attend_call(
                sp, s["q"], kv_own, kv_peer, hot2_all, matrix, tuple(s[n] for n in mixed)
            ))
        )
        names = ("n1", "h1", "g", "d", "n2", "r", "y")
        outs = dense_call(
            sp, s["a"], s["x"], w_out, w1, w2, gains, biases, eb, tuple(s[n] for n in names)
        )
        s.update(zip(names, outs[:-1]))
        return s, outs[-1]

    def dense_back(sp, s):
        names = ("db2", "df", "db1", "st", "se")
        outs = dense_back_call(
            sp, s["dy"], s["n2"], s["r"], s["d"], s["n1"], s["a"], s["rest"], w_out, w1, w2, gains, sel,
            tuple(s[n] for n in names),
        )
        s = dict(s)
        s.update(zip(names, outs[:5]))
        return s, tuple(outs[5:])

    def attend_back(sp, s, grads):
        cell, dq, keep, send = attend_back_call(
            sp, s["q"], s["kv"], s["peer"], hot2_all, matrix, s["lse"], *grads, hot_all, s["cell"]
        )
        return dict(s, cell=cell), (dq, keep), send

    def backward_pre(sp, s):
        s, grads = dense_back(sp, s)
        return attend_back(sp, s, grads)

    def backward_post(sp, s, own_parts, received):
        dj, sj, dx, fresh = input_back_call(
            sp, *own_parts, received, s["db1"], w_in, s["dj"], s["sj"], s["dx"]
        )
        return dict(s, dj=dj, sj=sj, dx=dx), fresh

    def put(name, s, sp, value, role):
        w = sp[0]
        old = lax.dynamic_index_in_dim(s[name], w, 0, keepdims=False)
        new = jnp.where(section == role, value, old)
        return dict(s, **{name: lax.dynamic_update_index_in_dim(s[name], new, w, 0)})

    blank_row = jnp.zeros((rows, width), bf16)
    blank_kv = jnp.zeros((rows, 2 * width), bf16)
    inbox = {}

    for number, (zero, one) in enumerate(SLOTS[:-1]):
        sp = infos[number]
        kinds = (zero[0] if zero else None, one[0] if one else None)
        if one and one[0] == "F":
            st = put("x", st, sp, inbox.pop(("F", one[1])), 1)
        if zero and zero[0] == "B":
            st = put("dy", st, sp, inbox.pop(("B", zero[1])), 0)
        if kinds == ("F", "F") or number == 0:
            st, fresh = forward_pre(sp, st)
            st, out = forward_post(sp, st, fresh, exchange(fresh))
        elif kinds == (None, "F"):
            active = section == 1
            st, fresh = lax.cond(
                active, lambda s: forward_pre(sp, s), lambda s: (s, blank_kv), st
            )
            peer = exchange(fresh)
            st, out = lax.cond(
                active, lambda s, a, b: forward_post(sp, s, a, b), lambda s, a, b: (s, blank_row),
                st, fresh, peer,
            )
        elif kinds == ("B", "B"):
            st, mine, send = backward_pre(sp, st)
            st, out = backward_post(sp, st, mine, exchange(send))
        else:

            def forward_start(s):
                s, fresh = forward_pre(sp, s)
                return s, (blank_row, blank_kv), fresh

            st, mine, send = lax.cond(
                section == 0, forward_start, lambda s: backward_pre(sp, s), st
            )
            send, inbox["F", 1] = lax.optimization_barrier((send, inbox["F", 1]))
            got = exchange(send)
            st, out = lax.cond(
                section == 0,
                lambda s, mine, send, got: forward_post(sp, s, send, got),
                lambda s, mine, send, got: backward_post(sp, s, mine, got),
                st, mine, send, got,
            )
        pairs = ([(0, 1)] if zero and zero[0] == "F" else []) + (
            [(1, 0)] if one and one[0] == "B" else []
        )
        if pairs:
            moved = lax.ppermute(out, "section", pairs)
            if (0, 1) in pairs:
                inbox[zero] = moved
            if (1, 0) in pairs:
                inbox[one] = moved

    def weight(a, b):
        left = st[a].reshape(windows * rows, st[a].shape[2])
        right = st[b].reshape(windows * rows, st[b].shape[2])
        half = left.shape[1] // 2
        part = lambda at: dot_tn(
            lax.dynamic_slice_in_dim(left, at * half, half, 1), right
        ).astype(bf16)
        return part(1 - core), part(core)

    def paired(give, keep):
        return keep + exchange(give)

    last = SLOTS[-1][0]
    sp = infos[-1]
    active = section == 0
    st = put("dy", st, sp, inbox.pop(last), 0)
    st, grads = lax.cond(
        active, lambda s: dense_back(sp, s), lambda s: (s, (blank_row,) * 2), st
    )
    sums_contract = ring.reduce(paired(*weight("db2", "g")))
    sums_expand = ring.reduce(paired(*weight("h1", "df")))
    st, mine, send = lax.cond(
        active, lambda s, g: attend_back(sp, s, g),
        lambda s, g: (s, (blank_row, blank_kv), blank_kv), st, grads,
    )
    got = exchange(send)
    st, out = lax.cond(
        active, lambda s, a, b: backward_post(sp, s, a, b), lambda s, a, b: (s, blank_row),
        st, mine, got,
    )
    (give_in, keep_in), (give_out, keep_out) = weight("x", "dj"), weight("a", "db1")
    beside = lambda a, b: jnp.concatenate([a, b], axis=1)
    sums_attend = ring.reduce(paired(beside(give_in, give_out), beside(keep_in, keep_out)))
    g_contract = ring.whole(ring.gather(sums_contract))
    g_expand = ring.whole(ring.gather(sums_expand))
    g_attend = ring.whole(ring.gather(sums_attend))
    g_in, g_out = g_attend[:, : 3 * width], g_attend[:, 3 * width :]

    sums = jnp.sum(st["st"], axis=0)
    joined_sums = jnp.sum(st["sj"], axis=0)
    wide = jnp.sum(st["se"], axis=0)
    small = [
        joined_sums[0:2], sums[0:6], wide,
    ] + table_grads(jnp.sum(st["cell"], axis=0), maps, counts)
    packed = jnp.concatenate([s.reshape(-1) for s in small])
    size = packed.shape[0]
    packed = jnp.pad(packed, (0, -size % 1024)).reshape(-1, PAIR)
    packed = ring.total(packed).reshape(-1)
    pieces = []
    begin = 0
    for s in small:
        count = math.prod(s.shape)
        pieces.append(packed[begin : begin + count].reshape(s.shape))
        begin += count
    joined_sums, sums, wide, table_p, table_h, table_v = pieces
    grad_bias = jnp.concatenate([joined_sums, sums[0:4]], axis=0)
    grad_gain = sums[4:6]

    result = jnp.where(section == 0, st["dx"], st["y"])
    mine_first, mine_second = result[:micro], result[micro:]
    keep = jnp.where(core == 0, mine_first, mine_second)
    give = exchange(jnp.where(core == 0, mine_second, mine_first))
    out_halves = jnp.stack(
        [jnp.where(core == 0, keep, give), jnp.where(core == 0, give, keep)], axis=1
    )
    boundary_out = out_halves.reshape(1, micro, slots, width)
    return (
        boundary_out, g_in[None], g_out[None], g_expand[None], g_contract[None], grad_gain[None], grad_bias[None], wide,
        table_p[None], table_h[None], table_v[None],
    )


def solution(mesh):
    section = P("section", None, None)
    placed = (
        P("section", "dp", None, None), P("dp"), P("dp", None), P("dp", None), section, section,
        section, section, section, section, P("section", None), section, section, section,
    )
    return jax.shard_map(
        on_device,
        mesh=mesh,
        in_specs=placed,
        out_specs=(
            P("section", "dp", None, None), section, section, section, section, section, section,
            P("section", None), section, section, section,
        ),
        check_vma=False,
    )
```

time: 2510 us -> 944 us (0.38)
  matrix products: 762 us -> 62.7 us
  waiting for transfers between devices: 953 us -> 283 us
  Pallas kernels: 0 us -> 369 us
  other arithmetic: 324 us -> 99.7 us
  local copies, waits for them, and re-layouts: 205 us -> 42.1 us
  starting transfers between devices: 201 us -> 68.4 us
  loops' own time: 39.7 us -> 2.14 us
    dot_general x100 -> x10, matrix products: 762 us -> 62.7 us  [the longest x8 59 us: lax.dot_general(a, b, (((0,), (0,)), ((), ())), preferred_element_type=f32)]
    pallas_call x0 -> x25, Pallas kernels: none -> 369 us  [the longest x24 369 us: call(): pl.pallas_call(run, grid_spec=pltpu.PrefetchScalarGridSpec(num_scalar_pre...]
    ppermute x6 -> x48, waiting for transfers between devices: 578 us -> 283 us  [the longest x18 156 us: send(): return lax.ppermute(a, 'dp', pairs)]
    reduce_scatter x1 -> x0, waiting for transfers between devices: 271 us -> none  [on_device(): grad_part = lax.psum_scatter(totals, 'dp', scatter_dimension=0, tiled=True)]
    ppermute x6 -> x48, starting transfers between devices: 201 us -> 68.4 us  [the longest x7 55.1 us: on_device(): moved = lax.ppermute(out, 'section', pairs)]
    all_gather x1 -> x0, waiting for transfers between devices: 105 us -> none  [on_device(): lax.all_gather(grad_part.astype(jnp.bfloat16), 'dp', axis=0, tiled=True)]
    convert_element_type x19 -> x5, other arithmetic: 108 us -> 3.85 us  [the longest x1 1.29 us: on_device(): (lane_ids[:, None] // HALF == lane_ids[None, :] // HALF ^ 1).astype(bf16)]
    reduce_sum x26 -> x4, other arithmetic: 66.5 us -> 1.94 us  [the longest x1 1.87 us: on_device(): jnp.sum(st['cell'], axis=0)]
  transfers between devices with their start and end apart: 8 -> 48, of which waited for: 8 -> 25; matrix products, arithmetic and copies ran while one was open for 0% -> 18% of each run, Pallas kernels for 0% -> 7%
where the time goes in v1:
time: 944 us; the launch traced here: 930 us
  Pallas kernels  369 us (39%)
  waiting for transfers between devices  283 us (30%)
  other arithmetic  99.7 us (11%)
  starting transfers between devices  68.4 us (7%)
  matrix products  62.7 us (7%)
  local copies, waits for them, and re-layouts  42.1 us (4%)
    pallas_call x24, Pallas kernels, call(): pl.pallas_call(run, grid_spec=pltpu.PrefetchScalarGridSpec(num_scalar_pre...  369 us
    ppermute x18, waiting for transfers between devices, send(): return lax.ppermute(a, 'dp', pairs)  156 us
    ppermute x7, waiting for transfers between devices, on_device(): moved = lax.ppermute(out, 'section', pairs)  109 us
    dot_general x8, matrix products, lax.dot_general(a, b, (((0,), (0,)), ((), ())), preferred_element_type=f32)  59 us
    ppermute x7, starting transfers between devices, on_device(): moved = lax.ppermute(out, 'section', pairs)  55.1 us
  transfers between devices with their start and end apart: 48, of which 25 were waited for; matrix products, arithmetic and copies ran while one was open for 18% of the time, Pallas kernels for 7%

profile of v1, /device:TPU:0, one launch (start us, length us, event | category | flops | bytes accessed | tf_op | source)
XLA Modules:
  0.0 930.0 jit_solution(16816716233079958140)
XLA Ops:
  31.8 17.4 %shard_map.223 = (bf16[4,512,768]{2,1,0:T(8,128)(2,1)}, bf16[4,512,768]{2,1,0:T(8,128)(2,1)}, bf16[4,512,768]{2,1,0:T(8,128)(2,1)}, bf16[4,512,1536]{2,1,0:T(8,128)(2,1)}) custom-call(s32[4]{0:T(128)} %pad_add_fusion.6.sp_ref, ...), custom_call_target="tpu_custom_call", output_to_operand_aliasing={{0}: (6, {}), {1}: (7, {}), {2}: (8, {}), {3}: (9, {})} | custom-call | flops 16999999488 | bytes 17000000 | tf_op jit(solution)/shard_map/pallas_call | solution.py:68
  49.2 18.0 %shard_map.224 = (bf16[4,512,768]{2,1,0:T(8,128)(2,1)}, bf16[4,512,768]{2,1,0:T(8,128)(2,1)}, bf16[4,512,3072]{2,1,0:T(8,128)(2,1)}, bf16[4,512,3072]{2,1,0:T(8,...) custom-call(s32[4]{0:T(128)} %pad_add_fusion.6.sp_ref, ...), custom_call_target="tpu_custom_call", output_to_operand_aliasing={{0}: (9, {}), {1}: (10, {}), {2}: (11, {}), {3}: (12, {}), ... | custom-call | flops 16000000000 | bytes 16000000 | tf_op jit(solution)/shard_map/pallas_call | solution.py:68
  78.3 12.0 %collective-permute-done.3 = bf16[512,768]{1,0:T(8,128)(2,1)} collective-permute-done((bf16[512,768]{1,0:T(8,128)(2,1)}, bf16[512,768]{1,0:T(8,128)(2,1)}, u32[]{:S(2)}, u32[]{:S(2)}) %collective-permute-start.3) | collective-permute-done | bytes 786464 | tf_op jit(solution)/shard_map/ppermute | solution.py:813
  103.7 14.7 %shard_map.226 = (bf16[4,512,768]{2,1,0:T(8,128)(2,1)}, bf16[4,512,768]{2,1,0:T(8,128)(2,1)}, bf16[4,512,768]{2,1,0:T(8,128)(2,1)}, bf16[4,512,1536]{2,1,0:T(8,128)(2,1)}) custom-call(s32[4]{0:T(128)} %pad_add_fusion.8.sp_ref, ...), custom_call_target="tpu_custom_call", output_to_operand_aliasing={{0}: (6, {}), {1}: (7, {}), {2}: (8, {}), {3}: (9, {})} | custom-call | flops 16999999488 | bytes 17000000 | tf_op jit(solution)/shard_map/pallas_call | solution.py:68
  118.4 30.5 %shard_map.227 = (bf16[4,512,768]{2,1,0:T(8,128)(2,1)}, bf16[4,512,768]{2,1,0:T(8,128)(2,1)}, bf16[4,512,3072]{2,1,0:T(8,128)(2,1)}, bf16[4,512,3072]{2,1,0:T(8,...) custom-call(s32[4]{0:T(128)} %pad_add_fusion.8.sp_ref, ...), custom_call_target="tpu_custom_call", output_to_operand_aliasing={{0}: (9, {}), {1}: (10, {}), {2}: (11, {}), {3}: (12, {}), ... | custom-call | flops 16000000000 | bytes 16000000 | tf_op jit(solution)/shard_map/pallas_call | solution.py:68
  179.4 38.8 %conditional.10 = (bf16[4,512,768]{2,1,0:T(8,128)(2,1)}, bf16[4,512,3072]{2,1,0:T(8,128)(2,1)}, bf16[4,512,2304]{2,1,0:T(8,128)(2,1)}, bf16[4,512,768]{2,1,0:T(8...) conditional(s32[]{:T(128)} %convert_element_type.96, ...), branch_computations={%region_2.3_spmd, %region_3.4_spmd} | conditional | flops 32999999488 | bytes 52398888 | solution.py:803
  180.5 18.8 %branch_1_fun.15 = (bf16[4,512,768]{2,1,0:T(8,128)(2,1)}, bf16[4,512,768]{2,1,0:T(8,128)(2,1)}, bf16[4,512,768]{2,1,0:T(8,128)(2,1)}, bf16[4,512,1536]{2,1,0:T(8,128)(2,1)}) custom-call(s32[4]{0:T(128)S(1)} %get-tuple-element.618.sp_ref, ...), custom_call_target="tpu_custom_call", output_to_operand_aliasing={{0}: (6, {}), {1}: (7, {}), {2}: (8, {}), {3}: (9, {})} | custom-call | flops 16999999488 | bytes 17000000 | tf_op jit(solution)/shard_map/cond/branch_1_fun/pallas_call | solution.py:68
  199.4 17.6 %branch_1_fun.16 = (bf16[4,512,768]{2,1,0:T(8,128)(2,1)}, bf16[4,512,768]{2,1,0:T(8,128)(2,1)}, bf16[4,512,3072]{2,1,0:T(8,128)(2,1)}, bf16[4,512,3072]{2,1,0:T(...) custom-call(s32[4]{0:T(128)S(1)} %get-tuple-element.618.sp_ref, ...), custom_call_target="tpu_custom_call", output_to_operand_aliasing={{0}: (9, {}), {1}: (10, {}), {2}: (11, {}), {3}: (12, {}), ... | custom-call | flops 16000000000 | bytes 16000000 | tf_op jit(solution)/shard_map/cond/branch_1_fun/pallas_call | solution.py:68
  233.5 18.9 %shard_map.229 = (bf16[4,512,768]{2,1,0:T(8,128)(2,1)}, bf16[4,512,768]{2,1,0:T(8,128)(2,1)}, bf16[4,512,768]{2,1,0:T(8,128)(2,1)}, bf16[4,512,1536]{2,1,0:T(8,128)(2,1)}) custom-call(s32[4]{0:T(128)} %pad_add_fusion.5.sp_ref, ...), custom_call_target="tpu_custom_call", output_to_operand_aliasing={{0}: (6, {}), {1}: (7, {}), {2}: (8, {}), {3}: (9, {})} | custom-call | flops 16999999488 | bytes 17000000 | tf_op jit(solution)/shard_map/pallas_call | solution.py:68
  252.4 18.3 %shard_map.230 = (bf16[4,512,768]{2,1,0:T(8,128)(2,1)}, bf16[4,512,768]{2,1,0:T(8,128)(2,1)}, bf16[4,512,3072]{2,1,0:T(8,128)(2,1)}, bf16[4,512,3072]{2,1,0:T(8,...) custom-call(s32[4]{0:T(128)} %pad_add_fusion.5.sp_ref, ...), custom_call_target="tpu_custom_call", output_to_operand_aliasing={{0}: (9, {}), {1}: (10, {}), {2}: (11, {}), {3}: (12, {}), ... | custom-call | flops 16000000000 | bytes 16000000 | tf_op jit(solution)/shard_map/pallas_call | solution.py:68
  274.4 17.0 %shard_map.231 = (bf16[4,512,768]{2,1,0:T(8,128)(2,1)}, bf16[4,512,3072]{2,1,0:T(8,128)(2,1)}, bf16[4,512,768]{2,1,0:T(8,128)(2,1)S(1)}, f32[4,8,768]{2,1,0:T(8,...) custom-call(s32[4]{0:T(128)} %get-tuple-element.1283.sp_ref, ...), custom_call_target="tpu_custom_call", output_to_operand_aliasing={{0}: (13, {}), {1}: (14, {}), {2}: (15, {}), {3}: (16, {}),... | custom-call | flops 16000000000 | bytes 16000000 | tf_op jit(solution)/shard_map/pallas_call | solution.py:68
  291.4 22.2 %shard_map.232 = (f32[4,64,768]{2,1,0:T(8,128)}, bf16[512,768]{1,0:T(8,128)(2,1)}, bf16[512,1536]{1,0:T(8,128)(2,1)}, bf16[512,1536]{1,0:T(8,128)(2,1)}) custom-call(s32[4]{0:T(128)} %get-tuple-element.1283.sp_ref, bf16[4,512,768]{2,1,0:T(8,128)(2,1)} %get-tuple-element.1049.refs_0_, ...), custom_call_target="tpu_custom_call", output_to_operand_aliasing={{0}: (10, {})} | custom-call | flops 24999999488 | bytes 25000000 | tf_op jit(solution)/shard_map/pallas_call | solution.py:68
  330.3 16.1 %collective-permute-done.13 = bf16[512,768]{1,0:T(8,128)(2,1)} collective-permute-done((bf16[512,768]{1,0:T(8,128)(2,1)}, bf16[512,768]{1,0:T(8,128)(2,1)}, u32[]{:S(2)}, u32[]{:S(2)}) %collective-permute-start.13) | collective-permute-done | bytes 786464 | tf_op jit(solution)/shard_map/ppermute | solution.py:813
  348.8 17.6 %shard_map.234 = (bf16[4,512,768]{2,1,0:T(8,128)(2,1)}, bf16[4,512,3072]{2,1,0:T(8,128)(2,1)}, bf16[4,512,768]{2,1,0:T(8,128)(2,1)S(1)}, f32[4,8,768]{2,1,0:T(8,...) custom-call(s32[4]{0:T(128)} %pad_add_fusion.12.sp_ref, ...), custom_call_target="tpu_custom_call", output_to_operand_aliasing={{0}: (13, {}), {1}: (14, {}), {2}: (15, {}), {3}: (16, {}),... | custom-call | flops 16000000000 | bytes 16000000 | tf_op jit(solution)/shard_map/pallas_call | solution.py:68
  366.5 17.8 %shard_map.235 = (f32[4,64,768]{2,1,0:T(8,128)}, bf16[512,768]{1,0:T(8,128)(2,1)}, bf16[512,1536]{1,0:T(8,128)(2,1)}, bf16[512,1536]{1,0:T(8,128)(2,1)}) custom-call(s32[4]{0:T(128)} %pad_add_fusion.12.sp_ref, bf16[4,512,768]{2,1,0:T(8,128)(2,1)} %get-tuple-element.1062.refs_0_, ...), custom_call_target="tpu_custom_call", output_to_operand_aliasing={{0}: (10, {})} | custom-call | flops 24999999488 | bytes 25000000 | tf_op jit(solution)/shard_map/pallas_call | solution.py:68
  384.4 36.6 %collective-permute-start.9 = (bf16[512,768]{1,0:T(8,128)(2,1)S(1)}, bf16[512,768]{1,0:T(8,128)(2,1)S(1)}, u32[]{:S(2)}, u32[]{:S(2)}) collective-permute-start(bf16[512,768]{1,0:T(8,128)(2,1)S(1)} %copy-done.74), channel_id=1, source_target_pairs={{0,16},{1,17},{2,18},{3,19},{4,20},{5,21},{6,22},{7,23},{8,24},{9,... | collective-permute-start | bytes 2359304 | tf_op jit(solution)/shard_map/ppermute | solution.py:813
  423.6 14.8 %collective-permute-done.9 = bf16[512,768]{1,0:T(8,128)(2,1)S(1)} collective-permute-done((bf16[512,768]{1,0:T(8,128)(2,1)S(1)}, bf16[512,768]{1,0:T(8,128)(2,1)S(1)}, u32[]{:S(2)}, u32[]{:S(2)}) %collective-permute-start.9) | collective-permute-done | bytes 786464 | tf_op jit(solution)/shard_map/ppermute | solution.py:813
  455.3 19.9 %collective-permute-done.15 = bf16[512,768]{1,0:T(8,128)(2,1)} collective-permute-done((bf16[512,768]{1,0:T(8,128)(2,1)}, bf16[512,768]{1,0:T(8,128)(2,1)}, u32[]{:S(2)}, u32[]{:S(2)}) %collective-permute-start.15) | collective-permute-done | bytes 786464 | tf_op jit(solution)/shard_map/ppermute | solution.py:813
  477.4 17.2 %shard_map.237 = (bf16[4,512,768]{2,1,0:T(8,128)(2,1)}, bf16[4,512,3072]{2,1,0:T(8,128)(2,1)}, bf16[4,512,768]{2,1,0:T(8,128)(2,1)S(1)}, f32[4,8,768]{2,1,0:T(8,...) custom-call(s32[4]{0:T(128)} %pad_add_fusion.4.sp_ref, ...), custom_call_target="tpu_custom_call", output_to_operand_aliasing={{0}: (13, {}), {1}: (14, {}), {2}: (15, {}), {3}: (16, {}),... | custom-call | flops 16000000000 | bytes 16000000 | tf_op jit(solution)/shard_map/pallas_call | solution.py:68
  494.6 26.5 %shard_map.238 = (f32[4,64,768]{2,1,0:T(8,128)}, bf16[512,768]{1,0:T(8,128)(2,1)}, bf16[512,1536]{1,0:T(8,128)(2,1)}, bf16[512,1536]{1,0:T(8,128)(2,1)}) custom-call(s32[4]{0:T(128)} %pad_add_fusion.4.sp_ref, bf16[4,512,768]{2,1,0:T(8,128)(2,1)} %get-tuple-element.1440.refs_0_, ...), custom_call_target="tpu_custom_call", output_to_operand_aliasing={{0}: (10, {})} | custom-call | flops 24999999488 | bytes 25000000 | tf_op jit(solution)/shard_map/pallas_call | solution.py:68
  535.9 40.7 %collective-permute-done.17 = bf16[512,768]{1,0:T(8,128)(2,1)} collective-permute-done((bf16[512,768]{1,0:T(8,128)(2,1)}, bf16[512,768]{1,0:T(8,128)(2,1)}, u32[]{:S(2)}, u32[]{:S(2)}) %collective-permute-start.17) | collective-permute-done | bytes 786464 | tf_op jit(solution)/shard_map/ppermute | solution.py:813
  576.6 20.7 %conditional.15 = (bf16[4,512,768]{2,1,0:T(8,128)(2,1)S(1)}, bf16[4,512,768]{2,1,0:T(8,128)(2,1)}, bf16[4,512,3072]{2,1,0:T(8,128)(2,1)}, f32[4,1,3072]{2,1,0:T(...) conditional(s32[]{:T(128)} %convert_element_type.96, ...), branch_computations={%region_12.13_spmd, %region_13.14_spmd} | conditional | flops 16000393216 | bytes 28846196 | solution.py:835
  580.1 16.9 %branch_1_fun.23 = (bf16[4,512,768]{2,1,0:T(8,128)(2,1)}, bf16[4,512,3072]{2,1,0:T(8,128)(2,1)}, bf16[4,512,768]{2,1,0:T(8,128)(2,1)S(1)}, f32[4,8,768]{2,1,0:T(...) custom-call(s32[4]{0:T(128)S(1)} %get-tuple-element.754.sp_ref, ...), custom_call_target="tpu_custom_call", output_to_operand_aliasing={{0}: (13, {}), {1}: (14, {}), {2}: (15, {}), {3}: (16, {}),... | custom-call | flops 16000000000 | bytes 16000000 | tf_op jit(solution)/shard_map/cond/branch_1_fun/pallas_call | solution.py:68
  597.3 26.8 %conditional.16 = ((f32[4,64,768]{2,1,0:T(8,128)}, bf16[512,768]{1,0:T(8,128)(2,1)}, bf16[512,1536]{1,0:T(8,128)(2,1)}, bf16[512,1536]{1,0:T(8,128)(2,1)})) conditional(s32[]{:T(128)} %convert_element_type.96, f32[4,64,768]{2,1,0:T(8,128)} %get-tuple-element.1157, (s32[4]{0:T(128)S(1)}, bf16[4,512,768]{2,1,0:T(8,128)(2,1)}, ...), branch_computations={%region_14.15_spmd, %region_15.16_spmd} | conditional | flops 24999999488 | bytes 25000008 | solution.py:840
  597.3 26.4 %branch_1_fun.24 = (f32[4,64,768]{2,1,0:T(8,128)}, bf16[512,768]{1,0:T(8,128)(2,1)}, bf16[512,1536]{1,0:T(8,128)(2,1)}, bf16[512,1536]{1,0:T(8,128)(2,1)}) custom-call(s32[4]{0:T(128)S(1)} %get-tuple-element.782.sp_ref, bf16[4,512,768]{2,1,0:T(8,128)(2,1)} %get-tuple-element.783.refs_0_, ...), custom_call_target="tpu_custom_call", output_to_operand_aliasing={{0}: (10, {})} | custom-call | flops 24999999488 | bytes 25000000 | tf_op jit(solution)/shard_map/cond/branch_1_fun/pallas_call | solution.py:68
  724.8 20.3 %collective-permute-done.29 = bf16[192,3072]{1,0:T(8,128)(2,1)S(1)} collective-permute-done((bf16[192,3072]{1,0:T(8,128)(2,1)S(1)}, bf16[192,3072]{1,0:T(8,128)(2,1)S(1)}, u32[]{:S(2)}, u32[]{:S(2)}) %collective-permute-start.29) | collective-permute-done | bytes 1179680 | tf_op jit(solution)/shard_map/ppermute | solution.py:582
  748.5 20.1 %collective-permute-done.30 = bf16[96,3072]{1,0:T(8,128)(2,1)S(1)} collective-permute-done((bf16[96,3072]{1,0:T(8,128)(2,1)S(1)}, bf16[96,3072]{1,0:T(8,128)(2,1)S(1)}, u32[]{:S(2)}, u32[]{:S(2)}) %collective-permute-start.30) | collective-permute-done | bytes 589856 | tf_op jit(solution)/shard_map/ppermute | solution.py:582
  771.9 21.3 %collective-permute-done.31 = bf16[48,3072]{1,0:T(8,128)(2,1)S(1)} collective-permute-done((bf16[48,3072]{1,0:T(8,128)(2,1)S(1)}, bf16[48,3072]{1,0:T(8,128)(2,1)S(1)}, u32[]{:S(2)}, u32[]{:S(2)}) %collective-permute-start.31) | collective-permute-done | bytes 294944 | tf_op jit(solution)/shard_map/ppermute | solution.py:582
  818.1 22.9 %collective-permute-done.22 = bf16[96,3072]{1,0:T(8,128)(2,1)S(1)} collective-permute-done((bf16[96,3072]{1,0:T(8,128)(2,1)S(1)}, bf16[96,3072]{1,0:T(8,128)(2,1)S(1)}, u32[]{:S(2)}, u32[]{:S(2)}) %collective-permute-start.22) | collective-permute-done | bytes 589856 | tf_op jit(solution)/shard_map/ppermute | solution.py:582
  841.6 12.6 %collective-permute-done.23 = bf16[48,3072]{1,0:T(8,128)(2,1)S(1)} collective-permute-done((bf16[48,3072]{1,0:T(8,128)(2,1)S(1)}, bf16[48,3072]{1,0:T(8,128)(2,1)S(1)}, u32[]{:S(2)}, u32[]{:S(2)}) %collective-permute-start.23) | collective-permute-done | bytes 294944 | tf_op jit(solution)/shard_map/ppermute | solution.py:582
  865.6 14.3 %collective-permute-done.25 = bf16[96,3072]{1,0:T(8,128)(2,1)S(1)} collective-permute-done((bf16[96,3072]{1,0:T(8,128)(2,1)S(1)}, bf16[96,3072]{1,0:T(8,128)(2,1)S(1)}, u32[]{:S(2)}, u32[]{:S(2)}) %collective-permute-start.25) | collective-permute-done | bytes 589856 | tf_op jit(solution)/shard_map/ppermute | solution.py:582
  885.2 11.3 %collective-permute-done.26 = bf16[192,3072]{1,0:T(8,128)(2,1)S(1)} collective-permute-done((bf16[192,3072]{1,0:T(8,128)(2,1)S(1)}, bf16[192,3072]{1,0:T(8,128)(2,1)S(1)}, u32[]{:S(2)}, u32[]{:S(2)}) %collective-permute-start.26) | collective-permute-done | bytes 1179680 | tf_op jit(solution)/shard_map/ppermute | solution.py:582
  (411 shorter events, 364.6 us)
Async XLA Ops:
  68.2 22.0 %collective-permute-start.3 = (bf16[512,768]{1,0:T(8,128)(2,1)}, bf16[512,768]{1,0:T(8,128)(2,1)}, u32[]{:S(2)}, u32[]{:S(2)}) collective-permute-start(bf16[512,768]{1,0:T(8,128)(2,1)} %get-tuple-element.1014), channel_id=1, source_target_pairs={{0,16},{1,17},{2,18},{3,19},{4,20},{5,21},{6,22},{7,23},{8,24},{9,... | collective-permute-start | bytes 2359304 | tf_op jit(solution)/shard_map/ppermute | solution.py:813
  149.9 25.6 %collective-permute-start.5 = (bf16[512,768]{1,0:T(8,128)(2,1)}, bf16[512,768]{1,0:T(8,128)(2,1)}, u32[]{:S(2)}, u32[]{:S(2)}) collective-permute-start(bf16[512,768]{1,0:T(8,128)(2,1)} %get-tuple-element.1044), channel_id=1, source_target_pairs={{0,16},{1,17},{2,18},{3,19},{4,20},{5,21},{6,22},{7,23},{8,24},{9,... | collective-permute-start | bytes 2359304 | tf_op jit(solution)/shard_map/ppermute | solution.py:813
  230.2 40.5 %collective-permute-start.7 = (bf16[512,768]{1,0:T(8,128)(2,1)}, bf16[512,768]{1,0:T(8,128)(2,1)}, u32[]{:S(2)}, u32[]{:S(2)}) collective-permute-start(bf16[512,768]{1,0:T(8,128)(2,1)} %get-tuple-element.1060), channel_id=1, source_target_pairs={{0,16},{16,0},{1,17},{17,1},{2,18},{18,2},{3,19},{19,3},{4,20},{20... | collective-permute-start | bytes 2359304 | tf_op jit(solution)/shard_map/ppermute | solution.py:813
  313.8 16.1 %collective-permute-start.10 = (bf16[512,1536]{1,0:T(8,128)(2,1)S(1)}, bf16[512,1536]{1,0:T(8,128)(2,1)}, u32[]{:S(2)}, u32[]{:S(2)}) collective-permute-start(bf16[512,1536]{1,0:T(8,128)(2,1)S(1)} %get-tuple-element.1089), channel_id=1, source_target_pairs={{0,1},{1,0},{2,3},{3,2},{4,5},{5,4},{6,7},{7,6},{8,9},{9,8},{10,11... | collective-permute-start | bytes 4718600 | tf_op jit(solution)/shard_map/ppermute | solution.py:640
  324.6 21.8 %collective-permute-start.13 = (bf16[512,768]{1,0:T(8,128)(2,1)}, bf16[512,768]{1,0:T(8,128)(2,1)}, u32[]{:S(2)}, u32[]{:S(2)}) collective-permute-start(bf16[512,768]{1,0:T(8,128)(2,1)} %get-tuple-element.1118), channel_id=1, source_target_pairs={{16,0},{17,1},{18,2},{19,3},{20,4},{21,5},{22,6},{23,7},{24,8},{25... | collective-permute-start | bytes 2359304 | tf_op jit(solution)/shard_map/ppermute | solution.py:813
  384.3 56.4 %collective-permute-start.14 = (bf16[512,1536]{1,0:T(8,128)(2,1)}, bf16[512,1536]{1,0:T(8,128)(2,1)}, u32[]{:S(2)}, u32[]{:S(2)}) collective-permute-start(bf16[512,1536]{1,0:T(8,128)(2,1)} %get-tuple-element.1128), channel_id=1, source_target_pairs={{0,1},{1,0},{2,3},{3,2},{4,5},{5,4},{6,7},{7,6},{8,9},{9,8},{10,11... | collective-permute-start | bytes 4718600 | tf_op jit(solution)/shard_map/ppermute | solution.py:640
  384.4 54.0 %collective-permute-start.9 = (bf16[512,768]{1,0:T(8,128)(2,1)S(1)}, bf16[512,768]{1,0:T(8,128)(2,1)S(1)}, u32[]{:S(2)}, u32[]{:S(2)}) collective-permute-start(bf16[512,768]{1,0:T(8,128)(2,1)S(1)} %copy-done.74), channel_id=1, source_target_pairs={{0,16},{1,17},{2,18},{3,19},{4,20},{5,21},{6,22},{7,23},{8,24},{9,... | collective-permute-start | bytes 2359304 | tf_op jit(solution)/shard_map/ppermute | solution.py:813
  448.0 27.1 %collective-permute-start.15 = (bf16[512,768]{1,0:T(8,128)(2,1)}, bf16[512,768]{1,0:T(8,128)(2,1)}, u32[]{:S(2)}, u32[]{:S(2)}) collective-permute-start(bf16[512,768]{1,0:T(8,128)(2,1)} %get-tuple-element.1133), channel_id=1, source_target_pairs={{16,0},{17,1},{18,2},{19,3},{20,4},{21,5},{22,6},{23,7},{24,8},{25... | collective-permute-start | bytes 2359304 | tf_op jit(solution)/shard_map/ppermute | solution.py:813
  533.2 43.4 %collective-permute-start.17 = (bf16[512,768]{1,0:T(8,128)(2,1)}, bf16[512,768]{1,0:T(8,128)(2,1)}, u32[]{:S(2)}, u32[]{:S(2)}) collective-permute-start(bf16[512,768]{1,0:T(8,128)(2,1)} %get-tuple-element.1162), channel_id=1, source_target_pairs={{16,0},{17,1},{18,2},{19,3},{20,4},{21,5},{22,6},{23,7},{24,8},{25... | collective-permute-start | bytes 2359304 | tf_op jit(solution)/shard_map/ppermute | solution.py:813
  624.1 30.7 %collective-permute-start.18 = (bf16[512,1536]{1,0:T(8,128)(2,1)}, bf16[512,1536]{1,0:T(8,128)(2,1)}, u32[]{:S(2)}, u32[]{:S(2)}) collective-permute-start(bf16[512,1536]{1,0:T(8,128)(2,1)} %get-tuple-element.1167), channel_id=1, source_target_pairs={{0,1},{1,0},{2,3},{3,2},{4,5},{5,4},{6,7},{7,6},{8,9},{9,8},{10,11... | collective-permute-start | bytes 4718600 | tf_op jit(solution)/shard_map/ppermute | solution.py:640
  642.8 53.7 %collective-permute-start.36 = (bf16[384,3072]{1,0:T(8,128)(2,1)}, bf16[384,3072]{1,0:T(8,128)(2,1)}, u32[]{:S(2)}, u32[]{:S(2)}) collective-permute-start(bf16[384,3072]{1,0:T(8,128)(2,1)} %convolution_convert_fusion), channel_id=1, source_target_pairs={{0,1},{1,0},{2,3},{3,2},{4,5},{5,4},{6,7},{7,6},{8,9},{9,8},{10,11... | collective-permute-start | bytes 7077896 | tf_op jit(solution)/shard_map/ppermute | solution.py:640
  649.8 57.6 %collective-permute-start.28 = (bf16[384,3072]{1,0:T(8,128)(2,1)}, bf16[384,3072]{1,0:T(8,128)(2,1)}, u32[]{:S(2)}, u32[]{:S(2)}) collective-permute-start(bf16[384,3072]{1,0:T(8,128)(2,1)} %convolution_convert_fusion.2), channel_id=1, source_target_pairs={{0,1},{1,0},{2,3},{3,2},{4,5},{5,4},{6,7},{7,6},{8,9},{9,8},{10,11... | collective-permute-start | bytes 7077896 | tf_op jit(solution)/shard_map/ppermute | solution.py:640
  661.5 17.2 %collective-permute-start.44 = (f32[88,128]{1,0:T(8,128)S(1)}, f32[88,128]{1,0:T(8,128)S(1)}, u32[]{:S(2)}, u32[]{:S(2)}) collective-permute-start(f32[88,128]{1,0:T(8,128)S(1)} %pad_bitcast_fusion), channel_id=1, source_target_pairs={{0,1},{1,0},{2,3},{3,2},{4,5},{5,4},{6,7},{7,6},{8,9},{9,8},{10,11... | collective-permute-start | bytes 135176 | tf_op jit(solution)/shard_map/ppermute | solution.py:613
  680.5 65.1 %collective-permute-start.20 = (bf16[384,3072]{1,0:T(8,128)(2,1)}, bf16[384,3072]{1,0:T(8,128)(2,1)}, u32[]{:S(2)}, u32[]{:S(2)}) collective-permute-start(bf16[384,3072]{1,0:T(8,128)(2,1)} %pad_maximum_fusion.3), channel_id=1, source_target_pairs={{0,1},{1,0},{2,3},{3,2},{4,5},{5,4},{6,7},{7,6},{8,9},{9,8},{10,11... | collective-permute-start | bytes 7077896 | tf_op jit(solution)/shard_map/ppermute | solution.py:640
  688.4 31.8 %collective-permute-start.19 = (bf16[2,512,768]{2,1,0:T(8,128)(2,1)}, bf16[2,512,768]{2,1,0:T(8,128)(2,1)}, u32[]{:S(2)}, u32[]{:S(2)}) collective-permute-start(bf16[2,512,768]{2,1,0:T(8,128)(2,1)} %broadcast_select_fusion.2), channel_id=1, source_target_pairs={{0,1},{1,0},{2,3},{3,2},{4,5},{5,4},{6,7},{7,6},{8,9},{9,8},{10,11... | collective-permute-start | bytes 4718600 | tf_op jit(solution)/shard_map/ppermute | solution.py:640
  707.1 17.1 %collective-permute-start.37 = (bf16[192,3072]{1,0:T(8,128)(2,1)S(1)}, bf16[192,3072]{1,0:T(8,128)(2,1)S(1)}, u32[]{:S(2)}, u32[]{:S(2)}) collective-permute-start(bf16[192,3072]{1,0:T(8,128)(2,1)S(1)} %constant_dynamic-slice_fusion.3), channel_id=1, source_target_pairs={{0,2},{1,5},{2,0},{3,7},{4,6},{5,1},{6,4},{7,3},{8,10},{9,13},{10,... | collective-permute-start | bytes 3538952 | tf_op jit(solution)/shard_map/ppermute | solution.py:582
  718.3 26.8 %collective-permute-start.29 = (bf16[192,3072]{1,0:T(8,128)(2,1)S(1)}, bf16[192,3072]{1,0:T(8,128)(2,1)S(1)}, u32[]{:S(2)}, u32[]{:S(2)}) collective-permute-start(bf16[192,3072]{1,0:T(8,128)(2,1)S(1)} %constant_dynamic-slice_fusion.6), channel_id=1, source_target_pairs={{0,2},{1,5},{2,0},{3,7},{4,6},{5,1},{6,4},{7,3},{8,10},{9,13},{10,... | collective-permute-start | bytes 3538952 | tf_op jit(solution)/shard_map/ppermute | solution.py:582
  724.7 23.5 %collective-permute-start.38 = (bf16[96,3072]{1,0:T(8,128)(2,1)S(1)}, bf16[96,3072]{1,0:T(8,128)(2,1)S(1)}, u32[]{:S(2)}, u32[]{:S(2)}) collective-permute-start(bf16[96,3072]{1,0:T(8,128)(2,1)S(1)} %constant_dynamic-slice_fusion.2), channel_id=1, source_target_pairs={{0,4},{1,3},{2,6},{3,1},{4,0},{5,7},{6,2},{7,5},{8,12},{9,11},{10,... | collective-permute-start | bytes 1769480 | tf_op jit(solution)/shard_map/ppermute | solution.py:582
  745.6 23.0 %collective-permute-start.30 = (bf16[96,3072]{1,0:T(8,128)(2,1)S(1)}, bf16[96,3072]{1,0:T(8,128)(2,1)S(1)}, u32[]{:S(2)}, u32[]{:S(2)}) collective-permute-start(bf16[96,3072]{1,0:T(8,128)(2,1)S(1)} %constant_dynamic-slice_fusion.5), channel_id=1, source_target_pairs={{0,4},{1,3},{2,6},{3,1},{4,0},{5,7},{6,2},{7,5},{8,12},{9,11},{10,... | collective-permute-start | bytes 1769480 | tf_op jit(solution)/shard_map/ppermute | solution.py:582
  748.1 57.8 %collective-permute-start.21 = (bf16[192,3072]{1,0:T(8,128)(2,1)S(1)}, bf16[192,3072]{1,0:T(8,128)(2,1)S(1)}, u32[]{:S(2)}, u32[]{:S(2)}) collective-permute-start(bf16[192,3072]{1,0:T(8,128)(2,1)S(1)} %constant_dynamic-slice_fusion.9), channel_id=1, source_target_pairs={{0,2},{1,5},{2,0},{3,7},{4,6},{5,1},{6,4},{7,3},{8,10},{9,13},{10,... | collective-permute-start | bytes 3538952 | tf_op jit(solution)/shard_map/ppermute | solution.py:582
  748.4 20.4 %collective-permute-start.39 = (bf16[48,3072]{1,0:T(8,128)(2,1)S(1)}, bf16[48,3072]{1,0:T(8,128)(2,1)S(1)}, u32[]{:S(2)}, u32[]{:S(2)}) collective-permute-start(bf16[48,3072]{1,0:T(8,128)(2,1)S(1)} %constant_dynamic-slice_fusion.1), channel_id=1, source_target_pairs={{0,8},{1,9},{2,10},{3,11},{4,12},{5,13},{6,14},{7,15},{8,0},{9,1},... | collective-permute-start | bytes 884744 | tf_op jit(solution)/shard_map/ppermute | solution.py:582
  768.8 24.4 %collective-permute-start.31 = (bf16[48,3072]{1,0:T(8,128)(2,1)S(1)}, bf16[48,3072]{1,0:T(8,128)(2,1)S(1)}, u32[]{:S(2)}, u32[]{:S(2)}) collective-permute-start(bf16[48,3072]{1,0:T(8,128)(2,1)S(1)} %constant_dynamic-slice_fusion.4), channel_id=1, source_target_pairs={{0,8},{1,9},{2,10},{3,11},{4,12},{5,13},{6,14},{7,15},{8,0},{9,1},... | collective-permute-start | bytes 884744 | tf_op jit(solution)/shard_map/ppermute | solution.py:582
  769.0 33.6 %collective-permute-start.40 = (bf16[48,3072]{1,0:T(8,128)(2,1)S(1)}, bf16[48,3072]{1,0:T(8,128)(2,1)S(1)}, u32[]{:S(2)}, u32[]{:S(2)}) collective-permute-start(bf16[48,3072]{1,0:T(8,128)(2,1)S(1)} %dynamic-slice_add_fusion.6), channel_id=1, source_target_pairs={{0,8},{1,9},{2,10},{3,11},{4,12},{5,13},{6,14},{7,15},{8,0},{9,1},... | collective-permute-start | bytes 884744 | tf_op jit(solution)/shard_map/ppermute | solution.py:582
  805.8 35.5 %collective-permute-start.33 = (bf16[96,3072]{1,0:T(8,128)(2,1)S(1)}, bf16[96,3072]{1,0:T(8,128)(2,1)S(1)}, u32[]{:S(2)}, u32[]{:S(2)}) collective-permute-start(bf16[96,3072]{1,0:T(8,128)(2,1)S(1)} %pad_maximum_fusion.11), channel_id=1, source_target_pairs={{0,4},{1,3},{2,6},{3,1},{4,0},{5,7},{6,2},{7,5},{8,12},{9,11},{10,... | collective-permute-start | bytes 1769480 | tf_op jit(solution)/shard_map/ppermute | solution.py:582
  806.4 34.7 %collective-permute-start.22 = (bf16[96,3072]{1,0:T(8,128)(2,1)S(1)}, bf16[96,3072]{1,0:T(8,128)(2,1)S(1)}, u32[]{:S(2)}, u32[]{:S(2)}) collective-permute-start(bf16[96,3072]{1,0:T(8,128)(2,1)S(1)} %constant_dynamic-slice_fusion.8), channel_id=1, source_target_pairs={{0,4},{1,3},{2,6},{3,1},{4,0},{5,7},{6,2},{7,5},{8,12},{9,11},{10,... | collective-permute-start | bytes 1769480 | tf_op jit(solution)/shard_map/ppermute | solution.py:582
  817.8 47.0 %collective-permute-start.42 = (bf16[192,3072]{1,0:T(8,128)(2,1)S(1)}, bf16[192,3072]{1,0:T(8,128)(2,1)S(1)}, u32[]{:S(2)}, u32[]{:S(2)}) collective-permute-start(bf16[192,3072]{1,0:T(8,128)(2,1)S(1)} %pad_maximum_fusion.9), channel_id=1, source_target_pairs={{0,2},{1,5},{2,0},{3,7},{4,6},{5,1},{6,4},{7,3},{8,10},{9,13},{10,... | collective-permute-start | bytes 3538952 | tf_op jit(solution)/shard_map/ppermute | solution.py:582
  854.4 28.6 %collective-permute-start.34 = (bf16[192,3072]{1,0:T(8,128)(2,1)S(1)}, bf16[192,3072]{1,0:T(8,128)(2,1)S(1)}, u32[]{:S(2)}, u32[]{:S(2)}) collective-permute-start(bf16[192,3072]{1,0:T(8,128)(2,1)S(1)} %pad_maximum_fusion.8), channel_id=1, source_target_pairs={{0,2},{1,5},{2,0},{3,7},{4,6},{5,1},{6,4},{7,3},{8,10},{9,13},{10,... | collective-permute-start | bytes 3538952 | tf_op jit(solution)/shard_map/ppermute | solution.py:582
  864.6 15.2 %collective-permute-start.25 = (bf16[96,3072]{1,0:T(8,128)(2,1)S(1)}, bf16[96,3072]{1,0:T(8,128)(2,1)S(1)}, u32[]{:S(2)}, u32[]{:S(2)}) collective-permute-start(bf16[96,3072]{1,0:T(8,128)(2,1)S(1)} %pad_maximum_fusion.10), channel_id=1, source_target_pairs={{0,4},{1,3},{2,6},{3,1},{4,0},{5,7},{6,2},{7,5},{8,12},{9,11},{10,... | collective-permute-start | bytes 1769480 | tf_op jit(solution)/shard_map/ppermute | solution.py:582
  865.5 33.3 %collective-permute-start.43 = (bf16[384,3072]{1,0:T(8,128)(2,1)S(1)}, bf16[384,3072]{1,0:T(8,128)(2,1)S(1)}, u32[]{:S(2)}, u32[]{:S(2)}) collective-permute-start(bf16[384,3072]{1,0:T(8,128)(2,1)S(1)} %pad_maximum_fusion.6), channel_id=1, source_target_pairs={{0,1},{1,0},{2,3},{3,2},{4,5},{5,4},{6,7},{7,6},{8,9},{9,8},{10,11... | collective-permute-start | bytes 7077896 | tf_op jit(solution)/shard_map/ppermute | solution.py:585
  880.2 16.3 %collective-permute-start.26 = (bf16[192,3072]{1,0:T(8,128)(2,1)S(1)}, bf16[192,3072]{1,0:T(8,128)(2,1)S(1)}, u32[]{:S(2)}, u32[]{:S(2)}) collective-permute-start(bf16[192,3072]{1,0:T(8,128)(2,1)S(1)} %pad_maximum_fusion.7), channel_id=1, source_target_pairs={{0,2},{1,5},{2,0},{3,7},{4,6},{5,1},{6,4},{7,3},{8,10},{9,13},{10,... | collective-permute-start | bytes 3538952 | tf_op jit(solution)/shard_map/ppermute | solution.py:582
  885.2 24.2 %collective-permute-start.35 = (bf16[384,3072]{1,0:T(8,128)(2,1)}, bf16[384,3072]{1,0:T(8,128)(2,1)}, u32[]{:S(2)}, u32[]{:S(2)}) collective-permute-start(bf16[384,3072]{1,0:T(8,128)(2,1)} %pad_maximum_fusion.5), channel_id=1, source_target_pairs={{0,1},{1,0},{2,3},{3,2},{4,5},{5,4},{6,7},{7,6},{8,9},{9,8},{10,11... | collective-permute-start | bytes 7077896 | tf_op jit(solution)/shard_map/ppermute | solution.py:585
  898.6 23.2 %collective-permute-start.27 = (bf16[384,3072]{1,0:T(8,128)(2,1)}, bf16[384,3072]{1,0:T(8,128)(2,1)}, u32[]{:S(2)}, u32[]{:S(2)}) collective-permute-start(bf16[384,3072]{1,0:T(8,128)(2,1)} %pad_maximum_fusion.4), channel_id=1, source_target_pairs={{0,1},{1,0},{2,3},{3,2},{4,5},{5,4},{6,7},{7,6},{8,9},{9,8},{10,11... | collective-permute-start | bytes 7077896 | tf_op jit(solution)/shard_map/ppermute | solution.py:585
  (89 other events, 909.6 us)

commit v2 on v1

v2 whole, which is shorter than its diff:
```python
import functools
import math

import jax
import jax.numpy as jnp
from jax import lax
from jax.experimental import pallas as pl
from jax.experimental.pallas import tpu as pltpu
from jax.sharding import PartitionSpec as P

GRID = 16
SPAN = 32
KEY_BLOCK = 256
ROW_BLOCK = 256
FF_BLOCK = 768
PAIRS = 2
HALF = 64
PAIR = 128

epsilon = 1e-05
masked = -1e30
score_scale = 0.125
VMEM_LIMIT = 40 * 1024 * 1024

f32 = jnp.float32
bf16 = jnp.bfloat16

dot_nn = lambda a, b: lax.dot_general(a, b, (((1,), (0,)), ((), ())), preferred_element_type=f32)
dot_nt = lambda a, b: lax.dot_general(a, b, (((1,), (1,)), ((), ())), preferred_element_type=f32)
dot_tn = lambda a, b: lax.dot_general(a, b, (((0,), (0,)), ((), ())), preferred_element_type=f32)


def params_for(axes):
    return pltpu.CompilerParams(
        dimension_semantics=("arbitrary",) * axes, vmem_limit_bytes=VMEM_LIMIT
    )


ANY = pl.BlockSpec(memory_space=pl.ANY)


def like(a):
    return jax.ShapeDtypeStruct(a.shape, a.dtype)


RESIDENT = pl.BlockSpec(memory_space=pltpu.VMEM)


def fixed(shape):
    return pl.BlockSpec(shape, lambda i, sp: (0,) * len(shape), pipeline_mode=pl.Buffered(1))


def this_step(count):
    return pl.ds(pl.multiple_of(pl.program_id(0) * count, count), count)


def stacked(rows, cols):
    return pl.BlockSpec((1, rows, cols), lambda i, sp: (sp[0], i, 0))


def plain(rows, cols):
    return pl.BlockSpec((rows, cols), lambda i, sp: (i, 0))


def call(body, sp, grid, ins, outs, aliased, scratch=(), us=10):
    operands = [a for a, _ in ins] + [a for a, _ in aliased]
    in_specs = [s for _, s in ins] + [ANY] * len(aliased)
    out_shape = [like(a) for a, _ in aliased] + [s for s, _ in outs]
    out_specs = [s for _, s in aliased] + [s for _, s in outs]
    kept = len(aliased)
    first = len(ins)

    def run(sp_ref, *refs):
        body(sp_ref, *refs[:first], *refs[first + kept :])

    return pl.pallas_call(
        run,
        grid_spec=pltpu.PrefetchScalarGridSpec(
            num_scalar_prefetch=1,
            grid=grid,
            in_specs=in_specs,
            out_specs=out_specs,
            scratch_shapes=list(scratch),
        ),
        out_shape=out_shape,
        input_output_aliases={1 + first + j: j for j in range(kept)},
        compiler_params=params_for(len(grid)),
        cost_estimate=pl.CostEstimate(
            flops=us * 1_000_000_000, bytes_accessed=us * 1_000_000, transcendentals=0
        ),
    )(sp, *operands)


def unwritten(shapes):
    return pl.pallas_call(
        lambda *refs: None, out_shape=shapes, out_specs=[ANY] * len(shapes),
        compiler_params=pltpu.CompilerParams(vmem_limit_bytes=2 * 1024 * 1024),
    )()


def in_vmem(arrays):
    def body(*refs):
        count = len(arrays)
        copies = [
            pltpu.make_async_copy(refs[j], refs[count + j], refs[-1].at[j]) for j in range(count)
        ]
        for copy in copies:
            copy.start()
        for copy in copies:
            copy.wait()

    return pl.pallas_call(
        body,
        out_shape=[pltpu.VMEM(a.shape, a.dtype) for a in arrays],
        in_specs=[ANY] * len(arrays),
        out_specs=[RESIDENT] * len(arrays),
        scratch_shapes=[pltpu.SemaphoreType.DMA((len(arrays),))],
        compiler_params=pltpu.CompilerParams(vmem_limit_bytes=2 * 1024 * 1024),
    )(*arrays)


def at_window(rows, cols):
    return pl.BlockSpec((1, rows, cols), lambda i, sp: (sp[0], 0, i))


def whole_window(rows, cols):
    return pl.BlockSpec((1, rows, cols), lambda i, sp: (sp[0], 0, 0))


def columns(rows, cols, begin=0):
    return pl.BlockSpec((rows, cols), lambda i, sp: (0, begin + i))


def qkv_body(sp, x_ref, got_ref, w_ref, b_ref, x_out, q_ref, kv_ref, fresh_ref):
    width = x_ref.shape[2]
    cols = q_ref.shape[2]
    x = jnp.where(sp[4] == 1, got_ref[...], x_ref[0])

    @pl.when(pl.program_id(0) == 0)
    def _():
        x_out[0] = x

    def part(j):
        at = pl.ds(pl.multiple_of(j * width + pl.program_id(0) * cols, cols), cols)
        return dot_nn(x, w_ref[:, at]) + b_ref[:, at]

    q_ref[0] = (part(0).astype(bf16) * score_scale).astype(bf16)
    k = part(1).astype(bf16)
    v = part(2).astype(bf16)
    for begin in range(0, cols, PAIR):
        for value, at in ((k, 0), (v, PAIR)):
            to = slice(2 * begin + at, 2 * begin + at + PAIR)
            kv_ref[0, :, to] = value[:, begin : begin + PAIR]
            fresh_ref[:, to] = value[:, begin : begin + PAIR]


def qkv_call(sp, own_all, got, weight, bias, x_all, q_all, kv_all):
    rows, width = x_all.shape[1], x_all.shape[2]
    cols = PAIRS * PAIR
    return call(
        qkv_body,
        sp,
        (width // cols,),
        [
            (own_all, whole_window(rows, width)), (got, fixed(got.shape)), (weight, RESIDENT),
            (bias, fixed(bias.shape)),
        ],
        [(jax.ShapeDtypeStruct((rows, 2 * width), bf16), columns(rows, 2 * cols))],
        [
            (x_all, whole_window(rows, width)), (q_all, at_window(rows, cols)),
            (kv_all, at_window(rows, 2 * cols)),
        ],
        us=4,
    )


def low_half(shape):
    return lax.broadcasted_iota(jnp.int32, shape, 1) < HALF


def split_three(value):
    place = lax.broadcasted_iota(jnp.int32, value.shape, 1) % HALF
    high = value.astype(bf16).astype(f32)
    rest = value - high
    mid = rest.astype(bf16).astype(f32)
    last = rest - mid
    out = jnp.where(place == 0, high, jnp.where(place == 1, mid, jnp.where(place == 2, last, 0.0)))
    return out.astype(bf16)


def in_order(first, own, peer):
    return jnp.concatenate([jnp.where(first, own, peer), jnp.where(first, peer, own)], axis=0)


def attend_body(
    sp, q_ref, own_ref, peer_ref, side_ref, hot_ref, m_ref, a_ref, rest_ref, lse_ref, kept_ref
):
    rows = q_ref.shape[1]
    first = sp[2] == 0
    kept_ref[0] = peer_ref[...]

    def variant(keys):
        low = low_half((rows, PAIR))
        key_low = low_half((keys, PAIR))
        one = jnp.ones((keys, PAIR), bf16)
        side = side_ref[0]
        hot = hot_ref[0, :keys, :]
        for n in range(PAIRS):
            cols = slice(n * PAIR, (n + 1) * PAIR)
            kv = slice(2 * n * PAIR, 2 * (n + 1) * PAIR)
            both = in_order(first, own_ref[:, kv], peer_ref[:, kv])[:keys]
            k, v = both[:, :PAIR], both[:, PAIR:]
            ks = dot_nn(hot, m_ref[:, cols]).astype(bf16)
            q = q_ref[0, :, cols]
            outs = []
            peaks = []
            for head in (0, 1):
                pick = (lambda m, x, y: jnp.where(m, x, y)) if head == 0 else (
                    lambda m, x, y: jnp.where(m, y, x)
                )
                s = dot_nt(pick(low, q, side), pick(key_low, k, ks))
                peak = jnp.max(s, axis=1, keepdims=True)
                e = jnp.exp(s - peak).astype(bf16)
                outs.append(dot_nn(e, pick(key_low, v, one)))
                peaks.append(peak)
            top = jnp.where(low, outs[0], outs[1])
            total = pltpu.roll(jnp.where(low, outs[1], outs[0]), HALF, 1)
            mixed = top / total
            mixed_low = mixed.astype(bf16)
            a_ref[0, :, cols] = mixed_low
            rest_ref[0, :, cols] = (mixed - mixed_low.astype(f32)).astype(bf16)
            lse = jnp.where(low, peaks[0], peaks[1]) + jnp.log(total)
            lse_ref[0, :, cols] = split_three(-lse)

    for blocks in range(1, 2 * rows // KEY_BLOCK + 1):
        pl.when(sp[1] == blocks)(functools.partial(variant, blocks * KEY_BLOCK))


def attend_call(sp, q_all, kv_own, kv_peer, side_all, hot_all, matrix, bufs):
    rows, width = q_all.shape[1], q_all.shape[2]
    cols = PAIRS * PAIR
    part = at_window(rows, cols)
    return call(
        attend_body,
        sp,
        (width // cols,),
        [
            (q_all, part),
            (kv_own, columns(rows, 2 * cols)),
            (kv_peer, columns(rows, 2 * cols)),
            (side_all, whole_window(rows, PAIR)),
            (hot_all, whole_window(2 * rows, PAIR)),
            (matrix, columns(PAIR, cols)),
        ],
        [],
        [(b, part) for b in bufs[:-1]] + [(bufs[-1], at_window(rows, 2 * cols))],
        us=14,
    )


def gelu_both(x):
    cdf = 0.5 + 0.5 * lax.erf(x * math.sqrt(0.5))
    bell = jnp.exp(x * x * -0.5)
    return x * cdf, cdf + x * bell * (1.0 / math.sqrt(2.0 * math.pi))


def centered(u):
    c = u - jnp.mean(u, axis=1, keepdims=True)
    r = lax.rsqrt(jnp.mean(c * c, axis=1, keepdims=True) + epsilon)
    return c * r, r


class Moves:
    def __init__(self, sems):
        self.sems = sems
        self.used = 0
        self.out = []

    def start(self, source, target):
        copy = pltpu.make_async_copy(source, target, self.sems.at[self.used])
        self.used += 1
        copy.start()
        return copy

    def write(self, source, target):
        self.out.append(self.start(source, target))

    def finish(self):
        for copy in self.out:
            copy.wait()


def chunks(width):
    return [slice(c, c + FF_BLOCK) for c in range(0, width, FF_BLOCK)]


def dense_body(
    sp, a_ref, x_ref, wo_ref, w1_ref, w2_ref, gain_ref, bias_ref, eb_ref,
    n1_hbm, h1_hbm, g_hbm, d_hbm, n2_hbm, r_hbm, fresh_ref,
    n1_ref, h1_ref, g_ref, d_ref, n2_ref, r_ref, sems,
):
    w = sp[0]
    moves = Moves(sems)
    parts = chunks(w1_ref.shape[1])
    u1 = dot_nn(a_ref[0], wo_ref[...]) + bias_ref[2:3, :] + x_ref[0].astype(f32)
    n1, r1 = centered(u1)
    h1 = n1 * gain_ref[0:1, :] + bias_ref[3:4, :]
    h1_low = h1.astype(bf16)
    n1_ref[...] = n1.astype(bf16)
    h1_ref[...] = h1_low
    moves.write(n1_ref, n1_hbm.at[w])
    moves.write(h1_ref, h1_hbm.at[w])
    u2 = h1 + bias_ref[4:5, :]
    for c in parts:
        g, d = gelu_both(dot_nn(h1_low, w1_ref[:, c]) + eb_ref[:, c])
        g = g.astype(bf16)
        g_ref[:, c] = g
        d_ref[:, c] = d.astype(bf16)
        moves.write(g_ref.at[:, c], g_hbm.at[w, :, c])
        moves.write(d_ref.at[:, c], d_hbm.at[w, :, c])
        u2 = u2 + dot_nt(g, w2_ref[:, c])
    n2, r2 = centered(u2)
    n2_ref[...] = n2.astype(bf16)
    moves.write(n2_ref, n2_hbm.at[w])
    r_ref[...] = jnp.where(low_half(r_ref.shape), r1, r2)
    moves.write(r_ref, r_hbm.at[w])
    fresh_ref[...] = (n2 * gain_ref[1:2, :] + bias_ref[5:6, :]).astype(bf16)
    moves.finish()


def dense_call(sp, a_all, x_all, wo, w1, w2, gains, biases, eb, bufs):
    rows, width = a_all.shape[1], a_all.shape[2]
    hidden = w1.shape[1]
    row = whole_window(rows, width)
    vmem = lambda *shape: pltpu.VMEM(shape, bf16)
    return call(
        dense_body,
        sp,
        (1,),
        [
            (a_all, row), (x_all, row), (wo, RESIDENT), (w1, RESIDENT), (w2, RESIDENT), (gains, fixed(gains.shape)),
            (biases, fixed(biases.shape)), (eb, fixed(eb.shape)),
        ],
        [(jax.ShapeDtypeStruct((rows, width), bf16), pl.BlockSpec((rows, width), lambda i, sp: (0, 0)))],
        [(b, ANY) for b in bufs],
        [
            vmem(rows, width), vmem(rows, width), vmem(rows, hidden), vmem(rows, hidden), vmem(rows, width),
            pltpu.VMEM((rows, PAIR), f32), pltpu.SemaphoreType.DMA((4 + 2 * (hidden // FF_BLOCK),)),
        ],
        us=10,
    )


def column_sum(v):
    return jnp.sum(v, axis=0, keepdims=True)


def norm_back(dy, n, r, gain):
    dn = dy * gain
    return r * (dn - jnp.mean(dn, axis=1, keepdims=True) - n * jnp.mean(dn * n, axis=1, keepdims=True))


def dense_back_body(
    sp, dy_ref, got_ref, n2_ref, r_ref, gain_ref, sel_ref, wo_ref, w1_ref, w2_ref, d_hbm, n1_hbm, a_hbm,
    rest_hbm, db2_hbm, df_hbm, db1_hbm, st_ref, se_ref, do_ref, dd_ref,
    d_ref, n1_ref, a_ref, rest_ref, db2_ref, df_ref, db1_ref, sems,
):
    w = sp[0]
    width = dy_ref.shape[2]
    moves = Moves(sems)
    parts = chunks(w1_ref.shape[1])
    loads = [moves.start(d_hbm.at[w, :, c], d_ref.at[:, c]) for c in parts]
    last = [
        moves.start(n1_hbm.at[w], n1_ref), moves.start(a_hbm.at[w], a_ref),
        moves.start(rest_hbm.at[w], rest_ref),
    ]
    r = r_ref[0]
    dy = jnp.where(sp[4] == 1, dy_ref[0], got_ref[...]).astype(f32)
    n2 = n2_ref[0].astype(f32)
    du2 = norm_back(dy, n2, r[:, HALF : HALF + 1], gain_ref[1:2, :])
    db2 = du2.astype(bf16)
    db2_ref[...] = db2
    moves.write(db2_ref, db2_hbm.at[w])
    st_ref[0, 2:3, :] = column_sum(du2)
    st_ref[0, 3:4, :] = column_sum(dy)
    st_ref[0, 5:6, :] = column_sum(dy * n2)
    st_ref[0, 6:8, :] = jnp.zeros((2, width), f32)
    dh1 = du2
    for c, load in zip(parts, loads):
        load.wait()
        df = dot_nn(db2, w2_ref[:, c]) * d_ref[:, c].astype(f32)
        se_ref[0, :, c] = column_sum(df)
        df = df.astype(bf16)
        df_ref[:, c] = df
        moves.write(df_ref.at[:, c], df_hbm.at[w, :, c])
        dh1 = dh1 + dot_nt(df, w1_ref[:, c])
    for load in last:
        load.wait()
    n1 = n1_ref[...].astype(f32)
    du1 = norm_back(dh1, n1, r[:, 0:1], gain_ref[0:1, :])
    db1 = du1.astype(bf16)
    db1_ref[...] = db1
    moves.write(db1_ref, db1_hbm.at[w])
    st_ref[0, 0:1, :] = column_sum(du1)
    st_ref[0, 1:2, :] = column_sum(dh1)
    st_ref[0, 4:5, :] = column_sum(dh1 * n1)
    do = dot_nt(db1, wo_ref[...]).astype(bf16)
    do_ref[...] = do
    mixed = do.astype(f32) * (a_ref[...].astype(f32) + rest_ref[...].astype(f32))
    high = mixed.astype(bf16)
    low = (mixed - high.astype(f32)).astype(bf16)
    for begin in range(0, width, PAIR):
        cols = slice(begin, begin + PAIR)
        inner = dot_nn(high[:, cols], sel_ref[...]) + dot_nn(low[:, cols], sel_ref[...])
        dd_ref[:, cols] = split_three(-inner)
    moves.finish()


def dense_back_call(
    sp, dy_all, got, n2_all, r_all, d_all, n1_all, a_all, rest_all, wo, w1, w2, gains, sel, bufs
):
    rows, width = got.shape
    hidden = w1.shape[1]
    row = whole_window(rows, width)
    db2_all, df_all, db1_all, st_all, se_all = bufs
    flat = (jax.ShapeDtypeStruct((rows, width), bf16), pl.BlockSpec((rows, width), lambda i, sp: (0, 0)))
    vmem = lambda *shape: pltpu.VMEM(shape, bf16)
    return call(
        dense_back_body,
        sp,
        (1,),
        [
            (dy_all, row), (got, fixed(got.shape)), (n2_all, row), (r_all, whole_window(rows, PAIR)),
            (gains, fixed(gains.shape)), (sel, fixed(sel.shape)), (wo, RESIDENT), (w1, RESIDENT),
            (w2, RESIDENT),
        ]
        + [(b, ANY) for b in (d_all, n1_all, a_all, rest_all)],
        [flat, flat],
        [
            (db2_all, ANY), (df_all, ANY), (db1_all, ANY), (st_all, whole_window(8, width)),
            (se_all, whole_window(1, hidden)),
        ],
        [
            vmem(rows, hidden), vmem(rows, width), vmem(rows, width), vmem(rows, width), vmem(rows, width),
            vmem(rows, hidden), vmem(rows, width), pltpu.SemaphoreType.DMA((5 + 2 * (hidden // FF_BLOCK),)),
        ],
        us=10,
    )


def attend_back_body(
    sp, q_ref, own_ref, peer_ref, side_ref, hot_ref, m_ref, lse_ref, do_ref, dd_ref, turned_ref,
    cell_ref, dq_ref, keep_ref, send_ref,
):
    rows = q_ref.shape[1]
    total = 2 * rows
    first = sp[2] == 0

    def variant(blocks):
        keys = blocks * KEY_BLOCK
        low = low_half((rows, PAIR))
        key_low = low_half((keys, PAIR))
        block_low = low_half((KEY_BLOCK, PAIR))
        place = lax.broadcasted_iota(jnp.int32, (KEY_BLOCK, PAIR), 1)
        three = jnp.where(place % HALF < 3, 1.0, 0.0).astype(bf16)
        lone = [
            jnp.where(place < 3, 1.0, 0.0).astype(bf16),
            jnp.where((place >= HALF) & (place < HALF + 3), 1.0, 0.0).astype(bf16),
        ]
        side = side_ref[0]
        hot = hot_ref[0, :keys, :]
        for n in range(PAIRS):
            cols = slice(n * PAIR, (n + 1) * PAIR)
            kv = slice(2 * n * PAIR, 2 * (n + 1) * PAIR)
            both = in_order(first, own_ref[0, :, kv], peer_ref[0, :, kv])[:keys]
            k, v = both[:, :PAIR], both[:, PAIR:]
            ks = dot_nn(hot, m_ref[:, cols]).astype(bf16)
            kt = k.T
            q = q_ref[0, :, cols]
            do = do_ref[:, cols]
            dd = dd_ref[:, cols]
            lse = lse_ref[0, :, cols]
            kc = (jnp.where(key_low, k, ks), jnp.where(key_low, ks, k))
            qc = (jnp.where(low, q, side), jnp.where(low, side, q))
            qe = tuple(jnp.concatenate([c, lse], axis=1) for c in qc)
            dc = (jnp.where(low, do, dd), jnp.where(low, dd, do))
            dq = [None, None]
            dks = []
            dvs = []
            gs = []
            for b in range(blocks):
                at = slice(b * KEY_BLOCK, (b + 1) * KEY_BLOCK)
                vb = v[at]
                vc = (jnp.where(block_low, vb, three), jnp.where(block_low, three, vb))
                part_v = []
                part_k = []
                for head in (0, 1):
                    kb = jnp.concatenate([kc[head][at], lone[head]], axis=1)
                    p = jnp.exp(dot_nt(kb, qe[head]))
                    dp = dot_nt(vc[head], dc[head])
                    ds = (p * dp).astype(bf16)
                    part_v.append(dot_nn(p.astype(bf16), do))
                    part_k.append(dot_nn(ds, qc[head]))
                    part = dot_nn(kt[head * HALF : (head + 1) * HALF, at], ds)
                    dq[head] = part if dq[head] is None else dq[head] + part
                dvs.append(jnp.where(block_low, part_v[0], part_v[1]).astype(bf16))
                dks.append(jnp.where(block_low, part_k[0], part_k[1]).astype(bf16))
                gs.append(jnp.where(block_low, part_k[1], part_k[0]).astype(bf16))
            dq_ref[:, cols] = (jnp.concatenate(dq, axis=0).T * score_scale).astype(bf16)
            cell_ref[0, :, cols] = dot_nn(turned_ref[0, :, :keys], jnp.concatenate(gs, axis=0))
            if keys < total:
                zero = [jnp.zeros((total - keys, PAIR), bf16)]
                dks = dks + zero
                dvs = dvs + zero
            grads = jnp.concatenate([jnp.concatenate(dks, axis=0), jnp.concatenate(dvs, axis=0)], axis=1)
            keep_ref[:, kv] = jnp.where(first, grads[:rows], grads[rows:])
            send_ref[:, kv] = jnp.where(first, grads[rows:], grads[:rows])

    for blocks in range(1, total // KEY_BLOCK + 1):
        pl.when(sp[1] == blocks)(functools.partial(variant, blocks))


def attend_back_call(
    sp, q_all, kv_all, peer_all, side_all, hot_all, matrix, lse_all, do, dd, turned_all, cell_all
):
    rows, width = q_all.shape[1], q_all.shape[2]
    cols = PAIRS * PAIR
    part = at_window(rows, cols)
    kv = at_window(rows, 2 * cols)
    flat = columns(rows, cols)
    flat_kv = columns(rows, 2 * cols)
    out_kv = jax.ShapeDtypeStruct((rows, 2 * width), bf16)
    return call(
        attend_back_body,
        sp,
        (width // cols,),
        [
            (q_all, part),
            (kv_all, kv),
            (peer_all, kv),
            (side_all, whole_window(rows, PAIR)),
            (hot_all, whole_window(2 * rows, PAIR)),
            (matrix, columns(PAIR, cols)),
            (lse_all, part),
            (do, flat),
            (dd, flat),
            (turned_all, whole_window(HALF, 2 * rows)),
        ],
        [(jax.ShapeDtypeStruct((rows, width), bf16), flat), (out_kv, flat_kv), (out_kv, flat_kv)],
        [(cell_all, at_window(HALF, cols))],
        us=20,
    )


def input_back_body(
    sp, dq_ref, own_ref, got_ref, db1_ref, w_ref, dj_ref, sj_ref, fresh_ref, total
):
    step = pl.program_id(0)
    dq = dq_ref[...]
    cols = dq.shape[1]
    both = own_ref[...].astype(f32) + got_ref[...].astype(f32)
    part = lambda at: jnp.concatenate(
        [both[:, p + at : p + at + PAIR] for p in range(0, 2 * cols, 2 * PAIR)], axis=1
    )
    dk = part(0).astype(bf16)
    dv32 = part(PAIR)
    dv = dv32.astype(bf16)
    dj_ref[0, :, :cols] = dq
    dj_ref[0, :, cols : 2 * cols] = dk
    dj_ref[0, :, 2 * cols :] = dv
    sj_ref[0] = jnp.concatenate(
        [column_sum(dq.astype(f32)), column_sum(dv32), jnp.zeros((6, cols), f32)], axis=0
    )
    width = w_ref.shape[0]
    dx = None
    for j, value in enumerate((dq, dk, dv)):
        at = pl.ds(pl.multiple_of(j * width + step * cols, cols), cols)
        term = dot_nt(value, w_ref[:, at])
        dx = term if dx is None else dx + term

    @pl.when(step == 0)
    def _():
        total[...] = dx + db1_ref[0].astype(f32)

    @pl.when(step > 0)
    def _():
        total[...] += dx

    @pl.when(step == pl.num_programs(0) - 1)
    def _():
        fresh_ref[...] = total[...].astype(bf16)


def input_back_call(sp, dq, own, got, db1_all, weight, dj_all, sj_all):
    rows, width = dq.shape
    cols = PAIRS * PAIR
    steps = width // cols
    return call(
        input_back_body,
        sp,
        (steps,),
        [
            (dq, columns(rows, cols)), (own, columns(rows, 2 * cols)), (got, columns(rows, 2 * cols)),
            (db1_all, whole_window(rows, width)), (weight, RESIDENT),
        ],
        [(jax.ShapeDtypeStruct((rows, width), bf16), pl.BlockSpec((rows, width), lambda i, sp: (0, 0)))],
        [
            (dj_all, at_window(rows, 3 * cols)), (sj_all, at_window(8, cols)),
        ],
        [pltpu.VMEM((rows, width), f32)],
        us=4,
    )


def weight_body(splits, sp, *refs):
    count = len(splits)
    lefts, rights = refs[:count], refs[count : 2 * count]
    give_ref, keep_ref = refs[2 * count : 2 * count + 2]
    turned = refs[2 * count + 2 :]
    step = pl.program_id(0)
    windows, rows, half = lefts[0].shape[0], lefts[0].shape[1], lefts[0].shape[2] // 2
    first = sp[2] == 0

    @pl.when(step == 0)
    def _():
        for left, scratch in zip(lefts, turned):
            for w in range(windows):
                at = slice(w * rows, (w + 1) * rows)
                low, high = left[w, :, :half], left[w, :, half:]
                scratch[:half, at] = jnp.where(first, high, low).T
                scratch[half:, at] = jnp.where(first, low, high).T

    for (begin, end), right, scratch in zip(splits, rights, turned):

        @pl.when((step >= begin) & (step < end))
        def _(right=right, scratch=scratch):
            out = dot_nn(scratch[...], right[...].reshape(windows * rows, right.shape[2])).astype(bf16)
            give_ref[...] = out[:half]
            keep_ref[...] = out[half:]


def weight_call(sp, windows, pairs):
    rows, width = pairs[0][0].shape[1:]
    splits = []
    begin = 0
    for _, right in pairs:
        splits.append((begin, begin + right.shape[2] // FF_BLOCK))
        begin = splits[-1][1]

    def left_spec():
        return pl.BlockSpec(
            (windows, rows, width), lambda i, sp: (0, 0, 0), pipeline_mode=pl.Buffered(1)
        )

    def right_spec(begin, end):
        return pl.BlockSpec(
            (windows, rows, FF_BLOCK), lambda i, sp: (0, 0, jnp.clip(i - begin, 0, end - begin - 1))
        )

    half = (
        jax.ShapeDtypeStruct((width // 2, begin * FF_BLOCK), bf16), columns(width // 2, FF_BLOCK)
    )
    return call(
        functools.partial(weight_body, tuple(splits)),
        sp,
        (begin,),
        [(left, left_spec()) for left, _ in pairs]
        + [(right, right_spec(*split)) for (_, right), split in zip(pairs, splits)],
        [half, half],
        [],
        [pltpu.VMEM((width, windows * rows), bf16)] * len(pairs),
        us=12,
    )


def spread_body(moves, sp, mine_ref, got_ref, *out_refs):
    half = pl.num_programs(0) // 2
    mine = (pl.program_id(0) // half) == sp[2]
    value = jnp.where(mine, mine_ref[...], got_ref[...]).astype(f32)
    for (out, to), begin, count in moves:
        out_refs[out][:, to : to + count] = value[:, begin : begin + count]


def spread_call(sp, mine, got, widths, moves):
    half, cols = mine.shape
    block = half // 4
    turn = lambda i, sp, core: jnp.where(i // 4 == core, i % 4, jnp.where(core == 0, 3, 0))
    return call(
        functools.partial(spread_body, moves),
        sp,
        (8,),
        [
            (mine, pl.BlockSpec((block, cols), lambda i, sp: (turn(i, sp, sp[2]), 0))),
            (got, pl.BlockSpec((block, cols), lambda i, sp: (turn(i, sp, 1 - sp[2]), 0))),
        ],
        [
            (jax.ShapeDtypeStruct((2 * half, w), f32), pl.BlockSpec((block, w), lambda i, sp: (i, 0)))
            for w in widths
        ],
        [],
        us=5,
    )


def bucket_maps(position_cells, counts):
    key = jnp.arange(HALF, dtype=jnp.int32)[:, None]
    query = jnp.arange(HALF, dtype=jnp.int32)[None, :]
    begins = (0, position_cells, position_cells + GRID, HALF)
    bucket = jnp.full((HALF, HALF), -1, jnp.int32)
    base = 0
    for j, offset in enumerate((counts[0] // 2, GRID - 1, GRID - 1)):
        inside = (key >= begins[j]) & (key < begins[j + 1]) & (query >= begins[j]) & (query < begins[j + 1])
        ids = jnp.clip(query - key, -offset, counts[j] - 1 - offset) + offset + base
        bucket = jnp.where(inside, ids, bucket)
        base += counts[j]
    return bucket[:, :, None] == jnp.arange(base, dtype=jnp.int32)


def cell_matrix(tables, maps, position_cells):
    whole = jnp.concatenate(tables, axis=0)
    heads = whole.shape[1]
    whole = whole.reshape(-1, heads // 2, 2)[:, :, ::-1].reshape(-1, heads)
    m = jnp.einsum("bh,xcb->xhc", whole, maps.astype(bf16), preferred_element_type=f32)
    m = m.reshape(HALF, heads * HALF).astype(bf16)
    lane = jnp.arange(heads * HALF, dtype=jnp.int32) % HALF
    dead = jnp.where(lane < position_cells, masked, 0.0).astype(bf16)[None]
    return jnp.concatenate([m, dead, jnp.zeros((HALF - 1, heads * HALF), bf16)], axis=0)


def table_grads(cells, maps, counts):
    heads = cells.shape[1] // HALF
    whole = jnp.einsum(
        "xcb,xhc->bh", maps.astype(f32), cells.reshape(HALF, heads, HALF), precision=lax.Precision.HIGHEST
    )
    whole = whole.reshape(-1, heads // 2, 2)[:, :, ::-1].reshape(-1, heads)
    a, b = counts[0], counts[0] + counts[1]
    return [whole[:a], whole[a:b], whole[b:]]


class Ring:
    def __init__(self, count):
        self.count = count
        self.index = lax.axis_index("dp")
        bits = list(range(1, count.bit_length() - 1))
        turned = bits[:2][::-1] + bits[2:]
        self.steps = list(zip(bits, turned))

    def bit(self, step):
        even, odd = step
        return jnp.where(self.index % 2 == 0, (self.index >> even) & 1, (self.index >> odd) & 1)

    def send(self, a, step):
        even, odd = step
        pairs = [(i, i ^ (1 << (even if i % 2 == 0 else odd))) for i in range(self.count)]
        return lax.ppermute(a, "dp", pairs)

    def swap(self, a):
        return lax.ppermute(a, "dp", [(i, i ^ 1) for i in range(self.count)])

    def reduce(self, part):
        for step in self.steps:
            half = part.shape[0] // 2
            bit = self.bit(step)
            keep = lax.dynamic_slice_in_dim(part, bit * half, half, 0)
            give = lax.dynamic_slice_in_dim(part, (1 - bit) * half, half, 0)
            part = keep + self.send(give, step)
        return part

    def gather(self, part):
        for step in self.steps[::-1]:
            first = self.bit(step) == 0
            got = self.send(part, step)
            part = jnp.concatenate(
                [jnp.where(first, part, got), jnp.where(first, got, part)], axis=0
            )
        return part

    def whole(self, part):
        got = self.swap(part).astype(f32)
        part = part.astype(f32)
        first = self.index % 2 == 0
        return jnp.concatenate([jnp.where(first, part, got), jnp.where(first, got, part)], axis=0)

    def total(self, part):
        for bit in range(self.count.bit_length() - 1):
            part = part + lax.ppermute(part, "dp", [(i, i ^ (1 << bit)) for i in range(self.count)])
        return part


SLOTS = (
    ("F", 0, None),
    ("F", 1, 0),
    ("B", None, 0),
    ("F", 2, 1),
    ("B", 0, 1),
    ("F", 3, 2),
    ("B", 1, 2),
    ("F", None, 3),
    ("B", 2, 3),
    ("B", 3, None),
)


def on_device(
    boundary, doc_lengths, horizontal, vertical, attention_in, attention_out, expand_weight,
    contract_weight, norm_gains, bias_rows, expand_bias, position_table, horizontal_table,
    vertical_table,
):
    section = lax.axis_index("section")
    dp_count = lax.axis_size("dp")
    core = lax.axis_index("dp") % 2
    swap = [(i, i ^ 1) for i in range(dp_count)]
    exchange = lambda a: lax.ppermute(a, "dp", swap)

    own = boundary[0]
    micro, slots, width = own.shape
    rows = slots // 2
    windows = 2 * micro
    hidden = expand_weight.shape[2]
    heads = position_table.shape[2]
    pairs = heads // 2
    w_in, w_out, w1, w2 = in_vmem([attention_in[0], attention_out[0], expand_weight[0], contract_weight[0]])
    gains = norm_gains[0].astype(f32)
    biases = bias_rows[0].astype(f32)
    eb = expand_bias.astype(f32)
    in_bias = jnp.concatenate([biases[0], jnp.zeros_like(biases[0]), biases[1]])[None]
    tables = (position_table[0], horizontal_table[0], vertical_table[0])
    counts = tuple(t.shape[0] for t in tables)
    position_cells = slots // SPAN
    maps = bucket_maps(position_cells, counts)
    ring = Ring(dp_count)

    def both(mine, theirs):
        return jnp.concatenate(
            [jnp.where(core == 0, mine, theirs), jnp.where(core == 0, theirs, mine)], axis=0
        )

    halves = own.reshape(micro, 2, rows, width)
    own_half = jnp.where(core == 0, halves[:, 0], halves[:, 1])
    other_half = jnp.where(core == 0, halves[:, 1], halves[:, 0])
    spare = lambda a: jnp.concatenate([a, a[:1]], axis=0)
    own_all = spare(both(own_half, exchange(other_half)))
    places = jnp.concatenate(
        [horizontal, vertical, jnp.broadcast_to(doc_lengths[:, None], (micro, PAIR))], axis=1
    )
    places = spare(both(places, exchange(places)))
    across_cell = places[:, :slots] // SPAN
    down_cell = places[:, slots : 2 * slots] // SPAN
    lengths = places[:, 2 * slots]
    ids = jnp.arange(slots, dtype=jnp.int32)
    position_cell = jnp.broadcast_to((ids // SPAN)[None], (windows + 1, slots))

    def hot_of(cells, lanes, axis):
        p, a, d = (jnp.expand_dims(c, axis) for c in cells)
        lanes = jnp.expand_dims(lanes, (0, 3 - axis))
        return (lanes == p) | (lanes == a + position_cells) | (lanes == d + position_cells + GRID)

    cells = (position_cell, across_cell, down_cell)
    cell_ids = jnp.arange(PAIR, dtype=jnp.int32)
    turned_all = hot_of(cells, cell_ids[:HALF], 1).astype(bf16)
    dead = (ids[None, :] >= lengths[:, None])[:, :, None] & (cell_ids == HALF)
    hot_all = (hot_of(cells, cell_ids, 2) | dead).astype(bf16)
    take = lambda c: jnp.where(core == 0, c[:, :rows], c[:, rows:])
    side_all = hot_of(tuple(take(c) for c in cells), cell_ids % HALF, 2).astype(bf16)
    matrix = cell_matrix(tables, maps, position_cells)

    sel = (cell_ids[:, None] // HALF != cell_ids[None, :] // HALF).astype(bf16)

    blocks_of = (lengths + KEY_BLOCK - 1) // KEY_BLOCK
    blocks_of = jnp.where(jnp.arange(windows + 1) < windows, blocks_of, 0)
    infos = []
    for _, zero, one in SLOTS:
        w = jnp.where(
            section == 0, windows if zero is None else zero, windows if one is None else one
        ).astype(jnp.int32)
        infos.append(jnp.stack([w, blocks_of[w], core.astype(jnp.int32), lengths[w], section.astype(jnp.int32)]))

    widths = dict(
        x=width, q=width, kv=2 * width, a=width, rest=width, lse=width, peer=2 * width, n1=width, h1=width,
        g=hidden, d=hidden, n2=width, db2=width, df=hidden, db1=width, dj=3 * width,
    )
    shapes = {n: jax.ShapeDtypeStruct((windows + 1, rows, c), bf16) for n, c in widths.items()}
    shapes["r"] = jax.ShapeDtypeStruct((windows + 1, rows, PAIR), f32)
    shapes["st"] = shapes["sj"] = jax.ShapeDtypeStruct((windows + 1, 8, width), f32)
    shapes["se"] = jax.ShapeDtypeStruct((windows + 1, 1, hidden), f32)
    shapes["cell"] = jax.ShapeDtypeStruct((windows + 1, HALF, width), f32)
    st = dict(zip(shapes, unwritten(list(shapes.values()))))

    def forward(sp, s, got):
        x, q, kv, fresh = qkv_call(sp, own_all, got, w_in, in_bias, s["x"], s["q"], s["kv"])
        s = dict(s, x=x, q=q, kv=kv)
        mixed = ("a", "rest", "lse", "peer")
        s.update(
            zip(mixed, attend_call(
                sp, q, fresh, exchange(fresh), side_all, hot_all, matrix, tuple(s[n] for n in mixed)
            ))
        )
        names = ("n1", "h1", "g", "d", "n2", "r")
        outs = dense_call(
            sp, s["a"], x, w_out, w1, w2, gains, biases, eb, tuple(s[n] for n in names)
        )
        s.update(zip(names, outs[:-1]))
        return s, outs[-1]

    def dense_back(sp, s, got):
        names = ("db2", "df", "db1", "st", "se")
        outs = dense_back_call(
            sp, own_all, got, s["n2"], s["r"], s["d"], s["n1"], s["a"], s["rest"], w_out, w1, w2, gains,
            sel, tuple(s[n] for n in names),
        )
        s = dict(s)
        s.update(zip(names, outs[:5]))
        return s, tuple(outs[5:])

    def attend_back(sp, s, grads):
        cell, dq, keep, send = attend_back_call(
            sp, s["q"], s["kv"], s["peer"], side_all, hot_all, matrix, s["lse"], *grads, turned_all,
            s["cell"],
        )
        s = dict(s, cell=cell)
        dj, sj, fresh = input_back_call(
            sp, dq, keep, exchange(send), s["db1"], w_in, s["dj"], s["sj"]
        )
        return dict(s, dj=dj, sj=sj), fresh

    got = {}
    finals = {}
    grads_in = {}
    nothing = jnp.zeros((rows, width), bf16)

    for number, (kind, zero, one) in enumerate(SLOTS[:-1]):
        sp = infos[number]
        if kind == "F":
            st, out = forward(sp, st, got.pop(("F", one), nothing))
            if one is not None:
                finals[one] = out
            if zero is not None:
                got["F", zero] = lax.ppermute(out, "section", [(0, 1)])
        else:
            st, grads = dense_back(sp, st, got.pop(("B", zero), nothing))
            st, out = attend_back(sp, st, grads)
            if zero is not None:
                grads_in[zero] = out
            if one is not None:
                got["B", one] = lax.ppermute(out, "section", [(1, 0)])

    sp = infos[-1]
    barrier = lax.optimization_barrier

    def start_sum(pairs):
        give, keep = weight_call(sp, windows, pairs)
        return keep + exchange(give)

    def spread(part, widths, moves):
        return spread_call(sp, part, exchange(part), widths, moves)

    st, grads = dense_back(sp, st, got.pop(("B", SLOTS[-1][1])))
    sums_contract = start_sum([(st["db2"], st["g"])])
    sums_expand = start_sum([(st["h1"], st["df"])])
    grads, sums_contract, sums_expand = barrier((grads, sums_contract, sums_expand))
    sums_contract = ring.reduce(sums_contract)
    sums_expand = ring.reduce(sums_expand)
    st, grads_in[SLOTS[-1][1]] = attend_back(sp, st, grads)
    sums_attend = ring.reduce(start_sum([(st["x"], st["dj"]), (st["a"], st["db1"])]))
    natural = [((0, 0), 0, hidden)]
    (g_contract,) = spread(ring.gather(sums_contract), [hidden], natural)
    (g_expand,) = spread(ring.gather(sums_expand), [hidden], natural)
    cols = PAIRS * PAIR
    moves = [
        ((0, j * width + i * cols), (3 * i + j) * cols, cols) for i in range(width // cols) for j in range(3)
    ] + [((1, 0), 3 * width, width)]
    g_in, g_out = spread(ring.gather(sums_attend), [3 * width, width], moves)

    sums = jnp.sum(st["st"][:windows], axis=0)
    joined_sums = jnp.sum(st["sj"][:windows], axis=0)
    wide = jnp.sum(st["se"][:windows], axis=0)
    small = [
        joined_sums[0:2], sums[0:6], wide,
    ] + table_grads(jnp.sum(st["cell"][:windows], axis=0), maps, counts)
    packed = jnp.concatenate([s.reshape(-1) for s in small])
    size = packed.shape[0]
    packed = jnp.pad(packed, (0, -size % 1024)).reshape(-1, PAIR)
    packed = ring.total(packed).reshape(-1)
    pieces = []
    begin = 0
    for s in small:
        count = math.prod(s.shape)
        pieces.append(packed[begin : begin + count].reshape(s.shape))
        begin += count
    joined_sums, sums, wide, table_p, table_h, table_v = pieces
    grad_bias = jnp.concatenate([joined_sums, sums[0:4]], axis=0)
    grad_gain = sums[4:6]

    result = [jnp.where(section == 0, grads_in[w], finals[w]) for w in range(windows)]
    mine_first, mine_second = jnp.stack(result[:micro]), jnp.stack(result[micro:])
    keep = jnp.where(core == 0, mine_first, mine_second)
    give = exchange(jnp.where(core == 0, mine_second, mine_first))
    out_halves = jnp.stack(
        [jnp.where(core == 0, keep, give), jnp.where(core == 0, give, keep)], axis=1
    )
    boundary_out = out_halves.reshape(1, micro, slots, width)
    return (
        boundary_out, g_in[None], g_out[None], g_expand[None], g_contract[None], grad_gain[None], grad_bias[None], wide,
        table_p[None], table_h[None], table_v[None],
    )


def solution(mesh):
    section = P("section", None, None)
    placed = (
        P("section", "dp", None, None), P("dp"), P("dp", None), P("dp", None), section, section,
        section, section, section, section, P("section", None), section, section, section,
    )
    return jax.shard_map(
        on_device,
        mesh=mesh,
        in_specs=placed,
        out_specs=(
            P("section", "dp", None, None), section, section, section, section, section, section,
            P("section", None), section, section, section,
        ),
        check_vma=False,
    )
```

time: 944 us -> 1040 us (1.10)
  local copies, waits for them, and re-layouts: 42.1 us -> 293 us
  waiting for transfers between devices: 283 us -> 170 us
  matrix products: 62.7 us -> 3.74 us
  Pallas kernels: 369 us -> 415 us
  other arithmetic: 99.7 us -> 60.9 us
  starting transfers between devices: 68.4 us -> 87.1 us
    unnamed x138 -> x617, local copies, waits for them, and re-layouts: 12.5 us -> 251 us
    ppermute x10 -> x8, waiting for transfers between devices: 109 us -> 41.5 us  [the longest x4 26.2 us: on_device(): got['B', one] = lax.ppermute(out, 'section', [(1, 0)])]
    dot_general x8 -> x0, matrix products: 59 us -> none  [lax.dot_general(a, b, (((0,), (0,)), ((), ())), preferred_element_type=f32)]
    pallas_call x24 -> x36, Pallas kernels: 369 us -> 414 us  [call(): pl.pallas_call(run, grid_spec=pltpu.PrefetchScalarGridSpec(num_scalar_pre...]
    ppermute x18, waiting for transfers between devices: 156 us -> 124 us  [send(): return lax.ppermute(a, 'dp', pairs)]
    ppermute x18, starting transfers between devices: 9.4 us -> 38 us  [send(): return lax.ppermute(a, 'dp', pairs)]
    ppermute x10 -> x8, starting transfers between devices: 55.2 us -> 26.9 us  [the longest x4 21.8 us: on_device(): got['F', zero] = lax.ppermute(out, 'section', [(0, 1)])]
    broadcast_in_dim x4 -> x0, other arithmetic: 20.2 us -> none  [the longest x1 7.73 us: on_device(): g_expand[None]]
  transfers between devices with their start and end apart: 48 -> 49, of which waited for: 25 -> 14; matrix products, arithmetic and copies ran while one was open for 18% -> 9% of each run, Pallas kernels for 7% -> 26%
where the time goes in v2:
time: 1040 us; the launch traced here: 1030 us
  Pallas kernels  415 us (40%)
  local copies, waits for them, and re-layouts  293 us (28%)
  waiting for transfers between devices  170 us (16%)
  starting transfers between devices  87.1 us (8%)
  other arithmetic  60.9 us (6%)
    pallas_call x36, Pallas kernels, call(): pl.pallas_call(run, grid_spec=pltpu.PrefetchScalarGridSpec(num_scalar_pre...  414 us
    unnamed x617, local copies, waits for them, and re-layouts  251 us
    ppermute x18, waiting for transfers between devices, send(): return lax.ppermute(a, 'dp', pairs)  124 us
    ppermute x18, starting transfers between devices, send(): return lax.ppermute(a, 'dp', pairs)  38 us
    ppermute x4, waiting for transfers between devices, on_device(): got['B', one] = lax.ppermute(out, 'section', [(1, 0)])  26.2 us
    ppermute x4, starting transfers between devices, on_device(): got['F', zero] = lax.ppermute(out, 'section', [(0, 1)])  21.8 us
  transfers between devices with their start and end apart: 49, of which 14 were waited for; matrix products, arithmetic and copies ran while one was open for 9% of the time, Pallas kernels for 26%

profile of v2, /device:TPU:0, one launch (start us, length us, event | category | flops | bytes accessed | tf_op | source)
XLA Modules:
  0.0 1033.3 jit_solution(3563096733315199809)
XLA Ops:
  86.5 12.3 %shard_map.224 = (bf16[5,512,768]{2,1,0:T(8,128)(2,1)S(1)}, bf16[5,512,768]{2,1,0:T(8,128)(2,1)S(1)}, bf16[5,512,768]{2,1,0:T(8,128)(2,1)}, bf16[5,512,1536]{2,1,0:T(8,128)(2,1)}) custom-call(s32[5]{0:T(128)S(1)} %stack.120.sp_ref, bf16[5,512,768]{2,1,0:T(8,128)(2,1)} %copy-done.86, ...), custom_call_target="tpu_custom_call", output_to_operand_aliasing={{0}: (7, {}), {1}: (8, {}), {2}: (9, {}), {3}: (10, {})} | custom-call | flops 14000000000 | bytes 14000000 | tf_op jit(solution)/shard_map/pallas_call | solution.py:76
  104.3 15.0 %shard_map.225 = (bf16[5,512,768]{2,1,0:T(8,128)(2,1)S(1)}, bf16[5,512,768]{2,1,0:T(8,128)(2,1)S(1)}, bf16[5,512,3072]{2,1,0:T(8,128)(2,1)}, bf16[5,512,3072]{2,...) custom-call(s32[5]{0:T(128)S(1)} %stack.120.sp_ref, ...), custom_call_target="tpu_custom_call", output_to_operand_aliasing={{0}: (9, {}), {1}: (10, {}), {2}: (11, {}), {3}: (12, {}), ... | custom-call | flops 10000000000 | bytes 10000000 | tf_op jit(solution)/shard_map/pallas_call | solution.py:76
  127.6 15.4 %collective-permute-done.3.refs_1_ = bf16[512,768]{1,0:T(8,128)(2,1)} collective-permute-done((bf16[512,768]{1,0:T(8,128)(2,1)}, bf16[512,768]{1,0:T(8,128)(2,1)}, u32[]{:S(2)}, u32[]{:S(2)}) %collective-permute-start.3) | collective-permute-done | bytes 786464 | tf_op jit(solution)/shard_map/ppermute | solution.py:938
  188.8 15.0 %shard_map.228 = (bf16[5,512,768]{2,1,0:T(8,128)(2,1)S(1)}, bf16[5,512,768]{2,1,0:T(8,128)(2,1)S(1)}, bf16[5,512,3072]{2,1,0:T(8,128)(2,1)}, bf16[5,512,3072]{2,...) custom-call(s32[5]{0:T(128)S(1)} %stack.118.sp_ref, ...), custom_call_target="tpu_custom_call", output_to_operand_aliasing={{0}: (9, {}), {1}: (10, {}), {2}: (11, {}), {3}: (12, {}), ... | custom-call | flops 10000000000 | bytes 10000000 | tf_op jit(solution)/shard_map/pallas_call | solution.py:76
  214.4 14.9 %shard_map.231 = (bf16[5,512,768]{2,1,0:T(8,128)(2,1)S(1)}, bf16[5,512,3072]{2,1,0:T(8,128)(2,1)}, bf16[5,512,768]{2,1,0:T(8,128)(2,1)S(1)}, f32[5,8,768]{2,1,0:...) custom-call(s32[5]{0:T(128)S(1)} %stack.122.sp_ref, ...), custom_call_target="tpu_custom_call", output_to_operand_aliasing={{0}: (14, {}), {1}: (15, {}), {2}: (16, {}), {3}: (17, {}),... | custom-call | flops 10000000000 | bytes 10000000 | tf_op jit(solution)/shard_map/pallas_call | solution.py:76
  242.6 10.5 %shard_map.232 = (f32[5,64,768]{2,1,0:T(8,128)S(1)}, bf16[512,768]{1,0:T(8,128)(2,1)S(1)}, bf16[512,1536]{1,0:T(8,128)(2,1)S(1)}, bf16[512,1536]{1,0:T(8,128)(2,1)}) custom-call(s32[5]{0:T(128)S(1)} %stack.122.sp_ref, bf16[5,512,768]{2,1,0:T(8,128)(2,1)S(1)} %copy-done.89, ...), custom_call_target="tpu_custom_call", output_to_operand_aliasing={{0}: (11, {})} | custom-call | flops 20000000000 | bytes 20000000 | tf_op jit(solution)/shard_map/pallas_call | solution.py:76
  291.3 14.0 %shard_map.230 = (bf16[5,512,768]{2,1,0:T(8,128)(2,1)S(1)}, bf16[5,512,768]{2,1,0:T(8,128)(2,1)S(1)}, bf16[5,512,768]{2,1,0:T(8,128)(2,1)}, bf16[5,512,1536]{2,1,0:T(8,128)(2,1)}) custom-call(s32[5]{0:T(128)S(1)} %copy-done.266, bf16[5,512,768]{2,1,0:T(8,128)(2,1)} %copy-done.91, ...), custom_call_target="tpu_custom_call", output_to_operand_aliasing={{0}: (7, {}), {1}: (8, {}), {2}: (9, {}), {3}: (10, {})} | custom-call | flops 14000000000 | bytes 14000000 | tf_op jit(solution)/shard_map/pallas_call | solution.py:76
  311.4 15.4 %shard_map.234 = (bf16[5,512,768]{2,1,0:T(8,128)(2,1)S(1)}, bf16[5,512,768]{2,1,0:T(8,128)(2,1)S(1)}, bf16[5,512,3072]{2,1,0:T(8,128)(2,1)}, bf16[5,512,3072]{2,...) custom-call(s32[5]{0:T(128)S(1)} %copy-done.266, ...), custom_call_target="tpu_custom_call", output_to_operand_aliasing={{0}: (9, {}), {1}: (10, {}), {2}: (11, {}), {3}: (12, {}), ... | custom-call | flops 10000000000 | bytes 10000000 | tf_op jit(solution)/shard_map/pallas_call | solution.py:76
  337.5 14.8 %shard_map.235 = (bf16[5,512,768]{2,1,0:T(8,128)(2,1)S(1)}, bf16[5,512,3072]{2,1,0:T(8,128)(2,1)}, bf16[5,512,768]{2,1,0:T(8,128)(2,1)S(1)}, f32[5,8,768]{2,1,0:...) custom-call(s32[5]{0:T(128)S(1)} %stack.114.sp_ref, ...), custom_call_target="tpu_custom_call", output_to_operand_aliasing={{0}: (14, {}), {1}: (15, {}), {2}: (16, {}), {3}: (17, {}),... | custom-call | flops 10000000000 | bytes 10000000 | tf_op jit(solution)/shard_map/pallas_call | solution.py:76
  360.9 17.9 %shard_map.236 = (f32[5,64,768]{2,1,0:T(8,128)S(1)}, bf16[512,768]{1,0:T(8,128)(2,1)S(1)}, bf16[512,1536]{1,0:T(8,128)(2,1)S(1)}, bf16[512,1536]{1,0:T(8,128)(2,1)}) custom-call(s32[5]{0:T(128)S(1)} %stack.114.sp_ref, bf16[5,512,768]{2,1,0:T(8,128)(2,1)S(1)} %copy-done.92, ...), custom_call_target="tpu_custom_call", output_to_operand_aliasing={{0}: (11, {})} | custom-call | flops 20000000000 | bytes 20000000 | tf_op jit(solution)/shard_map/pallas_call | solution.py:76
  417.0 11.9 %shard_map.239 = (bf16[5,512,768]{2,1,0:T(8,128)(2,1)S(1)}, bf16[5,512,768]{2,1,0:T(8,128)(2,1)S(1)}, bf16[5,512,768]{2,1,0:T(8,128)(2,1)}, bf16[5,512,1536]{2,1,0:T(8,128)(2,1)}) custom-call(s32[5]{0:T(128)S(1)} %copy-done.268, bf16[5,512,768]{2,1,0:T(8,128)(2,1)} %copy-done.94, ...), custom_call_target="tpu_custom_call", output_to_operand_aliasing={{0}: (7, {}), {1}: (8, {}), {2}: (9, {}), {3}: (10, {})} | custom-call | flops 14000000000 | bytes 14000000 | tf_op jit(solution)/shard_map/pallas_call | solution.py:76
  435.0 15.2 %shard_map.240 = (bf16[5,512,768]{2,1,0:T(8,128)(2,1)S(1)}, bf16[5,512,768]{2,1,0:T(8,128)(2,1)S(1)}, bf16[5,512,3072]{2,1,0:T(8,128)(2,1)}, bf16[5,512,3072]{2,...) custom-call(s32[5]{0:T(128)S(1)} %copy-done.268, ...), custom_call_target="tpu_custom_call", output_to_operand_aliasing={{0}: (9, {}), {1}: (10, {}), {2}: (11, {}), {3}: (12, {}), ... | custom-call | flops 10000000000 | bytes 10000000 | tf_op jit(solution)/shard_map/pallas_call | solution.py:76
  464.1 14.8 %shard_map.241 = (bf16[5,512,768]{2,1,0:T(8,128)(2,1)S(1)}, bf16[5,512,3072]{2,1,0:T(8,128)(2,1)}, bf16[5,512,768]{2,1,0:T(8,128)(2,1)S(1)}, f32[5,8,768]{2,1,0:...) custom-call(s32[5]{0:T(128)S(1)} %stack.125.sp_ref, ...), custom_call_target="tpu_custom_call", output_to_operand_aliasing={{0}: (14, {}), {1}: (15, {}), {2}: (16, {}), {3}: (17, {}),... | custom-call | flops 10000000000 | bytes 10000000 | tf_op jit(solution)/shard_map/pallas_call | solution.py:76
  487.6 13.2 %shard_map.242 = (f32[5,64,768]{2,1,0:T(8,128)S(1)}, bf16[512,768]{1,0:T(8,128)(2,1)S(1)}, bf16[512,1536]{1,0:T(8,128)(2,1)S(1)}, bf16[512,1536]{1,0:T(8,128)(2,1)}) custom-call(s32[5]{0:T(128)S(1)} %stack.125.sp_ref, bf16[5,512,768]{2,1,0:T(8,128)(2,1)S(1)} %copy-done.95, ...), custom_call_target="tpu_custom_call", output_to_operand_aliasing={{0}: (11, {})} | custom-call | flops 20000000000 | bytes 20000000 | tf_op jit(solution)/shard_map/pallas_call | solution.py:76
  548.7 14.5 %shard_map.246 = (bf16[5,512,768]{2,1,0:T(8,128)(2,1)S(1)}, bf16[5,512,768]{2,1,0:T(8,128)(2,1)S(1)}, bf16[5,512,3072]{2,1,0:T(8,128)(2,1)}, bf16[5,512,3072]{2,...) custom-call(s32[5]{0:T(128)S(1)} %copy-done.264, ...), custom_call_target="tpu_custom_call", output_to_operand_aliasing={{0}: (9, {}), {1}: (10, {}), {2}: (11, {}), {3}: (12, {}), ... | custom-call | flops 10000000000 | bytes 10000000 | tf_op jit(solution)/shard_map/pallas_call | solution.py:76
  569.9 15.2 %shard_map.247 = (bf16[5,512,768]{2,1,0:T(8,128)(2,1)S(1)}, bf16[5,512,3072]{2,1,0:T(8,128)(2,1)}, bf16[5,512,768]{2,1,0:T(8,128)(2,1)S(1)}, f32[5,8,768]{2,1,0:...) custom-call(s32[5]{0:T(128)S(1)} %stack.131.sp_ref, ...), custom_call_target="tpu_custom_call", output_to_operand_aliasing={{0}: (14, {}), {1}: (15, {}), {2}: (16, {}), {3}: (17, {}),... | custom-call | flops 10000000000 | bytes 10000000 | tf_op jit(solution)/shard_map/pallas_call | solution.py:76
  592.5 21.0 %shard_map.248 = (f32[5,64,768]{2,1,0:T(8,128)S(1)}, bf16[512,768]{1,0:T(8,128)(2,1)S(1)}, bf16[512,1536]{1,0:T(8,128)(2,1)S(1)}, bf16[512,1536]{1,0:T(8,128)(2,1)S(1)}) custom-call(s32[5]{0:T(128)S(1)} %stack.131.sp_ref, bf16[5,512,768]{2,1,0:T(8,128)(2,1)S(1)} %copy-done.98, ...), custom_call_target="tpu_custom_call", output_to_operand_aliasing={{0}: (11, {})} | custom-call | flops 20000000000 | bytes 20000000 | tf_op jit(solution)/shard_map/pallas_call | solution.py:76
  625.5 26.2 %collective-permute-done.18.refs_1_ = bf16[512,768]{1,0:T(8,128)(2,1)} collective-permute-done((bf16[512,768]{1,0:T(8,128)(2,1)}, bf16[512,768]{1,0:T(8,128)(2,1)}, u32[]{:S(2)}, u32[]{:S(2)}) %collective-permute-start.18) | collective-permute-done | bytes 786464 | tf_op jit(solution)/shard_map/ppermute | solution.py:945
  661.0 14.7 %shard_map.250 = (bf16[5,512,768]{2,1,0:T(8,128)(2,1)S(1)}, bf16[5,512,3072]{2,1,0:T(8,128)(2,1)}, bf16[5,512,768]{2,1,0:T(8,128)(2,1)S(1)}, f32[5,8,768]{2,1,0:...) custom-call(s32[5]{0:T(128)S(1)} %stack.136.sp_ref, ...), custom_call_target="tpu_custom_call", output_to_operand_aliasing={{0}: (14, {}), {1}: (15, {}), {2}: (16, {}), {3}: (17, {}),... | custom-call | flops 10000000000 | bytes 10000000 | tf_op jit(solution)/shard_map/pallas_call | solution.py:76
  684.2 15.1 %shard_map.251 = (bf16[384,3072]{1,0:T(8,128)(2,1)}, bf16[384,3072]{1,0:T(8,128)(2,1)S(1)}) custom-call(s32[5]{0:T(128)S(1)} %stack.136.sp_ref, bf16[5,512,768]{2,1,0:T(8,128)(2,1)S(1)} %copy-done.111, bf16[5,512,3072]{2,1,0:T(8,128)(2,1)} %get-tuple-element.346.refs_1_), custom_call_target="tpu_custom_call" | custom-call | flops 12000000000 | bytes 12000000 | tf_op jit(solution)/shard_map/pallas_call | solution.py:76
  699.3 15.0 %shard_map.252 = (bf16[384,3072]{1,0:T(8,128)(2,1)}, bf16[384,3072]{1,0:T(8,128)(2,1)S(1)}) custom-call(s32[5]{0:T(128)S(1)} %stack.136.sp_ref, bf16[5,512,768]{2,1,0:T(8,128)(2,1)S(1)} %copy-done.123, bf16[5,512,3072]{2,1,0:T(8,128)(2,1)} %get-tuple-element.350.refs_1_), custom_call_target="tpu_custom_call" | custom-call | flops 12000000000 | bytes 12000000 | tf_op jit(solution)/shard_map/pallas_call | solution.py:76
  734.8 17.4 %shard_map.253 = (f32[5,64,768]{2,1,0:T(8,128)S(1)}, bf16[512,768]{1,0:T(8,128)(2,1)S(1)}, bf16[512,1536]{1,0:T(8,128)(2,1)S(1)}, bf16[512,1536]{1,0:T(8,128)(2,1)}) custom-call(s32[5]{0:T(128)S(1)} %stack.136.sp_ref, bf16[5,512,768]{2,1,0:T(8,128)(2,1)S(1)} %copy-done.99, ...), custom_call_target="tpu_custom_call", output_to_operand_aliasing={{0}: (11, {})} | custom-call | flops 20000000000 | bytes 20000000 | tf_op jit(solution)/shard_map/pallas_call | solution.py:76
  755.6 15.1 %collective-permute-start.38 = (bf16[192,3072]{1,0:T(8,128)(2,1)}, bf16[192,3072]{1,0:T(8,128)(2,1)}, u32[]{:S(2)}, u32[]{:S(2)}) collective-permute-start(bf16[192,3072]{1,0:T(8,128)(2,1)} %constant_dynamic-slice_fusion.2), channel_id=1, source_target_pairs={{0,2},{1,5},{2,0},{3,7},{4,6},{5,1},{6,4},{7,3},{8,10},{9,13},{10,... | collective-permute-start | bytes 3538952 | tf_op jit(solution)/shard_map/ppermute | solution.py:755
  813.3 16.3 %shard_map.255 = (bf16[384,3072]{1,0:T(8,128)(2,1)S(1)}, bf16[384,3072]{1,0:T(8,128)(2,1)S(1)}) custom-call(s32[5]{0:T(128)S(1)} %stack.136.sp_ref, bf16[5,512,768]{2,1,0:T(8,128)(2,1)S(1)} %copy-done.13, bf16[5,512,768]{2,1,0:T(8,128)(2,1)S(1)} %copy-done.52, bf16[5,512,2304]{2,1,0:T(8,128)(2,1)} %get-tuple-element.364.refs_2_, bf16[5,512,768]{2,1,0:T(8,128)(2,1)} %copy-done.27), custom_call_target="tpu_custom_call" | custom-call | flops 12000000000 | bytes 12000000 | tf_op jit(solution)/shard_map/pallas_call | solution.py:76
  829.7 15.1 %collective-permute-start.48 = (f32[88,128]{1,0:T(8,128)S(1)}, f32[88,128]{1,0:T(8,128)S(1)}, u32[]{:S(2)}, u32[]{:S(2)}) collective-permute-start(f32[88,128]{1,0:T(8,128)S(1)} %add.289), channel_id=1, source_target_pairs={{0,8},{1,9},{2,10},{3,11},{4,12},{5,13},{6,14},{7,15},{8,0},{9,1},... | collective-permute-start | bytes 135176 | tf_op jit(solution)/shard_map/ppermute | solution.py:786
  850.4 19.0 %collective-permute-done.33 = bf16[48,3072]{1,0:T(8,128)(2,1)S(1)} collective-permute-done((bf16[48,3072]{1,0:T(8,128)(2,1)S(1)}, bf16[48,3072]{1,0:T(8,128)(2,1)S(1)}, u32[]{:S(2)}, u32[]{:S(2)}) %collective-permute-start.33) | collective-permute-done | bytes 294944 | tf_op jit(solution)/shard_map/ppermute | solution.py:755
  869.6 12.5 %collective-permute-done.40 = bf16[48,3072]{1,0:T(8,128)(2,1)S(1)} collective-permute-done((bf16[48,3072]{1,0:T(8,128)(2,1)S(1)}, bf16[48,3072]{1,0:T(8,128)(2,1)S(1)}, u32[]{:S(2)}, u32[]{:S(2)}) %collective-permute-start.40) | collective-permute-done | bytes 294944 | tf_op jit(solution)/shard_map/ppermute | solution.py:755
  882.2 12.5 %collective-permute-done.34 = bf16[48,3072]{1,0:T(8,128)(2,1)S(1)} collective-permute-done((bf16[48,3072]{1,0:T(8,128)(2,1)S(1)}, bf16[48,3072]{1,0:T(8,128)(2,1)S(1)}, u32[]{:S(2)}, u32[]{:S(2)}) %collective-permute-start.34) | collective-permute-done | bytes 294944 | tf_op jit(solution)/shard_map/ppermute | solution.py:755
  900.7 22.1 %collective-permute-done.24 = bf16[192,3072]{1,0:T(8,128)(2,1)S(1)} collective-permute-done((bf16[192,3072]{1,0:T(8,128)(2,1)S(1)}, bf16[192,3072]{1,0:T(8,128)(2,1)S(1)}, u32[]{:S(2)}, u32[]{:S(2)}) %collective-permute-start.24) | collective-permute-done | bytes 1179680 | tf_op jit(solution)/shard_map/ppermute | solution.py:755
  925.5 10.6 %collective-permute-done.25 = bf16[96,3072]{1,0:T(8,128)(2,1)S(1)} collective-permute-done((bf16[96,3072]{1,0:T(8,128)(2,1)S(1)}, bf16[96,3072]{1,0:T(8,128)(2,1)S(1)}, u32[]{:S(2)}, u32[]{:S(2)}) %collective-permute-start.25) | collective-permute-done | bytes 589856 | tf_op jit(solution)/shard_map/ppermute | solution.py:755
  960.3 18.2 %collective-permute-done.28 = bf16[96,3072]{1,0:T(8,128)(2,1)S(1)} collective-permute-done((bf16[96,3072]{1,0:T(8,128)(2,1)S(1)}, bf16[96,3072]{1,0:T(8,128)(2,1)S(1)}, u32[]{:S(2)}, u32[]{:S(2)}) %collective-permute-start.28) | collective-permute-done | bytes 589856 | tf_op jit(solution)/shard_map/ppermute | solution.py:755
  985.6 11.3 %collective-permute-done.29 = bf16[192,3072]{1,0:T(8,128)(2,1)S(1)} collective-permute-done((bf16[192,3072]{1,0:T(8,128)(2,1)S(1)}, bf16[192,3072]{1,0:T(8,128)(2,1)S(1)}, u32[]{:S(2)}, u32[]{:S(2)}) %collective-permute-start.29) | collective-permute-done | bytes 1179680 | tf_op jit(solution)/shard_map/ppermute | solution.py:755
  (868 shorter events, 537.8 us)
Async XLA Ops:
  2.7 46.6 %collective-permute-start = (s32[2,2176]{1,0:T(2,128)}, s32[2,2176]{1,0:T(2,128)}, u32[]{:S(2)}, u32[]{:S(2)}) collective-permute-start(s32[2,2176]{1,0:T(2,128)} %pad_add_fusion.3), channel_id=1, source_target_pairs={{0,1},{1,0},{2,3},{3,2},{4,5},{5,4},{6,7},{7,6},{8,9},{9,8},{10,11... | collective-permute-start | bytes 52232 | tf_op jit(solution)/shard_map/ppermute | solution.py:813
  6.4 46.7 %collective-permute-start.1 = (bf16[2,512,768]{2,1,0:T(8,128)(2,1)}, bf16[2,512,768]{2,1,0:T(8,128)(2,1)}, u32[]{:S(2)}, u32[]{:S(2)}) collective-permute-start(bf16[2,512,768]{2,1,0:T(8,128)(2,1)} %select_bitcast_fusion.2), channel_id=1, source_target_pairs={{0,1},{1,0},{2,3},{3,2},{4,5},{5,4},{6,7},{7,6},{8,9},{9,8},{10,11... | collective-permute-start | bytes 4718600 | tf_op jit(solution)/shard_map/ppermute | solution.py:813
  124.1 18.9 %collective-permute-start.3 = (bf16[512,768]{1,0:T(8,128)(2,1)}, bf16[512,768]{1,0:T(8,128)(2,1)}, u32[]{:S(2)}, u32[]{:S(2)}) collective-permute-start(bf16[512,768]{1,0:T(8,128)(2,1)} %get-tuple-element.214), channel_id=1, source_target_pairs={{0,16},{1,17},{2,18},{3,19},{4,20},{5,21},{6,22},{7,23},{8,24},{9,... | collective-permute-start | bytes 2359304 | tf_op jit(solution)/shard_map/ppermute | solution.py:938
  205.6 52.0 %collective-permute-start.5 = (bf16[512,768]{1,0:T(8,128)(2,1)}, bf16[512,768]{1,0:T(8,128)(2,1)}, u32[]{:S(2)}, u32[]{:S(2)}) collective-permute-start(bf16[512,768]{1,0:T(8,128)(2,1)} %get-tuple-element.229), channel_id=1, source_target_pairs={{0,16},{1,17},{2,18},{3,19},{4,20},{5,21},{6,22},{7,23},{8,24},{9,... | collective-permute-start | bytes 2359304 | tf_op jit(solution)/shard_map/ppermute | solution.py:938
  287.8 48.3 %collective-permute-start.8 = (bf16[512,768]{1,0:T(8,128)(2,1)S(1)}, bf16[512,768]{1,0:T(8,128)(2,1)S(1)}, u32[]{:S(2)}, u32[]{:S(2)}) collective-permute-start(bf16[512,768]{1,0:T(8,128)(2,1)S(1)} %get-tuple-element.257), channel_id=1, source_target_pairs={{16,0},{17,1},{18,2},{19,3},{20,4},{21,5},{22,6},{23,7},{24,8},{25... | collective-permute-start | bytes 2359304 | tf_op jit(solution)/shard_map/ppermute | solution.py:945
  331.6 51.7 %collective-permute-start.10 = (bf16[512,768]{1,0:T(8,128)(2,1)}, bf16[512,768]{1,0:T(8,128)(2,1)}, u32[]{:S(2)}, u32[]{:S(2)}) collective-permute-start(bf16[512,768]{1,0:T(8,128)(2,1)} %get-tuple-element.281), channel_id=1, source_target_pairs={{0,16},{1,17},{2,18},{3,19},{4,20},{5,21},{6,22},{7,23},{8,24},{9,... | collective-permute-start | bytes 2359304 | tf_op jit(solution)/shard_map/ppermute | solution.py:938
  413.5 49.3 %collective-permute-start.12 = (bf16[512,768]{1,0:T(8,128)(2,1)S(1)}, bf16[512,768]{1,0:T(8,128)(2,1)S(1)}, u32[]{:S(2)}, u32[]{:S(2)}) collective-permute-start(bf16[512,768]{1,0:T(8,128)(2,1)S(1)} %get-tuple-element.280), channel_id=1, source_target_pairs={{16,0},{17,1},{18,2},{19,3},{20,4},{21,5},{22,6},{23,7},{24,8},{25... | collective-permute-start | bytes 2359304 | tf_op jit(solution)/shard_map/ppermute | solution.py:945
  455.2 49.8 %collective-permute-start.14 = (bf16[512,768]{1,0:T(8,128)(2,1)}, bf16[512,768]{1,0:T(8,128)(2,1)}, u32[]{:S(2)}, u32[]{:S(2)}) collective-permute-start(bf16[512,768]{1,0:T(8,128)(2,1)} %get-tuple-element.310), channel_id=1, source_target_pairs={{0,16},{1,17},{2,18},{3,19},{4,20},{5,21},{6,22},{7,23},{8,24},{9,... | collective-permute-start | bytes 2359304 | tf_op jit(solution)/shard_map/ppermute | solution.py:938
  535.6 32.6 %collective-permute-start.16 = (bf16[512,768]{1,0:T(8,128)(2,1)S(1)}, bf16[512,768]{1,0:T(8,128)(2,1)S(1)}, u32[]{:S(2)}, u32[]{:S(2)}) collective-permute-start(bf16[512,768]{1,0:T(8,128)(2,1)S(1)} %get-tuple-element.309), channel_id=1, source_target_pairs={{16,0},{17,1},{18,2},{19,3},{20,4},{21,5},{22,6},{23,7},{24,8},{25... | collective-permute-start | bytes 2359304 | tf_op jit(solution)/shard_map/ppermute | solution.py:945
  622.9 28.8 %collective-permute-start.18 = (bf16[512,768]{1,0:T(8,128)(2,1)}, bf16[512,768]{1,0:T(8,128)(2,1)}, u32[]{:S(2)}, u32[]{:S(2)}) collective-permute-start(bf16[512,768]{1,0:T(8,128)(2,1)} %get-tuple-element.338), channel_id=1, source_target_pairs={{16,0},{17,1},{18,2},{19,3},{20,4},{21,5},{22,6},{23,7},{24,8},{25... | collective-permute-start | bytes 2359304 | tf_op jit(solution)/shard_map/ppermute | solution.py:945
  699.3 25.4 %collective-permute-start.19 = (bf16[384,3072]{1,0:T(8,128)(2,1)}, bf16[384,3072]{1,0:T(8,128)(2,1)}, u32[]{:S(2)}, u32[]{:S(2)}) collective-permute-start(bf16[384,3072]{1,0:T(8,128)(2,1)} %get-tuple-element.348), channel_id=1, source_target_pairs={{0,1},{1,0},{2,3},{3,2},{4,5},{5,4},{6,7},{7,6},{8,9},{9,8},{10,11... | collective-permute-start | bytes 7077896 | tf_op jit(solution)/shard_map/ppermute | solution.py:813
  732.8 54.0 %collective-permute-start.31 = (bf16[192,3072]{1,0:T(8,128)(2,1)}, bf16[192,3072]{1,0:T(8,128)(2,1)}, u32[]{:S(2)}, u32[]{:S(2)}) collective-permute-start(bf16[192,3072]{1,0:T(8,128)(2,1)} %constant_dynamic-slice_fusion.5), channel_id=1, source_target_pairs={{0,2},{1,5},{2,0},{3,7},{4,6},{5,1},{6,4},{7,3},{8,10},{9,13},{10,... | collective-permute-start | bytes 3538952 | tf_op jit(solution)/shard_map/ppermute | solution.py:755
  754.3 41.6 %collective-permute-start.21 = (bf16[512,1536]{1,0:T(8,128)(2,1)}, bf16[512,1536]{1,0:T(8,128)(2,1)}, u32[]{:S(2)}, u32[]{:S(2)}) collective-permute-start(bf16[512,1536]{1,0:T(8,128)(2,1)} %get-tuple-element.358), channel_id=1, source_target_pairs={{0,1},{1,0},{2,3},{3,2},{4,5},{5,4},{6,7},{7,6},{8,9},{9,8},{10,11... | collective-permute-start | bytes 4718600 | tf_op jit(solution)/shard_map/ppermute | solution.py:813
  755.6 37.4 %collective-permute-start.38 = (bf16[192,3072]{1,0:T(8,128)(2,1)}, bf16[192,3072]{1,0:T(8,128)(2,1)}, u32[]{:S(2)}, u32[]{:S(2)}) collective-permute-start(bf16[192,3072]{1,0:T(8,128)(2,1)} %constant_dynamic-slice_fusion.2), channel_id=1, source_target_pairs={{0,2},{1,5},{2,0},{3,7},{4,6},{5,1},{6,4},{7,3},{8,10},{9,13},{10,... | collective-permute-start | bytes 3538952 | tf_op jit(solution)/shard_map/ppermute | solution.py:755
  790.9 53.9 %collective-permute-start.32 = (bf16[96,3072]{1,0:T(8,128)(2,1)}, bf16[96,3072]{1,0:T(8,128)(2,1)}, u32[]{:S(2)}, u32[]{:S(2)}) collective-permute-start(bf16[96,3072]{1,0:T(8,128)(2,1)} %constant_dynamic-slice_fusion.4), channel_id=1, source_target_pairs={{0,4},{1,3},{2,6},{3,1},{4,0},{5,7},{6,2},{7,5},{8,12},{9,11},{10,... | collective-permute-start | bytes 1769480 | tf_op jit(solution)/shard_map/ppermute | solution.py:755
  795.7 50.6 %collective-permute-start.39 = (bf16[96,3072]{1,0:T(8,128)(2,1)}, bf16[96,3072]{1,0:T(8,128)(2,1)}, u32[]{:S(2)}, u32[]{:S(2)}) collective-permute-start(bf16[96,3072]{1,0:T(8,128)(2,1)} %constant_dynamic-slice_fusion.1), channel_id=1, source_target_pairs={{0,4},{1,3},{2,6},{3,1},{4,0},{5,7},{6,2},{7,5},{8,12},{9,11},{10,... | collective-permute-start | bytes 1769480 | tf_op jit(solution)/shard_map/ppermute | solution.py:755
  807.9 195.5 %collective-permute-start.22 = (bf16[2,512,768]{2,1,0:T(8,128)(2,1)}, bf16[2,512,768]{2,1,0:T(8,128)(2,1)}, u32[]{:S(2)}, u32[]{:S(2)}) collective-permute-start(bf16[2,512,768]{2,1,0:T(8,128)(2,1)} %broadcast_select_fusion.1), channel_id=1, source_target_pairs={{0,1},{1,0},{2,3},{3,2},{4,5},{5,4},{6,7},{7,6},{8,9},{9,8},{10,11... | collective-permute-start | bytes 4718600 | tf_op jit(solution)/shard_map/ppermute | solution.py:813
  809.2 20.4 %collective-permute-start.47 = (f32[88,128]{1,0:T(8,128)S(1)}, f32[88,128]{1,0:T(8,128)S(1)}, u32[]{:S(2)}, u32[]{:S(2)}) collective-permute-start(f32[88,128]{1,0:T(8,128)S(1)} %fusion.38), channel_id=1, source_target_pairs={{0,4},{1,5},{2,6},{3,7},{4,0},{5,1},{6,2},{7,3},{8,12},{9,13},{10,... | collective-permute-start | bytes 135176 | tf_op jit(solution)/shard_map/ppermute | solution.py:786
  829.6 65.1 %collective-permute-start.23 = (bf16[384,3072]{1,0:T(8,128)(2,1)S(1)}, bf16[384,3072]{1,0:T(8,128)(2,1)S(1)}, u32[]{:S(2)}, u32[]{:S(2)}) collective-permute-start(bf16[384,3072]{1,0:T(8,128)(2,1)S(1)} %get-tuple-element.366), channel_id=1, source_target_pairs={{0,1},{1,0},{2,3},{3,2},{4,5},{5,4},{6,7},{7,6},{8,9},{9,8},{10,11... | collective-permute-start | bytes 7077896 | tf_op jit(solution)/shard_map/ppermute | solution.py:813
  829.7 169.4 %collective-permute-start.48 = (f32[88,128]{1,0:T(8,128)S(1)}, f32[88,128]{1,0:T(8,128)S(1)}, u32[]{:S(2)}, u32[]{:S(2)}) collective-permute-start(f32[88,128]{1,0:T(8,128)S(1)} %add.289), channel_id=1, source_target_pairs={{0,8},{1,9},{2,10},{3,11},{4,12},{5,13},{6,14},{7,15},{8,0},{9,1},... | collective-permute-start | bytes 135176 | tf_op jit(solution)/shard_map/ppermute | solution.py:786
  846.1 23.4 %collective-permute-start.33 = (bf16[48,3072]{1,0:T(8,128)(2,1)S(1)}, bf16[48,3072]{1,0:T(8,128)(2,1)S(1)}, u32[]{:S(2)}, u32[]{:S(2)}) collective-permute-start(bf16[48,3072]{1,0:T(8,128)(2,1)S(1)} %constant_dynamic-slice_fusion.3), channel_id=1, source_target_pairs={{0,8},{1,9},{2,10},{3,11},{4,12},{5,13},{6,14},{7,15},{8,0},{9,1},... | collective-permute-start | bytes 884744 | tf_op jit(solution)/shard_map/ppermute | solution.py:755
  847.5 34.5 %collective-permute-start.40 = (bf16[48,3072]{1,0:T(8,128)(2,1)S(1)}, bf16[48,3072]{1,0:T(8,128)(2,1)S(1)}, u32[]{:S(2)}, u32[]{:S(2)}) collective-permute-start(bf16[48,3072]{1,0:T(8,128)(2,1)S(1)} %constant_dynamic-slice_fusion), channel_id=1, source_target_pairs={{0,8},{1,9},{2,10},{3,11},{4,12},{5,13},{6,14},{7,15},{8,0},{9,1},... | collective-permute-start | bytes 884744 | tf_op jit(solution)/shard_map/ppermute | solution.py:755
  869.5 25.2 %collective-permute-start.34 = (bf16[48,3072]{1,0:T(8,128)(2,1)S(1)}, bf16[48,3072]{1,0:T(8,128)(2,1)S(1)}, u32[]{:S(2)}, u32[]{:S(2)}) collective-permute-start(bf16[48,3072]{1,0:T(8,128)(2,1)S(1)} %dynamic-slice_add_fusion.7), channel_id=1, source_target_pairs={{0,8},{1,9},{2,10},{3,11},{4,12},{5,13},{6,14},{7,15},{8,0},{9,1},... | collective-permute-start | bytes 884744 | tf_op jit(solution)/shard_map/ppermute | solution.py:755
  895.7 27.1 %collective-permute-start.24 = (bf16[192,3072]{1,0:T(8,128)(2,1)S(1)}, bf16[192,3072]{1,0:T(8,128)(2,1)S(1)}, u32[]{:S(2)}, u32[]{:S(2)}) collective-permute-start(bf16[192,3072]{1,0:T(8,128)(2,1)S(1)} %constant_dynamic-slice_fusion.8), channel_id=1, source_target_pairs={{0,2},{1,5},{2,0},{3,7},{4,6},{5,1},{6,4},{7,3},{8,10},{9,13},{10,... | collective-permute-start | bytes 3538952 | tf_op jit(solution)/shard_map/ppermute | solution.py:755
  896.6 26.8 %collective-permute-start.35 = (bf16[96,3072]{1,0:T(8,128)(2,1)S(1)}, bf16[96,3072]{1,0:T(8,128)(2,1)S(1)}, u32[]{:S(2)}, u32[]{:S(2)}) collective-permute-start(bf16[96,3072]{1,0:T(8,128)(2,1)S(1)} %pad_maximum_fusion.11), channel_id=1, source_target_pairs={{0,4},{1,3},{2,6},{3,1},{4,0},{5,7},{6,2},{7,5},{8,12},{9,11},{10,... | collective-permute-start | bytes 1769480 | tf_op jit(solution)/shard_map/ppermute | solution.py:755
  900.6 37.8 %collective-permute-start.42 = (bf16[96,3072]{1,0:T(8,128)(2,1)S(1)}, bf16[96,3072]{1,0:T(8,128)(2,1)S(1)}, u32[]{:S(2)}, u32[]{:S(2)}) collective-permute-start(bf16[96,3072]{1,0:T(8,128)(2,1)S(1)} %pad_maximum_fusion.12), channel_id=1, source_target_pairs={{0,4},{1,3},{2,6},{3,1},{4,0},{5,7},{6,2},{7,5},{8,12},{9,11},{10,... | collective-permute-start | bytes 1769480 | tf_op jit(solution)/shard_map/ppermute | solution.py:755
  923.7 36.0 %collective-permute-start.36 = (bf16[192,3072]{1,0:T(8,128)(2,1)S(1)}, bf16[192,3072]{1,0:T(8,128)(2,1)S(1)}, u32[]{:S(2)}, u32[]{:S(2)}) collective-permute-start(bf16[192,3072]{1,0:T(8,128)(2,1)S(1)} %pad_maximum_fusion.8), channel_id=1, source_target_pairs={{0,2},{1,5},{2,0},{3,7},{4,6},{5,1},{6,4},{7,3},{8,10},{9,13},{10,... | collective-permute-start | bytes 3538952 | tf_op jit(solution)/shard_map/ppermute | solution.py:755
  949.4 33.5 %collective-permute-start.43 = (bf16[192,3072]{1,0:T(8,128)(2,1)S(1)}, bf16[192,3072]{1,0:T(8,128)(2,1)S(1)}, u32[]{:S(2)}, u32[]{:S(2)}) collective-permute-start(bf16[192,3072]{1,0:T(8,128)(2,1)S(1)} %pad_maximum_fusion.9), channel_id=1, source_target_pairs={{0,2},{1,5},{2,0},{3,7},{4,6},{5,1},{6,4},{7,3},{8,10},{9,13},{10,... | collective-permute-start | bytes 3538952 | tf_op jit(solution)/shard_map/ppermute | solution.py:755
  959.6 18.9 %collective-permute-start.28 = (bf16[96,3072]{1,0:T(8,128)(2,1)S(1)}, bf16[96,3072]{1,0:T(8,128)(2,1)S(1)}, u32[]{:S(2)}, u32[]{:S(2)}) collective-permute-start(bf16[96,3072]{1,0:T(8,128)(2,1)S(1)} %pad_maximum_fusion.10), channel_id=1, source_target_pairs={{0,4},{1,3},{2,6},{3,1},{4,0},{5,7},{6,2},{7,5},{8,12},{9,11},{10,... | collective-permute-start | bytes 1769480 | tf_op jit(solution)/shard_map/ppermute | solution.py:755
  982.8 25.2 %collective-permute-start.37 = (bf16[384,3072]{1,0:T(8,128)(2,1)S(1)}, bf16[384,3072]{1,0:T(8,128)(2,1)}, u32[]{:S(2)}, u32[]{:S(2)}) collective-permute-start(bf16[384,3072]{1,0:T(8,128)(2,1)S(1)} %pad_maximum_fusion.3.refs_0_), channel_id=1, source_target_pairs={{0,1},{1,0},{2,3},{3,2},{4,5},{5,4},{6,7},{7,6},{8,9},{9,8},{10,11... | collective-permute-start | bytes 7077896 | tf_op jit(solution)/shard_map/ppermute | solution.py:813
  985.1 30.7 %collective-permute-start.44 = (bf16[384,3072]{1,0:T(8,128)(2,1)}, bf16[384,3072]{1,0:T(8,128)(2,1)}, u32[]{:S(2)}, u32[]{:S(2)}) collective-permute-start(bf16[384,3072]{1,0:T(8,128)(2,1)} %pad_maximum_fusion.4.refs_0_), channel_id=1, source_target_pairs={{0,1},{1,0},{2,3},{3,2},{4,5},{5,4},{6,7},{7,6},{8,9},{9,8},{10,11... | collective-permute-start | bytes 7077896 | tf_op jit(solution)/shard_map/ppermute | solution.py:813
  999.1 25.3 %collective-permute-start.30 = (bf16[384,3072]{1,0:T(8,128)(2,1)}, bf16[384,3072]{1,0:T(8,128)(2,1)}, u32[]{:S(2)}, u32[]{:S(2)}) collective-permute-start(bf16[384,3072]{1,0:T(8,128)(2,1)} %pad_maximum_fusion.2.refs_0_), channel_id=1, source_target_pairs={{0,1},{1,0},{2,3},{3,2},{4,5},{5,4},{6,7},{7,6},{8,9},{9,8},{10,11... | collective-permute-start | bytes 7077896 | tf_op jit(solution)/shard_map/ppermute | solution.py:813
  (324 other events, 2761.5 us)

commit v3 on v2

--- a/solution.py
+++ b/solution.py
@@ -62,16 +62,36 @@
     return pl.BlockSpec((rows, cols), lambda i, sp: (i, 0))
 
 
+class Row:
+    def __init__(self, table, base):
+        self.table = table
+        self.base = base
+
+    def __getitem__(self, at):
+        return self.table[self.base + at]
+
+
+def shifted(spec, base):
+    if spec.index_map is None:
+        return spec
+    inner = spec.index_map
+    return pl.BlockSpec(
+        spec.block_shape, lambda i, sp: inner(i, Row(sp, base)), pipeline_mode=spec.pipeline_mode
+    )
+
+
 def call(body, sp, grid, ins, outs, aliased, scratch=(), us=10):
-    operands = [a for a, _ in ins] + [a for a, _ in aliased]
-    in_specs = [s for _, s in ins] + [ANY] * len(aliased)
-    out_shape = [like(a) for a, _ in aliased] + [s for s, _ in outs]
-    out_specs = [s for _, s in aliased] + [s for _, s in outs]
+    held = lambda a, s: pltpu.with_memory_space_constraint(a, pltpu.HBM) if a.ndim == 3 else a
+    operands = [held(a, s) for a, s in ins] + [held(a, s) for a, s in aliased]
+    table, base = sp
+    in_specs = [shifted(s, base) for _, s in ins] + [ANY] * len(aliased)
+    out_shape = [pltpu.HBM(a.shape, a.dtype) for a, _ in aliased] + [s for s, _ in outs]
+    out_specs = [shifted(s, base) for _, s in aliased] + [shifted(s, base) for _, s in outs]
     kept = len(aliased)
     first = len(ins)
 
     def run(sp_ref, *refs):
-        body(sp_ref, *refs[:first], *refs[first + kept :])
+        body(Row(sp_ref, base), *refs[:first], *refs[first + kept :])
 
     return pl.pallas_call(
         run,
@@ -88,12 +108,12 @@
         cost_estimate=pl.CostEstimate(
             flops=us * 1_000_000_000, bytes_accessed=us * 1_000_000, transcendentals=0
         ),
-    )(sp, *operands)
+    )(table, *operands)
 
 
 def unwritten(shapes):
     return pl.pallas_call(
-        lambda *refs: None, out_shape=shapes, out_specs=[ANY] * len(shapes),
+        lambda *refs: None, out_shape=[pltpu.HBM(s.shape, s.dtype) for s in shapes], out_specs=[ANY] * len(shapes),
         compiler_params=pltpu.CompilerParams(vmem_limit_bytes=2 * 1024 * 1024),
     )()
 
@@ -116,7 +136,7 @@
         out_specs=[RESIDENT] * len(arrays),
         scratch_shapes=[pltpu.SemaphoreType.DMA((len(arrays),))],
         compiler_params=pltpu.CompilerParams(vmem_limit_bytes=2 * 1024 * 1024),
-    )(*arrays)
+    )(*[pltpu.with_memory_space_constraint(a, pltpu.HBM) for a in arrays])
 
 
 def at_window(rows, cols):
@@ -737,6 +757,10 @@
     return [whole[:a], whole[a:b], whole[b:]]
 
 
+def after(value, earlier):
+    return lax.optimization_barrier((value, earlier))[0]
+
+
 class Ring:
     def __init__(self, count):
         self.count = count
@@ -757,34 +781,40 @@
     def swap(self, a):
         return lax.ppermute(a, "dp", [(i, i ^ 1) for i in range(self.count)])
 
-    def reduce(self, part):
+    def halve(self, part, step):
+        half = part.shape[0] // 2
+        bit = self.bit(step)
+        keep = lax.dynamic_slice_in_dim(part, bit * half, half, 0)
+        give = lax.dynamic_slice_in_dim(part, (1 - bit) * half, half, 0)
+        return keep, self.send(give, step)
+
+    def join(self, part, got, step):
+        first = self.bit(step) == 0
+        return jnp.concatenate([jnp.where(first, part, got), jnp.where(first, got, part)], axis=0)
+
+    def stages(self, give, keep):
+        got = self.swap(give)
+        order = yield
+        part = keep + order(got)
         for step in self.steps:
-            half = part.shape[0] // 2
-            bit = self.bit(step)
-            keep = lax.dynamic_slice_in_dim(part, bit * half, half, 0)
-            give = lax.dynamic_slice_in_dim(part, (1 - bit) * half, half, 0)
-            part = keep + self.send(give, step)
-        return part
-
-    def gather(self, part):
+            keep, got = self.halve(part, step)
+            order = yield part
+            part = keep + order(got)
         for step in self.steps[::-1]:
-            first = self.bit(step) == 0
             got = self.send(part, step)
-            part = jnp.concatenate(
-                [jnp.where(first, part, got), jnp.where(first, got, part)], axis=0
-            )
-        return part
-
-    def whole(self, part):
-        got = self.swap(part).astype(f32)
-        part = part.astype(f32)
-        first = self.index % 2 == 0
-        return jnp.concatenate([jnp.where(first, part, got), jnp.where(first, got, part)], axis=0)
-
-    def total(self, part):
+            order = yield part
+            part = self.join(part, order(got), step)
+        got = self.swap(part)
+        order = yield part
+        self.result = (part, order(got))
+        yield self.result[1]
+
+    def totals(self, part):
         for bit in range(self.count.bit_length() - 1):
-            part = part + lax.ppermute(part, "dp", [(i, i ^ (1 << bit)) for i in range(self.count)])
-        return part
+            got = lax.ppermute(part, "dp", [(i, i ^ (1 << bit)) for i in range(self.count)])
+            order = yield part
+            part = part + order(got)
+        yield part
 
 
 SLOTS = (
@@ -873,7 +903,14 @@
         w = jnp.where(
             section == 0, windows if zero is None else zero, windows if one is None else one
         ).astype(jnp.int32)
-        infos.append(jnp.stack([w, blocks_of[w], core.astype(jnp.int32), lengths[w], section.astype(jnp.int32)]))
+        infos.append(w)
+    infos = jnp.stack(infos)
+    infos = jnp.stack(
+        [infos, blocks_of[infos], jnp.full_like(infos, core), lengths[infos], jnp.full_like(infos, section)],
+        axis=1,
+    )
+    facts = infos.shape[1]
+    infos = infos.reshape(-1)
 
     widths = dict(
         x=width, q=width, kv=2 * width, a=width, rest=width, lse=width, peer=2 * width, n1=width, h1=width,
@@ -912,16 +949,19 @@
         s.update(zip(names, outs[:5]))
         return s, tuple(outs[5:])
 
-    def attend_back(sp, s, grads):
-        cell, dq, keep, send = attend_back_call(
+    def attend_back_kernel(sp, s, grads):
+        return attend_back_call(
             sp, s["q"], s["kv"], s["peer"], side_all, hot_all, matrix, s["lse"], *grads, turned_all,
             s["cell"],
         )
-        s = dict(s, cell=cell)
-        dj, sj, fresh = input_back_call(
-            sp, dq, keep, exchange(send), s["db1"], w_in, s["dj"], s["sj"]
-        )
+
+    def input_back(sp, s, dq, keep, got):
+        dj, sj, fresh = input_back_call(sp, dq, keep, got, s["db1"], w_in, s["dj"], s["sj"])
         return dict(s, dj=dj, sj=sj), fresh
+
+    def attend_back(sp, s, grads):
+        cell, dq, keep, send = attend_back_kernel(sp, s, grads)
+        return input_back(sp, dict(s, cell=cell), dq, keep, exchange(send))
 
     got = {}
     finals = {}
@@ -929,7 +969,7 @@
     nothing = jnp.zeros((rows, width), bf16)
 
     for number, (kind, zero, one) in enumerate(SLOTS[:-1]):
-        sp = infos[number]
+        sp = (infos, number * facts)
         if kind == "F":
             st, out = forward(sp, st, got.pop(("F", one), nothing))
             if one is not None:
@@ -944,64 +984,91 @@
             if one is not None:
                 got["B", one] = lax.ppermute(out, "section", [(1, 0)])
 
-    sp = infos[-1]
-    barrier = lax.optimization_barrier
-
-    def start_sum(pairs):
+    sp = (infos, (len(SLOTS) - 1) * facts)
+
+    class Chain:
+        def __init__(self, stages, count):
+            self.stages = stages
+            self.left = count
+            next(stages)
+
+        def advance(self, earlier):
+            self.last = self.stages.send(lambda got: after(got, earlier))
+            self.left -= 1
+            return self.last
+
+    def weight_sum(pairs):
         give, keep = weight_call(sp, windows, pairs)
-        return keep + exchange(give)
-
-    def spread(part, widths, moves):
-        return spread_call(sp, part, exchange(part), widths, moves)
-
-    st, grads = dense_back(sp, st, got.pop(("B", SLOTS[-1][1])))
-    sums_contract = start_sum([(st["db2"], st["g"])])
-    sums_expand = start_sum([(st["h1"], st["df"])])
-    grads, sums_contract, sums_expand = barrier((grads, sums_contract, sums_expand))
-    sums_contract = ring.reduce(sums_contract)
-    sums_expand = ring.reduce(sums_expand)
-    st, grads_in[SLOTS[-1][1]] = attend_back(sp, st, grads)
-    sums_attend = ring.reduce(start_sum([(st["x"], st["dj"]), (st["a"], st["db1"])]))
+        return give, Chain(ring.stages(give, keep), 2 * len(ring.steps) + 2)
+
     natural = [((0, 0), 0, hidden)]
-    (g_contract,) = spread(ring.gather(sums_contract), [hidden], natural)
-    (g_expand,) = spread(ring.gather(sums_expand), [hidden], natural)
     cols = PAIRS * PAIR
     moves = [
         ((0, j * width + i * cols), (3 * i + j) * cols, cols) for i in range(width // cols) for j in range(3)
     ] + [((1, 0), 3 * width, width)]
-    g_in, g_out = spread(ring.gather(sums_attend), [3 * width, width], moves)
-
-    sums = jnp.sum(st["st"][:windows], axis=0)
-    joined_sums = jnp.sum(st["sj"][:windows], axis=0)
-    wide = jnp.sum(st["se"][:windows], axis=0)
-    small = [
-        joined_sums[0:2], sums[0:6], wide,
-    ] + table_grads(jnp.sum(st["cell"][:windows], axis=0), maps, counts)
-    packed = jnp.concatenate([s.reshape(-1) for s in small])
-    size = packed.shape[0]
-    packed = jnp.pad(packed, (0, -size % 1024)).reshape(-1, PAIR)
-    packed = ring.total(packed).reshape(-1)
+
+    st, grads = dense_back(sp, st, got.pop(("B", SLOTS[-1][1])))
+    given, contract = weight_sum([(st["db2"], st["g"])])
+    given, expand = weight_sum([(after(st["h1"], given), st["df"])])
+    done = contract.advance(given)
+    grads = tuple(after(g, done) for g in grads)
+    cell, dq, keep, send = attend_back_kernel(sp, st, grads)
+    got = exchange(send)
+    done = expand.advance(dq)
+    done = contract.advance(done)
+    got = after(got, done)
+    st, grads_in[SLOTS[-1][1]] = input_back(sp, dict(st, cell=cell), dq, keep, got)
+    done = contract.advance(st["dj"])
+    given, attend = weight_sum([(after(st["x"], done), st["dj"]), (st["a"], st["db1"])])
+
+    later = lambda a: after(a, given)
+    of_windows = lambda name: jnp.sum(later(st[name])[:windows], axis=0)
+    small = [of_windows("sj")[0:2], of_windows("st")[0:6], of_windows("se")] + table_grads(
+        of_windows("cell"), maps, counts
+    )
+    packed = jnp.concatenate([p.reshape(-1) for p in small])
+    packed = jnp.pad(packed, (0, -packed.shape[0] % (8 * PAIR))).reshape(-1, PAIR)
+    totals = Chain(ring.totals(packed), dp_count.bit_length() - 1)
+    result = [later(jnp.where(section == 0, grads_in[w], finals[w])) for w in range(windows)]
+    mine_first, mine_second = jnp.stack(result[:micro]), jnp.stack(result[micro:])
+    keep_rows = jnp.where(core == 0, mine_first, mine_second)
+    got_rows = exchange(jnp.where(core == 0, mine_second, mine_first))
+
+    def assembled(got_rows):
+        out_halves = jnp.stack(
+            [jnp.where(core == 0, keep_rows, got_rows), jnp.where(core == 0, got_rows, keep_rows)], axis=1
+        )
+        return out_halves.reshape(1, micro, slots, width)
+
+    done = expand.advance(packed)
+    chains = {"contract": contract, "expand": expand, "attend": attend, "totals": totals}
+    kinds = {"contract": ([hidden], natural), "expand": ([hidden], natural), "attend": ([3 * width, width], moves)}
+    outputs = {}
+    boundary_out = None
+    while any(chain.left for chain in chains.values()):
+        for name, chain in chains.items():
+            if chain.left:
+                done = chain.advance(done)
+                if not chain.left and name in kinds:
+                    outputs[name] = spread_call(sp, *ring.result, *kinds[name])
+                    done = outputs[name][0]
+        if boundary_out is None and not totals.left:
+            boundary_out = assembled(after(got_rows, done))
+            done = boundary_out
+    (g_contract,), (g_expand,), (g_in, g_out) = (outputs[n] for n in ("contract", "expand", "attend"))
+    packed = totals.last.reshape(-1)
     pieces = []
     begin = 0
-    for s in small:
-        count = math.prod(s.shape)
-        pieces.append(packed[begin : begin + count].reshape(s.shape))
+    for p in small:
+        count = math.prod(p.shape)
+        pieces.append(packed[begin : begin + count].reshape(p.shape))
         begin += count
     joined_sums, sums, wide, table_p, table_h, table_v = pieces
     grad_bias = jnp.concatenate([joined_sums, sums[0:4]], axis=0)
     grad_gain = sums[4:6]
-
-    result = [jnp.where(section == 0, grads_in[w], finals[w]) for w in range(windows)]
-    mine_first, mine_second = jnp.stack(result[:micro]), jnp.stack(result[micro:])
-    keep = jnp.where(core == 0, mine_first, mine_second)
-    give = exchange(jnp.where(core == 0, mine_second, mine_first))
-    out_halves = jnp.stack(
-        [jnp.where(core == 0, keep, give), jnp.where(core == 0, give, keep)], axis=1
-    )
-    boundary_out = out_halves.reshape(1, micro, slots, width)
     return (
-        boundary_out, g_in[None], g_out[None], g_expand[None], g_contract[None], grad_gain[None], grad_bias[None], wide,
-        table_p[None], table_h[None], table_v[None],
+        boundary_out, g_in[None], g_out[None], g_expand[None], g_contract[None], grad_gain[None],
+        grad_bias[None], wide, table_p[None], table_h[None], table_v[None],
     )
 
 

time: 1040 us -> 736 us (0.71)
  local copies, waits for them, and re-layouts: 293 us -> 38.6 us
  starting transfers between devices: 87.1 us -> 60.3 us
  Pallas kernels: 415 us -> 392 us
  other arithmetic: 60.9 us -> 50 us
    unnamed x617 -> x135, local copies, waits for them, and re-layouts: 251 us -> 16.2 us
    pallas_call x36, Pallas kernels: 414 us -> 387 us  [call(): pl.pallas_call(run, grid_spec=pltpu.PrefetchScalarGridSpec(num_scalar_pre...]
    ppermute x18, starting transfers between devices: 38 us -> 12.7 us  [send(): return lax.ppermute(a, 'dp', pairs)]
  transfers between devices with their start and end apart: 49 -> 49, of which waited for: 14 -> 16; matrix products, arithmetic and copies ran while one was open for 9% -> 10% of each run, Pallas kernels for 26% -> 36%
where the time goes in v3:
time: 736 us; the launch traced here: 726 us
  Pallas kernels  392 us (53%)
  waiting for transfers between devices  178 us (24%)
  starting transfers between devices  60.3 us (8%)
  other arithmetic  50 us (7%)
  local copies, waits for them, and re-layouts  38.6 us (5%)
    pallas_call x36, Pallas kernels, call(): pl.pallas_call(run, grid_spec=pltpu.PrefetchScalarGridSpec(num_scalar_pre...  387 us
    ppermute x18, waiting for transfers between devices, send(): return lax.ppermute(a, 'dp', pairs)  125 us
    ppermute x4, waiting for transfers between devices, on_device(): got['B', one] = lax.ppermute(out, 'section', [(1, 0)])  30.3 us
    ppermute x4, starting transfers between devices, on_device(): got['F', zero] = lax.ppermute(out, 'section', [(0, 1)])  18.1 us
    ppermute x4, waiting for transfers between devices, on_device(): got['F', zero] = lax.ppermute(out, 'section', [(0, 1)])  17.2 us
    unnamed x135, local copies, waits for them, and re-layouts  16.2 us
  transfers between devices with their start and end apart: 49, of which 16 were waited for; matrix products, arithmetic and copies ran while one was open for 10% of the time, Pallas kernels for 36%

profile of v3, /device:TPU:0, one launch (start us, length us, event | category | flops | bytes accessed | tf_op | source)
XLA Modules:
  0.0 726.0 jit_solution(17875067927341596830)
XLA Ops:
  57.4 12.6 %shard_map.224 = (bf16[5,512,768]{2,1,0:T(8,128)(2,1)}, bf16[5,512,768]{2,1,0:T(8,128)(2,1)}, bf16[5,512,768]{2,1,0:T(8,128)(2,1)}, bf16[5,512,1536]{2,1,0:T(8,128)(2,1)}) custom-call(s32[50]{0:T(128)S(1)} %reshape.890.sp_ref, ...), custom_call_target="tpu_custom_call", output_to_operand_aliasing={{0}: (7, {}), {1}: (8, {}), {2}: (9, {}), {3}: (10, {})} | custom-call | flops 14000000000 | bytes 14000000 | tf_op jit(solution)/shard_map/pallas_call | solution.py:96
  70.1 11.1 %shard_map.225 = (bf16[5,512,768]{2,1,0:T(8,128)(2,1)}, bf16[5,512,768]{2,1,0:T(8,128)(2,1)}, bf16[5,512,3072]{2,1,0:T(8,128)(2,1)}, bf16[5,512,3072]{2,1,0:T(8,...) custom-call(s32[50]{0:T(128)S(1)} %reshape.890.sp_ref, ...), custom_call_target="tpu_custom_call", output_to_operand_aliasing={{0}: (9, {}), {1}: (10, {}), {2}: (11, {}), {3}: (12, {}), ... | custom-call | flops 10000000000 | bytes 10000000 | tf_op jit(solution)/shard_map/pallas_call | solution.py:96
  82.6 17.2 %collective-permute-done.3.refs_1_ = bf16[512,768]{1,0:T(8,128)(2,1)S(1)} collective-permute-done((bf16[512,768]{1,0:T(8,128)(2,1)S(1)}, bf16[512,768]{1,0:T(8,128)(2,1)S(1)}, u32[]{:S(2)}, u32[]{:S(2)}) %collective-permute-start.3) | collective-permute-done | bytes 786464 | tf_op jit(solution)/shard_map/ppermute | solution.py:978
  109.1 11.8 %shard_map.227 = (bf16[5,512,768]{2,1,0:T(8,128)(2,1)}, bf16[5,512,768]{2,1,0:T(8,128)(2,1)}, bf16[5,512,768]{2,1,0:T(8,128)(2,1)}, bf16[5,512,1536]{2,1,0:T(8,128)(2,1)}) custom-call(s32[50]{0:T(128)S(1)} %reshape.890.sp_ref, ...), custom_call_target="tpu_custom_call", output_to_operand_aliasing={{0}: (7, {}), {1}: (8, {}), {2}: (9, {}), {3}: (10, {})} | custom-call | flops 14000000000 | bytes 14000000 | tf_op jit(solution)/shard_map/pallas_call | solution.py:96
  120.9 10.9 %shard_map.228 = (bf16[5,512,768]{2,1,0:T(8,128)(2,1)}, bf16[5,512,768]{2,1,0:T(8,128)(2,1)}, bf16[5,512,3072]{2,1,0:T(8,128)(2,1)}, bf16[5,512,3072]{2,1,0:T(8,...) custom-call(s32[50]{0:T(128)S(1)} %reshape.890.sp_ref, ...), custom_call_target="tpu_custom_call", output_to_operand_aliasing={{0}: (9, {}), {1}: (10, {}), {2}: (11, {}), {3}: (12, {}), ... | custom-call | flops 10000000000 | bytes 10000000 | tf_op jit(solution)/shard_map/pallas_call | solution.py:96
  136.3 12.2 %shard_map.231 = (bf16[5,512,768]{2,1,0:T(8,128)(2,1)}, bf16[5,512,3072]{2,1,0:T(8,128)(2,1)}, bf16[5,512,768]{2,1,0:T(8,128)(2,1)}, f32[5,8,768]{2,1,0:T(8,128)...) custom-call(s32[50]{0:T(128)S(1)} %reshape.890.sp_ref, ...), custom_call_target="tpu_custom_call", output_to_operand_aliasing={{0}: (14, {}), {1}: (15, {}), {2}: (16, {}), {3}: (17, {}),... | custom-call | flops 10000000000 | bytes 10000000 | tf_op jit(solution)/shard_map/pallas_call | solution.py:96
  148.5 9.5 %shard_map.232 = (f32[5,64,768]{2,1,0:T(8,128)}, bf16[512,768]{1,0:T(8,128)(2,1)S(1)}, bf16[512,1536]{1,0:T(8,128)(2,1)S(1)}, bf16[512,1536]{1,0:T(8,128)(2,1)}) custom-call(s32[50]{0:T(128)S(1)} %reshape.890.sp_ref, bf16[5,512,768]{2,1,0:T(8,128)(2,1)} %get-tuple-element.254.refs_0_.refs_5_, ...), custom_call_target="tpu_custom_call", output_to_operand_aliasing={{0}: (11, {})} | custom-call | flops 20000000000 | bytes 20000000 | tf_op jit(solution)/shard_map/pallas_call | solution.py:96
  172.4 14.1 %shard_map.230 = (bf16[5,512,768]{2,1,0:T(8,128)(2,1)}, bf16[5,512,768]{2,1,0:T(8,128)(2,1)}, bf16[5,512,768]{2,1,0:T(8,128)(2,1)}, bf16[5,512,1536]{2,1,0:T(8,128)(2,1)}) custom-call(s32[50]{0:T(128)S(1)} %reshape.890.sp_ref, ...), custom_call_target="tpu_custom_call", output_to_operand_aliasing={{0}: (7, {}), {1}: (8, {}), {2}: (9, {}), {3}: (10, {})} | custom-call | flops 14000000000 | bytes 14000000 | tf_op jit(solution)/shard_map/pallas_call | solution.py:96
  186.6 10.9 %shard_map.234 = (bf16[5,512,768]{2,1,0:T(8,128)(2,1)}, bf16[5,512,768]{2,1,0:T(8,128)(2,1)}, bf16[5,512,3072]{2,1,0:T(8,128)(2,1)}, bf16[5,512,3072]{2,1,0:T(8,...) custom-call(s32[50]{0:T(128)S(1)} %reshape.890.sp_ref, ...), custom_call_target="tpu_custom_call", output_to_operand_aliasing={{0}: (9, {}), {1}: (10, {}), {2}: (11, {}), {3}: (12, {}), ... | custom-call | flops 10000000000 | bytes 10000000 | tf_op jit(solution)/shard_map/pallas_call | solution.py:96
  205.1 12.3 %shard_map.235 = (bf16[5,512,768]{2,1,0:T(8,128)(2,1)}, bf16[5,512,3072]{2,1,0:T(8,128)(2,1)}, bf16[5,512,768]{2,1,0:T(8,128)(2,1)}, f32[5,8,768]{2,1,0:T(8,128)...) custom-call(s32[50]{0:T(128)S(1)} %reshape.890.sp_ref, ...), custom_call_target="tpu_custom_call", output_to_operand_aliasing={{0}: (14, {}), {1}: (15, {}), {2}: (16, {}), {3}: (17, {}),... | custom-call | flops 10000000000 | bytes 10000000 | tf_op jit(solution)/shard_map/pallas_call | solution.py:96
  217.4 18.0 %shard_map.236 = (f32[5,64,768]{2,1,0:T(8,128)}, bf16[512,768]{1,0:T(8,128)(2,1)S(1)}, bf16[512,1536]{1,0:T(8,128)(2,1)S(1)}, bf16[512,1536]{1,0:T(8,128)(2,1)S(1)}) custom-call(s32[50]{0:T(128)S(1)} %reshape.890.sp_ref, bf16[5,512,768]{2,1,0:T(8,128)(2,1)} %get-tuple-element.269.refs_0_.refs_5_, ...), custom_call_target="tpu_custom_call", output_to_operand_aliasing={{0}: (11, {})} | custom-call | flops 20000000000 | bytes 20000000 | tf_op jit(solution)/shard_map/pallas_call | solution.py:96
  249.8 13.9 %shard_map.239 = (bf16[5,512,768]{2,1,0:T(8,128)(2,1)}, bf16[5,512,768]{2,1,0:T(8,128)(2,1)}, bf16[5,512,768]{2,1,0:T(8,128)(2,1)}, bf16[5,512,1536]{2,1,0:T(8,128)(2,1)}) custom-call(s32[50]{0:T(128)S(1)} %reshape.890.sp_ref, ...), custom_call_target="tpu_custom_call", output_to_operand_aliasing={{0}: (7, {}), {1}: (8, {}), {2}: (9, {}), {3}: (10, {})} | custom-call | flops 14000000000 | bytes 14000000 | tf_op jit(solution)/shard_map/pallas_call | solution.py:96
  263.7 10.9 %shard_map.240 = (bf16[5,512,768]{2,1,0:T(8,128)(2,1)}, bf16[5,512,768]{2,1,0:T(8,128)(2,1)}, bf16[5,512,3072]{2,1,0:T(8,128)(2,1)}, bf16[5,512,3072]{2,1,0:T(8,...) custom-call(s32[50]{0:T(128)S(1)} %reshape.890.sp_ref, ...), custom_call_target="tpu_custom_call", output_to_operand_aliasing={{0}: (9, {}), {1}: (10, {}), {2}: (11, {}), {3}: (12, {}), ... | custom-call | flops 10000000000 | bytes 10000000 | tf_op jit(solution)/shard_map/pallas_call | solution.py:96
  279.2 12.3 %shard_map.243 = (bf16[5,512,768]{2,1,0:T(8,128)(2,1)}, bf16[5,512,3072]{2,1,0:T(8,128)(2,1)}, bf16[5,512,768]{2,1,0:T(8,128)(2,1)}, f32[5,8,768]{2,1,0:T(8,128)...) custom-call(s32[50]{0:T(128)S(1)} %reshape.890.sp_ref, ...), custom_call_target="tpu_custom_call", output_to_operand_aliasing={{0}: (14, {}), {1}: (15, {}), {2}: (16, {}), {3}: (17, {}),... | custom-call | flops 10000000000 | bytes 10000000 | tf_op jit(solution)/shard_map/pallas_call | solution.py:96
  291.5 18.0 %shard_map.244 = (f32[5,64,768]{2,1,0:T(8,128)}, bf16[512,768]{1,0:T(8,128)(2,1)S(1)}, bf16[512,1536]{1,0:T(8,128)(2,1)S(1)}, bf16[512,1536]{1,0:T(8,128)(2,1)}) custom-call(s32[50]{0:T(128)S(1)} %reshape.890.sp_ref, bf16[5,512,768]{2,1,0:T(8,128)(2,1)} %get-tuple-element.320.refs_0_.refs_5_, ...), custom_call_target="tpu_custom_call", output_to_operand_aliasing={{0}: (11, {})} | custom-call | flops 20000000000 | bytes 20000000 | tf_op jit(solution)/shard_map/pallas_call | solution.py:96
  328.4 10.9 %shard_map.246 = (bf16[5,512,768]{2,1,0:T(8,128)(2,1)}, bf16[5,512,768]{2,1,0:T(8,128)(2,1)}, bf16[5,512,3072]{2,1,0:T(8,128)(2,1)}, bf16[5,512,3072]{2,1,0:T(8,...) custom-call(s32[50]{0:T(128)S(1)} %reshape.890.sp_ref, ...), custom_call_target="tpu_custom_call", output_to_operand_aliasing={{0}: (9, {}), {1}: (10, {}), {2}: (11, {}), {3}: (12, {}), ... | custom-call | flops 10000000000 | bytes 10000000 | tf_op jit(solution)/shard_map/pallas_call | solution.py:96
  344.5 12.3 %shard_map.247 = (bf16[5,512,768]{2,1,0:T(8,128)(2,1)}, bf16[5,512,3072]{2,1,0:T(8,128)(2,1)}, bf16[5,512,768]{2,1,0:T(8,128)(2,1)}, f32[5,8,768]{2,1,0:T(8,128)...) custom-call(s32[50]{0:T(128)S(1)} %reshape.890.sp_ref, ...), custom_call_target="tpu_custom_call", output_to_operand_aliasing={{0}: (14, {}), {1}: (15, {}), {2}: (16, {}), {3}: (17, {}),... | custom-call | flops 10000000000 | bytes 10000000 | tf_op jit(solution)/shard_map/pallas_call | solution.py:96
  356.8 21.7 %shard_map.248 = (f32[5,64,768]{2,1,0:T(8,128)}, bf16[512,768]{1,0:T(8,128)(2,1)S(1)}, bf16[512,1536]{1,0:T(8,128)(2,1)S(1)}, bf16[512,1536]{1,0:T(8,128)(2,1)S(1)}) custom-call(s32[50]{0:T(128)S(1)} %reshape.890.sp_ref, bf16[5,512,768]{2,1,0:T(8,128)(2,1)} %get-tuple-element.329.refs_0_, ...), custom_call_target="tpu_custom_call", output_to_operand_aliasing={{0}: (11, {})} | custom-call | flops 20000000000 | bytes 20000000 | tf_op jit(solution)/shard_map/pallas_call | solution.py:96
  391.7 26.0 %collective-permute-done.18.refs_1_ = bf16[512,768]{1,0:T(8,128)(2,1)S(1)} collective-permute-done((bf16[512,768]{1,0:T(8,128)(2,1)S(1)}, bf16[512,768]{1,0:T(8,128)(2,1)S(1)}, u32[]{:S(2)}, u32[]{:S(2)}) %collective-permute-start.18) | collective-permute-done | bytes 786464 | tf_op jit(solution)/shard_map/ppermute | solution.py:985
  417.7 12.2 %shard_map.250 = (bf16[5,512,768]{2,1,0:T(8,128)(2,1)}, bf16[5,512,3072]{2,1,0:T(8,128)(2,1)}, bf16[5,512,768]{2,1,0:T(8,128)(2,1)}, f32[5,8,768]{2,1,0:T(8,128)...) custom-call(s32[50]{0:T(128)S(1)} %reshape.890.sp_ref, ...), custom_call_target="tpu_custom_call", output_to_operand_aliasing={{0}: (14, {}), {1}: (15, {}), {2}: (16, {}), {3}: (17, {}),... | custom-call | flops 10000000000 | bytes 10000000 | tf_op jit(solution)/shard_map/pallas_call | solution.py:96
  430.0 16.0 %shard_map.251 = (bf16[384,3072]{1,0:T(8,128)(2,1)}, bf16[384,3072]{1,0:T(8,128)(2,1)S(1)}) custom-call(s32[50]{0:T(128)S(1)} %reshape.890.sp_ref, bf16[5,512,768]{2,1,0:T(8,128)(2,1)} %get-tuple-element.381.refs_0_, bf16[5,512,3072]{2,1,0:T(8,128)(2,1)} %get-tuple-element.382.refs_1_), custom_call_target="tpu_custom_call" | custom-call | flops 12000000000 | bytes 12000000 | tf_op jit(solution)/shard_map/pallas_call | solution.py:96
  447.8 15.2 %shard_map.252 = (bf16[384,3072]{1,0:T(8,128)(2,1)S(1)}, bf16[384,3072]{1,0:T(8,128)(2,1)S(1)}) custom-call(s32[50]{0:T(128)S(1)} %reshape.890.sp_ref, bf16[5,512,768]{2,1,0:T(8,128)(2,1)} %get-tuple-element.386.refs_0_, bf16[5,512,3072]{2,1,0:T(8,128)(2,1)} %get-tuple-element.387.refs_1_), custom_call_target="tpu_custom_call" | custom-call | flops 12000000000 | bytes 12000000 | tf_op jit(solution)/shard_map/pallas_call | solution.py:96
  467.4 21.2 %shard_map.253 = (f32[5,64,768]{2,1,0:T(8,128)}, bf16[512,768]{1,0:T(8,128)(2,1)S(1)}, bf16[512,1536]{1,0:T(8,128)(2,1)S(1)}, bf16[512,1536]{1,0:T(8,128)(2,1)S(1)}) custom-call(s32[50]{0:T(128)S(1)} %reshape.890.sp_ref, bf16[5,512,768]{2,1,0:T(8,128)(2,1)} %get-tuple-element.329.refs_0_, ...), custom_call_target="tpu_custom_call", output_to_operand_aliasing={{0}: (11, {})} | custom-call | flops 20000000000 | bytes 20000000 | tf_op jit(solution)/shard_map/pallas_call | solution.py:96
  488.6 10.7 %collective-permute-start.23 = (bf16[512,1536]{1,0:T(8,128)(2,1)S(1)}, bf16[512,1536]{1,0:T(8,128)(2,1)S(1)}, u32[]{:S(2)}, u32[]{:S(2)}) collective-permute-start(bf16[512,1536]{1,0:T(8,128)(2,1)S(1)} %get-tuple-element.400), channel_id=1, source_target_pairs={{0,1},{1,0},{2,3},{3,2},{4,5},{5,4},{6,7},{7,6},{8,9},{9,8},{10,11... | collective-permute-start | bytes 4718600 | tf_op jit(solution)/shard_map/ppermute | solution.py:843
  521.9 18.7 %shard_map.255 = (bf16[384,3072]{1,0:T(8,128)(2,1)}, bf16[384,3072]{1,0:T(8,128)(2,1)S(1)}) custom-call(s32[50]{0:T(128)S(1)} %reshape.890.sp_ref, bf16[5,512,768]{2,1,0:T(8,128)(2,1)} %get-tuple-element.407.refs_1_.refs_0_, bf16[5,512,768]{2,1,0:T(8,128)(2,1)} %get-tuple-element.355.refs_0_.refs_11_.refs_1_, ...), custom_call_target="tpu_custom_call" | custom-call | flops 12000000000 | bytes 12000000 | tf_op jit(solution)/shard_map/pallas_call | solution.py:96
  556.0 13.9 %collective-permute-done.29 = bf16[48,3072]{1,0:T(8,128)(2,1)S(1)} collective-permute-done((bf16[48,3072]{1,0:T(8,128)(2,1)S(1)}, bf16[48,3072]{1,0:T(8,128)(2,1)S(1)}, u32[]{:S(2)}, u32[]{:S(2)}) %collective-permute-start.29) | collective-permute-done | bytes 294944 | tf_op jit(solution)/shard_map/ppermute | solution.py:779
  578.1 13.5 %collective-permute-done.33 = bf16[48,3072]{1,0:T(8,128)(2,1)S(1)} collective-permute-done((bf16[48,3072]{1,0:T(8,128)(2,1)S(1)}, bf16[48,3072]{1,0:T(8,128)(2,1)S(1)}, u32[]{:S(2)}, u32[]{:S(2)}) %collective-permute-start.33) | collective-permute-done | bytes 294944 | tf_op jit(solution)/shard_map/ppermute | solution.py:779
  601.1 15.7 %collective-permute-done.37 = bf16[96,3072]{1,0:T(8,128)(2,1)S(1)} collective-permute-done((bf16[96,3072]{1,0:T(8,128)(2,1)S(1)}, bf16[96,3072]{1,0:T(8,128)(2,1)S(1)}, u32[]{:S(2)}, u32[]{:S(2)}) %collective-permute-start.37) | collective-permute-done | bytes 589856 | tf_op jit(solution)/shard_map/ppermute | solution.py:779
  617.8 9.3 %collective-permute-done.35 = bf16[96,3072]{1,0:T(8,128)(2,1)S(1)} collective-permute-done((bf16[96,3072]{1,0:T(8,128)(2,1)S(1)}, bf16[96,3072]{1,0:T(8,128)(2,1)S(1)}, u32[]{:S(2)}, u32[]{:S(2)}) %collective-permute-start.35) | collective-permute-done | bytes 589856 | tf_op jit(solution)/shard_map/ppermute | solution.py:779
  630.4 15.2 %collective-permute-done.41 = bf16[192,3072]{1,0:T(8,128)(2,1)S(1)} collective-permute-done((bf16[192,3072]{1,0:T(8,128)(2,1)S(1)}, bf16[192,3072]{1,0:T(8,128)(2,1)S(1)}, u32[]{:S(2)}, u32[]{:S(2)}) %collective-permute-start.41) | collective-permute-done | bytes 1179680 | tf_op jit(solution)/shard_map/ppermute | solution.py:779
  668.6 15.8 %collective-permute-done.42 = bf16[48,3072]{1,0:T(8,128)(2,1)S(1)} collective-permute-done((bf16[48,3072]{1,0:T(8,128)(2,1)S(1)}, bf16[48,3072]{1,0:T(8,128)(2,1)S(1)}, u32[]{:S(2)}, u32[]{:S(2)}) %collective-permute-start.42) | collective-permute-done | bytes 294944 | tf_op jit(solution)/shard_map/ppermute | solution.py:779
  695.3 15.9 %collective-permute-done.47 = bf16[192,3072]{1,0:T(8,128)(2,1)S(1)} collective-permute-done((bf16[192,3072]{1,0:T(8,128)(2,1)S(1)}, bf16[192,3072]{1,0:T(8,128)(2,1)S(1)}, u32[]{:S(2)}, u32[]{:S(2)}) %collective-permute-start.47) | collective-permute-done | bytes 1179680 | tf_op jit(solution)/shard_map/ppermute | solution.py:779
  (387 shorter events, 263.3 us)
Async XLA Ops:
  3.3 20.9 %collective-permute-start = (s32[2,2176]{1,0:T(2,128)}, s32[2,2176]{1,0:T(2,128)}, u32[]{:S(2)}, u32[]{:S(2)}) collective-permute-start(s32[2,2176]{1,0:T(2,128)} %pad_add_fusion.3), channel_id=1, source_target_pairs={{0,1},{1,0},{2,3},{3,2},{4,5},{5,4},{6,7},{7,6},{8,9},{9,8},{10,11... | collective-permute-start | bytes 52232 | tf_op jit(solution)/shard_map/ppermute | solution.py:843
  7.0 26.7 %collective-permute-start.1 = (bf16[2,512,768]{2,1,0:T(8,128)(2,1)}, bf16[2,512,768]{2,1,0:T(8,128)(2,1)}, u32[]{:S(2)}, u32[]{:S(2)}) collective-permute-start(bf16[2,512,768]{2,1,0:T(8,128)(2,1)} %select_bitcast_fusion.2), channel_id=1, source_target_pairs={{0,1},{1,0},{2,3},{3,2},{4,5},{5,4},{6,7},{7,6},{8,9},{9,8},{10,11... | collective-permute-start | bytes 4718600 | tf_op jit(solution)/shard_map/ppermute | solution.py:843
  81.3 18.6 %collective-permute-start.3 = (bf16[512,768]{1,0:T(8,128)(2,1)S(1)}, bf16[512,768]{1,0:T(8,128)(2,1)S(1)}, u32[]{:S(2)}, u32[]{:S(2)}) collective-permute-start(bf16[512,768]{1,0:T(8,128)(2,1)S(1)} %get-tuple-element.252), channel_id=1, source_target_pairs={{0,16},{1,17},{2,18},{3,19},{4,20},{5,21},{6,22},{7,23},{8,24},{9,... | collective-permute-start | bytes 2359304 | tf_op jit(solution)/shard_map/ppermute | solution.py:978
  131.8 27.1 %collective-permute-start.5 = (bf16[512,768]{1,0:T(8,128)(2,1)S(1)}, bf16[512,768]{1,0:T(8,128)(2,1)S(1)}, u32[]{:S(2)}, u32[]{:S(2)}) collective-permute-start(bf16[512,768]{1,0:T(8,128)(2,1)S(1)} %get-tuple-element.267), channel_id=1, source_target_pairs={{0,16},{1,17},{2,18},{3,19},{4,20},{5,21},{6,22},{7,23},{8,24},{9,... | collective-permute-start | bytes 2359304 | tf_op jit(solution)/shard_map/ppermute | solution.py:978
  171.1 34.0 %collective-permute-start.8 = (bf16[512,768]{1,0:T(8,128)(2,1)S(1)}, bf16[512,768]{1,0:T(8,128)(2,1)S(1)}, u32[]{:S(2)}, u32[]{:S(2)}) collective-permute-start(bf16[512,768]{1,0:T(8,128)(2,1)S(1)} %get-tuple-element.295), channel_id=1, source_target_pairs={{16,0},{17,1},{18,2},{19,3},{20,4},{21,5},{22,6},{23,7},{24,8},{25... | collective-permute-start | bytes 2359304 | tf_op jit(solution)/shard_map/ppermute | solution.py:985
  197.4 39.1 %collective-permute-start.10 = (bf16[512,768]{1,0:T(8,128)(2,1)S(1)}, bf16[512,768]{1,0:T(8,128)(2,1)S(1)}, u32[]{:S(2)}, u32[]{:S(2)}) collective-permute-start(bf16[512,768]{1,0:T(8,128)(2,1)S(1)} %get-tuple-element.319), channel_id=1, source_target_pairs={{0,16},{1,17},{2,18},{3,19},{4,20},{5,21},{6,22},{7,23},{8,24},{9,... | collective-permute-start | bytes 2359304 | tf_op jit(solution)/shard_map/ppermute | solution.py:978
  248.5 30.8 %collective-permute-start.14 = (bf16[512,768]{1,0:T(8,128)(2,1)S(1)}, bf16[512,768]{1,0:T(8,128)(2,1)S(1)}, u32[]{:S(2)}, u32[]{:S(2)}) collective-permute-start(bf16[512,768]{1,0:T(8,128)(2,1)S(1)} %get-tuple-element.318), channel_id=1, source_target_pairs={{16,0},{17,1},{18,2},{19,3},{20,4},{21,5},{22,6},{23,7},{24,8},{25... | collective-permute-start | bytes 2359304 | tf_op jit(solution)/shard_map/ppermute | solution.py:985
  274.6 36.1 %collective-permute-start.12 = (bf16[512,768]{1,0:T(8,128)(2,1)S(1)}, bf16[512,768]{1,0:T(8,128)(2,1)S(1)}, u32[]{:S(2)}, u32[]{:S(2)}) collective-permute-start(bf16[512,768]{1,0:T(8,128)(2,1)S(1)} %get-tuple-element.326), channel_id=1, source_target_pairs={{0,16},{1,17},{2,18},{3,19},{4,20},{5,21},{6,22},{7,23},{8,24},{9,... | collective-permute-start | bytes 2359304 | tf_op jit(solution)/shard_map/ppermute | solution.py:978
  322.5 22.0 %collective-permute-start.16 = (bf16[512,768]{1,0:T(8,128)(2,1)S(1)}, bf16[512,768]{1,0:T(8,128)(2,1)S(1)}, u32[]{:S(2)}, u32[]{:S(2)}) collective-permute-start(bf16[512,768]{1,0:T(8,128)(2,1)S(1)} %get-tuple-element.354), channel_id=1, source_target_pairs={{16,0},{17,1},{18,2},{19,3},{20,4},{21,5},{22,6},{23,7},{24,8},{25... | collective-permute-start | bytes 2359304 | tf_op jit(solution)/shard_map/ppermute | solution.py:985
  390.4 27.3 %collective-permute-start.18 = (bf16[512,768]{1,0:T(8,128)(2,1)S(1)}, bf16[512,768]{1,0:T(8,128)(2,1)S(1)}, u32[]{:S(2)}, u32[]{:S(2)}) collective-permute-start(bf16[512,768]{1,0:T(8,128)(2,1)S(1)} %get-tuple-element.376), channel_id=1, source_target_pairs={{16,0},{17,1},{18,2},{19,3},{20,4},{21,5},{22,6},{23,7},{24,8},{25... | collective-permute-start | bytes 2359304 | tf_op jit(solution)/shard_map/ppermute | solution.py:985
  446.0 17.4 %collective-permute-start.19 = (bf16[384,3072]{1,0:T(8,128)(2,1)}, bf16[384,3072]{1,0:T(8,128)(2,1)}, u32[]{:S(2)}, u32[]{:S(2)}) collective-permute-start(bf16[384,3072]{1,0:T(8,128)(2,1)} %get-tuple-element.384), channel_id=1, source_target_pairs={{0,1},{1,0},{2,3},{3,2},{4,5},{5,4},{6,7},{7,6},{8,9},{9,8},{10,11... | collective-permute-start | bytes 7077896 | tf_op jit(solution)/shard_map/ppermute | solution.py:782
  463.0 36.5 %collective-permute-start.21 = (bf16[384,3072]{1,0:T(8,128)(2,1)S(1)}, bf16[384,3072]{1,0:T(8,128)(2,1)S(1)}, u32[]{:S(2)}, u32[]{:S(2)}) collective-permute-start(bf16[384,3072]{1,0:T(8,128)(2,1)S(1)} %get-tuple-element.388), channel_id=1, source_target_pairs={{0,1},{1,0},{2,3},{3,2},{4,5},{5,4},{6,7},{7,6},{8,9},{9,8},{10,11... | collective-permute-start | bytes 7077896 | tf_op jit(solution)/shard_map/ppermute | solution.py:782
  466.2 38.0 %collective-permute-start.20 = (bf16[192,3072]{1,0:T(8,128)(2,1)S(1)}, bf16[192,3072]{1,0:T(8,128)(2,1)S(1)}, u32[]{:S(2)}, u32[]{:S(2)}) collective-permute-start(bf16[192,3072]{1,0:T(8,128)(2,1)S(1)} %constant_dynamic-slice_fusion.8), channel_id=1, source_target_pairs={{0,2},{1,5},{2,0},{3,7},{4,6},{5,1},{6,4},{7,3},{8,10},{9,13},{10,... | collective-permute-start | bytes 3538952 | tf_op jit(solution)/shard_map/ppermute | solution.py:779
  488.6 17.5 %collective-permute-start.23 = (bf16[512,1536]{1,0:T(8,128)(2,1)S(1)}, bf16[512,1536]{1,0:T(8,128)(2,1)S(1)}, u32[]{:S(2)}, u32[]{:S(2)}) collective-permute-start(bf16[512,1536]{1,0:T(8,128)(2,1)S(1)} %get-tuple-element.400), channel_id=1, source_target_pairs={{0,1},{1,0},{2,3},{3,2},{4,5},{5,4},{6,7},{7,6},{8,9},{9,8},{10,11... | collective-permute-start | bytes 4718600 | tf_op jit(solution)/shard_map/ppermute | solution.py:843
  504.1 47.5 %collective-permute-start.27 = (bf16[192,3072]{1,0:T(8,128)(2,1)}, bf16[192,3072]{1,0:T(8,128)(2,1)}, u32[]{:S(2)}, u32[]{:S(2)}) collective-permute-start(bf16[192,3072]{1,0:T(8,128)(2,1)} %constant_dynamic-slice_fusion.6), channel_id=1, source_target_pairs={{0,2},{1,5},{2,0},{3,7},{4,6},{5,1},{6,4},{7,3},{8,10},{9,13},{10,... | collective-permute-start | bytes 3538952 | tf_op jit(solution)/shard_map/ppermute | solution.py:779
  504.6 16.3 %collective-permute-start.22 = (bf16[96,3072]{1,0:T(8,128)(2,1)S(1)}, bf16[96,3072]{1,0:T(8,128)(2,1)S(1)}, u32[]{:S(2)}, u32[]{:S(2)}) collective-permute-start(bf16[96,3072]{1,0:T(8,128)(2,1)S(1)} %constant_dynamic-slice_fusion.7), channel_id=1, source_target_pairs={{0,4},{1,3},{2,6},{3,1},{4,0},{5,7},{6,2},{7,5},{8,12},{9,11},{10,... | collective-permute-start | bytes 1769480 | tf_op jit(solution)/shard_map/ppermute | solution.py:779
  540.6 32.7 %collective-permute-start.26 = (bf16[384,3072]{1,0:T(8,128)(2,1)}, bf16[384,3072]{1,0:T(8,128)(2,1)}, u32[]{:S(2)}, u32[]{:S(2)}) collective-permute-start(bf16[384,3072]{1,0:T(8,128)(2,1)} %get-tuple-element.408), channel_id=1, source_target_pairs={{0,1},{1,0},{2,3},{3,2},{4,5},{5,4},{6,7},{7,6},{8,9},{9,8},{10,11... | collective-permute-start | bytes 7077896 | tf_op jit(solution)/shard_map/ppermute | solution.py:782
  543.0 109.0 %collective-permute-start.24 = (bf16[2,512,768]{2,1,0:T(8,128)(2,1)}, bf16[2,512,768]{2,1,0:T(8,128)(2,1)}, u32[]{:S(2)}, u32[]{:S(2)}) collective-permute-start(bf16[2,512,768]{2,1,0:T(8,128)(2,1)} %broadcast_select_fusion.1), channel_id=1, source_target_pairs={{0,1},{1,0},{2,3},{3,2},{4,5},{5,4},{6,7},{7,6},{8,9},{9,8},{10,11... | collective-permute-start | bytes 4718600 | tf_op jit(solution)/shard_map/ppermute | solution.py:843
  551.0 24.8 %collective-permute-start.25 = (f32[88,128]{1,0:T(8,128)S(1)}, f32[88,128]{1,0:T(8,128)S(1)}, u32[]{:S(2)}, u32[]{:S(2)}) collective-permute-start(f32[88,128]{1,0:T(8,128)S(1)} %pad_bitcast_fusion), channel_id=1, source_target_pairs={{0,1},{1,0},{2,3},{3,2},{4,5},{5,4},{6,7},{7,6},{8,9},{9,8},{10,11... | collective-permute-start | bytes 135176 | tf_op jit(solution)/shard_map/ppermute | solution.py:814
  553.6 16.3 %collective-permute-start.29 = (bf16[48,3072]{1,0:T(8,128)(2,1)S(1)}, bf16[48,3072]{1,0:T(8,128)(2,1)S(1)}, u32[]{:S(2)}, u32[]{:S(2)}) collective-permute-start(bf16[48,3072]{1,0:T(8,128)(2,1)S(1)} %constant_dynamic-slice_fusion.4), channel_id=1, source_target_pairs={{0,8},{1,9},{2,10},{3,11},{4,12},{5,13},{6,14},{7,15},{8,0},{9,1},... | collective-permute-start | bytes 884744 | tf_op jit(solution)/shard_map/ppermute | solution.py:779
  570.0 21.6 %collective-permute-start.33 = (bf16[48,3072]{1,0:T(8,128)(2,1)S(1)}, bf16[48,3072]{1,0:T(8,128)(2,1)S(1)}, u32[]{:S(2)}, u32[]{:S(2)}) collective-permute-start(bf16[48,3072]{1,0:T(8,128)(2,1)S(1)} %dynamic-slice_add_fusion.8), channel_id=1, source_target_pairs={{0,8},{1,9},{2,10},{3,11},{4,12},{5,13},{6,14},{7,15},{8,0},{9,1},... | collective-permute-start | bytes 884744 | tf_op jit(solution)/shard_map/ppermute | solution.py:779
  570.3 27.5 %collective-permute-start.32 = (bf16[48,3072]{1,0:T(8,128)(2,1)S(1)}, bf16[48,3072]{1,0:T(8,128)(2,1)S(1)}, u32[]{:S(2)}, u32[]{:S(2)}) collective-permute-start(bf16[48,3072]{1,0:T(8,128)(2,1)S(1)} %constant_dynamic-slice_fusion.2), channel_id=1, source_target_pairs={{0,8},{1,9},{2,10},{3,11},{4,12},{5,13},{6,14},{7,15},{8,0},{9,1},... | collective-permute-start | bytes 884744 | tf_op jit(solution)/shard_map/ppermute | solution.py:779
  575.8 22.6 %collective-permute-start.30 = (f32[88,128]{1,0:T(8,128)S(1)}, f32[88,128]{1,0:T(8,128)S(1)}, u32[]{:S(2)}, u32[]{:S(2)}) collective-permute-start(f32[88,128]{1,0:T(8,128)S(1)} %fusion.31), channel_id=1, source_target_pairs={{0,2},{1,3},{2,0},{3,1},{4,6},{5,7},{6,4},{7,5},{8,10},{9,11},{10,... | collective-permute-start | bytes 135176 | tf_op jit(solution)/shard_map/ppermute | solution.py:814
  577.6 20.4 %collective-permute-start.31 = (bf16[192,3072]{1,0:T(8,128)(2,1)S(1)}, bf16[192,3072]{1,0:T(8,128)(2,1)S(1)}, u32[]{:S(2)}, u32[]{:S(2)}) collective-permute-start(bf16[192,3072]{1,0:T(8,128)(2,1)S(1)} %constant_dynamic-slice_fusion.3), channel_id=1, source_target_pairs={{0,2},{1,5},{2,0},{3,7},{4,6},{5,1},{6,4},{7,3},{8,10},{9,13},{10,... | collective-permute-start | bytes 3538952 | tf_op jit(solution)/shard_map/ppermute | solution.py:779
  591.7 25.2 %collective-permute-start.37 = (bf16[96,3072]{1,0:T(8,128)(2,1)S(1)}, bf16[96,3072]{1,0:T(8,128)(2,1)S(1)}, u32[]{:S(2)}, u32[]{:S(2)}) collective-permute-start(bf16[96,3072]{1,0:T(8,128)(2,1)S(1)} %pad_maximum_fusion.10), channel_id=1, source_target_pairs={{0,4},{1,3},{2,6},{3,1},{4,0},{5,7},{6,2},{7,5},{8,12},{9,11},{10,... | collective-permute-start | bytes 1769480 | tf_op jit(solution)/shard_map/ppermute | solution.py:779
  597.9 19.7 %collective-permute-start.36 = (bf16[48,3072]{1,0:T(8,128)(2,1)S(1)}, bf16[48,3072]{1,0:T(8,128)(2,1)S(1)}, u32[]{:S(2)}, u32[]{:S(2)}) collective-permute-start(bf16[48,3072]{1,0:T(8,128)(2,1)S(1)} %dynamic-slice_add_fusion.7), channel_id=1, source_target_pairs={{0,8},{1,9},{2,10},{3,11},{4,12},{5,13},{6,14},{7,15},{8,0},{9,1},... | collective-permute-start | bytes 884744 | tf_op jit(solution)/shard_map/ppermute | solution.py:779
  598.5 28.9 %collective-permute-start.34 = (f32[88,128]{1,0:T(8,128)S(1)}, f32[88,128]{1,0:T(8,128)S(1)}, u32[]{:S(2)}, u32[]{:S(2)}) collective-permute-start(f32[88,128]{1,0:T(8,128)S(1)} %fusion.37), channel_id=1, source_target_pairs={{0,4},{1,5},{2,6},{3,7},{4,0},{5,1},{6,2},{7,3},{8,12},{9,13},{10,... | collective-permute-start | bytes 135176 | tf_op jit(solution)/shard_map/ppermute | solution.py:814
  601.0 26.2 %collective-permute-start.35 = (bf16[96,3072]{1,0:T(8,128)(2,1)S(1)}, bf16[96,3072]{1,0:T(8,128)(2,1)S(1)}, u32[]{:S(2)}, u32[]{:S(2)}) collective-permute-start(bf16[96,3072]{1,0:T(8,128)(2,1)S(1)} %constant_dynamic-slice_fusion.1), channel_id=1, source_target_pairs={{0,4},{1,3},{2,6},{3,1},{4,0},{5,7},{6,2},{7,5},{8,12},{9,11},{10,... | collective-permute-start | bytes 1769480 | tf_op jit(solution)/shard_map/ppermute | solution.py:779
  617.2 28.4 %collective-permute-start.41 = (bf16[192,3072]{1,0:T(8,128)(2,1)S(1)}, bf16[192,3072]{1,0:T(8,128)(2,1)S(1)}, u32[]{:S(2)}, u32[]{:S(2)}) collective-permute-start(bf16[192,3072]{1,0:T(8,128)(2,1)S(1)} %pad_maximum_fusion.7), channel_id=1, source_target_pairs={{0,2},{1,5},{2,0},{3,7},{4,6},{5,1},{6,4},{7,3},{8,10},{9,13},{10,... | collective-permute-start | bytes 3538952 | tf_op jit(solution)/shard_map/ppermute | solution.py:779
  617.8 33.4 %collective-permute-start.40 = (bf16[96,3072]{1,0:T(8,128)(2,1)S(1)}, bf16[96,3072]{1,0:T(8,128)(2,1)S(1)}, u32[]{:S(2)}, u32[]{:S(2)}) collective-permute-start(bf16[96,3072]{1,0:T(8,128)(2,1)S(1)} %pad_maximum_fusion.11), channel_id=1, source_target_pairs={{0,4},{1,3},{2,6},{3,1},{4,0},{5,7},{6,2},{7,5},{8,12},{9,11},{10,... | collective-permute-start | bytes 1769480 | tf_op jit(solution)/shard_map/ppermute | solution.py:779
  627.3 24.6 %collective-permute-start.38 = (f32[88,128]{1,0:T(8,128)S(1)}, f32[88,128]{1,0:T(8,128)S(1)}, u32[]{:S(2)}, u32[]{:S(2)}) collective-permute-start(f32[88,128]{1,0:T(8,128)S(1)} %add.280), channel_id=1, source_target_pairs={{0,8},{1,9},{2,10},{3,11},{4,12},{5,13},{6,14},{7,15},{8,0},{9,1},... | collective-permute-start | bytes 135176 | tf_op jit(solution)/shard_map/ppermute | solution.py:814
  627.5 24.4 %collective-permute-start.39 = (bf16[48,3072]{1,0:T(8,128)(2,1)S(1)}, bf16[48,3072]{1,0:T(8,128)(2,1)S(1)}, u32[]{:S(2)}, u32[]{:S(2)}) collective-permute-start(bf16[48,3072]{1,0:T(8,128)(2,1)S(1)} %constant_dynamic-slice_fusion), channel_id=1, source_target_pairs={{0,8},{1,9},{2,10},{3,11},{4,12},{5,13},{6,14},{7,15},{8,0},{9,1},... | collective-permute-start | bytes 884744 | tf_op jit(solution)/shard_map/ppermute | solution.py:779
  (83 other events, 960.8 us)

commit v4 on v3

--- a/solution.py
+++ b/solution.py
@@ -147,6 +147,10 @@
     return pl.BlockSpec((1, rows, cols), lambda i, sp: (sp[0], 0, 0))
 
 
+def as_given(rows, cols):
+    return pl.BlockSpec((1, rows, cols), lambda i, sp: (sp[5], 0, 0))
+
+
 def columns(rows, cols, begin=0):
     return pl.BlockSpec((rows, cols), lambda i, sp: (0, begin + i))
 
@@ -182,7 +186,7 @@
         sp,
         (width // cols,),
         [
-            (own_all, whole_window(rows, width)), (got, fixed(got.shape)), (weight, RESIDENT),
+            (own_all, as_given(rows, width)), (got, fixed(got.shape)), (weight, RESIDENT),
             (bias, fixed(bias.shape)),
         ],
         [(jax.ShapeDtypeStruct((rows, 2 * width), bf16), columns(rows, 2 * cols))],
@@ -268,8 +272,8 @@
             (q_all, part),
             (kv_own, columns(rows, 2 * cols)),
             (kv_peer, columns(rows, 2 * cols)),
-            (side_all, whole_window(rows, PAIR)),
-            (hot_all, whole_window(2 * rows, PAIR)),
+            (side_all, as_given(rows, PAIR)),
+            (hot_all, as_given(2 * rows, PAIR)),
             (matrix, columns(PAIR, cols)),
         ],
         [],
@@ -450,7 +454,7 @@
         sp,
         (1,),
         [
-            (dy_all, row), (got, fixed(got.shape)), (n2_all, row), (r_all, whole_window(rows, PAIR)),
+            (dy_all, as_given(rows, width)), (got, fixed(got.shape)), (n2_all, row), (r_all, whole_window(rows, PAIR)),
             (gains, fixed(gains.shape)), (sel, fixed(sel.shape)), (wo, RESIDENT), (w1, RESIDENT),
             (w2, RESIDENT),
         ]
@@ -558,13 +562,13 @@
             (q_all, part),
             (kv_all, kv),
             (peer_all, kv),
-            (side_all, whole_window(rows, PAIR)),
-            (hot_all, whole_window(2 * rows, PAIR)),
+            (side_all, as_given(rows, PAIR)),
+            (hot_all, as_given(2 * rows, PAIR)),
             (matrix, columns(PAIR, cols)),
             (lse_all, part),
             (do, flat),
             (dd, flat),
-            (turned_all, whole_window(HALF, 2 * rows)),
+            (turned_all, as_given(HALF, 2 * rows)),
         ],
         [(jax.ShapeDtypeStruct((rows, width), bf16), flat), (out_kv, flat_kv), (out_kv, flat_kv)],
         [(cell_all, at_window(HALF, cols))],
@@ -632,34 +636,32 @@
     )
 
 
-def weight_body(splits, sp, *refs):
+def weight_body(splits, based, sp, *refs):
     count = len(splits)
     lefts, rights = refs[:count], refs[count : 2 * count]
-    give_ref, keep_ref = refs[2 * count : 2 * count + 2]
-    turned = refs[2 * count + 2 :]
+    base_refs = refs[2 * count : 2 * count + 2] if based else ()
+    give_ref, keep_ref = refs[-2:]
     step = pl.program_id(0)
-    windows, rows, half = lefts[0].shape[0], lefts[0].shape[1], lefts[0].shape[2] // 2
+    windows, rows, width = lefts[0].shape
+    half = width // 2
     first = sp[2] == 0
 
-    @pl.when(step == 0)
-    def _():
-        for left, scratch in zip(lefts, turned):
-            for w in range(windows):
-                at = slice(w * rows, (w + 1) * rows)
-                low, high = left[w, :, :half], left[w, :, half:]
-                scratch[:half, at] = jnp.where(first, high, low).T
-                scratch[half:, at] = jnp.where(first, low, high).T
-
-    for (begin, end), right, scratch in zip(splits, rights, turned):
+    for (begin, end), left, right in zip(splits, lefts, rights):
 
         @pl.when((step >= begin) & (step < end))
-        def _(right=right, scratch=scratch):
-            out = dot_nn(scratch[...], right[...].reshape(windows * rows, right.shape[2])).astype(bf16)
-            give_ref[...] = out[:half]
-            keep_ref[...] = out[half:]
-
-
-def weight_call(sp, windows, pairs):
+        def _(left=left, right=right):
+            flat = left[...].reshape(windows * rows, width)
+            out = dot_tn(flat, right[...].reshape(windows * rows, right.shape[2]))
+            give = jnp.where(first, out[half:], out[:half])
+            keep = jnp.where(first, out[:half], out[half:])
+            if based:
+                give = give + base_refs[0][...].astype(f32)
+                keep = keep + base_refs[1][...].astype(f32)
+            give_ref[...] = give.astype(bf16)
+            keep_ref[...] = keep.astype(bf16)
+
+
+def weight_call(sp, at, windows, pairs, base=()):
     rows, width = pairs[0][0].shape[1:]
     splits = []
     begin = 0
@@ -669,27 +671,26 @@
 
     def left_spec():
         return pl.BlockSpec(
-            (windows, rows, width), lambda i, sp: (0, 0, 0), pipeline_mode=pl.Buffered(1)
+            (windows, rows, width), lambda i, sp: (at, 0, 0), pipeline_mode=pl.Buffered(1)
         )
 
     def right_spec(begin, end):
         return pl.BlockSpec(
-            (windows, rows, FF_BLOCK), lambda i, sp: (0, 0, jnp.clip(i - begin, 0, end - begin - 1))
+            (windows, rows, FF_BLOCK), lambda i, sp: (at, 0, jnp.clip(i - begin, 0, end - begin - 1))
         )
 
-    half = (
-        jax.ShapeDtypeStruct((width // 2, begin * FF_BLOCK), bf16), columns(width // 2, FF_BLOCK)
-    )
+    half = columns(width // 2, FF_BLOCK)
+    shape = jax.ShapeDtypeStruct((width // 2, begin * FF_BLOCK), bf16)
     return call(
-        functools.partial(weight_body, tuple(splits)),
+        functools.partial(weight_body, tuple(splits), bool(base)),
         sp,
         (begin,),
         [(left, left_spec()) for left, _ in pairs]
-        + [(right, right_spec(*split)) for (_, right), split in zip(pairs, splits)],
-        [half, half],
+        + [(right, right_spec(*split)) for (_, right), split in zip(pairs, splits)]
+        + [(b, half) for b in base],
+        [(shape, half), (shape, half)],
         [],
-        [pltpu.VMEM((width, windows * rows), bf16)] * len(pairs),
-        us=12,
+        us=5 + 3 * windows,
     )
 
 
@@ -767,7 +768,8 @@
         self.index = lax.axis_index("dp")
         bits = list(range(1, count.bit_length() - 1))
         turned = bits[:2][::-1] + bits[2:]
-        self.steps = list(zip(bits, turned))
+        self.mixed = list(zip(bits, turned))
+        self.plain = list(zip(bits, bits))
 
     def bit(self, step):
         even, odd = step
@@ -792,15 +794,15 @@
         first = self.bit(step) == 0
         return jnp.concatenate([jnp.where(first, part, got), jnp.where(first, got, part)], axis=0)
 
-    def stages(self, give, keep):
+    def stages(self, give, keep, steps):
         got = self.swap(give)
         order = yield
         part = keep + order(got)
-        for step in self.steps:
+        for step in steps:
             keep, got = self.halve(part, step)
             order = yield part
             part = keep + order(got)
-        for step in self.steps[::-1]:
+        for step in steps[::-1]:
             got = self.send(part, step)
             order = yield part
             part = self.join(part, order(got), step)
@@ -868,17 +870,16 @@
     halves = own.reshape(micro, 2, rows, width)
     own_half = jnp.where(core == 0, halves[:, 0], halves[:, 1])
     other_half = jnp.where(core == 0, halves[:, 1], halves[:, 0])
-    spare = lambda a: jnp.concatenate([a, a[:1]], axis=0)
-    own_all = spare(both(own_half, exchange(other_half)))
+    own_all = both(own_half, exchange(other_half))
     places = jnp.concatenate(
         [horizontal, vertical, jnp.broadcast_to(doc_lengths[:, None], (micro, PAIR))], axis=1
     )
-    places = spare(both(places, exchange(places)))
+    places = both(places, exchange(places))
     across_cell = places[:, :slots] // SPAN
     down_cell = places[:, slots : 2 * slots] // SPAN
     lengths = places[:, 2 * slots]
     ids = jnp.arange(slots, dtype=jnp.int32)
-    position_cell = jnp.broadcast_to((ids // SPAN)[None], (windows + 1, slots))
+    position_cell = jnp.broadcast_to((ids // SPAN)[None], (windows, slots))
 
     def hot_of(cells, lanes, axis):
         p, a, d = (jnp.expand_dims(c, axis) for c in cells)
@@ -896,17 +897,22 @@
 
     sel = (cell_ids[:, None] // HALF != cell_ids[None, :] // HALF).astype(bf16)
 
-    blocks_of = (lengths + KEY_BLOCK - 1) // KEY_BLOCK
-    blocks_of = jnp.where(jnp.arange(windows + 1) < windows, blocks_of, 0)
-    infos = []
-    for _, zero, one in SLOTS:
-        w = jnp.where(
-            section == 0, windows if zero is None else zero, windows if one is None else one
-        ).astype(jnp.int32)
-        infos.append(w)
-    infos = jnp.stack(infos)
+    window_ids = jnp.arange(windows, dtype=jnp.int32)
+    mine, theirs = lengths[:windows][:, None], lengths[:windows][None, :]
+    ahead = (theirs > mine) | ((theirs == mine) & (window_ids[None, :] < window_ids[:, None]))
+    rank = jnp.sum(ahead.astype(jnp.int32), axis=1)
+    picks = jnp.stack(
+        [jnp.array([windows if w is None else w for w in slots_of], jnp.int32) for slots_of in zip(*[s[1:] for s in SLOTS])]
+    )
+    infos = jnp.where(section == 0, picks[0], picks[1])
+    hits = infos[:, None] == rank[None, :]
+    given_ids = jnp.sum(jnp.where(hits, window_ids[None, :], 0), axis=1)
+    given_lengths = jnp.sum(jnp.where(hits, lengths[None, :windows], 0), axis=1)
     infos = jnp.stack(
-        [infos, blocks_of[infos], jnp.full_like(infos, core), lengths[infos], jnp.full_like(infos, section)],
+        [
+            infos, (given_lengths + KEY_BLOCK - 1) // KEY_BLOCK, jnp.full_like(infos, core),
+            given_lengths, jnp.full_like(infos, section), given_ids,
+        ],
         axis=1,
     )
     facts = infos.shape[1]
@@ -997,9 +1003,8 @@
             self.left -= 1
             return self.last
 
-    def weight_sum(pairs):
-        give, keep = weight_call(sp, windows, pairs)
-        return give, Chain(ring.stages(give, keep), 2 * len(ring.steps) + 2)
+    def weight_sum(steps, give, keep):
+        return give, Chain(ring.stages(give, keep, steps), 2 * len(steps) + 2)
 
     natural = [((0, 0), 0, hidden)]
     cols = PAIRS * PAIR
@@ -1007,9 +1012,15 @@
         ((0, j * width + i * cols), (3 * i + j) * cols, cols) for i in range(width // cols) for j in range(3)
     ] + [((1, 0), 3 * width, width)]
 
-    st, grads = dense_back(sp, st, got.pop(("B", SLOTS[-1][1])))
-    given, contract = weight_sum([(st["db2"], st["g"])])
-    given, expand = weight_sum([(after(st["h1"], given), st["df"])])
+    others = windows - 1
+    part_contract = weight_call(sp, 0, others, [(after(st["db2"], out), st["g"])])
+    part_expand = weight_call(sp, 0, others, [(after(st["h1"], part_contract[0]), st["df"])])
+    rows_in = after(got.pop(("B", SLOTS[-1][1])), part_expand[0])
+    st, grads = dense_back(sp, st, rows_in)
+    halves = weight_call(sp, others, 1, [(st["db2"], st["g"])], part_contract)
+    given, contract = weight_sum(ring.mixed, *halves)
+    halves = weight_call(sp, others, 1, [(after(st["h1"], given), st["df"])], part_expand)
+    given, expand = weight_sum(ring.plain, *halves)
     done = contract.advance(given)
     grads = tuple(after(g, done) for g in grads)
     cell, dq, keep, send = attend_back_kernel(sp, st, grads)
@@ -1019,7 +1030,8 @@
     got = after(got, done)
     st, grads_in[SLOTS[-1][1]] = input_back(sp, dict(st, cell=cell), dq, keep, got)
     done = contract.advance(st["dj"])
-    given, attend = weight_sum([(after(st["x"], done), st["dj"]), (st["a"], st["db1"])])
+    halves = weight_call(sp, 0, windows, [(after(st["x"], done), st["dj"]), (st["a"], st["db1"])])
+    given, attend = weight_sum(ring.mixed, *halves)
 
     later = lambda a: after(a, given)
     of_windows = lambda name: jnp.sum(later(st[name])[:windows], axis=0)
@@ -1030,7 +1042,9 @@
     packed = jnp.pad(packed, (0, -packed.shape[0] % (8 * PAIR))).reshape(-1, PAIR)
     totals = Chain(ring.totals(packed), dp_count.bit_length() - 1)
     result = [later(jnp.where(section == 0, grads_in[w], finals[w])) for w in range(windows)]
-    mine_first, mine_second = jnp.stack(result[:micro]), jnp.stack(result[micro:])
+    result = jnp.stack(result)
+    ordered = [lax.dynamic_index_in_dim(result, rank[w], 0, keepdims=False) for w in range(windows)]
+    mine_first, mine_second = jnp.stack(ordered[:micro]), jnp.stack(ordered[micro:])
     keep_rows = jnp.where(core == 0, mine_first, mine_second)
     got_rows = exchange(jnp.where(core == 0, mine_second, mine_first))
 

time: 736 us -> 749 us (1.018)
  starting transfers between devices: 60.3 us -> 117 us
  waiting for transfers between devices: 178 us -> 144 us
  Pallas kernels: 392 us -> 380 us
  between operations: 2.74 us -> 10.7 us
    ppermute x6, starting transfers between devices: 6.3 us -> 42.2 us  [swap(): return lax.ppermute(a, 'dp', [(i, i ^ 1) for i in range(self.count)])]
    ppermute x18, starting transfers between devices: 12.7 us -> 44.4 us  [send(): return lax.ppermute(a, 'dp', pairs)]
    ppermute x4, waiting for transfers between devices: 30.3 us -> 3.69 us  [on_device(): got['B', one] = lax.ppermute(out, 'section', [(1, 0)])]
    pallas_call x36 -> x38, Pallas kernels: 387 us -> 375 us  [call(): pl.pallas_call(run, grid_spec=pltpu.PrefetchScalarGridSpec(num_scalar_pre...]
    ppermute x13, starting transfers between devices: 13.2 us -> 2.5 us  [on_device(): exchange = lambda a: lax.ppermute(a, 'dp', swap)]
    ppermute x18, waiting for transfers between devices: 125 us -> 117 us  [send(): return lax.ppermute(a, 'dp', pairs)]
    unnamed x135 -> x179, local copies, waits for them, and re-layouts: 16.2 us -> 19.8 us
  transfers between devices with their start and end apart: 49 -> 49, of which waited for: 16 -> 17; matrix products, arithmetic and copies ran while one was open for 10% -> 8% of each run, Pallas kernels for 36% -> 35%
where the time goes in v4:
time: 749 us; the launch traced here: 741 us
  Pallas kernels  380 us (51%)
  waiting for transfers between devices  144 us (19%)
  starting transfers between devices  117 us (16%)
  other arithmetic  44.8 us (6%)
  local copies, waits for them, and re-layouts  40.9 us (5%)
  between operations  10.7 us (1%)
    pallas_call x38, Pallas kernels, call(): pl.pallas_call(run, grid_spec=pltpu.PrefetchScalarGridSpec(num_scalar_pre...  375 us
    ppermute x18, waiting for transfers between devices, send(): return lax.ppermute(a, 'dp', pairs)  117 us
    ppermute x18, starting transfers between devices, send(): return lax.ppermute(a, 'dp', pairs)  44.4 us
    ppermute x6, starting transfers between devices, swap(): return lax.ppermute(a, 'dp', [(i, i ^ 1) for i in range(self.count)])  42.2 us
    ppermute x4, starting transfers between devices, on_device(): got['F', zero] = lax.ppermute(out, 'section', [(0, 1)])  22.4 us
    unnamed x179, local copies, waits for them, and re-layouts  19.8 us
    ppermute x4, waiting for transfers between devices, on_device(): got['F', zero] = lax.ppermute(out, 'section', [(0, 1)])  17.2 us
  transfers between devices with their start and end apart: 49, of which 17 were waited for; matrix products, arithmetic and copies ran while one was open for 8% of the time, Pallas kernels for 35%

profile of v4, /device:TPU:0, one launch (start us, length us, event | category | flops | bytes accessed | tf_op | source)
XLA Modules:
  0.0 740.5 jit_solution(13161142762011013631)
XLA Ops:
  48.0 12.6 %shard_map.242 = (bf16[5,512,768]{2,1,0:T(8,128)(2,1)}, bf16[5,512,768]{2,1,0:T(8,128)(2,1)}, bf16[5,512,768]{2,1,0:T(8,128)(2,1)}, bf16[5,512,1536]{2,1,0:T(8,128)(2,1)}) custom-call(s32[60]{0:T(128)S(1)} %reshape.556.sp_ref, ...), custom_call_target="tpu_custom_call", output_to_operand_aliasing={{0}: (7, {}), {1}: (8, {}), {2}: (9, {}), {3}: (10, {})} | custom-call | flops 14000000000 | bytes 14000000 | tf_op jit(solution)/shard_map/pallas_call | solution.py:96
  60.6 11.1 %shard_map.243 = (bf16[5,512,768]{2,1,0:T(8,128)(2,1)}, bf16[5,512,768]{2,1,0:T(8,128)(2,1)}, bf16[5,512,3072]{2,1,0:T(8,128)(2,1)}, bf16[5,512,3072]{2,1,0:T(8,...) custom-call(s32[60]{0:T(128)S(1)} %reshape.556.sp_ref, ...), custom_call_target="tpu_custom_call", output_to_operand_aliasing={{0}: (9, {}), {1}: (10, {}), {2}: (11, {}), {3}: (12, {}), ... | custom-call | flops 10000000000 | bytes 10000000 | tf_op jit(solution)/shard_map/pallas_call | solution.py:96
  73.1 17.2 %collective-permute-done.3.refs_1_ = bf16[512,768]{1,0:T(8,128)(2,1)S(1)} collective-permute-done((bf16[512,768]{1,0:T(8,128)(2,1)S(1)}, bf16[512,768]{1,0:T(8,128)(2,1)S(1)}, u32[]{:S(2)}, u32[]{:S(2)}) %collective-permute-start.3) | collective-permute-done | bytes 786464 | tf_op jit(solution)/shard_map/ppermute | solution.py:984
  99.6 11.8 %shard_map.245 = (bf16[5,512,768]{2,1,0:T(8,128)(2,1)}, bf16[5,512,768]{2,1,0:T(8,128)(2,1)}, bf16[5,512,768]{2,1,0:T(8,128)(2,1)}, bf16[5,512,1536]{2,1,0:T(8,128)(2,1)}) custom-call(s32[60]{0:T(128)S(1)} %reshape.556.sp_ref, ...), custom_call_target="tpu_custom_call", output_to_operand_aliasing={{0}: (7, {}), {1}: (8, {}), {2}: (9, {}), {3}: (10, {})} | custom-call | flops 14000000000 | bytes 14000000 | tf_op jit(solution)/shard_map/pallas_call | solution.py:96
  111.5 10.9 %shard_map.246 = (bf16[5,512,768]{2,1,0:T(8,128)(2,1)}, bf16[5,512,768]{2,1,0:T(8,128)(2,1)}, bf16[5,512,3072]{2,1,0:T(8,128)(2,1)}, bf16[5,512,3072]{2,1,0:T(8,...) custom-call(s32[60]{0:T(128)S(1)} %reshape.556.sp_ref, ...), custom_call_target="tpu_custom_call", output_to_operand_aliasing={{0}: (9, {}), {1}: (10, {}), {2}: (11, {}), {3}: (12, {}), ... | custom-call | flops 10000000000 | bytes 10000000 | tf_op jit(solution)/shard_map/pallas_call | solution.py:96
  126.8 12.3 %shard_map.249 = (bf16[5,512,768]{2,1,0:T(8,128)(2,1)}, bf16[5,512,3072]{2,1,0:T(8,128)(2,1)}, bf16[5,512,768]{2,1,0:T(8,128)(2,1)}, f32[5,8,768]{2,1,0:T(8,128)...) custom-call(s32[60]{0:T(128)S(1)} %reshape.556.sp_ref, ...), custom_call_target="tpu_custom_call", output_to_operand_aliasing={{0}: (14, {}), {1}: (15, {}), {2}: (16, {}), {3}: (17, {}),... | custom-call | flops 10000000000 | bytes 10000000 | tf_op jit(solution)/shard_map/pallas_call | solution.py:96
  163.0 12.1 %shard_map.248 = (bf16[5,512,768]{2,1,0:T(8,128)(2,1)}, bf16[5,512,768]{2,1,0:T(8,128)(2,1)}, bf16[5,512,768]{2,1,0:T(8,128)(2,1)}, bf16[5,512,1536]{2,1,0:T(8,128)(2,1)}) custom-call(s32[60]{0:T(128)S(1)} %reshape.556.sp_ref, ...), custom_call_target="tpu_custom_call", output_to_operand_aliasing={{0}: (7, {}), {1}: (8, {}), {2}: (9, {}), {3}: (10, {})} | custom-call | flops 14000000000 | bytes 14000000 | tf_op jit(solution)/shard_map/pallas_call | solution.py:96
  175.1 10.8 %shard_map.252 = (bf16[5,512,768]{2,1,0:T(8,128)(2,1)}, bf16[5,512,768]{2,1,0:T(8,128)(2,1)}, bf16[5,512,3072]{2,1,0:T(8,128)(2,1)}, bf16[5,512,3072]{2,1,0:T(8,...) custom-call(s32[60]{0:T(128)S(1)} %reshape.556.sp_ref, ...), custom_call_target="tpu_custom_call", output_to_operand_aliasing={{0}: (9, {}), {1}: (10, {}), {2}: (11, {}), {3}: (12, {}), ... | custom-call | flops 10000000000 | bytes 10000000 | tf_op jit(solution)/shard_map/pallas_call | solution.py:96
  186.0 9.7 %collective-permute-start.10 = (bf16[512,768]{1,0:T(8,128)(2,1)S(1)}, bf16[512,768]{1,0:T(8,128)(2,1)S(1)}, u32[]{:S(2)}, u32[]{:S(2)}) collective-permute-start(bf16[512,768]{1,0:T(8,128)(2,1)S(1)} %get-tuple-element.326), channel_id=1, source_target_pairs={{0,16},{1,17},{2,18},{3,19},{4,20},{5,21},{6,22},{7,23},{8,24},{9,... | collective-permute-start | bytes 2359304 | tf_op jit(solution)/shard_map/ppermute | solution.py:984
  195.7 12.3 %shard_map.253 = (bf16[5,512,768]{2,1,0:T(8,128)(2,1)}, bf16[5,512,3072]{2,1,0:T(8,128)(2,1)}, bf16[5,512,768]{2,1,0:T(8,128)(2,1)}, f32[5,8,768]{2,1,0:T(8,128)...) custom-call(s32[60]{0:T(128)S(1)} %reshape.556.sp_ref, ...), custom_call_target="tpu_custom_call", output_to_operand_aliasing={{0}: (14, {}), {1}: (15, {}), {2}: (16, {}), {3}: (17, {}),... | custom-call | flops 10000000000 | bytes 10000000 | tf_op jit(solution)/shard_map/pallas_call | solution.py:96
  208.0 18.0 %shard_map.254 = (f32[5,64,768]{2,1,0:T(8,128)}, bf16[512,768]{1,0:T(8,128)(2,1)S(1)}, bf16[512,1536]{1,0:T(8,128)(2,1)S(1)}, bf16[512,1536]{1,0:T(8,128)(2,1)S(1)}) custom-call(s32[60]{0:T(128)S(1)} %reshape.556.sp_ref, bf16[5,512,768]{2,1,0:T(8,128)(2,1)} %get-tuple-element.276.refs_0_.refs_5_, ...), custom_call_target="tpu_custom_call", output_to_operand_aliasing={{0}: (11, {})} | custom-call | flops 20000000000 | bytes 20000000 | tf_op jit(solution)/shard_map/pallas_call | solution.py:96
  240.3 9.5 %shard_map.257 = (bf16[5,512,768]{2,1,0:T(8,128)(2,1)}, bf16[5,512,768]{2,1,0:T(8,128)(2,1)}, bf16[5,512,768]{2,1,0:T(8,128)(2,1)}, bf16[5,512,1536]{2,1,0:T(8,128)(2,1)}) custom-call(s32[60]{0:T(128)S(1)} %reshape.556.sp_ref, ...), custom_call_target="tpu_custom_call", output_to_operand_aliasing={{0}: (7, {}), {1}: (8, {}), {2}: (9, {}), {3}: (10, {})} | custom-call | flops 14000000000 | bytes 14000000 | tf_op jit(solution)/shard_map/pallas_call | solution.py:96
  249.9 10.9 %shard_map.258 = (bf16[5,512,768]{2,1,0:T(8,128)(2,1)}, bf16[5,512,768]{2,1,0:T(8,128)(2,1)}, bf16[5,512,3072]{2,1,0:T(8,128)(2,1)}, bf16[5,512,3072]{2,1,0:T(8,...) custom-call(s32[60]{0:T(128)S(1)} %reshape.556.sp_ref, ...), custom_call_target="tpu_custom_call", output_to_operand_aliasing={{0}: (9, {}), {1}: (10, {}), {2}: (11, {}), {3}: (12, {}), ... | custom-call | flops 10000000000 | bytes 10000000 | tf_op jit(solution)/shard_map/pallas_call | solution.py:96
  267.7 12.3 %shard_map.261 = (bf16[5,512,768]{2,1,0:T(8,128)(2,1)}, bf16[5,512,3072]{2,1,0:T(8,128)(2,1)}, bf16[5,512,768]{2,1,0:T(8,128)(2,1)}, f32[5,8,768]{2,1,0:T(8,128)...) custom-call(s32[60]{0:T(128)S(1)} %reshape.556.sp_ref, ...), custom_call_target="tpu_custom_call", output_to_operand_aliasing={{0}: (14, {}), {1}: (15, {}), {2}: (16, {}), {3}: (17, {}),... | custom-call | flops 10000000000 | bytes 10000000 | tf_op jit(solution)/shard_map/pallas_call | solution.py:96
  280.0 17.9 %shard_map.262 = (f32[5,64,768]{2,1,0:T(8,128)}, bf16[512,768]{1,0:T(8,128)(2,1)S(1)}, bf16[512,1536]{1,0:T(8,128)(2,1)S(1)}, bf16[512,1536]{1,0:T(8,128)(2,1)}) custom-call(s32[60]{0:T(128)S(1)} %reshape.556.sp_ref, bf16[5,512,768]{2,1,0:T(8,128)(2,1)} %get-tuple-element.327.refs_0_.refs_5_, ...), custom_call_target="tpu_custom_call", output_to_operand_aliasing={{0}: (11, {})} | custom-call | flops 20000000000 | bytes 20000000 | tf_op jit(solution)/shard_map/pallas_call | solution.py:96
  316.9 10.9 %shard_map.264 = (bf16[5,512,768]{2,1,0:T(8,128)(2,1)}, bf16[5,512,768]{2,1,0:T(8,128)(2,1)}, bf16[5,512,3072]{2,1,0:T(8,128)(2,1)}, bf16[5,512,3072]{2,1,0:T(8,...) custom-call(s32[60]{0:T(128)S(1)} %reshape.556.sp_ref, ...), custom_call_target="tpu_custom_call", output_to_operand_aliasing={{0}: (9, {}), {1}: (10, {}), {2}: (11, {}), {3}: (12, {}), ... | custom-call | flops 10000000000 | bytes 10000000 | tf_op jit(solution)/shard_map/pallas_call | solution.py:96
  332.4 12.3 %shard_map.265 = (bf16[5,512,768]{2,1,0:T(8,128)(2,1)}, bf16[5,512,3072]{2,1,0:T(8,128)(2,1)}, bf16[5,512,768]{2,1,0:T(8,128)(2,1)}, f32[5,8,768]{2,1,0:T(8,128)...) custom-call(s32[60]{0:T(128)S(1)} %reshape.556.sp_ref, ...), custom_call_target="tpu_custom_call", output_to_operand_aliasing={{0}: (14, {}), {1}: (15, {}), {2}: (16, {}), {3}: (17, {}),... | custom-call | flops 10000000000 | bytes 10000000 | tf_op jit(solution)/shard_map/pallas_call | solution.py:96
  344.7 18.0 %shard_map.266 = (f32[5,64,768]{2,1,0:T(8,128)}, bf16[512,768]{1,0:T(8,128)(2,1)S(1)}, bf16[512,1536]{1,0:T(8,128)(2,1)S(1)}, bf16[512,1536]{1,0:T(8,128)(2,1)S(1)}) custom-call(s32[60]{0:T(128)S(1)} %reshape.556.sp_ref, bf16[5,512,768]{2,1,0:T(8,128)(2,1)} %get-tuple-element.336.refs_0_, ...), custom_call_target="tpu_custom_call", output_to_operand_aliasing={{0}: (11, {})} | custom-call | flops 20000000000 | bytes 20000000 | tf_op jit(solution)/shard_map/pallas_call | solution.py:96
  375.9 11.5 %shard_map.268 = (bf16[384,3072]{1,0:T(8,128)(2,1)S(1)}, bf16[384,3072]{1,0:T(8,128)(2,1)S(1)}) custom-call(s32[60]{0:T(128)S(1)} %reshape.556.sp_ref, bf16[5,512,768]{2,1,0:T(8,128)(2,1)} %get-tuple-element.386.refs_0_.refs_13_, bf16[5,512,3072]{2,1,0:T(8,128)(2,1)} %get-tuple-element.387.refs_1_), custom_call_target="tpu_custom_call" | custom-call | flops 14000000000 | bytes 14000000 | tf_op jit(solution)/shard_map/pallas_call | solution.py:96
  387.4 11.8 %shard_map.269 = (bf16[384,3072]{1,0:T(8,128)(2,1)S(1)}, bf16[384,3072]{1,0:T(8,128)(2,1)S(1)}) custom-call(s32[60]{0:T(128)S(1)} %reshape.556.sp_ref, bf16[5,512,768]{2,1,0:T(8,128)(2,1)} %get-tuple-element.399.refs_0_, bf16[5,512,3072]{2,1,0:T(8,128)(2,1)} %get-tuple-element.390.refs_1_.refs_14_), custom_call_target="tpu_custom_call" | custom-call | flops 14000000000 | bytes 14000000 | tf_op jit(solution)/shard_map/pallas_call | solution.py:96
  400.7 13.3 %shard_map.270 = (bf16[5,512,768]{2,1,0:T(8,128)(2,1)}, bf16[5,512,3072]{2,1,0:T(8,128)(2,1)}, bf16[5,512,768]{2,1,0:T(8,128)(2,1)}, f32[5,8,768]{2,1,0:T(8,128)...) custom-call(s32[60]{0:T(128)S(1)} %reshape.556.sp_ref, ...), custom_call_target="tpu_custom_call", output_to_operand_aliasing={{0}: (14, {}), {1}: (15, {}), {2}: (16, {}), {3}: (17, {}),... | custom-call | flops 10000000000 | bytes 10000000 | tf_op jit(solution)/shard_map/pallas_call | solution.py:96
  450.9 13.9 %shard_map.273 = (f32[5,64,768]{2,1,0:T(8,128)}, bf16[512,768]{1,0:T(8,128)(2,1)S(1)}, bf16[512,1536]{1,0:T(8,128)(2,1)S(1)}, bf16[512,1536]{1,0:T(8,128)(2,1)S(1)}) custom-call(s32[60]{0:T(128)S(1)} %reshape.556.sp_ref, bf16[5,512,768]{2,1,0:T(8,128)(2,1)} %get-tuple-element.336.refs_0_, ...), custom_call_target="tpu_custom_call", output_to_operand_aliasing={{0}: (11, {})} | custom-call | flops 20000000000 | bytes 20000000 | tf_op jit(solution)/shard_map/pallas_call | solution.py:96
  482.4 16.9 %shard_map.275 = (bf16[384,3072]{1,0:T(8,128)(2,1)}, bf16[384,3072]{1,0:T(8,128)(2,1)S(1)}) custom-call(s32[60]{0:T(128)S(1)} %reshape.556.sp_ref, bf16[5,512,768]{2,1,0:T(8,128)(2,1)} %get-tuple-element.421.refs_1_.refs_0_, bf16[5,512,768]{2,1,0:T(8,128)(2,1)} %get-tuple-element.362.refs_0_.refs_11_.refs_1_, ...), custom_call_target="tpu_custom_call" | custom-call | flops 16999999488 | bytes 17000000 | tf_op jit(solution)/shard_map/pallas_call | solution.py:96
  499.3 23.0 %collective-permute-start.26 = (bf16[384,3072]{1,0:T(8,128)(2,1)}, bf16[384,3072]{1,0:T(8,128)(2,1)}, u32[]{:S(2)}, u32[]{:S(2)}) collective-permute-start(bf16[384,3072]{1,0:T(8,128)(2,1)} %get-tuple-element.422), channel_id=1, source_target_pairs={{0,1},{1,0},{2,3},{3,2},{4,5},{5,4},{6,7},{7,6},{8,9},{9,8},{10,11... | collective-permute-start | bytes 7077896 | tf_op jit(solution)/shard_map/ppermute | solution.py:784
  534.6 21.0 %collective-permute-start.29 = (bf16[48,3072]{1,0:T(8,128)(2,1)S(1)}, bf16[48,3072]{1,0:T(8,128)(2,1)S(1)}, u32[]{:S(2)}, u32[]{:S(2)}) collective-permute-start(bf16[48,3072]{1,0:T(8,128)(2,1)S(1)} %constant_dynamic-slice_fusion.4), channel_id=1, source_target_pairs={{0,8},{1,9},{2,10},{3,11},{4,12},{5,13},{6,14},{7,15},{8,0},{9,1},... | collective-permute-start | bytes 884744 | tf_op jit(solution)/shard_map/ppermute | solution.py:781
  557.8 10.6 %collective-permute-done.29 = bf16[48,3072]{1,0:T(8,128)(2,1)S(1)} collective-permute-done((bf16[48,3072]{1,0:T(8,128)(2,1)S(1)}, bf16[48,3072]{1,0:T(8,128)(2,1)S(1)}, u32[]{:S(2)}, u32[]{:S(2)}) %collective-permute-start.29) | collective-permute-done | bytes 294944 | tf_op jit(solution)/shard_map/ppermute | solution.py:781
  568.5 15.4 %collective-permute-done.28 = bf16[96,3072]{1,0:T(8,128)(2,1)S(1)} collective-permute-done((bf16[96,3072]{1,0:T(8,128)(2,1)S(1)}, bf16[96,3072]{1,0:T(8,128)(2,1)S(1)}, u32[]{:S(2)}, u32[]{:S(2)}) %collective-permute-start.28) | collective-permute-done | bytes 589856 | tf_op jit(solution)/shard_map/ppermute | solution.py:781
  597.6 12.2 %collective-permute-done.31 = bf16[192,3072]{1,0:T(8,128)(2,1)S(1)} collective-permute-done((bf16[192,3072]{1,0:T(8,128)(2,1)S(1)}, bf16[192,3072]{1,0:T(8,128)(2,1)S(1)}, u32[]{:S(2)}, u32[]{:S(2)}) %collective-permute-start.31) | collective-permute-done | bytes 1179680 | tf_op jit(solution)/shard_map/ppermute | solution.py:781
  640.2 13.5 %collective-permute-start.44 = (bf16[384,3072]{1,0:T(8,128)(2,1)S(1)}, bf16[384,3072]{1,0:T(8,128)(2,1)S(1)}, u32[]{:S(2)}, u32[]{:S(2)}) collective-permute-start(bf16[384,3072]{1,0:T(8,128)(2,1)S(1)} %pad_maximum_fusion.3.refs_0_), channel_id=1, source_target_pairs={{0,1},{1,0},{2,3},{3,2},{4,5},{5,4},{6,7},{7,6},{8,9},{9,8},{10,11... | collective-permute-start | bytes 7077896 | tf_op jit(solution)/shard_map/ppermute | solution.py:784
  665.5 12.3 %collective-permute-done.43 = bf16[192,3072]{1,0:T(8,128)(2,1)S(1)} collective-permute-done((bf16[192,3072]{1,0:T(8,128)(2,1)S(1)}, bf16[192,3072]{1,0:T(8,128)(2,1)S(1)}, u32[]{:S(2)}, u32[]{:S(2)}) %collective-permute-start.43) | collective-permute-done | bytes 1179680 | tf_op jit(solution)/shard_map/ppermute | solution.py:781
  683.8 15.2 %collective-permute-done.42 = bf16[48,3072]{1,0:T(8,128)(2,1)S(1)} collective-permute-done((bf16[48,3072]{1,0:T(8,128)(2,1)S(1)}, bf16[48,3072]{1,0:T(8,128)(2,1)S(1)}, u32[]{:S(2)}, u32[]{:S(2)}) %collective-permute-start.42) | collective-permute-done | bytes 294944 | tf_op jit(solution)/shard_map/ppermute | solution.py:781
  711.5 14.2 %collective-permute-done.47 = bf16[192,3072]{1,0:T(8,128)(2,1)S(1)} collective-permute-done((bf16[192,3072]{1,0:T(8,128)(2,1)S(1)}, bf16[192,3072]{1,0:T(8,128)(2,1)S(1)}, u32[]{:S(2)}, u32[]{:S(2)}) %collective-permute-start.47) | collective-permute-done | bytes 1179680 | tf_op jit(solution)/shard_map/ppermute | solution.py:781
  (431 shorter events, 294.4 us)
Async XLA Ops:
  2.7 22.1 %collective-permute-start = (s32[2,2176]{1,0:T(2,128)}, s32[2,2176]{1,0:T(2,128)}, u32[]{:S(2)}, u32[]{:S(2)}) collective-permute-start(s32[2,2176]{1,0:T(2,128)} %pad_add_fusion), channel_id=1, source_target_pairs={{0,1},{1,0},{2,3},{3,2},{4,5},{5,4},{6,7},{7,6},{8,9},{9,8},{10,11... | collective-permute-start | bytes 52232 | tf_op jit(solution)/shard_map/ppermute | solution.py:845
  6.4 24.9 %collective-permute-start.1 = (bf16[2,512,768]{2,1,0:T(8,128)(2,1)}, bf16[2,512,768]{2,1,0:T(8,128)(2,1)}, u32[]{:S(2)}, u32[]{:S(2)}) collective-permute-start(bf16[2,512,768]{2,1,0:T(8,128)(2,1)} %select_bitcast_fusion.2), channel_id=1, source_target_pairs={{0,1},{1,0},{2,3},{3,2},{4,5},{5,4},{6,7},{7,6},{8,9},{9,8},{10,11... | collective-permute-start | bytes 4718600 | tf_op jit(solution)/shard_map/ppermute | solution.py:845
  71.8 18.6 %collective-permute-start.3 = (bf16[512,768]{1,0:T(8,128)(2,1)S(1)}, bf16[512,768]{1,0:T(8,128)(2,1)S(1)}, u32[]{:S(2)}, u32[]{:S(2)}) collective-permute-start(bf16[512,768]{1,0:T(8,128)(2,1)S(1)} %get-tuple-element.259), channel_id=1, source_target_pairs={{0,16},{1,17},{2,18},{3,19},{4,20},{5,21},{6,22},{7,23},{8,24},{9,... | collective-permute-start | bytes 2359304 | tf_op jit(solution)/shard_map/ppermute | solution.py:984
  122.3 27.1 %collective-permute-start.5 = (bf16[512,768]{1,0:T(8,128)(2,1)S(1)}, bf16[512,768]{1,0:T(8,128)(2,1)S(1)}, u32[]{:S(2)}, u32[]{:S(2)}) collective-permute-start(bf16[512,768]{1,0:T(8,128)(2,1)S(1)} %get-tuple-element.274), channel_id=1, source_target_pairs={{0,16},{1,17},{2,18},{3,19},{4,20},{5,21},{6,22},{7,23},{8,24},{9,... | collective-permute-start | bytes 2359304 | tf_op jit(solution)/shard_map/ppermute | solution.py:984
  161.7 34.0 %collective-permute-start.8 = (bf16[512,768]{1,0:T(8,128)(2,1)S(1)}, bf16[512,768]{1,0:T(8,128)(2,1)S(1)}, u32[]{:S(2)}, u32[]{:S(2)}) collective-permute-start(bf16[512,768]{1,0:T(8,128)(2,1)S(1)} %get-tuple-element.302), channel_id=1, source_target_pairs={{16,0},{17,1},{18,2},{19,3},{20,4},{21,5},{22,6},{23,7},{24,8},{25... | collective-permute-start | bytes 2359304 | tf_op jit(solution)/shard_map/ppermute | solution.py:991
  186.0 41.2 %collective-permute-start.10 = (bf16[512,768]{1,0:T(8,128)(2,1)S(1)}, bf16[512,768]{1,0:T(8,128)(2,1)S(1)}, u32[]{:S(2)}, u32[]{:S(2)}) collective-permute-start(bf16[512,768]{1,0:T(8,128)(2,1)S(1)} %get-tuple-element.326), channel_id=1, source_target_pairs={{0,16},{1,17},{2,18},{3,19},{4,20},{5,21},{6,22},{7,23},{8,24},{9,... | collective-permute-start | bytes 2359304 | tf_op jit(solution)/shard_map/ppermute | solution.py:984
  239.1 28.7 %collective-permute-start.14 = (bf16[512,768]{1,0:T(8,128)(2,1)S(1)}, bf16[512,768]{1,0:T(8,128)(2,1)S(1)}, u32[]{:S(2)}, u32[]{:S(2)}) collective-permute-start(bf16[512,768]{1,0:T(8,128)(2,1)S(1)} %get-tuple-element.325), channel_id=1, source_target_pairs={{16,0},{17,1},{18,2},{19,3},{20,4},{21,5},{22,6},{23,7},{24,8},{25... | collective-permute-start | bytes 2359304 | tf_op jit(solution)/shard_map/ppermute | solution.py:991
  260.8 38.3 %collective-permute-start.12 = (bf16[512,768]{1,0:T(8,128)(2,1)S(1)}, bf16[512,768]{1,0:T(8,128)(2,1)S(1)}, u32[]{:S(2)}, u32[]{:S(2)}) collective-permute-start(bf16[512,768]{1,0:T(8,128)(2,1)S(1)} %get-tuple-element.333), channel_id=1, source_target_pairs={{0,16},{1,17},{2,18},{3,19},{4,20},{5,21},{6,22},{7,23},{8,24},{9,... | collective-permute-start | bytes 2359304 | tf_op jit(solution)/shard_map/ppermute | solution.py:984
  311.0 21.3 %collective-permute-start.16 = (bf16[512,768]{1,0:T(8,128)(2,1)S(1)}, bf16[512,768]{1,0:T(8,128)(2,1)S(1)}, u32[]{:S(2)}, u32[]{:S(2)}) collective-permute-start(bf16[512,768]{1,0:T(8,128)(2,1)S(1)} %get-tuple-element.361), channel_id=1, source_target_pairs={{16,0},{17,1},{18,2},{19,3},{20,4},{21,5},{22,6},{23,7},{24,8},{25... | collective-permute-start | bytes 2359304 | tf_op jit(solution)/shard_map/ppermute | solution.py:991
  374.6 26.1 %collective-permute-start.18 = (bf16[512,768]{1,0:T(8,128)(2,1)S(1)}, bf16[512,768]{1,0:T(8,128)(2,1)S(1)}, u32[]{:S(2)}, u32[]{:S(2)}) collective-permute-start(bf16[512,768]{1,0:T(8,128)(2,1)S(1)} %get-tuple-element.383), channel_id=1, source_target_pairs={{16,0},{17,1},{18,2},{19,3},{20,4},{21,5},{22,6},{23,7},{24,8},{25... | collective-permute-start | bytes 2359304 | tf_op jit(solution)/shard_map/ppermute | solution.py:991
  421.3 19.3 %collective-permute-start.19 = (bf16[384,3072]{1,0:T(8,128)(2,1)}, bf16[384,3072]{1,0:T(8,128)(2,1)}, u32[]{:S(2)}, u32[]{:S(2)}) collective-permute-start(bf16[384,3072]{1,0:T(8,128)(2,1)} %get-tuple-element.398), channel_id=1, source_target_pairs={{0,1},{1,0},{2,3},{3,2},{4,5},{5,4},{6,7},{7,6},{8,9},{9,8},{10,11... | collective-permute-start | bytes 7077896 | tf_op jit(solution)/shard_map/ppermute | solution.py:784
  440.1 24.9 %collective-permute-start.21 = (bf16[384,3072]{1,0:T(8,128)(2,1)S(1)}, bf16[384,3072]{1,0:T(8,128)(2,1)S(1)}, u32[]{:S(2)}, u32[]{:S(2)}) collective-permute-start(bf16[384,3072]{1,0:T(8,128)(2,1)S(1)} %get-tuple-element.402), channel_id=1, source_target_pairs={{0,1},{1,0},{2,3},{3,2},{4,5},{5,4},{6,7},{7,6},{8,9},{9,8},{10,11... | collective-permute-start | bytes 7077896 | tf_op jit(solution)/shard_map/ppermute | solution.py:784
  443.2 27.8 %collective-permute-start.20 = (bf16[192,3072]{1,0:T(8,128)(2,1)S(1)}, bf16[192,3072]{1,0:T(8,128)(2,1)S(1)}, u32[]{:S(2)}, u32[]{:S(2)}) collective-permute-start(bf16[192,3072]{1,0:T(8,128)(2,1)S(1)} %constant_dynamic-slice_fusion.12), channel_id=1, source_target_pairs={{0,2},{1,5},{2,0},{3,7},{4,6},{5,1},{6,4},{7,3},{8,10},{9,13},{10,... | collective-permute-start | bytes 3538952 | tf_op jit(solution)/shard_map/ppermute | solution.py:781
  469.7 63.9 %collective-permute-start.27 = (bf16[192,3072]{1,0:T(8,128)(2,1)}, bf16[192,3072]{1,0:T(8,128)(2,1)}, u32[]{:S(2)}, u32[]{:S(2)}) collective-permute-start(bf16[192,3072]{1,0:T(8,128)(2,1)} %constant_dynamic-slice_fusion.6), channel_id=1, source_target_pairs={{0,2},{1,3},{2,0},{3,1},{4,6},{5,7},{6,4},{7,5},{8,10},{9,11},{10,... | collective-permute-start | bytes 3538952 | tf_op jit(solution)/shard_map/ppermute | solution.py:781
  499.3 84.9 %collective-permute-start.26 = (bf16[384,3072]{1,0:T(8,128)(2,1)}, bf16[384,3072]{1,0:T(8,128)(2,1)}, u32[]{:S(2)}, u32[]{:S(2)}) collective-permute-start(bf16[384,3072]{1,0:T(8,128)(2,1)} %get-tuple-element.422), channel_id=1, source_target_pairs={{0,1},{1,0},{2,3},{3,2},{4,5},{5,4},{6,7},{7,6},{8,9},{9,8},{10,11... | collective-permute-start | bytes 7077896 | tf_op jit(solution)/shard_map/ppermute | solution.py:784
  524.9 131.3 %collective-permute-start.24 = (bf16[2,512,768]{2,1,0:T(8,128)(2,1)}, bf16[2,512,768]{2,1,0:T(8,128)(2,1)}, u32[]{:S(2)}, u32[]{:S(2)}) collective-permute-start(bf16[2,512,768]{2,1,0:T(8,128)(2,1)} %broadcast_select_fusion.1), channel_id=1, source_target_pairs={{0,1},{1,0},{2,3},{3,2},{4,5},{5,4},{6,7},{7,6},{8,9},{9,8},{10,11... | collective-permute-start | bytes 4718600 | tf_op jit(solution)/shard_map/ppermute | solution.py:845
  533.1 53.7 %collective-permute-start.25 = (f32[88,128]{1,0:T(8,128)S(1)}, f32[88,128]{1,0:T(8,128)S(1)}, u32[]{:S(2)}, u32[]{:S(2)}) collective-permute-start(f32[88,128]{1,0:T(8,128)S(1)} %pad_bitcast_fusion), channel_id=1, source_target_pairs={{0,1},{1,0},{2,3},{3,2},{4,5},{5,4},{6,7},{7,6},{8,9},{9,8},{10,11... | collective-permute-start | bytes 135176 | tf_op jit(solution)/shard_map/ppermute | solution.py:816
  534.6 33.7 %collective-permute-start.29 = (bf16[48,3072]{1,0:T(8,128)(2,1)S(1)}, bf16[48,3072]{1,0:T(8,128)(2,1)S(1)}, u32[]{:S(2)}, u32[]{:S(2)}) collective-permute-start(bf16[48,3072]{1,0:T(8,128)(2,1)S(1)} %constant_dynamic-slice_fusion.4), channel_id=1, source_target_pairs={{0,8},{1,9},{2,10},{3,11},{4,12},{5,13},{6,14},{7,15},{8,0},{9,1},... | collective-permute-start | bytes 884744 | tf_op jit(solution)/shard_map/ppermute | solution.py:781
  557.7 26.2 %collective-permute-start.28 = (bf16[96,3072]{1,0:T(8,128)(2,1)S(1)}, bf16[96,3072]{1,0:T(8,128)(2,1)S(1)}, u32[]{:S(2)}, u32[]{:S(2)}) collective-permute-start(bf16[96,3072]{1,0:T(8,128)(2,1)S(1)} %constant_dynamic-slice_fusion.5), channel_id=1, source_target_pairs={{0,4},{1,5},{2,6},{3,7},{4,0},{5,1},{6,2},{7,3},{8,12},{9,13},{10,... | collective-permute-start | bytes 1769480 | tf_op jit(solution)/shard_map/ppermute | solution.py:781
  568.4 23.1 %collective-permute-start.33 = (bf16[48,3072]{1,0:T(8,128)(2,1)S(1)}, bf16[48,3072]{1,0:T(8,128)(2,1)S(1)}, u32[]{:S(2)}, u32[]{:S(2)}) collective-permute-start(bf16[48,3072]{1,0:T(8,128)(2,1)S(1)} %dynamic-slice_add_fusion.8), channel_id=1, source_target_pairs={{0,8},{1,9},{2,10},{3,11},{4,12},{5,13},{6,14},{7,15},{8,0},{9,1},... | collective-permute-start | bytes 884744 | tf_op jit(solution)/shard_map/ppermute | solution.py:781
  586.8 23.5 %collective-permute-start.30 = (f32[88,128]{1,0:T(8,128)S(1)}, f32[88,128]{1,0:T(8,128)S(1)}, u32[]{:S(2)}, u32[]{:S(2)}) collective-permute-start(f32[88,128]{1,0:T(8,128)S(1)} %fusion.35), channel_id=1, source_target_pairs={{0,2},{1,3},{2,0},{3,1},{4,6},{5,7},{6,4},{7,5},{8,10},{9,11},{10,... | collective-permute-start | bytes 135176 | tf_op jit(solution)/shard_map/ppermute | solution.py:816
  586.9 22.9 %collective-permute-start.31 = (bf16[192,3072]{1,0:T(8,128)(2,1)S(1)}, bf16[192,3072]{1,0:T(8,128)(2,1)S(1)}, u32[]{:S(2)}, u32[]{:S(2)}) collective-permute-start(bf16[192,3072]{1,0:T(8,128)(2,1)S(1)} %constant_dynamic-slice_fusion.3), channel_id=1, source_target_pairs={{0,2},{1,5},{2,0},{3,7},{4,6},{5,1},{6,4},{7,3},{8,10},{9,13},{10,... | collective-permute-start | bytes 3538952 | tf_op jit(solution)/shard_map/ppermute | solution.py:781
  591.6 24.9 %collective-permute-start.37 = (bf16[96,3072]{1,0:T(8,128)(2,1)S(1)}, bf16[96,3072]{1,0:T(8,128)(2,1)S(1)}, u32[]{:S(2)}, u32[]{:S(2)}) collective-permute-start(bf16[96,3072]{1,0:T(8,128)(2,1)S(1)} %pad_maximum_fusion.11), channel_id=1, source_target_pairs={{0,4},{1,3},{2,6},{3,1},{4,0},{5,7},{6,2},{7,5},{8,12},{9,11},{10,... | collective-permute-start | bytes 1769480 | tf_op jit(solution)/shard_map/ppermute | solution.py:781
  597.5 21.0 %collective-permute-start.36 = (bf16[48,3072]{1,0:T(8,128)(2,1)S(1)}, bf16[48,3072]{1,0:T(8,128)(2,1)S(1)}, u32[]{:S(2)}, u32[]{:S(2)}) collective-permute-start(bf16[48,3072]{1,0:T(8,128)(2,1)S(1)} %dynamic-slice_add_fusion.7), channel_id=1, source_target_pairs={{0,8},{1,9},{2,10},{3,11},{4,12},{5,13},{6,14},{7,15},{8,0},{9,1},... | collective-permute-start | bytes 884744 | tf_op jit(solution)/shard_map/ppermute | solution.py:781
  610.3 16.6 %collective-permute-start.34 = (f32[88,128]{1,0:T(8,128)S(1)}, f32[88,128]{1,0:T(8,128)S(1)}, u32[]{:S(2)}, u32[]{:S(2)}) collective-permute-start(f32[88,128]{1,0:T(8,128)S(1)} %fusion.42), channel_id=1, source_target_pairs={{0,4},{1,5},{2,6},{3,7},{4,0},{5,1},{6,2},{7,3},{8,12},{9,13},{10,... | collective-permute-start | bytes 135176 | tf_op jit(solution)/shard_map/ppermute | solution.py:816
  616.8 22.6 %collective-permute-start.41 = (bf16[192,3072]{1,0:T(8,128)(2,1)S(1)}, bf16[192,3072]{1,0:T(8,128)(2,1)S(1)}, u32[]{:S(2)}, u32[]{:S(2)}) collective-permute-start(bf16[192,3072]{1,0:T(8,128)(2,1)S(1)} %pad_maximum_fusion.8), channel_id=1, source_target_pairs={{0,2},{1,5},{2,0},{3,7},{4,6},{5,1},{6,4},{7,3},{8,10},{9,13},{10,... | collective-permute-start | bytes 3538952 | tf_op jit(solution)/shard_map/ppermute | solution.py:781
  618.6 35.0 %collective-permute-start.40 = (bf16[96,3072]{1,0:T(8,128)(2,1)S(1)}, bf16[96,3072]{1,0:T(8,128)(2,1)S(1)}, u32[]{:S(2)}, u32[]{:S(2)}) collective-permute-start(bf16[96,3072]{1,0:T(8,128)(2,1)S(1)} %pad_maximum_fusion.12), channel_id=1, source_target_pairs={{0,4},{1,5},{2,6},{3,7},{4,0},{5,1},{6,2},{7,3},{8,12},{9,13},{10,... | collective-permute-start | bytes 1769480 | tf_op jit(solution)/shard_map/ppermute | solution.py:781
  626.9 29.3 %collective-permute-start.38 = (f32[88,128]{1,0:T(8,128)S(1)}, f32[88,128]{1,0:T(8,128)S(1)}, u32[]{:S(2)}, u32[]{:S(2)}) collective-permute-start(f32[88,128]{1,0:T(8,128)S(1)} %add.312), channel_id=1, source_target_pairs={{0,8},{1,9},{2,10},{3,11},{4,12},{5,13},{6,14},{7,15},{8,0},{9,1},... | collective-permute-start | bytes 135176 | tf_op jit(solution)/shard_map/ppermute | solution.py:816
  627.0 29.1 %collective-permute-start.39 = (bf16[48,3072]{1,0:T(8,128)(2,1)S(1)}, bf16[48,3072]{1,0:T(8,128)(2,1)S(1)}, u32[]{:S(2)}, u32[]{:S(2)}) collective-permute-start(bf16[48,3072]{1,0:T(8,128)(2,1)S(1)} %constant_dynamic-slice_fusion), channel_id=1, source_target_pairs={{0,8},{1,9},{2,10},{3,11},{4,12},{5,13},{6,14},{7,15},{8,0},{9,1},... | collective-permute-start | bytes 884744 | tf_op jit(solution)/shard_map/ppermute | solution.py:781
  640.2 20.0 %collective-permute-start.44 = (bf16[384,3072]{1,0:T(8,128)(2,1)S(1)}, bf16[384,3072]{1,0:T(8,128)(2,1)S(1)}, u32[]{:S(2)}, u32[]{:S(2)}) collective-permute-start(bf16[384,3072]{1,0:T(8,128)(2,1)S(1)} %pad_maximum_fusion.3.refs_0_), channel_id=1, source_target_pairs={{0,1},{1,0},{2,3},{3,2},{4,5},{5,4},{6,7},{7,6},{8,9},{9,8},{10,11... | collective-permute-start | bytes 7077896 | tf_op jit(solution)/shard_map/ppermute | solution.py:784
  654.0 23.8 %collective-permute-start.43 = (bf16[192,3072]{1,0:T(8,128)(2,1)S(1)}, bf16[192,3072]{1,0:T(8,128)(2,1)S(1)}, u32[]{:S(2)}, u32[]{:S(2)}) collective-permute-start(bf16[192,3072]{1,0:T(8,128)(2,1)S(1)} %pad_maximum_fusion.9), channel_id=1, source_target_pairs={{0,2},{1,3},{2,0},{3,1},{4,6},{5,7},{6,4},{7,5},{8,10},{9,11},{10,... | collective-permute-start | bytes 3538952 | tf_op jit(solution)/shard_map/ppermute | solution.py:781
  678.6 20.7 %collective-permute-start.46 = (bf16[384,3072]{1,0:T(8,128)(2,1)S(1)}, bf16[384,3072]{1,0:T(8,128)(2,1)S(1)}, u32[]{:S(2)}, u32[]{:S(2)}) collective-permute-start(bf16[384,3072]{1,0:T(8,128)(2,1)S(1)} %pad_maximum_fusion.4.refs_0_), channel_id=1, source_target_pairs={{0,1},{1,0},{2,3},{3,2},{4,5},{5,4},{6,7},{7,6},{8,9},{9,8},{10,11... | collective-permute-start | bytes 7077896 | tf_op jit(solution)/shard_map/ppermute | solution.py:784
  (105 other events, 922.6 us)

commit v5 on v4

--- a/solution.py
+++ b/solution.py
@@ -1029,9 +1029,9 @@
     done = contract.advance(done)
     got = after(got, done)
     st, grads_in[SLOTS[-1][1]] = input_back(sp, dict(st, cell=cell), dq, keep, got)
-    done = contract.advance(st["dj"])
-    halves = weight_call(sp, 0, windows, [(after(st["x"], done), st["dj"]), (st["a"], st["db1"])])
+    halves = weight_call(sp, 0, windows, [(st["x"], st["dj"]), (st["a"], st["db1"])])
     given, attend = weight_sum(ring.mixed, *halves)
+    done = contract.advance(given)
 
     later = lambda a: after(a, given)
     of_windows = lambda name: jnp.sum(later(st[name])[:windows], axis=0)
@@ -1041,9 +1041,10 @@
     packed = jnp.concatenate([p.reshape(-1) for p in small])
     packed = jnp.pad(packed, (0, -packed.shape[0] % (8 * PAIR))).reshape(-1, PAIR)
     totals = Chain(ring.totals(packed), dp_count.bit_length() - 1)
-    result = [later(jnp.where(section == 0, grads_in[w], finals[w])) for w in range(windows)]
+    result = [jnp.where(section == 0, later(grads_in[w]), later(finals[w])) for w in range(windows)]
     result = jnp.stack(result)
-    ordered = [lax.dynamic_index_in_dim(result, rank[w], 0, keepdims=False) for w in range(windows)]
+    ranks = later(rank)
+    ordered = [lax.dynamic_index_in_dim(result, ranks[w], 0, keepdims=False) for w in range(windows)]
     mine_first, mine_second = jnp.stack(ordered[:micro]), jnp.stack(ordered[micro:])
     keep_rows = jnp.where(core == 0, mine_first, mine_second)
     got_rows = exchange(jnp.where(core == 0, mine_second, mine_first))
@@ -1054,21 +1055,26 @@
         )
         return out_halves.reshape(1, micro, slots, width)
 
-    done = expand.advance(packed)
-    chains = {"contract": contract, "expand": expand, "attend": attend, "totals": totals}
+    done = expand.advance(done)
+    chains = {"attend": attend, "contract": contract, "expand": expand, "totals": totals}
     kinds = {"contract": ([hidden], natural), "expand": ([hidden], natural), "attend": ([3 * width, width], moves)}
     outputs = {}
+    waiting = []
     boundary_out = None
     while any(chain.left for chain in chains.values()):
         for name, chain in chains.items():
-            if chain.left:
-                done = chain.advance(done)
-                if not chain.left and name in kinds:
-                    outputs[name] = spread_call(sp, *ring.result, *kinds[name])
-                    done = outputs[name][0]
+            if not chain.left:
+                continue
+            done = chain.advance(done)
+            for other, (mine, theirs) in waiting:
+                outputs[other] = spread_call(sp, after(mine, done), theirs, *kinds[other])
+                done = outputs[other][0]
+            waiting = [(name, ring.result)] if not chain.left and name in kinds else []
         if boundary_out is None and not totals.left:
             boundary_out = assembled(after(got_rows, done))
             done = boundary_out
+    for other, halves in waiting:
+        outputs[other] = spread_call(sp, *halves, *kinds[other])
     (g_contract,), (g_expand,), (g_in, g_out) = (outputs[n] for n in ("contract", "expand", "attend"))
     packed = totals.last.reshape(-1)
     pieces = []

time: 749 us -> 721 us (0.963)
  waiting for transfers between devices: 144 us -> 123 us
  starting transfers between devices: 117 us -> 99.4 us
  other arithmetic: 44.8 us -> 53.2 us
    ppermute x18, starting transfers between devices: 44.4 us -> 20 us  [send(): return lax.ppermute(a, 'dp', pairs)]
    ppermute x18, waiting for transfers between devices: 117 us -> 96.9 us  [send(): return lax.ppermute(a, 'dp', pairs)]
    ppermute x13, starting transfers between devices: 2.5 us -> 21.1 us  [on_device(): exchange = lambda a: lax.ppermute(a, 'dp', swap)]
    ppermute x6, starting transfers between devices: 42.2 us -> 26.1 us  [swap(): return lax.ppermute(a, 'dp', [(i, i ^ 1) for i in range(self.count)])]
    unnamed x179 -> x203, local copies, waits for them, and re-layouts: 19.8 us -> 26.2 us
  transfers between devices with their start and end apart: 49 -> 49, of which waited for: 17 -> 12; matrix products, arithmetic and copies ran while one was open for 8% -> 10% of each run, Pallas kernels for 35% -> 36%
where the time goes in v5:
time: 721 us; the launch traced here: 711 us
  Pallas kernels  374 us (52%)
  waiting for transfers between devices  123 us (17%)
  starting transfers between devices  99.4 us (14%)
  other arithmetic  53.2 us (7%)
  local copies, waits for them, and re-layouts  47.1 us (7%)
  between operations  10.7 us (1%)
    pallas_call x38, Pallas kernels, call(): pl.pallas_call(run, grid_spec=pltpu.PrefetchScalarGridSpec(num_scalar_pre...  368 us
    ppermute x18, waiting for transfers between devices, send(): return lax.ppermute(a, 'dp', pairs)  96.9 us
    unnamed x203, local copies, waits for them, and re-layouts  26.2 us
    ppermute x6, starting transfers between devices, swap(): return lax.ppermute(a, 'dp', [(i, i ^ 1) for i in range(self.count)])  26.1 us
    ppermute x4, starting transfers between devices, on_device(): got['F', zero] = lax.ppermute(out, 'section', [(0, 1)])  22.4 us
    ppermute x13, starting transfers between devices, on_device(): exchange = lambda a: lax.ppermute(a, 'dp', swap)  21.1 us
    ppermute x18, starting transfers between devices, send(): return lax.ppermute(a, 'dp', pairs)  20 us
    ppermute x4, waiting for transfers between devices, on_device(): got['F', zero] = lax.ppermute(out, 'section', [(0, 1)])  17.2 us
  transfers between devices with their start and end apart: 49, of which 12 were waited for; matrix products, arithmetic and copies ran while one was open for 10% of the time, Pallas kernels for 36%

profile of v5, /device:TPU:0, one launch (start us, length us, event | category | flops | bytes accessed | tf_op | source)
XLA Modules:
  0.0 710.5 jit_solution(16227821861389217014)
XLA Ops:
  48.0 12.6 %shard_map.242 = (bf16[5,512,768]{2,1,0:T(8,128)(2,1)}, bf16[5,512,768]{2,1,0:T(8,128)(2,1)}, bf16[5,512,768]{2,1,0:T(8,128)(2,1)}, bf16[5,512,1536]{2,1,0:T(8,128)(2,1)}) custom-call(s32[60]{0:T(128)S(1)} %reshape.556.sp_ref, ...), custom_call_target="tpu_custom_call", output_to_operand_aliasing={{0}: (7, {}), {1}: (8, {}), {2}: (9, {}), {3}: (10, {})} | custom-call | flops 14000000000 | bytes 14000000 | tf_op jit(solution)/shard_map/pallas_call | solution.py:96
  60.6 11.1 %shard_map.243 = (bf16[5,512,768]{2,1,0:T(8,128)(2,1)}, bf16[5,512,768]{2,1,0:T(8,128)(2,1)}, bf16[5,512,3072]{2,1,0:T(8,128)(2,1)}, bf16[5,512,3072]{2,1,0:T(8,...) custom-call(s32[60]{0:T(128)S(1)} %reshape.556.sp_ref, ...), custom_call_target="tpu_custom_call", output_to_operand_aliasing={{0}: (9, {}), {1}: (10, {}), {2}: (11, {}), {3}: (12, {}), ... | custom-call | flops 10000000000 | bytes 10000000 | tf_op jit(solution)/shard_map/pallas_call | solution.py:96
  73.1 17.2 %collective-permute-done.3.refs_1_ = bf16[512,768]{1,0:T(8,128)(2,1)S(1)} collective-permute-done((bf16[512,768]{1,0:T(8,128)(2,1)S(1)}, bf16[512,768]{1,0:T(8,128)(2,1)S(1)}, u32[]{:S(2)}, u32[]{:S(2)}) %collective-permute-start.3) | collective-permute-done | bytes 786464 | tf_op jit(solution)/shard_map/ppermute | solution.py:984
  99.6 11.8 %shard_map.245 = (bf16[5,512,768]{2,1,0:T(8,128)(2,1)}, bf16[5,512,768]{2,1,0:T(8,128)(2,1)}, bf16[5,512,768]{2,1,0:T(8,128)(2,1)}, bf16[5,512,1536]{2,1,0:T(8,128)(2,1)}) custom-call(s32[60]{0:T(128)S(1)} %reshape.556.sp_ref, ...), custom_call_target="tpu_custom_call", output_to_operand_aliasing={{0}: (7, {}), {1}: (8, {}), {2}: (9, {}), {3}: (10, {})} | custom-call | flops 14000000000 | bytes 14000000 | tf_op jit(solution)/shard_map/pallas_call | solution.py:96
  111.5 10.8 %shard_map.246 = (bf16[5,512,768]{2,1,0:T(8,128)(2,1)}, bf16[5,512,768]{2,1,0:T(8,128)(2,1)}, bf16[5,512,3072]{2,1,0:T(8,128)(2,1)}, bf16[5,512,3072]{2,1,0:T(8,...) custom-call(s32[60]{0:T(128)S(1)} %reshape.556.sp_ref, ...), custom_call_target="tpu_custom_call", output_to_operand_aliasing={{0}: (9, {}), {1}: (10, {}), {2}: (11, {}), {3}: (12, {}), ... | custom-call | flops 10000000000 | bytes 10000000 | tf_op jit(solution)/shard_map/pallas_call | solution.py:96
  126.8 12.3 %shard_map.249 = (bf16[5,512,768]{2,1,0:T(8,128)(2,1)}, bf16[5,512,3072]{2,1,0:T(8,128)(2,1)}, bf16[5,512,768]{2,1,0:T(8,128)(2,1)}, f32[5,8,768]{2,1,0:T(8,128)...) custom-call(s32[60]{0:T(128)S(1)} %reshape.556.sp_ref, ...), custom_call_target="tpu_custom_call", output_to_operand_aliasing={{0}: (14, {}), {1}: (15, {}), {2}: (16, {}), {3}: (17, {}),... | custom-call | flops 10000000000 | bytes 10000000 | tf_op jit(solution)/shard_map/pallas_call | solution.py:96
  139.1 9.5 %shard_map.250 = (f32[5,64,768]{2,1,0:T(8,128)}, bf16[512,768]{1,0:T(8,128)(2,1)S(1)}, bf16[512,1536]{1,0:T(8,128)(2,1)S(1)}, bf16[512,1536]{1,0:T(8,128)(2,1)}) custom-call(s32[60]{0:T(128)S(1)} %reshape.556.sp_ref, bf16[5,512,768]{2,1,0:T(8,128)(2,1)} %get-tuple-element.267.refs_0_.refs_5_, ...), custom_call_target="tpu_custom_call", output_to_operand_aliasing={{0}: (11, {})} | custom-call | flops 20000000000 | bytes 20000000 | tf_op jit(solution)/shard_map/pallas_call | solution.py:96
  163.1 9.8 %shard_map.248 = (bf16[5,512,768]{2,1,0:T(8,128)(2,1)}, bf16[5,512,768]{2,1,0:T(8,128)(2,1)}, bf16[5,512,768]{2,1,0:T(8,128)(2,1)}, bf16[5,512,1536]{2,1,0:T(8,128)(2,1)}) custom-call(s32[60]{0:T(128)S(1)} %reshape.556.sp_ref, ...), custom_call_target="tpu_custom_call", output_to_operand_aliasing={{0}: (7, {}), {1}: (8, {}), {2}: (9, {}), {3}: (10, {})} | custom-call | flops 14000000000 | bytes 14000000 | tf_op jit(solution)/shard_map/pallas_call | solution.py:96
  172.9 10.8 %shard_map.252 = (bf16[5,512,768]{2,1,0:T(8,128)(2,1)}, bf16[5,512,768]{2,1,0:T(8,128)(2,1)}, bf16[5,512,3072]{2,1,0:T(8,128)(2,1)}, bf16[5,512,3072]{2,1,0:T(8,...) custom-call(s32[60]{0:T(128)S(1)} %reshape.556.sp_ref, ...), custom_call_target="tpu_custom_call", output_to_operand_aliasing={{0}: (9, {}), {1}: (10, {}), {2}: (11, {}), {3}: (12, {}), ... | custom-call | flops 10000000000 | bytes 10000000 | tf_op jit(solution)/shard_map/pallas_call | solution.py:96
  183.7 12.0 %collective-permute-start.10 = (bf16[512,768]{1,0:T(8,128)(2,1)S(1)}, bf16[512,768]{1,0:T(8,128)(2,1)S(1)}, u32[]{:S(2)}, u32[]{:S(2)}) collective-permute-start(bf16[512,768]{1,0:T(8,128)(2,1)S(1)} %get-tuple-element.430), channel_id=1, source_target_pairs={{0,16},{1,17},{2,18},{3,19},{4,20},{5,21},{6,22},{7,23},{8,24},{9,... | collective-permute-start | bytes 2359304 | tf_op jit(solution)/shard_map/ppermute | solution.py:984
  195.7 12.3 %shard_map.253 = (bf16[5,512,768]{2,1,0:T(8,128)(2,1)}, bf16[5,512,3072]{2,1,0:T(8,128)(2,1)}, bf16[5,512,768]{2,1,0:T(8,128)(2,1)}, f32[5,8,768]{2,1,0:T(8,128)...) custom-call(s32[60]{0:T(128)S(1)} %reshape.556.sp_ref, ...), custom_call_target="tpu_custom_call", output_to_operand_aliasing={{0}: (14, {}), {1}: (15, {}), {2}: (16, {}), {3}: (17, {}),... | custom-call | flops 10000000000 | bytes 10000000 | tf_op jit(solution)/shard_map/pallas_call | solution.py:96
  208.1 18.0 %shard_map.254 = (f32[5,64,768]{2,1,0:T(8,128)}, bf16[512,768]{1,0:T(8,128)(2,1)S(1)}, bf16[512,1536]{1,0:T(8,128)(2,1)S(1)}, bf16[512,1536]{1,0:T(8,128)(2,1)S(1)}) custom-call(s32[60]{0:T(128)S(1)} %reshape.556.sp_ref, bf16[5,512,768]{2,1,0:T(8,128)(2,1)} %get-tuple-element.282.refs_0_.refs_5_, ...), custom_call_target="tpu_custom_call", output_to_operand_aliasing={{0}: (11, {})} | custom-call | flops 20000000000 | bytes 20000000 | tf_op jit(solution)/shard_map/pallas_call | solution.py:96
  240.4 9.5 %shard_map.257 = (bf16[5,512,768]{2,1,0:T(8,128)(2,1)}, bf16[5,512,768]{2,1,0:T(8,128)(2,1)}, bf16[5,512,768]{2,1,0:T(8,128)(2,1)}, bf16[5,512,1536]{2,1,0:T(8,128)(2,1)}) custom-call(s32[60]{0:T(128)S(1)} %reshape.556.sp_ref, ...), custom_call_target="tpu_custom_call", output_to_operand_aliasing={{0}: (7, {}), {1}: (8, {}), {2}: (9, {}), {3}: (10, {})} | custom-call | flops 14000000000 | bytes 14000000 | tf_op jit(solution)/shard_map/pallas_call | solution.py:96
  249.9 10.9 %shard_map.258 = (bf16[5,512,768]{2,1,0:T(8,128)(2,1)}, bf16[5,512,768]{2,1,0:T(8,128)(2,1)}, bf16[5,512,3072]{2,1,0:T(8,128)(2,1)}, bf16[5,512,3072]{2,1,0:T(8,...) custom-call(s32[60]{0:T(128)S(1)} %reshape.556.sp_ref, ...), custom_call_target="tpu_custom_call", output_to_operand_aliasing={{0}: (9, {}), {1}: (10, {}), {2}: (11, {}), {3}: (12, {}), ... | custom-call | flops 10000000000 | bytes 10000000 | tf_op jit(solution)/shard_map/pallas_call | solution.py:96
  265.5 12.3 %shard_map.261 = (bf16[5,512,768]{2,1,0:T(8,128)(2,1)}, bf16[5,512,3072]{2,1,0:T(8,128)(2,1)}, bf16[5,512,768]{2,1,0:T(8,128)(2,1)}, f32[5,8,768]{2,1,0:T(8,128)...) custom-call(s32[60]{0:T(128)S(1)} %reshape.556.sp_ref, ...), custom_call_target="tpu_custom_call", output_to_operand_aliasing={{0}: (14, {}), {1}: (15, {}), {2}: (16, {}), {3}: (17, {}),... | custom-call | flops 10000000000 | bytes 10000000 | tf_op jit(solution)/shard_map/pallas_call | solution.py:96
  277.8 17.8 %shard_map.262 = (f32[5,64,768]{2,1,0:T(8,128)}, bf16[512,768]{1,0:T(8,128)(2,1)S(1)}, bf16[512,1536]{1,0:T(8,128)(2,1)S(1)}, bf16[512,1536]{1,0:T(8,128)(2,1)S(1)}) custom-call(s32[60]{0:T(128)S(1)} %reshape.556.sp_ref, bf16[5,512,768]{2,1,0:T(8,128)(2,1)} %get-tuple-element.333.refs_0_.refs_5_, ...), custom_call_target="tpu_custom_call", output_to_operand_aliasing={{0}: (11, {})} | custom-call | flops 20000000000 | bytes 20000000 | tf_op jit(solution)/shard_map/pallas_call | solution.py:96
  314.4 10.9 %shard_map.264 = (bf16[5,512,768]{2,1,0:T(8,128)(2,1)}, bf16[5,512,768]{2,1,0:T(8,128)(2,1)}, bf16[5,512,3072]{2,1,0:T(8,128)(2,1)}, bf16[5,512,3072]{2,1,0:T(8,...) custom-call(s32[60]{0:T(128)S(1)} %reshape.556.sp_ref, ...), custom_call_target="tpu_custom_call", output_to_operand_aliasing={{0}: (9, {}), {1}: (10, {}), {2}: (11, {}), {3}: (12, {}), ... | custom-call | flops 10000000000 | bytes 10000000 | tf_op jit(solution)/shard_map/pallas_call | solution.py:96
  329.9 12.3 %shard_map.265 = (bf16[5,512,768]{2,1,0:T(8,128)(2,1)}, bf16[5,512,3072]{2,1,0:T(8,128)(2,1)}, bf16[5,512,768]{2,1,0:T(8,128)(2,1)}, f32[5,8,768]{2,1,0:T(8,128)...) custom-call(s32[60]{0:T(128)S(1)} %reshape.556.sp_ref, ...), custom_call_target="tpu_custom_call", output_to_operand_aliasing={{0}: (14, {}), {1}: (15, {}), {2}: (16, {}), {3}: (17, {}),... | custom-call | flops 10000000000 | bytes 10000000 | tf_op jit(solution)/shard_map/pallas_call | solution.py:96
  342.2 13.5 %shard_map.266 = (f32[5,64,768]{2,1,0:T(8,128)}, bf16[512,768]{1,0:T(8,128)(2,1)S(1)}, bf16[512,1536]{1,0:T(8,128)(2,1)S(1)}, bf16[512,1536]{1,0:T(8,128)(2,1)S(1)}) custom-call(s32[60]{0:T(128)S(1)} %reshape.556.sp_ref, bf16[5,512,768]{2,1,0:T(8,128)(2,1)} %get-tuple-element.342.refs_0_, ...), custom_call_target="tpu_custom_call", output_to_operand_aliasing={{0}: (11, {})} | custom-call | flops 20000000000 | bytes 20000000 | tf_op jit(solution)/shard_map/pallas_call | solution.py:96
  368.9 11.6 %shard_map.268 = (bf16[384,3072]{1,0:T(8,128)(2,1)S(1)}, bf16[384,3072]{1,0:T(8,128)(2,1)S(1)}) custom-call(s32[60]{0:T(128)S(1)} %reshape.556.sp_ref, bf16[5,512,768]{2,1,0:T(8,128)(2,1)} %get-tuple-element.392.refs_0_.refs_13_, bf16[5,512,3072]{2,1,0:T(8,128)(2,1)} %get-tuple-element.393.refs_1_), custom_call_target="tpu_custom_call" | custom-call | flops 14000000000 | bytes 14000000 | tf_op jit(solution)/shard_map/pallas_call | solution.py:96
  380.6 11.5 %shard_map.269 = (bf16[384,3072]{1,0:T(8,128)(2,1)S(1)}, bf16[384,3072]{1,0:T(8,128)(2,1)S(1)}) custom-call(s32[60]{0:T(128)S(1)} %reshape.556.sp_ref, bf16[5,512,768]{2,1,0:T(8,128)(2,1)} %get-tuple-element.406.refs_0_, bf16[5,512,3072]{2,1,0:T(8,128)(2,1)} %get-tuple-element.396.refs_1_.refs_14_), custom_call_target="tpu_custom_call" | custom-call | flops 14000000000 | bytes 14000000 | tf_op jit(solution)/shard_map/pallas_call | solution.py:96
  393.5 12.5 %shard_map.270 = (bf16[5,512,768]{2,1,0:T(8,128)(2,1)}, bf16[5,512,3072]{2,1,0:T(8,128)(2,1)}, bf16[5,512,768]{2,1,0:T(8,128)(2,1)}, f32[5,8,768]{2,1,0:T(8,128)...) custom-call(s32[60]{0:T(128)S(1)} %reshape.556.sp_ref, ...), custom_call_target="tpu_custom_call", output_to_operand_aliasing={{0}: (14, {}), {1}: (15, {}), {2}: (16, {}), {3}: (17, {}),... | custom-call | flops 10000000000 | bytes 10000000 | tf_op jit(solution)/shard_map/pallas_call | solution.py:96
  432.3 14.2 %shard_map.273 = (f32[5,64,768]{2,1,0:T(8,128)}, bf16[512,768]{1,0:T(8,128)(2,1)S(1)}, bf16[512,1536]{1,0:T(8,128)(2,1)S(1)}, bf16[512,1536]{1,0:T(8,128)(2,1)}) custom-call(s32[60]{0:T(128)S(1)} %reshape.556.sp_ref, bf16[5,512,768]{2,1,0:T(8,128)(2,1)} %get-tuple-element.342.refs_0_, ...), custom_call_target="tpu_custom_call", output_to_operand_aliasing={{0}: (11, {})} | custom-call | flops 20000000000 | bytes 20000000 | tf_op jit(solution)/shard_map/pallas_call | solution.py:96
  447.7 18.3 %collective-permute-start.20 = (bf16[512,1536]{1,0:T(8,128)(2,1)}, bf16[512,1536]{1,0:T(8,128)(2,1)}, u32[]{:S(2)}, u32[]{:S(2)}) collective-permute-start(bf16[512,1536]{1,0:T(8,128)(2,1)} %get-tuple-element.417), channel_id=1, source_target_pairs={{0,1},{1,0},{2,3},{3,2},{4,5},{5,4},{6,7},{7,6},{8,9},{9,8},{10,11... | collective-permute-start | bytes 4718600 | tf_op jit(solution)/shard_map/ppermute | solution.py:845
  481.8 16.3 %shard_map.275 = (bf16[384,3072]{1,0:T(8,128)(2,1)S(1)}, bf16[384,3072]{1,0:T(8,128)(2,1)S(1)}) custom-call(s32[60]{0:T(128)S(1)} %reshape.556.sp_ref, bf16[5,512,768]{2,1,0:T(8,128)(2,1)} %get-tuple-element.341.refs_1_.refs_0_, bf16[5,512,768]{2,1,0:T(8,128)(2,1)} %get-tuple-element.347.refs_0_.refs_11_.refs_1_, ...), custom_call_target="tpu_custom_call" | custom-call | flops 16999999488 | bytes 17000000 | tf_op jit(solution)/shard_map/pallas_call | solution.py:96
  547.1 12.0 %collective-permute-done.27 = bf16[96,3072]{1,0:T(8,128)(2,1)S(1)} collective-permute-done((bf16[96,3072]{1,0:T(8,128)(2,1)S(1)}, bf16[96,3072]{1,0:T(8,128)(2,1)S(1)}, u32[]{:S(2)}, u32[]{:S(2)}) %collective-permute-start.27) | collective-permute-done | bytes 589856 | tf_op jit(solution)/shard_map/ppermute | solution.py:781
  561.4 13.8 %collective-permute-done.33 = bf16[192,3072]{1,0:T(8,128)(2,1)S(1)} collective-permute-done((bf16[192,3072]{1,0:T(8,128)(2,1)S(1)}, bf16[192,3072]{1,0:T(8,128)(2,1)S(1)}, u32[]{:S(2)}, u32[]{:S(2)}) %collective-permute-start.33) | collective-permute-done | bytes 1179680 | tf_op jit(solution)/shard_map/ppermute | solution.py:781
  580.1 18.6 %collective-permute-done.37 = bf16[96,3072]{1,0:T(8,128)(2,1)S(1)} collective-permute-done((bf16[96,3072]{1,0:T(8,128)(2,1)S(1)}, bf16[96,3072]{1,0:T(8,128)(2,1)S(1)}, u32[]{:S(2)}, u32[]{:S(2)}) %collective-permute-start.37) | collective-permute-done | bytes 589856 | tf_op jit(solution)/shard_map/ppermute | solution.py:781
  617.0 17.8 %collective-permute-start.45 = (bf16[384,3072]{1,0:T(8,128)(2,1)S(1)}, bf16[384,3072]{1,0:T(8,128)(2,1)S(1)}, u32[]{:S(2)}, u32[]{:S(2)}) collective-permute-start(bf16[384,3072]{1,0:T(8,128)(2,1)S(1)} %pad_maximum_fusion.3.refs_0_), channel_id=1, source_target_pairs={{0,1},{1,0},{2,3},{3,2},{4,5},{5,4},{6,7},{7,6},{8,9},{9,8},{10,11... | collective-permute-start | bytes 7077896 | tf_op jit(solution)/shard_map/ppermute | solution.py:784
  639.9 16.3 %collective-permute-done.44 = bf16[192,3072]{1,0:T(8,128)(2,1)S(1)} collective-permute-done((bf16[192,3072]{1,0:T(8,128)(2,1)S(1)}, bf16[192,3072]{1,0:T(8,128)(2,1)S(1)}, u32[]{:S(2)}, u32[]{:S(2)}) %collective-permute-start.44) | collective-permute-done | bytes 1179680 | tf_op jit(solution)/shard_map/ppermute | solution.py:781
  671.0 15.6 %collective-permute-done.46 = bf16[192,3072]{1,0:T(8,128)(2,1)S(1)} collective-permute-done((bf16[192,3072]{1,0:T(8,128)(2,1)S(1)}, bf16[192,3072]{1,0:T(8,128)(2,1)S(1)}, u32[]{:S(2)}, u32[]{:S(2)}) %collective-permute-start.46) | collective-permute-done | bytes 1179680 | tf_op jit(solution)/shard_map/ppermute | solution.py:781
  701.6 8.6 %shard_map.278 = (f32[768,2304]{1,0:T(8,128)}, f32[768,768]{1,0:T(8,128)}) custom-call(s32[60]{0:T(128)S(1)} %reshape.556.sp_ref, bf16[384,3072]{1,0:T(8,128)(2,1)} %pad_maximum_fusion.5.refs_0_, bf16[384,3072]{1,0:T(8,128)(2,1)} %collective-permute-done.48.refs_1_), custom_call_target="tpu_custom_call" | custom-call | flops 5000000000 | bytes 5000000 | tf_op jit(solution)/shard_map/pallas_call | solution.py:96
  (455 shorter events, 277.4 us)
Async XLA Ops:
  2.7 22.2 %collective-permute-start = (s32[2,2176]{1,0:T(2,128)}, s32[2,2176]{1,0:T(2,128)}, u32[]{:S(2)}, u32[]{:S(2)}) collective-permute-start(s32[2,2176]{1,0:T(2,128)} %pad_add_fusion), channel_id=1, source_target_pairs={{0,1},{1,0},{2,3},{3,2},{4,5},{5,4},{6,7},{7,6},{8,9},{9,8},{10,11... | collective-permute-start | bytes 52232 | tf_op jit(solution)/shard_map/ppermute | solution.py:845
  6.4 25.0 %collective-permute-start.1 = (bf16[2,512,768]{2,1,0:T(8,128)(2,1)}, bf16[2,512,768]{2,1,0:T(8,128)(2,1)}, u32[]{:S(2)}, u32[]{:S(2)}) collective-permute-start(bf16[2,512,768]{2,1,0:T(8,128)(2,1)} %select_bitcast_fusion.2), channel_id=1, source_target_pairs={{0,1},{1,0},{2,3},{3,2},{4,5},{5,4},{6,7},{7,6},{8,9},{9,8},{10,11... | collective-permute-start | bytes 4718600 | tf_op jit(solution)/shard_map/ppermute | solution.py:845
  71.8 18.6 %collective-permute-start.3 = (bf16[512,768]{1,0:T(8,128)(2,1)S(1)}, bf16[512,768]{1,0:T(8,128)(2,1)S(1)}, u32[]{:S(2)}, u32[]{:S(2)}) collective-permute-start(bf16[512,768]{1,0:T(8,128)(2,1)S(1)} %get-tuple-element.265), channel_id=1, source_target_pairs={{0,16},{1,17},{2,18},{3,19},{4,20},{5,21},{6,22},{7,23},{8,24},{9,... | collective-permute-start | bytes 2359304 | tf_op jit(solution)/shard_map/ppermute | solution.py:984
  122.3 27.2 %collective-permute-start.5 = (bf16[512,768]{1,0:T(8,128)(2,1)S(1)}, bf16[512,768]{1,0:T(8,128)(2,1)S(1)}, u32[]{:S(2)}, u32[]{:S(2)}) collective-permute-start(bf16[512,768]{1,0:T(8,128)(2,1)S(1)} %get-tuple-element.428), channel_id=1, source_target_pairs={{0,16},{1,17},{2,18},{3,19},{4,20},{5,21},{6,22},{7,23},{8,24},{9,... | collective-permute-start | bytes 2359304 | tf_op jit(solution)/shard_map/ppermute | solution.py:984
  161.8 33.9 %collective-permute-start.8 = (bf16[512,768]{1,0:T(8,128)(2,1)S(1)}, bf16[512,768]{1,0:T(8,128)(2,1)S(1)}, u32[]{:S(2)}, u32[]{:S(2)}) collective-permute-start(bf16[512,768]{1,0:T(8,128)(2,1)S(1)} %get-tuple-element.308), channel_id=1, source_target_pairs={{16,0},{17,1},{18,2},{19,3},{20,4},{21,5},{22,6},{23,7},{24,8},{25... | collective-permute-start | bytes 2359304 | tf_op jit(solution)/shard_map/ppermute | solution.py:991
  183.7 43.4 %collective-permute-start.10 = (bf16[512,768]{1,0:T(8,128)(2,1)S(1)}, bf16[512,768]{1,0:T(8,128)(2,1)S(1)}, u32[]{:S(2)}, u32[]{:S(2)}) collective-permute-start(bf16[512,768]{1,0:T(8,128)(2,1)S(1)} %get-tuple-element.430), channel_id=1, source_target_pairs={{0,16},{1,17},{2,18},{3,19},{4,20},{5,21},{6,22},{7,23},{8,24},{9,... | collective-permute-start | bytes 2359304 | tf_op jit(solution)/shard_map/ppermute | solution.py:984
  239.1 26.4 %collective-permute-start.14 = (bf16[512,768]{1,0:T(8,128)(2,1)S(1)}, bf16[512,768]{1,0:T(8,128)(2,1)S(1)}, u32[]{:S(2)}, u32[]{:S(2)}) collective-permute-start(bf16[512,768]{1,0:T(8,128)(2,1)S(1)} %get-tuple-element.427), channel_id=1, source_target_pairs={{16,0},{17,1},{18,2},{19,3},{20,4},{21,5},{22,6},{23,7},{24,8},{25... | collective-permute-start | bytes 2359304 | tf_op jit(solution)/shard_map/ppermute | solution.py:991
  260.8 35.8 %collective-permute-start.12 = (bf16[512,768]{1,0:T(8,128)(2,1)S(1)}, bf16[512,768]{1,0:T(8,128)(2,1)S(1)}, u32[]{:S(2)}, u32[]{:S(2)}) collective-permute-start(bf16[512,768]{1,0:T(8,128)(2,1)S(1)} %get-tuple-element.432), channel_id=1, source_target_pairs={{0,16},{1,17},{2,18},{3,19},{4,20},{5,21},{6,22},{7,23},{8,24},{9,... | collective-permute-start | bytes 2359304 | tf_op jit(solution)/shard_map/ppermute | solution.py:984
  308.5 21.3 %collective-permute-start.16 = (bf16[512,768]{1,0:T(8,128)(2,1)S(1)}, bf16[512,768]{1,0:T(8,128)(2,1)S(1)}, u32[]{:S(2)}, u32[]{:S(2)}) collective-permute-start(bf16[512,768]{1,0:T(8,128)(2,1)S(1)} %get-tuple-element.429), channel_id=1, source_target_pairs={{16,0},{17,1},{18,2},{19,3},{20,4},{21,5},{22,6},{23,7},{24,8},{25... | collective-permute-start | bytes 2359304 | tf_op jit(solution)/shard_map/ppermute | solution.py:991
  367.7 25.9 %collective-permute-start.18 = (bf16[512,768]{1,0:T(8,128)(2,1)S(1)}, bf16[512,768]{1,0:T(8,128)(2,1)S(1)}, u32[]{:S(2)}, u32[]{:S(2)}) collective-permute-start(bf16[512,768]{1,0:T(8,128)(2,1)S(1)} %get-tuple-element.431), channel_id=1, source_target_pairs={{16,0},{17,1},{18,2},{19,3},{20,4},{21,5},{22,6},{23,7},{24,8},{25... | collective-permute-start | bytes 2359304 | tf_op jit(solution)/shard_map/ppermute | solution.py:991
  425.3 40.7 %collective-permute-start.22 = (bf16[384,3072]{1,0:T(8,128)(2,1)}, bf16[384,3072]{1,0:T(8,128)(2,1)}, u32[]{:S(2)}, u32[]{:S(2)}) collective-permute-start(bf16[384,3072]{1,0:T(8,128)(2,1)} %get-tuple-element.409), channel_id=1, source_target_pairs={{0,1},{1,0},{2,3},{3,2},{4,5},{5,4},{6,7},{7,6},{8,9},{9,8},{10,11... | collective-permute-start | bytes 7077896 | tf_op jit(solution)/shard_map/ppermute | solution.py:784
  429.4 40.4 %collective-permute-start.21 = (bf16[192,3072]{1,0:T(8,128)(2,1)}, bf16[192,3072]{1,0:T(8,128)(2,1)}, u32[]{:S(2)}, u32[]{:S(2)}) collective-permute-start(bf16[192,3072]{1,0:T(8,128)(2,1)} %constant_dynamic-slice_fusion.12), channel_id=1, source_target_pairs={{0,2},{1,5},{2,0},{3,7},{4,6},{5,1},{6,4},{7,3},{8,10},{9,13},{10,... | collective-permute-start | bytes 3538952 | tf_op jit(solution)/shard_map/ppermute | solution.py:781
  447.7 27.8 %collective-permute-start.20 = (bf16[512,1536]{1,0:T(8,128)(2,1)}, bf16[512,1536]{1,0:T(8,128)(2,1)}, u32[]{:S(2)}, u32[]{:S(2)}) collective-permute-start(bf16[512,1536]{1,0:T(8,128)(2,1)} %get-tuple-element.417), channel_id=1, source_target_pairs={{0,1},{1,0},{2,3},{3,2},{4,5},{5,4},{6,7},{7,6},{8,9},{9,8},{10,11... | collective-permute-start | bytes 4718600 | tf_op jit(solution)/shard_map/ppermute | solution.py:845
  469.8 57.4 %collective-permute-start.25 = (bf16[192,3072]{1,0:T(8,128)(2,1)}, bf16[192,3072]{1,0:T(8,128)(2,1)}, u32[]{:S(2)}, u32[]{:S(2)}) collective-permute-start(bf16[192,3072]{1,0:T(8,128)(2,1)} %constant_dynamic-slice_fusion.7), channel_id=1, source_target_pairs={{0,2},{1,3},{2,0},{3,1},{4,6},{5,7},{6,4},{7,5},{8,10},{9,11},{10,... | collective-permute-start | bytes 3538952 | tf_op jit(solution)/shard_map/ppermute | solution.py:781
  473.1 52.6 %collective-permute-start.26 = (bf16[96,3072]{1,0:T(8,128)(2,1)}, bf16[96,3072]{1,0:T(8,128)(2,1)}, u32[]{:S(2)}, u32[]{:S(2)}) collective-permute-start(bf16[96,3072]{1,0:T(8,128)(2,1)} %constant_dynamic-slice_fusion.6), channel_id=1, source_target_pairs={{0,4},{1,3},{2,6},{3,1},{4,0},{5,7},{6,2},{7,5},{8,12},{9,11},{10,... | collective-permute-start | bytes 1769480 | tf_op jit(solution)/shard_map/ppermute | solution.py:781
  505.3 30.5 %collective-permute-start.29 = (bf16[384,3072]{1,0:T(8,128)(2,1)}, bf16[384,3072]{1,0:T(8,128)(2,1)}, u32[]{:S(2)}, u32[]{:S(2)}) collective-permute-start(bf16[384,3072]{1,0:T(8,128)(2,1)} %copy-done.40), channel_id=1, source_target_pairs={{0,1},{1,0},{2,3},{3,2},{4,5},{5,4},{6,7},{7,6},{8,9},{9,8},{10,11... | collective-permute-start | bytes 7077896 | tf_op jit(solution)/shard_map/ppermute | solution.py:784
  517.2 118.5 %collective-permute-start.23 = (bf16[2,512,768]{2,1,0:T(8,128)(2,1)}, bf16[2,512,768]{2,1,0:T(8,128)(2,1)}, u32[]{:S(2)}, u32[]{:S(2)}) collective-permute-start(bf16[2,512,768]{2,1,0:T(8,128)(2,1)} %broadcast_select_fusion.1), channel_id=1, source_target_pairs={{0,1},{1,0},{2,3},{3,2},{4,5},{5,4},{6,7},{7,6},{8,9},{9,8},{10,11... | collective-permute-start | bytes 4718600 | tf_op jit(solution)/shard_map/ppermute | solution.py:845
  525.5 34.8 %collective-permute-start.24 = (f32[88,128]{1,0:T(8,128)S(1)}, f32[88,128]{1,0:T(8,128)S(1)}, u32[]{:S(2)}, u32[]{:S(2)}) collective-permute-start(f32[88,128]{1,0:T(8,128)S(1)} %pad_bitcast_fusion), channel_id=1, source_target_pairs={{0,1},{1,0},{2,3},{3,2},{4,5},{5,4},{6,7},{7,6},{8,9},{9,8},{10,11... | collective-permute-start | bytes 135176 | tf_op jit(solution)/shard_map/ppermute | solution.py:816
  527.2 19.6 %collective-permute-start.28 = (bf16[48,3072]{1,0:T(8,128)(2,1)S(1)}, bf16[48,3072]{1,0:T(8,128)(2,1)S(1)}, u32[]{:S(2)}, u32[]{:S(2)}) collective-permute-start(bf16[48,3072]{1,0:T(8,128)(2,1)S(1)} %constant_dynamic-slice_fusion.4), channel_id=1, source_target_pairs={{0,8},{1,9},{2,10},{3,11},{4,12},{5,13},{6,14},{7,15},{8,0},{9,1},... | collective-permute-start | bytes 884744 | tf_op jit(solution)/shard_map/ppermute | solution.py:781
  534.5 24.6 %collective-permute-start.27 = (bf16[96,3072]{1,0:T(8,128)(2,1)S(1)}, bf16[96,3072]{1,0:T(8,128)(2,1)S(1)}, u32[]{:S(2)}, u32[]{:S(2)}) collective-permute-start(bf16[96,3072]{1,0:T(8,128)(2,1)S(1)} %constant_dynamic-slice_fusion.5), channel_id=1, source_target_pairs={{0,4},{1,5},{2,6},{3,7},{4,0},{5,1},{6,2},{7,3},{8,12},{9,13},{10,... | collective-permute-start | bytes 1769480 | tf_op jit(solution)/shard_map/ppermute | solution.py:781
  546.9 28.7 %collective-permute-start.32 = (bf16[48,3072]{1,0:T(8,128)(2,1)S(1)}, bf16[48,3072]{1,0:T(8,128)(2,1)S(1)}, u32[]{:S(2)}, u32[]{:S(2)}) collective-permute-start(bf16[48,3072]{1,0:T(8,128)(2,1)S(1)} %dynamic-slice_add_fusion.8), channel_id=1, source_target_pairs={{0,8},{1,9},{2,10},{3,11},{4,12},{5,13},{6,14},{7,15},{8,0},{9,1},... | collective-permute-start | bytes 884744 | tf_op jit(solution)/shard_map/ppermute | solution.py:781
  560.4 17.8 %collective-permute-start.30 = (f32[88,128]{1,0:T(8,128)S(1)}, f32[88,128]{1,0:T(8,128)S(1)}, u32[]{:S(2)}, u32[]{:S(2)}) collective-permute-start(f32[88,128]{1,0:T(8,128)S(1)} %fusion.35), channel_id=1, source_target_pairs={{0,2},{1,3},{2,0},{3,1},{4,6},{5,7},{6,4},{7,5},{8,10},{9,11},{10,... | collective-permute-start | bytes 135176 | tf_op jit(solution)/shard_map/ppermute | solution.py:816
  575.8 23.0 %collective-permute-start.36 = (bf16[96,3072]{1,0:T(8,128)(2,1)S(1)}, bf16[96,3072]{1,0:T(8,128)(2,1)S(1)}, u32[]{:S(2)}, u32[]{:S(2)}) collective-permute-start(bf16[96,3072]{1,0:T(8,128)(2,1)S(1)} %pad_maximum_fusion.11), channel_id=1, source_target_pairs={{0,4},{1,3},{2,6},{3,1},{4,0},{5,7},{6,2},{7,5},{8,12},{9,11},{10,... | collective-permute-start | bytes 1769480 | tf_op jit(solution)/shard_map/ppermute | solution.py:781
  575.9 22.7 %collective-permute-start.37 = (bf16[96,3072]{1,0:T(8,128)(2,1)S(1)}, bf16[96,3072]{1,0:T(8,128)(2,1)S(1)}, u32[]{:S(2)}, u32[]{:S(2)}) collective-permute-start(bf16[96,3072]{1,0:T(8,128)(2,1)S(1)} %constant_dynamic-slice_fusion.1), channel_id=1, source_target_pairs={{0,4},{1,3},{2,6},{3,1},{4,0},{5,7},{6,2},{7,5},{8,12},{9,11},{10,... | collective-permute-start | bytes 1769480 | tf_op jit(solution)/shard_map/ppermute | solution.py:781
  578.0 22.6 %collective-permute-start.35 = (bf16[48,3072]{1,0:T(8,128)(2,1)S(1)}, bf16[48,3072]{1,0:T(8,128)(2,1)S(1)}, u32[]{:S(2)}, u32[]{:S(2)}) collective-permute-start(bf16[48,3072]{1,0:T(8,128)(2,1)S(1)} %dynamic-slice_add_fusion.7), channel_id=1, source_target_pairs={{0,8},{1,9},{2,10},{3,11},{4,12},{5,13},{6,14},{7,15},{8,0},{9,1},... | collective-permute-start | bytes 884744 | tf_op jit(solution)/shard_map/ppermute | solution.py:781
  578.2 24.0 %collective-permute-start.34 = (f32[88,128]{1,0:T(8,128)S(1)}, f32[88,128]{1,0:T(8,128)S(1)}, u32[]{:S(2)}, u32[]{:S(2)}) collective-permute-start(f32[88,128]{1,0:T(8,128)S(1)} %fusion.42), channel_id=1, source_target_pairs={{0,4},{1,5},{2,6},{3,7},{4,0},{5,1},{6,2},{7,3},{8,12},{9,13},{10,... | collective-permute-start | bytes 135176 | tf_op jit(solution)/shard_map/ppermute | solution.py:816
  600.9 33.9 %collective-permute-start.39 = (bf16[96,3072]{1,0:T(8,128)(2,1)S(1)}, bf16[96,3072]{1,0:T(8,128)(2,1)S(1)}, u32[]{:S(2)}, u32[]{:S(2)}) collective-permute-start(bf16[96,3072]{1,0:T(8,128)(2,1)S(1)} %pad_maximum_fusion.12), channel_id=1, source_target_pairs={{0,4},{1,5},{2,6},{3,7},{4,0},{5,1},{6,2},{7,3},{8,12},{9,13},{10,... | collective-permute-start | bytes 1769480 | tf_op jit(solution)/shard_map/ppermute | solution.py:781
  602.2 33.6 %collective-permute-start.38 = (f32[88,128]{1,0:T(8,128)S(1)}, f32[88,128]{1,0:T(8,128)S(1)}, u32[]{:S(2)}, u32[]{:S(2)}) collective-permute-start(f32[88,128]{1,0:T(8,128)S(1)} %add.312), channel_id=1, source_target_pairs={{0,8},{1,9},{2,10},{3,11},{4,12},{5,13},{6,14},{7,15},{8,0},{9,1},... | collective-permute-start | bytes 135176 | tf_op jit(solution)/shard_map/ppermute | solution.py:816
  612.5 27.3 %collective-permute-start.42 = (bf16[48,3072]{1,0:T(8,128)(2,1)S(1)}, bf16[48,3072]{1,0:T(8,128)(2,1)S(1)}, u32[]{:S(2)}, u32[]{:S(2)}) collective-permute-start(bf16[48,3072]{1,0:T(8,128)(2,1)S(1)} %dynamic-slice_add_fusion.6), channel_id=1, source_target_pairs={{0,8},{1,9},{2,10},{3,11},{4,12},{5,13},{6,14},{7,15},{8,0},{9,1},... | collective-permute-start | bytes 884744 | tf_op jit(solution)/shard_map/ppermute | solution.py:781
  617.0 22.9 %collective-permute-start.45 = (bf16[384,3072]{1,0:T(8,128)(2,1)S(1)}, bf16[384,3072]{1,0:T(8,128)(2,1)S(1)}, u32[]{:S(2)}, u32[]{:S(2)}) collective-permute-start(bf16[384,3072]{1,0:T(8,128)(2,1)S(1)} %pad_maximum_fusion.3.refs_0_), channel_id=1, source_target_pairs={{0,1},{1,0},{2,3},{3,2},{4,5},{5,4},{6,7},{7,6},{8,9},{9,8},{10,11... | collective-permute-start | bytes 7077896 | tf_op jit(solution)/shard_map/ppermute | solution.py:784
  635.1 21.1 %collective-permute-start.44 = (bf16[192,3072]{1,0:T(8,128)(2,1)S(1)}, bf16[192,3072]{1,0:T(8,128)(2,1)S(1)}, u32[]{:S(2)}, u32[]{:S(2)}) collective-permute-start(bf16[192,3072]{1,0:T(8,128)(2,1)S(1)} %pad_maximum_fusion.9), channel_id=1, source_target_pairs={{0,2},{1,3},{2,0},{3,1},{4,6},{5,7},{6,4},{7,5},{8,10},{9,11},{10,... | collective-permute-start | bytes 3538952 | tf_op jit(solution)/shard_map/ppermute | solution.py:781
  639.8 30.2 %collective-permute-start.43 = (bf16[96,3072]{1,0:T(8,128)(2,1)S(1)}, bf16[96,3072]{1,0:T(8,128)(2,1)S(1)}, u32[]{:S(2)}, u32[]{:S(2)}) collective-permute-start(bf16[96,3072]{1,0:T(8,128)(2,1)S(1)} %pad_maximum_fusion.13), channel_id=1, source_target_pairs={{0,4},{1,3},{2,6},{3,1},{4,0},{5,7},{6,2},{7,5},{8,12},{9,11},{10,... | collective-permute-start | bytes 1769480 | tf_op jit(solution)/shard_map/ppermute | solution.py:781
  (117 other events, 937.5 us)

commit v6 on v5

--- a/solution.py
+++ b/solution.py
@@ -1018,7 +1018,7 @@
     rows_in = after(got.pop(("B", SLOTS[-1][1])), part_expand[0])
     st, grads = dense_back(sp, st, rows_in)
     halves = weight_call(sp, others, 1, [(st["db2"], st["g"])], part_contract)
-    given, contract = weight_sum(ring.mixed, *halves)
+    given, contract = weight_sum(ring.plain, *halves)
     halves = weight_call(sp, others, 1, [(after(st["h1"], given), st["df"])], part_expand)
     given, expand = weight_sum(ring.plain, *halves)
     done = contract.advance(given)
@@ -1032,22 +1032,17 @@
     halves = weight_call(sp, 0, windows, [(st["x"], st["dj"]), (st["a"], st["db1"])])
     given, attend = weight_sum(ring.mixed, *halves)
     done = contract.advance(given)
-
-    later = lambda a: after(a, given)
-    of_windows = lambda name: jnp.sum(later(st[name])[:windows], axis=0)
-    small = [of_windows("sj")[0:2], of_windows("st")[0:6], of_windows("se")] + table_grads(
-        of_windows("cell"), maps, counts
-    )
-    packed = jnp.concatenate([p.reshape(-1) for p in small])
-    packed = jnp.pad(packed, (0, -packed.shape[0] % (8 * PAIR))).reshape(-1, PAIR)
-    totals = Chain(ring.totals(packed), dp_count.bit_length() - 1)
-    result = [jnp.where(section == 0, later(grads_in[w]), later(finals[w])) for w in range(windows)]
+    done = expand.advance(done)
+    done = attend.advance(done)
+
+    result = [jnp.where(section == 0, after(grads_in[w], done), after(finals[w], done)) for w in range(windows)]
     result = jnp.stack(result)
-    ranks = later(rank)
+    ranks = after(rank, done)
     ordered = [lax.dynamic_index_in_dim(result, ranks[w], 0, keepdims=False) for w in range(windows)]
     mine_first, mine_second = jnp.stack(ordered[:micro]), jnp.stack(ordered[micro:])
     keep_rows = jnp.where(core == 0, mine_first, mine_second)
-    got_rows = exchange(jnp.where(core == 0, mine_second, mine_first))
+    give_rows = jnp.where(core == 0, mine_second, mine_first)
+    got_rows = exchange(give_rows)
 
     def assembled(got_rows):
         out_halves = jnp.stack(
@@ -1055,7 +1050,18 @@
         )
         return out_halves.reshape(1, micro, slots, width)
 
+    done = attend.advance(give_rows)
+    done = contract.advance(done)
     done = expand.advance(done)
+
+    of_windows = lambda name: jnp.sum(after(st[name], done)[:windows], axis=0)
+    small = [of_windows("sj")[0:2], of_windows("st")[0:6], of_windows("se")] + table_grads(
+        of_windows("cell"), maps, counts
+    )
+    packed = jnp.concatenate([p.reshape(-1) for p in small])
+    packed = jnp.pad(packed, (0, -packed.shape[0] % (8 * PAIR))).reshape(-1, PAIR)
+    totals = Chain(ring.totals(packed), dp_count.bit_length() - 1)
+    done = packed
     chains = {"attend": attend, "contract": contract, "expand": expand, "totals": totals}
     kinds = {"contract": ([hidden], natural), "expand": ([hidden], natural), "attend": ([3 * width, width], moves)}
     outputs = {}

time: 721 us -> 722 us (level)
  starting transfers between devices: 99.4 us -> 54.6 us
  Pallas kernels: 374 us -> 411 us
    pallas_call x38, Pallas kernels: 368 us -> 406 us  [call(): pl.pallas_call(run, grid_spec=pltpu.PrefetchScalarGridSpec(num_scalar_pre...]
    ppermute x6, starting transfers between devices: 26.1 us -> 5.03 us  [swap(): return lax.ppermute(a, 'dp', [(i, i ^ 1) for i in range(self.count)])]
    ppermute x13, starting transfers between devices: 21.1 us -> 2.63 us  [on_device(): exchange = lambda a: lax.ppermute(a, 'dp', swap)]
    ppermute x18, starting transfers between devices: 20 us -> 11.6 us  [send(): return lax.ppermute(a, 'dp', pairs)]
    ppermute x18, waiting for transfers between devices: 96.9 us -> 89.3 us  [send(): return lax.ppermute(a, 'dp', pairs)]
    unnamed x203 -> x231, local copies, waits for them, and re-layouts: 26.2 us -> 28.7 us
  transfers between devices with their start and end apart: 49 -> 49, of which waited for: 12 -> 14; matrix products, arithmetic and copies ran while one was open for 10% -> 11% of each run, Pallas kernels for 36% -> 38%
where the time goes in v6:
time: 722 us; the launch traced here: 713 us
  Pallas kernels  411 us (57%)
  waiting for transfers between devices  122 us (17%)
  other arithmetic  59.7 us (8%)
  starting transfers between devices  54.6 us (8%)
  local copies, waits for them, and re-layouts  51.6 us (7%)
  between operations  10.9 us (2%)
    pallas_call x38, Pallas kernels, call(): pl.pallas_call(run, grid_spec=pltpu.PrefetchScalarGridSpec(num_scalar_pre...  406 us
    ppermute x18, waiting for transfers between devices, send(): return lax.ppermute(a, 'dp', pairs)  89.3 us
    unnamed x231, local copies, waits for them, and re-layouts  28.7 us
    ppermute x4, starting transfers between devices, on_device(): got['F', zero] = lax.ppermute(out, 'section', [(0, 1)])  25.9 us
    add x12, other arithmetic, stages(): part = keep + order(got)  20.3 us
    ppermute x4, waiting for transfers between devices, on_device(): got['F', zero] = lax.ppermute(out, 'section', [(0, 1)])  17.2 us
  transfers between devices with their start and end apart: 49, of which 14 were waited for; matrix products, arithmetic and copies ran while one was open for 11% of the time, Pallas kernels for 38%

profile of v6, /device:TPU:0, one launch (start us, length us, event | category | flops | bytes accessed | tf_op | source)
XLA Modules:
  0.0 712.9 jit_solution(1007503795632238634)
XLA Ops:
  47.8 14.7 %shard_map.242 = (bf16[5,512,768]{2,1,0:T(8,128)(2,1)}, bf16[5,512,768]{2,1,0:T(8,128)(2,1)}, bf16[5,512,768]{2,1,0:T(8,128)(2,1)}, bf16[5,512,1536]{2,1,0:T(8,128)(2,1)}) custom-call(s32[60]{0:T(128)S(1)} %reshape.556.sp_ref, ...), custom_call_target="tpu_custom_call", output_to_operand_aliasing={{0}: (7, {}), {1}: (8, {}), {2}: (9, {}), {3}: (10, {})} | custom-call | flops 14000000000 | bytes 14000000 | tf_op jit(solution)/shard_map/pallas_call | solution.py:96
  62.6 11.3 %shard_map.243 = (bf16[5,512,768]{2,1,0:T(8,128)(2,1)}, bf16[5,512,768]{2,1,0:T(8,128)(2,1)}, bf16[5,512,3072]{2,1,0:T(8,128)(2,1)}, bf16[5,512,3072]{2,1,0:T(8,...) custom-call(s32[60]{0:T(128)S(1)} %reshape.556.sp_ref, ...), custom_call_target="tpu_custom_call", output_to_operand_aliasing={{0}: (9, {}), {1}: (10, {}), {2}: (11, {}), {3}: (12, {}), ... | custom-call | flops 10000000000 | bytes 10000000 | tf_op jit(solution)/shard_map/pallas_call | solution.py:96
  75.2 17.2 %collective-permute-done.3.refs_1_ = bf16[512,768]{1,0:T(8,128)(2,1)S(1)} collective-permute-done((bf16[512,768]{1,0:T(8,128)(2,1)S(1)}, bf16[512,768]{1,0:T(8,128)(2,1)S(1)}, u32[]{:S(2)}, u32[]{:S(2)}) %collective-permute-start.3) | collective-permute-done | bytes 786464 | tf_op jit(solution)/shard_map/ppermute | solution.py:984
  101.6 13.9 %shard_map.245 = (bf16[5,512,768]{2,1,0:T(8,128)(2,1)}, bf16[5,512,768]{2,1,0:T(8,128)(2,1)}, bf16[5,512,768]{2,1,0:T(8,128)(2,1)}, bf16[5,512,1536]{2,1,0:T(8,128)(2,1)}) custom-call(s32[60]{0:T(128)S(1)} %reshape.556.sp_ref, ...), custom_call_target="tpu_custom_call", output_to_operand_aliasing={{0}: (7, {}), {1}: (8, {}), {2}: (9, {}), {3}: (10, {})} | custom-call | flops 14000000000 | bytes 14000000 | tf_op jit(solution)/shard_map/pallas_call | solution.py:96
  115.5 11.0 %shard_map.246 = (bf16[5,512,768]{2,1,0:T(8,128)(2,1)}, bf16[5,512,768]{2,1,0:T(8,128)(2,1)}, bf16[5,512,3072]{2,1,0:T(8,128)(2,1)}, bf16[5,512,3072]{2,1,0:T(8,...) custom-call(s32[60]{0:T(128)S(1)} %reshape.556.sp_ref, ...), custom_call_target="tpu_custom_call", output_to_operand_aliasing={{0}: (9, {}), {1}: (10, {}), {2}: (11, {}), {3}: (12, {}), ... | custom-call | flops 10000000000 | bytes 10000000 | tf_op jit(solution)/shard_map/pallas_call | solution.py:96
  131.0 12.4 %shard_map.249 = (bf16[5,512,768]{2,1,0:T(8,128)(2,1)}, bf16[5,512,3072]{2,1,0:T(8,128)(2,1)}, bf16[5,512,768]{2,1,0:T(8,128)(2,1)}, f32[5,8,768]{2,1,0:T(8,128)...) custom-call(s32[60]{0:T(128)S(1)} %reshape.556.sp_ref, ...), custom_call_target="tpu_custom_call", output_to_operand_aliasing={{0}: (14, {}), {1}: (15, {}), {2}: (16, {}), {3}: (17, {}),... | custom-call | flops 10000000000 | bytes 10000000 | tf_op jit(solution)/shard_map/pallas_call | solution.py:96
  143.5 9.5 %shard_map.250 = (f32[5,64,768]{2,1,0:T(8,128)}, bf16[512,768]{1,0:T(8,128)(2,1)S(1)}, bf16[512,1536]{1,0:T(8,128)(2,1)S(1)}, bf16[512,1536]{1,0:T(8,128)(2,1)}) custom-call(s32[60]{0:T(128)S(1)} %reshape.556.sp_ref, bf16[5,512,768]{2,1,0:T(8,128)(2,1)} %get-tuple-element.267.refs_0_.refs_5_, ...), custom_call_target="tpu_custom_call", output_to_operand_aliasing={{0}: (11, {})} | custom-call | flops 20000000000 | bytes 20000000 | tf_op jit(solution)/shard_map/pallas_call | solution.py:96
  167.3 14.2 %shard_map.248 = (bf16[5,512,768]{2,1,0:T(8,128)(2,1)}, bf16[5,512,768]{2,1,0:T(8,128)(2,1)}, bf16[5,512,768]{2,1,0:T(8,128)(2,1)}, bf16[5,512,1536]{2,1,0:T(8,128)(2,1)}) custom-call(s32[60]{0:T(128)S(1)} %reshape.556.sp_ref, ...), custom_call_target="tpu_custom_call", output_to_operand_aliasing={{0}: (7, {}), {1}: (8, {}), {2}: (9, {}), {3}: (10, {})} | custom-call | flops 14000000000 | bytes 14000000 | tf_op jit(solution)/shard_map/pallas_call | solution.py:96
  181.5 11.0 %shard_map.252 = (bf16[5,512,768]{2,1,0:T(8,128)(2,1)}, bf16[5,512,768]{2,1,0:T(8,128)(2,1)}, bf16[5,512,3072]{2,1,0:T(8,128)(2,1)}, bf16[5,512,3072]{2,1,0:T(8,...) custom-call(s32[60]{0:T(128)S(1)} %reshape.556.sp_ref, ...), custom_call_target="tpu_custom_call", output_to_operand_aliasing={{0}: (9, {}), {1}: (10, {}), {2}: (11, {}), {3}: (12, {}), ... | custom-call | flops 10000000000 | bytes 10000000 | tf_op jit(solution)/shard_map/pallas_call | solution.py:96
  192.5 13.3 %collective-permute-start.10 = (bf16[512,768]{1,0:T(8,128)(2,1)S(1)}, bf16[512,768]{1,0:T(8,128)(2,1)S(1)}, u32[]{:S(2)}, u32[]{:S(2)}) collective-permute-start(bf16[512,768]{1,0:T(8,128)(2,1)S(1)} %get-tuple-element.434), channel_id=1, source_target_pairs={{0,16},{1,17},{2,18},{3,19},{4,20},{5,21},{6,22},{7,23},{8,24},{9,... | collective-permute-start | bytes 2359304 | tf_op jit(solution)/shard_map/ppermute | solution.py:984
  205.9 12.5 %shard_map.253 = (bf16[5,512,768]{2,1,0:T(8,128)(2,1)}, bf16[5,512,3072]{2,1,0:T(8,128)(2,1)}, bf16[5,512,768]{2,1,0:T(8,128)(2,1)}, f32[5,8,768]{2,1,0:T(8,128)...) custom-call(s32[60]{0:T(128)S(1)} %reshape.556.sp_ref, ...), custom_call_target="tpu_custom_call", output_to_operand_aliasing={{0}: (14, {}), {1}: (15, {}), {2}: (16, {}), {3}: (17, {}),... | custom-call | flops 10000000000 | bytes 10000000 | tf_op jit(solution)/shard_map/pallas_call | solution.py:96
  218.3 21.8 %shard_map.254 = (f32[5,64,768]{2,1,0:T(8,128)}, bf16[512,768]{1,0:T(8,128)(2,1)S(1)}, bf16[512,1536]{1,0:T(8,128)(2,1)S(1)}, bf16[512,1536]{1,0:T(8,128)(2,1)}) custom-call(s32[60]{0:T(128)S(1)} %reshape.556.sp_ref, bf16[5,512,768]{2,1,0:T(8,128)(2,1)} %get-tuple-element.282.refs_0_.refs_5_, ...), custom_call_target="tpu_custom_call", output_to_operand_aliasing={{0}: (11, {})} | custom-call | flops 20000000000 | bytes 20000000 | tf_op jit(solution)/shard_map/pallas_call | solution.py:96
  254.4 11.9 %shard_map.257 = (bf16[5,512,768]{2,1,0:T(8,128)(2,1)}, bf16[5,512,768]{2,1,0:T(8,128)(2,1)}, bf16[5,512,768]{2,1,0:T(8,128)(2,1)}, bf16[5,512,1536]{2,1,0:T(8,128)(2,1)}) custom-call(s32[60]{0:T(128)S(1)} %reshape.556.sp_ref, ...), custom_call_target="tpu_custom_call", output_to_operand_aliasing={{0}: (7, {}), {1}: (8, {}), {2}: (9, {}), {3}: (10, {})} | custom-call | flops 14000000000 | bytes 14000000 | tf_op jit(solution)/shard_map/pallas_call | solution.py:96
  266.3 11.0 %shard_map.258 = (bf16[5,512,768]{2,1,0:T(8,128)(2,1)}, bf16[5,512,768]{2,1,0:T(8,128)(2,1)}, bf16[5,512,3072]{2,1,0:T(8,128)(2,1)}, bf16[5,512,3072]{2,1,0:T(8,...) custom-call(s32[60]{0:T(128)S(1)} %reshape.556.sp_ref, ...), custom_call_target="tpu_custom_call", output_to_operand_aliasing={{0}: (9, {}), {1}: (10, {}), {2}: (11, {}), {3}: (12, {}), ... | custom-call | flops 10000000000 | bytes 10000000 | tf_op jit(solution)/shard_map/pallas_call | solution.py:96
  284.1 12.4 %shard_map.261 = (bf16[5,512,768]{2,1,0:T(8,128)(2,1)}, bf16[5,512,3072]{2,1,0:T(8,128)(2,1)}, bf16[5,512,768]{2,1,0:T(8,128)(2,1)}, f32[5,8,768]{2,1,0:T(8,128)...) custom-call(s32[60]{0:T(128)S(1)} %reshape.556.sp_ref, ...), custom_call_target="tpu_custom_call", output_to_operand_aliasing={{0}: (14, {}), {1}: (15, {}), {2}: (16, {}), {3}: (17, {}),... | custom-call | flops 10000000000 | bytes 10000000 | tf_op jit(solution)/shard_map/pallas_call | solution.py:96
  296.5 21.6 %shard_map.262 = (f32[5,64,768]{2,1,0:T(8,128)}, bf16[512,768]{1,0:T(8,128)(2,1)S(1)}, bf16[512,1536]{1,0:T(8,128)(2,1)S(1)}, bf16[512,1536]{1,0:T(8,128)(2,1)}) custom-call(s32[60]{0:T(128)S(1)} %reshape.556.sp_ref, bf16[5,512,768]{2,1,0:T(8,128)(2,1)} %get-tuple-element.333.refs_0_.refs_5_, ...), custom_call_target="tpu_custom_call", output_to_operand_aliasing={{0}: (11, {})} | custom-call | flops 20000000000 | bytes 20000000 | tf_op jit(solution)/shard_map/pallas_call | solution.py:96
  337.8 11.0 %shard_map.264 = (bf16[5,512,768]{2,1,0:T(8,128)(2,1)}, bf16[5,512,768]{2,1,0:T(8,128)(2,1)}, bf16[5,512,3072]{2,1,0:T(8,128)(2,1)}, bf16[5,512,3072]{2,1,0:T(8,...) custom-call(s32[60]{0:T(128)S(1)} %reshape.556.sp_ref, ...), custom_call_target="tpu_custom_call", output_to_operand_aliasing={{0}: (9, {}), {1}: (10, {}), {2}: (11, {}), {3}: (12, {}), ... | custom-call | flops 10000000000 | bytes 10000000 | tf_op jit(solution)/shard_map/pallas_call | solution.py:96
  352.6 12.4 %shard_map.265 = (bf16[5,512,768]{2,1,0:T(8,128)(2,1)}, bf16[5,512,3072]{2,1,0:T(8,128)(2,1)}, bf16[5,512,768]{2,1,0:T(8,128)(2,1)}, f32[5,8,768]{2,1,0:T(8,128)...) custom-call(s32[60]{0:T(128)S(1)} %reshape.556.sp_ref, ...), custom_call_target="tpu_custom_call", output_to_operand_aliasing={{0}: (14, {}), {1}: (15, {}), {2}: (16, {}), {3}: (17, {}),... | custom-call | flops 10000000000 | bytes 10000000 | tf_op jit(solution)/shard_map/pallas_call | solution.py:96
  365.0 21.7 %shard_map.266 = (f32[5,64,768]{2,1,0:T(8,128)}, bf16[512,768]{1,0:T(8,128)(2,1)S(1)}, bf16[512,1536]{1,0:T(8,128)(2,1)S(1)}, bf16[512,1536]{1,0:T(8,128)(2,1)S(1)}) custom-call(s32[60]{0:T(128)S(1)} %reshape.556.sp_ref, bf16[5,512,768]{2,1,0:T(8,128)(2,1)} %get-tuple-element.342.refs_0_, ...), custom_call_target="tpu_custom_call", output_to_operand_aliasing={{0}: (11, {})} | custom-call | flops 20000000000 | bytes 20000000 | tf_op jit(solution)/shard_map/pallas_call | solution.py:96
  399.9 11.5 %shard_map.268 = (bf16[384,3072]{1,0:T(8,128)(2,1)S(1)}, bf16[384,3072]{1,0:T(8,128)(2,1)S(1)}) custom-call(s32[60]{0:T(128)S(1)} %reshape.556.sp_ref, bf16[5,512,768]{2,1,0:T(8,128)(2,1)} %get-tuple-element.392.refs_0_.refs_13_, bf16[5,512,3072]{2,1,0:T(8,128)(2,1)} %get-tuple-element.393.refs_1_), custom_call_target="tpu_custom_call" | custom-call | flops 14000000000 | bytes 14000000 | tf_op jit(solution)/shard_map/pallas_call | solution.py:96
  411.5 11.8 %shard_map.269 = (bf16[384,3072]{1,0:T(8,128)(2,1)S(1)}, bf16[384,3072]{1,0:T(8,128)(2,1)S(1)}) custom-call(s32[60]{0:T(128)S(1)} %reshape.556.sp_ref, bf16[5,512,768]{2,1,0:T(8,128)(2,1)} %get-tuple-element.406.refs_0_, bf16[5,512,3072]{2,1,0:T(8,128)(2,1)} %get-tuple-element.396.refs_1_.refs_14_), custom_call_target="tpu_custom_call" | custom-call | flops 14000000000 | bytes 14000000 | tf_op jit(solution)/shard_map/pallas_call | solution.py:96
  424.7 12.7 %shard_map.270 = (bf16[5,512,768]{2,1,0:T(8,128)(2,1)}, bf16[5,512,3072]{2,1,0:T(8,128)(2,1)}, bf16[5,512,768]{2,1,0:T(8,128)(2,1)}, f32[5,8,768]{2,1,0:T(8,128)...) custom-call(s32[60]{0:T(128)S(1)} %reshape.556.sp_ref, ...), custom_call_target="tpu_custom_call", output_to_operand_aliasing={{0}: (14, {}), {1}: (15, {}), {2}: (16, {}), {3}: (17, {}),... | custom-call | flops 10000000000 | bytes 10000000 | tf_op jit(solution)/shard_map/pallas_call | solution.py:96
  452.3 7.2 %shard_map.272 = (bf16[384,3072]{1,0:T(8,128)(2,1)}, bf16[384,3072]{1,0:T(8,128)(2,1)S(1)}) custom-call(s32[60]{0:T(128)S(1)} %reshape.556.sp_ref, bf16[5,512,768]{2,1,0:T(8,128)(2,1)} %get-tuple-element.406.refs_0_, bf16[5,512,3072]{2,1,0:T(8,128)(2,1)} %get-tuple-element.407.refs_1_, bf16[384,3072]{1,0:T(8,128)(2,1)S(1)} %copy-done.49, ...), custom_call_target="tpu_custom_call" | custom-call | flops 8000000000 | bytes 8000000 | tf_op jit(solution)/shard_map/pallas_call | solution.py:96
  465.0 17.7 %shard_map.273 = (f32[5,64,768]{2,1,0:T(8,128)}, bf16[512,768]{1,0:T(8,128)(2,1)S(1)}, bf16[512,1536]{1,0:T(8,128)(2,1)S(1)}, bf16[512,1536]{1,0:T(8,128)(2,1)}) custom-call(s32[60]{0:T(128)S(1)} %reshape.556.sp_ref, bf16[5,512,768]{2,1,0:T(8,128)(2,1)} %get-tuple-element.342.refs_0_, ...), custom_call_target="tpu_custom_call", output_to_operand_aliasing={{0}: (11, {})} | custom-call | flops 20000000000 | bytes 20000000 | tf_op jit(solution)/shard_map/pallas_call | solution.py:96
  501.6 17.0 %shard_map.275 = (bf16[384,3072]{1,0:T(8,128)(2,1)}, bf16[384,3072]{1,0:T(8,128)(2,1)S(1)}) custom-call(s32[60]{0:T(128)S(1)} %reshape.556.sp_ref, bf16[5,512,768]{2,1,0:T(8,128)(2,1)} %get-tuple-element.341.refs_1_.refs_0_, bf16[5,512,768]{2,1,0:T(8,128)(2,1)} %get-tuple-element.347.refs_0_.refs_11_.refs_1_, ...), custom_call_target="tpu_custom_call" | custom-call | flops 16999999488 | bytes 17000000 | tf_op jit(solution)/shard_map/pallas_call | solution.py:96
  547.0 7.6 %collective-permute-done.29 = bf16[192,3072]{1,0:T(8,128)(2,1)} collective-permute-done((bf16[192,3072]{1,0:T(8,128)(2,1)}, bf16[192,3072]{1,0:T(8,128)(2,1)}, u32[]{:S(2)}, u32[]{:S(2)}) %collective-permute-start.29) | collective-permute-done | bytes 1179680 | tf_op jit(solution)/shard_map/ppermute | solution.py:781
  570.9 17.2 %collective-permute-done.33 = bf16[96,3072]{1,0:T(8,128)(2,1)} collective-permute-done((bf16[96,3072]{1,0:T(8,128)(2,1)}, bf16[96,3072]{1,0:T(8,128)(2,1)}, u32[]{:S(2)}, u32[]{:S(2)}) %collective-permute-start.33) | collective-permute-done | bytes 589856 | tf_op jit(solution)/shard_map/ppermute | solution.py:781
  594.0 26.5 %collective-permute-done.37 = bf16[48,3072]{1,0:T(8,128)(2,1)S(1)} collective-permute-done((bf16[48,3072]{1,0:T(8,128)(2,1)S(1)}, bf16[48,3072]{1,0:T(8,128)(2,1)S(1)}, u32[]{:S(2)}, u32[]{:S(2)}) %collective-permute-start.37) | collective-permute-done | bytes 294944 | tf_op jit(solution)/shard_map/ppermute | solution.py:781
  655.0 16.2 %collective-permute-done.43 = bf16[192,3072]{1,0:T(8,128)(2,1)} collective-permute-done((bf16[192,3072]{1,0:T(8,128)(2,1)}, bf16[192,3072]{1,0:T(8,128)(2,1)}, u32[]{:S(2)}, u32[]{:S(2)}) %collective-permute-start.43) | collective-permute-done | bytes 1179680 | tf_op jit(solution)/shard_map/ppermute | solution.py:781
  677.1 7.8 %shard_map.276 = f32[768,3072]{1,0:T(8,128)} custom-call(s32[60]{0:T(128)S(1)} %reshape.556.sp_ref, bf16[384,3072]{1,0:T(8,128)(2,1)S(1)} %copy-done.14, bf16[384,3072]{1,0:T(8,128)(2,1)} %collective-permute-done.44.refs_1_), custom_call_target="tpu_custom_call" | custom-call | flops 5000000000 | bytes 5000000 | tf_op jit(solution)/shard_map/pallas_call | solution.py:96
  696.1 8.6 %shard_map.277 = (f32[768,2304]{1,0:T(8,128)}, f32[768,768]{1,0:T(8,128)}) custom-call(s32[60]{0:T(128)S(1)} %reshape.556.sp_ref, bf16[384,3072]{1,0:T(8,128)(2,1)} %pad_maximum_fusion.5.refs_0_, bf16[384,3072]{1,0:T(8,128)(2,1)} %collective-permute-done.47.refs_1_), custom_call_target="tpu_custom_call" | custom-call | flops 5000000000 | bytes 5000000 | tf_op jit(solution)/shard_map/pallas_call | solution.py:96
  704.7 7.8 %shard_map.278 = f32[768,3072]{1,0:T(8,128)} custom-call(s32[60]{0:T(128)S(1)} %reshape.556.sp_ref, bf16[384,3072]{1,0:T(8,128)(2,1)S(1)} %pad_maximum_fusion.4.refs_0_, bf16[384,3072]{1,0:T(8,128)(2,1)} %collective-permute-done.48.refs_1_), custom_call_target="tpu_custom_call" | custom-call | flops 5000000000 | bytes 5000000 | tf_op jit(solution)/shard_map/pallas_call | solution.py:96
  (483 shorter events, 267.6 us)
Async XLA Ops:
  2.7 22.1 %collective-permute-start = (s32[2,2176]{1,0:T(2,128)}, s32[2,2176]{1,0:T(2,128)}, u32[]{:S(2)}, u32[]{:S(2)}) collective-permute-start(s32[2,2176]{1,0:T(2,128)} %pad_add_fusion), channel_id=1, source_target_pairs={{0,1},{1,0},{2,3},{3,2},{4,5},{5,4},{6,7},{7,6},{8,9},{9,8},{10,11... | collective-permute-start | bytes 52232 | tf_op jit(solution)/shard_map/ppermute | solution.py:845
  6.4 24.9 %collective-permute-start.1 = (bf16[2,512,768]{2,1,0:T(8,128)(2,1)}, bf16[2,512,768]{2,1,0:T(8,128)(2,1)}, u32[]{:S(2)}, u32[]{:S(2)}) collective-permute-start(bf16[2,512,768]{2,1,0:T(8,128)(2,1)} %select_bitcast_fusion.2), channel_id=1, source_target_pairs={{0,1},{1,0},{2,3},{3,2},{4,5},{5,4},{6,7},{7,6},{8,9},{9,8},{10,11... | collective-permute-start | bytes 4718600 | tf_op jit(solution)/shard_map/ppermute | solution.py:845
  73.8 18.6 %collective-permute-start.3 = (bf16[512,768]{1,0:T(8,128)(2,1)S(1)}, bf16[512,768]{1,0:T(8,128)(2,1)S(1)}, u32[]{:S(2)}, u32[]{:S(2)}) collective-permute-start(bf16[512,768]{1,0:T(8,128)(2,1)S(1)} %get-tuple-element.265), channel_id=1, source_target_pairs={{0,16},{1,17},{2,18},{3,19},{4,20},{5,21},{6,22},{7,23},{8,24},{9,... | collective-permute-start | bytes 2359304 | tf_op jit(solution)/shard_map/ppermute | solution.py:984
  126.5 27.4 %collective-permute-start.5 = (bf16[512,768]{1,0:T(8,128)(2,1)S(1)}, bf16[512,768]{1,0:T(8,128)(2,1)S(1)}, u32[]{:S(2)}, u32[]{:S(2)}) collective-permute-start(bf16[512,768]{1,0:T(8,128)(2,1)S(1)} %get-tuple-element.432), channel_id=1, source_target_pairs={{0,16},{1,17},{2,18},{3,19},{4,20},{5,21},{6,22},{7,23},{8,24},{9,... | collective-permute-start | bytes 2359304 | tf_op jit(solution)/shard_map/ppermute | solution.py:984
  166.0 39.9 %collective-permute-start.8 = (bf16[512,768]{1,0:T(8,128)(2,1)S(1)}, bf16[512,768]{1,0:T(8,128)(2,1)S(1)}, u32[]{:S(2)}, u32[]{:S(2)}) collective-permute-start(bf16[512,768]{1,0:T(8,128)(2,1)S(1)} %get-tuple-element.308), channel_id=1, source_target_pairs={{16,0},{17,1},{18,2},{19,3},{20,4},{21,5},{22,6},{23,7},{24,8},{25... | collective-permute-start | bytes 2359304 | tf_op jit(solution)/shard_map/ppermute | solution.py:991
  192.5 48.8 %collective-permute-start.10 = (bf16[512,768]{1,0:T(8,128)(2,1)S(1)}, bf16[512,768]{1,0:T(8,128)(2,1)S(1)}, u32[]{:S(2)}, u32[]{:S(2)}) collective-permute-start(bf16[512,768]{1,0:T(8,128)(2,1)S(1)} %get-tuple-element.434), channel_id=1, source_target_pairs={{0,16},{1,17},{2,18},{3,19},{4,20},{5,21},{6,22},{7,23},{8,24},{9,... | collective-permute-start | bytes 2359304 | tf_op jit(solution)/shard_map/ppermute | solution.py:984
  253.1 30.9 %collective-permute-start.14 = (bf16[512,768]{1,0:T(8,128)(2,1)S(1)}, bf16[512,768]{1,0:T(8,128)(2,1)S(1)}, u32[]{:S(2)}, u32[]{:S(2)}) collective-permute-start(bf16[512,768]{1,0:T(8,128)(2,1)S(1)} %get-tuple-element.431), channel_id=1, source_target_pairs={{16,0},{17,1},{18,2},{19,3},{20,4},{21,5},{22,6},{23,7},{24,8},{25... | collective-permute-start | bytes 2359304 | tf_op jit(solution)/shard_map/ppermute | solution.py:991
  277.3 42.0 %collective-permute-start.12 = (bf16[512,768]{1,0:T(8,128)(2,1)S(1)}, bf16[512,768]{1,0:T(8,128)(2,1)S(1)}, u32[]{:S(2)}, u32[]{:S(2)}) collective-permute-start(bf16[512,768]{1,0:T(8,128)(2,1)S(1)} %get-tuple-element.436), channel_id=1, source_target_pairs={{0,16},{1,17},{2,18},{3,19},{4,20},{5,21},{6,22},{7,23},{8,24},{9,... | collective-permute-start | bytes 2359304 | tf_op jit(solution)/shard_map/ppermute | solution.py:984
  331.2 21.3 %collective-permute-start.16 = (bf16[512,768]{1,0:T(8,128)(2,1)S(1)}, bf16[512,768]{1,0:T(8,128)(2,1)S(1)}, u32[]{:S(2)}, u32[]{:S(2)}) collective-permute-start(bf16[512,768]{1,0:T(8,128)(2,1)S(1)} %get-tuple-element.433), channel_id=1, source_target_pairs={{16,0},{17,1},{18,2},{19,3},{20,4},{21,5},{22,6},{23,7},{24,8},{25... | collective-permute-start | bytes 2359304 | tf_op jit(solution)/shard_map/ppermute | solution.py:991
  398.7 26.1 %collective-permute-start.18 = (bf16[512,768]{1,0:T(8,128)(2,1)S(1)}, bf16[512,768]{1,0:T(8,128)(2,1)S(1)}, u32[]{:S(2)}, u32[]{:S(2)}) collective-permute-start(bf16[512,768]{1,0:T(8,128)(2,1)S(1)} %get-tuple-element.435), channel_id=1, source_target_pairs={{16,0},{17,1},{18,2},{19,3},{20,4},{21,5},{22,6},{23,7},{24,8},{25... | collective-permute-start | bytes 2359304 | tf_op jit(solution)/shard_map/ppermute | solution.py:991
  459.5 24.5 %collective-permute-start.22 = (bf16[384,3072]{1,0:T(8,128)(2,1)}, bf16[384,3072]{1,0:T(8,128)(2,1)}, u32[]{:S(2)}, u32[]{:S(2)}) collective-permute-start(bf16[384,3072]{1,0:T(8,128)(2,1)} %get-tuple-element.409), channel_id=1, source_target_pairs={{0,1},{1,0},{2,3},{3,2},{4,5},{5,4},{6,7},{7,6},{8,9},{9,8},{10,11... | collective-permute-start | bytes 7077896 | tf_op jit(solution)/shard_map/ppermute | solution.py:784
  463.6 29.0 %collective-permute-start.21 = (bf16[192,3072]{1,0:T(8,128)(2,1)}, bf16[192,3072]{1,0:T(8,128)(2,1)}, u32[]{:S(2)}, u32[]{:S(2)}) collective-permute-start(bf16[192,3072]{1,0:T(8,128)(2,1)} %constant_dynamic-slice_fusion.12), channel_id=1, source_target_pairs={{0,2},{1,3},{2,0},{3,1},{4,6},{5,7},{6,4},{7,5},{8,10},{9,11},{10,... | collective-permute-start | bytes 3538952 | tf_op jit(solution)/shard_map/ppermute | solution.py:781
  487.8 32.0 %collective-permute-start.24 = (bf16[192,3072]{1,0:T(8,128)(2,1)}, bf16[192,3072]{1,0:T(8,128)(2,1)}, u32[]{:S(2)}, u32[]{:S(2)}) collective-permute-start(bf16[192,3072]{1,0:T(8,128)(2,1)} %constant_dynamic-slice_fusion.11), channel_id=1, source_target_pairs={{0,2},{1,3},{2,0},{3,1},{4,6},{5,7},{6,4},{7,5},{8,10},{9,11},{10,... | collective-permute-start | bytes 3538952 | tf_op jit(solution)/shard_map/ppermute | solution.py:781
  495.3 23.3 %collective-permute-start.25 = (bf16[96,3072]{1,0:T(8,128)(2,1)}, bf16[96,3072]{1,0:T(8,128)(2,1)}, u32[]{:S(2)}, u32[]{:S(2)}) collective-permute-start(bf16[96,3072]{1,0:T(8,128)(2,1)} %constant_dynamic-slice_fusion.10), channel_id=1, source_target_pairs={{0,4},{1,5},{2,6},{3,7},{4,0},{5,1},{6,2},{7,3},{8,12},{9,13},{10,... | collective-permute-start | bytes 1769480 | tf_op jit(solution)/shard_map/ppermute | solution.py:781
  523.0 37.9 %collective-permute-start.27 = (bf16[96,3072]{1,0:T(8,128)(2,1)}, bf16[96,3072]{1,0:T(8,128)(2,1)}, u32[]{:S(2)}, u32[]{:S(2)}) collective-permute-start(bf16[96,3072]{1,0:T(8,128)(2,1)} %constant_dynamic-slice_fusion.5), channel_id=1, source_target_pairs={{0,4},{1,5},{2,6},{3,7},{4,0},{5,1},{6,2},{7,3},{8,12},{9,13},{10,... | collective-permute-start | bytes 1769480 | tf_op jit(solution)/shard_map/ppermute | solution.py:781
  525.8 30.5 %collective-permute-start.28 = (bf16[48,3072]{1,0:T(8,128)(2,1)}, bf16[48,3072]{1,0:T(8,128)(2,1)}, u32[]{:S(2)}, u32[]{:S(2)}) collective-permute-start(bf16[48,3072]{1,0:T(8,128)(2,1)} %constant_dynamic-slice_fusion.4), channel_id=1, source_target_pairs={{0,8},{1,9},{2,10},{3,11},{4,12},{5,13},{6,14},{7,15},{8,0},{9,1},... | collective-permute-start | bytes 884744 | tf_op jit(solution)/shard_map/ppermute | solution.py:781
  538.1 16.5 %collective-permute-start.29 = (bf16[192,3072]{1,0:T(8,128)(2,1)}, bf16[192,3072]{1,0:T(8,128)(2,1)}, u32[]{:S(2)}, u32[]{:S(2)}) collective-permute-start(bf16[192,3072]{1,0:T(8,128)(2,1)} %constant_dynamic-slice_fusion.3), channel_id=1, source_target_pairs={{0,2},{1,5},{2,0},{3,7},{4,6},{5,1},{6,4},{7,3},{8,10},{9,13},{10,... | collective-permute-start | bytes 3538952 | tf_op jit(solution)/shard_map/ppermute | solution.py:781
  558.0 31.2 %collective-permute-start.32 = (bf16[48,3072]{1,0:T(8,128)(2,1)}, bf16[48,3072]{1,0:T(8,128)(2,1)}, u32[]{:S(2)}, u32[]{:S(2)}) collective-permute-start(bf16[48,3072]{1,0:T(8,128)(2,1)} %dynamic-slice_add_fusion.8), channel_id=1, source_target_pairs={{0,8},{1,9},{2,10},{3,11},{4,12},{5,13},{6,14},{7,15},{8,0},{9,1},... | collective-permute-start | bytes 884744 | tf_op jit(solution)/shard_map/ppermute | solution.py:781
  566.4 21.7 %collective-permute-start.33 = (bf16[96,3072]{1,0:T(8,128)(2,1)}, bf16[96,3072]{1,0:T(8,128)(2,1)}, u32[]{:S(2)}, u32[]{:S(2)}) collective-permute-start(bf16[96,3072]{1,0:T(8,128)(2,1)} %constant_dynamic-slice_fusion.1), channel_id=1, source_target_pairs={{0,4},{1,3},{2,6},{3,1},{4,0},{5,7},{6,2},{7,5},{8,12},{9,11},{10,... | collective-permute-start | bytes 1769480 | tf_op jit(solution)/shard_map/ppermute | solution.py:781
  567.5 26.2 %collective-permute-start.30 = (f32[88,128]{1,0:T(8,128)S(1)}, f32[88,128]{1,0:T(8,128)S(1)}, u32[]{:S(2)}, u32[]{:S(2)}) collective-permute-start(f32[88,128]{1,0:T(8,128)S(1)} %pad_bitcast_fusion), channel_id=1, source_target_pairs={{0,1},{1,0},{2,3},{3,2},{4,5},{5,4},{6,7},{7,6},{8,9},{9,8},{10,11... | collective-permute-start | bytes 135176 | tf_op jit(solution)/shard_map/ppermute | solution.py:816
  568.2 22.3 %collective-permute-start.31 = (bf16[48,3072]{1,0:T(8,128)(2,1)S(1)}, bf16[48,3072]{1,0:T(8,128)(2,1)S(1)}, u32[]{:S(2)}, u32[]{:S(2)}) collective-permute-start(bf16[48,3072]{1,0:T(8,128)(2,1)S(1)} %constant_dynamic-slice_fusion.2), channel_id=1, source_target_pairs={{0,8},{1,9},{2,10},{3,11},{4,12},{5,13},{6,14},{7,15},{8,0},{9,1},... | collective-permute-start | bytes 884744 | tf_op jit(solution)/shard_map/ppermute | solution.py:781
  590.4 30.3 %collective-permute-start.36 = (bf16[96,3072]{1,0:T(8,128)(2,1)S(1)}, bf16[96,3072]{1,0:T(8,128)(2,1)S(1)}, u32[]{:S(2)}, u32[]{:S(2)}) collective-permute-start(bf16[96,3072]{1,0:T(8,128)(2,1)S(1)} %pad_maximum_fusion.11), channel_id=1, source_target_pairs={{0,4},{1,5},{2,6},{3,7},{4,0},{5,1},{6,2},{7,3},{8,12},{9,13},{10,... | collective-permute-start | bytes 1769480 | tf_op jit(solution)/shard_map/ppermute | solution.py:781
  590.5 30.0 %collective-permute-start.37 = (bf16[48,3072]{1,0:T(8,128)(2,1)S(1)}, bf16[48,3072]{1,0:T(8,128)(2,1)S(1)}, u32[]{:S(2)}, u32[]{:S(2)}) collective-permute-start(bf16[48,3072]{1,0:T(8,128)(2,1)S(1)} %constant_dynamic-slice_fusion), channel_id=1, source_target_pairs={{0,8},{1,9},{2,10},{3,11},{4,12},{5,13},{6,14},{7,15},{8,0},{9,1},... | collective-permute-start | bytes 884744 | tf_op jit(solution)/shard_map/ppermute | solution.py:781
  590.7 35.2 %collective-permute-start.35 = (bf16[48,3072]{1,0:T(8,128)(2,1)S(1)}, bf16[48,3072]{1,0:T(8,128)(2,1)S(1)}, u32[]{:S(2)}, u32[]{:S(2)}) collective-permute-start(bf16[48,3072]{1,0:T(8,128)(2,1)S(1)} %dynamic-slice_add_fusion.7), channel_id=1, source_target_pairs={{0,8},{1,9},{2,10},{3,11},{4,12},{5,13},{6,14},{7,15},{8,0},{9,1},... | collective-permute-start | bytes 884744 | tf_op jit(solution)/shard_map/ppermute | solution.py:781
  593.7 32.4 %collective-permute-start.34 = (f32[88,128]{1,0:T(8,128)S(1)}, f32[88,128]{1,0:T(8,128)S(1)}, u32[]{:S(2)}, u32[]{:S(2)}) collective-permute-start(f32[88,128]{1,0:T(8,128)S(1)} %fusion.35), channel_id=1, source_target_pairs={{0,2},{1,3},{2,0},{3,1},{4,6},{5,7},{6,4},{7,5},{8,10},{9,11},{10,... | collective-permute-start | bytes 135176 | tf_op jit(solution)/shard_map/ppermute | solution.py:816
  621.0 16.3 %collective-permute-start.40 = (bf16[192,3072]{1,0:T(8,128)(2,1)S(1)}, bf16[192,3072]{1,0:T(8,128)(2,1)S(1)}, u32[]{:S(2)}, u32[]{:S(2)}) collective-permute-start(bf16[192,3072]{1,0:T(8,128)(2,1)S(1)} %pad_maximum_fusion.8), channel_id=1, source_target_pairs={{0,2},{1,3},{2,0},{3,1},{4,6},{5,7},{6,4},{7,5},{8,10},{9,11},{10,... | collective-permute-start | bytes 3538952 | tf_op jit(solution)/shard_map/ppermute | solution.py:781
  638.0 17.0 %collective-permute-start.44 = (bf16[384,3072]{1,0:T(8,128)(2,1)S(1)}, bf16[384,3072]{1,0:T(8,128)(2,1)}, u32[]{:S(2)}, u32[]{:S(2)}) collective-permute-start(bf16[384,3072]{1,0:T(8,128)(2,1)S(1)} %pad_maximum_fusion.3.refs_0_), channel_id=1, source_target_pairs={{0,1},{1,0},{2,3},{3,2},{4,5},{5,4},{6,7},{7,6},{8,9},{9,8},{10,11... | collective-permute-start | bytes 7077896 | tf_op jit(solution)/shard_map/ppermute | solution.py:784
  642.1 29.2 %collective-permute-start.43 = (bf16[192,3072]{1,0:T(8,128)(2,1)}, bf16[192,3072]{1,0:T(8,128)(2,1)}, u32[]{:S(2)}, u32[]{:S(2)}) collective-permute-start(bf16[192,3072]{1,0:T(8,128)(2,1)} %pad_maximum_fusion.9), channel_id=1, source_target_pairs={{0,2},{1,3},{2,0},{3,1},{4,6},{5,7},{6,4},{7,5},{8,10},{9,11},{10,... | collective-permute-start | bytes 3538952 | tf_op jit(solution)/shard_map/ppermute | solution.py:781
  642.5 42.4 %collective-permute-start.26 = (bf16[2,512,768]{2,1,0:T(8,128)(2,1)}, bf16[2,512,768]{2,1,0:T(8,128)(2,1)S(1)}, u32[]{:S(2)}, u32[]{:S(2)}) collective-permute-start(bf16[2,512,768]{2,1,0:T(8,128)(2,1)} %broadcast_select_fusion.1), channel_id=1, source_target_pairs={{0,1},{1,0},{2,3},{3,2},{4,5},{5,4},{6,7},{7,6},{8,9},{9,8},{10,11... | collective-permute-start | bytes 4718600 | tf_op jit(solution)/shard_map/ppermute | solution.py:845
  650.0 34.9 %collective-permute-start.42 = (f32[88,128]{1,0:T(8,128)S(1)}, f32[88,128]{1,0:T(8,128)S(1)}, u32[]{:S(2)}, u32[]{:S(2)}) collective-permute-start(f32[88,128]{1,0:T(8,128)S(1)} %add.313), channel_id=1, source_target_pairs={{0,8},{1,9},{2,10},{3,11},{4,12},{5,13},{6,14},{7,15},{8,0},{9,1},... | collective-permute-start | bytes 135176 | tf_op jit(solution)/shard_map/ppermute | solution.py:816
  654.9 32.6 %collective-permute-start.46 = (bf16[192,3072]{1,0:T(8,128)(2,1)S(1)}, bf16[192,3072]{1,0:T(8,128)(2,1)S(1)}, u32[]{:S(2)}, u32[]{:S(2)}) collective-permute-start(bf16[192,3072]{1,0:T(8,128)(2,1)S(1)} %pad_maximum_fusion.10), channel_id=1, source_target_pairs={{0,2},{1,5},{2,0},{3,7},{4,6},{5,1},{6,4},{7,3},{8,10},{9,13},{10,... | collective-permute-start | bytes 3538952 | tf_op jit(solution)/shard_map/ppermute | solution.py:781
  673.4 22.7 %collective-permute-start.48 = (bf16[384,3072]{1,0:T(8,128)(2,1)S(1)}, bf16[384,3072]{1,0:T(8,128)(2,1)}, u32[]{:S(2)}, u32[]{:S(2)}) collective-permute-start(bf16[384,3072]{1,0:T(8,128)(2,1)S(1)} %pad_maximum_fusion.4.refs_0_), channel_id=1, source_target_pairs={{0,1},{1,0},{2,3},{3,2},{4,5},{5,4},{6,7},{7,6},{8,9},{9,8},{10,11... | collective-permute-start | bytes 7077896 | tf_op jit(solution)/shard_map/ppermute | solution.py:784
  (131 other events, 994.7 us)

commit v7 on v6

--- a/solution.py
+++ b/solution.py
@@ -798,11 +798,15 @@
         got = self.swap(give)
         order = yield
         part = keep + order(got)
-        for step in steps:
+        for step in steps[:-1]:
             keep, got = self.halve(part, step)
             order = yield part
             part = keep + order(got)
-        for step in steps[::-1]:
+        for step in steps[-1:]:
+            got = self.send(part, step)
+            order = yield part
+            part = part + order(got)
+        for step in steps[:-1][::-1]:
             got = self.send(part, step)
             order = yield part
             part = self.join(part, order(got), step)
@@ -1004,7 +1008,7 @@
             return self.last
 
     def weight_sum(steps, give, keep):
-        return give, Chain(ring.stages(give, keep, steps), 2 * len(steps) + 2)
+        return give, Chain(ring.stages(give, keep, steps), 2 * len(steps) + 1)
 
     natural = [((0, 0), 0, hidden)]
     cols = PAIRS * PAIR

time: 722 us -> 742 us (1.028)
  waiting for transfers between devices: 122 us -> 147 us
  Pallas kernels: 411 us -> 392 us
  starting transfers between devices: 54.6 us -> 71.6 us
    ppermute x18 -> x15, waiting for transfers between devices: 89.3 us -> 117 us  [send(): return lax.ppermute(a, 'dp', pairs)]
    ppermute x18 -> x15, starting transfers between devices: 11.6 us -> 34.6 us  [send(): return lax.ppermute(a, 'dp', pairs)]
    pallas_call x38, Pallas kernels: 406 us -> 387 us  [call(): pl.pallas_call(run, grid_spec=pltpu.PrefetchScalarGridSpec(num_scalar_pre...]
    unnamed x231 -> x211, local copies, waits for them, and re-layouts: 28.7 us -> 27.5 us
    add x12 -> x9, other arithmetic: 20.3 us -> 20.8 us  [stages(): part = keep + order(got)]
  transfers between devices with their start and end apart: 49 -> 46, of which waited for: 14 -> 15; matrix products, arithmetic and copies ran while one was open for 11% -> 10% of each run, Pallas kernels for 38% -> 37%
where the time goes in v7:
time: 742 us; the launch traced here: 737 us
  Pallas kernels  392 us (53%)
  waiting for transfers between devices  147 us (20%)
  starting transfers between devices  71.6 us (10%)
  other arithmetic  61.5 us (8%)
  local copies, waits for them, and re-layouts  50.8 us (7%)
  between operations  10.6 us (1%)
    pallas_call x38, Pallas kernels, call(): pl.pallas_call(run, grid_spec=pltpu.PrefetchScalarGridSpec(num_scalar_pre...  387 us
    ppermute x15, waiting for transfers between devices, send(): return lax.ppermute(a, 'dp', pairs)  117 us
    ppermute x15, starting transfers between devices, send(): return lax.ppermute(a, 'dp', pairs)  34.6 us
    unnamed x211, local copies, waits for them, and re-layouts  27.5 us
    ppermute x4, starting transfers between devices, on_device(): got['F', zero] = lax.ppermute(out, 'section', [(0, 1)])  25.8 us
    add x9, other arithmetic, stages(): part = keep + order(got)  20.8 us
    ppermute x4, waiting for transfers between devices, on_device(): got['F', zero] = lax.ppermute(out, 'section', [(0, 1)])  17.2 us
  transfers between devices with their start and end apart: 46, of which 15 were waited for; matrix products, arithmetic and copies ran while one was open for 10% of the time, Pallas kernels for 37%

profile of v7, /device:TPU:0, one launch (start us, length us, event | category | flops | bytes accessed | tf_op | source)
XLA Modules:
  0.0 736.5 jit_solution(15909675359928988371)
XLA Ops:
  47.9 14.7 %shard_map.242 = (bf16[5,512,768]{2,1,0:T(8,128)(2,1)}, bf16[5,512,768]{2,1,0:T(8,128)(2,1)}, bf16[5,512,768]{2,1,0:T(8,128)(2,1)}, bf16[5,512,1536]{2,1,0:T(8,128)(2,1)}) custom-call(s32[60]{0:T(128)S(1)} %reshape.556.sp_ref, ...), custom_call_target="tpu_custom_call", output_to_operand_aliasing={{0}: (7, {}), {1}: (8, {}), {2}: (9, {}), {3}: (10, {})} | custom-call | flops 14000000000 | bytes 14000000 | tf_op jit(solution)/shard_map/pallas_call | solution.py:96
  62.6 11.3 %shard_map.243 = (bf16[5,512,768]{2,1,0:T(8,128)(2,1)}, bf16[5,512,768]{2,1,0:T(8,128)(2,1)}, bf16[5,512,3072]{2,1,0:T(8,128)(2,1)}, bf16[5,512,3072]{2,1,0:T(8,...) custom-call(s32[60]{0:T(128)S(1)} %reshape.556.sp_ref, ...), custom_call_target="tpu_custom_call", output_to_operand_aliasing={{0}: (9, {}), {1}: (10, {}), {2}: (11, {}), {3}: (12, {}), ... | custom-call | flops 10000000000 | bytes 10000000 | tf_op jit(solution)/shard_map/pallas_call | solution.py:96
  75.3 17.2 %collective-permute-done.3.refs_1_ = bf16[512,768]{1,0:T(8,128)(2,1)S(1)} collective-permute-done((bf16[512,768]{1,0:T(8,128)(2,1)S(1)}, bf16[512,768]{1,0:T(8,128)(2,1)S(1)}, u32[]{:S(2)}, u32[]{:S(2)}) %collective-permute-start.3) | collective-permute-done | bytes 786464 | tf_op jit(solution)/shard_map/ppermute | solution.py:988
  101.7 11.8 %shard_map.245 = (bf16[5,512,768]{2,1,0:T(8,128)(2,1)}, bf16[5,512,768]{2,1,0:T(8,128)(2,1)}, bf16[5,512,768]{2,1,0:T(8,128)(2,1)}, bf16[5,512,1536]{2,1,0:T(8,128)(2,1)}) custom-call(s32[60]{0:T(128)S(1)} %reshape.556.sp_ref, ...), custom_call_target="tpu_custom_call", output_to_operand_aliasing={{0}: (7, {}), {1}: (8, {}), {2}: (9, {}), {3}: (10, {})} | custom-call | flops 14000000000 | bytes 14000000 | tf_op jit(solution)/shard_map/pallas_call | solution.py:96
  113.5 11.0 %shard_map.246 = (bf16[5,512,768]{2,1,0:T(8,128)(2,1)}, bf16[5,512,768]{2,1,0:T(8,128)(2,1)}, bf16[5,512,3072]{2,1,0:T(8,128)(2,1)}, bf16[5,512,3072]{2,1,0:T(8,...) custom-call(s32[60]{0:T(128)S(1)} %reshape.556.sp_ref, ...), custom_call_target="tpu_custom_call", output_to_operand_aliasing={{0}: (9, {}), {1}: (10, {}), {2}: (11, {}), {3}: (12, {}), ... | custom-call | flops 10000000000 | bytes 10000000 | tf_op jit(solution)/shard_map/pallas_call | solution.py:96
  131.1 12.4 %shard_map.249 = (bf16[5,512,768]{2,1,0:T(8,128)(2,1)}, bf16[5,512,3072]{2,1,0:T(8,128)(2,1)}, bf16[5,512,768]{2,1,0:T(8,128)(2,1)}, f32[5,8,768]{2,1,0:T(8,128)...) custom-call(s32[60]{0:T(128)S(1)} %reshape.556.sp_ref, ...), custom_call_target="tpu_custom_call", output_to_operand_aliasing={{0}: (14, {}), {1}: (15, {}), {2}: (16, {}), {3}: (17, {}),... | custom-call | flops 10000000000 | bytes 10000000 | tf_op jit(solution)/shard_map/pallas_call | solution.py:96
  143.5 9.5 %shard_map.250 = (f32[5,64,768]{2,1,0:T(8,128)}, bf16[512,768]{1,0:T(8,128)(2,1)S(1)}, bf16[512,1536]{1,0:T(8,128)(2,1)S(1)}, bf16[512,1536]{1,0:T(8,128)(2,1)}) custom-call(s32[60]{0:T(128)S(1)} %reshape.556.sp_ref, bf16[5,512,768]{2,1,0:T(8,128)(2,1)} %get-tuple-element.264.refs_0_.refs_5_, ...), custom_call_target="tpu_custom_call", output_to_operand_aliasing={{0}: (11, {})} | custom-call | flops 20000000000 | bytes 20000000 | tf_op jit(solution)/shard_map/pallas_call | solution.py:96
  167.4 12.1 %shard_map.248 = (bf16[5,512,768]{2,1,0:T(8,128)(2,1)}, bf16[5,512,768]{2,1,0:T(8,128)(2,1)}, bf16[5,512,768]{2,1,0:T(8,128)(2,1)}, bf16[5,512,1536]{2,1,0:T(8,128)(2,1)}) custom-call(s32[60]{0:T(128)S(1)} %reshape.556.sp_ref, ...), custom_call_target="tpu_custom_call", output_to_operand_aliasing={{0}: (7, {}), {1}: (8, {}), {2}: (9, {}), {3}: (10, {})} | custom-call | flops 14000000000 | bytes 14000000 | tf_op jit(solution)/shard_map/pallas_call | solution.py:96
  179.5 11.0 %shard_map.252 = (bf16[5,512,768]{2,1,0:T(8,128)(2,1)}, bf16[5,512,768]{2,1,0:T(8,128)(2,1)}, bf16[5,512,3072]{2,1,0:T(8,128)(2,1)}, bf16[5,512,3072]{2,1,0:T(8,...) custom-call(s32[60]{0:T(128)S(1)} %reshape.556.sp_ref, ...), custom_call_target="tpu_custom_call", output_to_operand_aliasing={{0}: (9, {}), {1}: (10, {}), {2}: (11, {}), {3}: (12, {}), ... | custom-call | flops 10000000000 | bytes 10000000 | tf_op jit(solution)/shard_map/pallas_call | solution.py:96
  190.4 13.4 %collective-permute-start.10 = (bf16[512,768]{1,0:T(8,128)(2,1)S(1)}, bf16[512,768]{1,0:T(8,128)(2,1)S(1)}, u32[]{:S(2)}, u32[]{:S(2)}) collective-permute-start(bf16[512,768]{1,0:T(8,128)(2,1)S(1)} %get-tuple-element.431), channel_id=1, source_target_pairs={{0,16},{1,17},{2,18},{3,19},{4,20},{5,21},{6,22},{7,23},{8,24},{9,... | collective-permute-start | bytes 2359304 | tf_op jit(solution)/shard_map/ppermute | solution.py:988
  203.8 12.5 %shard_map.253 = (bf16[5,512,768]{2,1,0:T(8,128)(2,1)}, bf16[5,512,3072]{2,1,0:T(8,128)(2,1)}, bf16[5,512,768]{2,1,0:T(8,128)(2,1)}, f32[5,8,768]{2,1,0:T(8,128)...) custom-call(s32[60]{0:T(128)S(1)} %reshape.556.sp_ref, ...), custom_call_target="tpu_custom_call", output_to_operand_aliasing={{0}: (14, {}), {1}: (15, {}), {2}: (16, {}), {3}: (17, {}),... | custom-call | flops 10000000000 | bytes 10000000 | tf_op jit(solution)/shard_map/pallas_call | solution.py:96
  216.3 21.8 %shard_map.254 = (f32[5,64,768]{2,1,0:T(8,128)}, bf16[512,768]{1,0:T(8,128)(2,1)S(1)}, bf16[512,1536]{1,0:T(8,128)(2,1)S(1)}, bf16[512,1536]{1,0:T(8,128)(2,1)}) custom-call(s32[60]{0:T(128)S(1)} %reshape.556.sp_ref, bf16[5,512,768]{2,1,0:T(8,128)(2,1)} %get-tuple-element.279.refs_0_.refs_5_, ...), custom_call_target="tpu_custom_call", output_to_operand_aliasing={{0}: (11, {})} | custom-call | flops 20000000000 | bytes 20000000 | tf_op jit(solution)/shard_map/pallas_call | solution.py:96
  252.4 11.9 %shard_map.257 = (bf16[5,512,768]{2,1,0:T(8,128)(2,1)}, bf16[5,512,768]{2,1,0:T(8,128)(2,1)}, bf16[5,512,768]{2,1,0:T(8,128)(2,1)}, bf16[5,512,1536]{2,1,0:T(8,128)(2,1)}) custom-call(s32[60]{0:T(128)S(1)} %reshape.556.sp_ref, ...), custom_call_target="tpu_custom_call", output_to_operand_aliasing={{0}: (7, {}), {1}: (8, {}), {2}: (9, {}), {3}: (10, {})} | custom-call | flops 14000000000 | bytes 14000000 | tf_op jit(solution)/shard_map/pallas_call | solution.py:96
  264.3 11.0 %shard_map.258 = (bf16[5,512,768]{2,1,0:T(8,128)(2,1)}, bf16[5,512,768]{2,1,0:T(8,128)(2,1)}, bf16[5,512,3072]{2,1,0:T(8,128)(2,1)}, bf16[5,512,3072]{2,1,0:T(8,...) custom-call(s32[60]{0:T(128)S(1)} %reshape.556.sp_ref, ...), custom_call_target="tpu_custom_call", output_to_operand_aliasing={{0}: (9, {}), {1}: (10, {}), {2}: (11, {}), {3}: (12, {}), ... | custom-call | flops 10000000000 | bytes 10000000 | tf_op jit(solution)/shard_map/pallas_call | solution.py:96
  279.9 12.4 %shard_map.261 = (bf16[5,512,768]{2,1,0:T(8,128)(2,1)}, bf16[5,512,3072]{2,1,0:T(8,128)(2,1)}, bf16[5,512,768]{2,1,0:T(8,128)(2,1)}, f32[5,8,768]{2,1,0:T(8,128)...) custom-call(s32[60]{0:T(128)S(1)} %reshape.556.sp_ref, ...), custom_call_target="tpu_custom_call", output_to_operand_aliasing={{0}: (14, {}), {1}: (15, {}), {2}: (16, {}), {3}: (17, {}),... | custom-call | flops 10000000000 | bytes 10000000 | tf_op jit(solution)/shard_map/pallas_call | solution.py:96
  292.4 17.9 %shard_map.262 = (f32[5,64,768]{2,1,0:T(8,128)}, bf16[512,768]{1,0:T(8,128)(2,1)S(1)}, bf16[512,1536]{1,0:T(8,128)(2,1)S(1)}, bf16[512,1536]{1,0:T(8,128)(2,1)}) custom-call(s32[60]{0:T(128)S(1)} %reshape.556.sp_ref, bf16[5,512,768]{2,1,0:T(8,128)(2,1)} %get-tuple-element.330.refs_0_.refs_5_, ...), custom_call_target="tpu_custom_call", output_to_operand_aliasing={{0}: (11, {})} | custom-call | flops 20000000000 | bytes 20000000 | tf_op jit(solution)/shard_map/pallas_call | solution.py:96
  330.0 11.0 %shard_map.264 = (bf16[5,512,768]{2,1,0:T(8,128)(2,1)}, bf16[5,512,768]{2,1,0:T(8,128)(2,1)}, bf16[5,512,3072]{2,1,0:T(8,128)(2,1)}, bf16[5,512,3072]{2,1,0:T(8,...) custom-call(s32[60]{0:T(128)S(1)} %reshape.556.sp_ref, ...), custom_call_target="tpu_custom_call", output_to_operand_aliasing={{0}: (9, {}), {1}: (10, {}), {2}: (11, {}), {3}: (12, {}), ... | custom-call | flops 10000000000 | bytes 10000000 | tf_op jit(solution)/shard_map/pallas_call | solution.py:96
  344.8 12.4 %shard_map.265 = (bf16[5,512,768]{2,1,0:T(8,128)(2,1)}, bf16[5,512,3072]{2,1,0:T(8,128)(2,1)}, bf16[5,512,768]{2,1,0:T(8,128)(2,1)}, f32[5,8,768]{2,1,0:T(8,128)...) custom-call(s32[60]{0:T(128)S(1)} %reshape.556.sp_ref, ...), custom_call_target="tpu_custom_call", output_to_operand_aliasing={{0}: (14, {}), {1}: (15, {}), {2}: (16, {}), {3}: (17, {}),... | custom-call | flops 10000000000 | bytes 10000000 | tf_op jit(solution)/shard_map/pallas_call | solution.py:96
  357.2 18.0 %shard_map.266 = (f32[5,64,768]{2,1,0:T(8,128)}, bf16[512,768]{1,0:T(8,128)(2,1)S(1)}, bf16[512,1536]{1,0:T(8,128)(2,1)S(1)}, bf16[512,1536]{1,0:T(8,128)(2,1)S(1)}) custom-call(s32[60]{0:T(128)S(1)} %reshape.556.sp_ref, bf16[5,512,768]{2,1,0:T(8,128)(2,1)} %get-tuple-element.339.refs_0_, ...), custom_call_target="tpu_custom_call", output_to_operand_aliasing={{0}: (11, {})} | custom-call | flops 20000000000 | bytes 20000000 | tf_op jit(solution)/shard_map/pallas_call | solution.py:96
  388.4 11.6 %shard_map.268 = (bf16[384,3072]{1,0:T(8,128)(2,1)S(1)}, bf16[384,3072]{1,0:T(8,128)(2,1)S(1)}) custom-call(s32[60]{0:T(128)S(1)} %reshape.556.sp_ref, bf16[5,512,768]{2,1,0:T(8,128)(2,1)} %get-tuple-element.389.refs_0_.refs_13_, bf16[5,512,3072]{2,1,0:T(8,128)(2,1)} %get-tuple-element.390.refs_1_), custom_call_target="tpu_custom_call" | custom-call | flops 14000000000 | bytes 14000000 | tf_op jit(solution)/shard_map/pallas_call | solution.py:96
  400.0 11.8 %shard_map.269 = (bf16[384,3072]{1,0:T(8,128)(2,1)S(1)}, bf16[384,3072]{1,0:T(8,128)(2,1)S(1)}) custom-call(s32[60]{0:T(128)S(1)} %reshape.556.sp_ref, bf16[5,512,768]{2,1,0:T(8,128)(2,1)} %get-tuple-element.403.refs_0_, bf16[5,512,3072]{2,1,0:T(8,128)(2,1)} %get-tuple-element.393.refs_1_.refs_14_), custom_call_target="tpu_custom_call" | custom-call | flops 14000000000 | bytes 14000000 | tf_op jit(solution)/shard_map/pallas_call | solution.py:96
  413.2 12.7 %shard_map.270 = (bf16[5,512,768]{2,1,0:T(8,128)(2,1)}, bf16[5,512,3072]{2,1,0:T(8,128)(2,1)}, bf16[5,512,768]{2,1,0:T(8,128)(2,1)}, f32[5,8,768]{2,1,0:T(8,128)...) custom-call(s32[60]{0:T(128)S(1)} %reshape.556.sp_ref, ...), custom_call_target="tpu_custom_call", output_to_operand_aliasing={{0}: (14, {}), {1}: (15, {}), {2}: (16, {}), {3}: (17, {}),... | custom-call | flops 10000000000 | bytes 10000000 | tf_op jit(solution)/shard_map/pallas_call | solution.py:96
  440.8 7.2 shard_map.272
  455.1 17.8 %shard_map.273 = (f32[5,64,768]{2,1,0:T(8,128)}, bf16[512,768]{1,0:T(8,128)(2,1)S(1)}, bf16[512,1536]{1,0:T(8,128)(2,1)S(1)}, bf16[512,1536]{1,0:T(8,128)(2,1)}) custom-call(s32[60]{0:T(128)S(1)} %reshape.556.sp_ref, bf16[5,512,768]{2,1,0:T(8,128)(2,1)} %get-tuple-element.339.refs_0_, ...), custom_call_target="tpu_custom_call", output_to_operand_aliasing={{0}: (11, {})} | custom-call | flops 20000000000 | bytes 20000000 | tf_op jit(solution)/shard_map/pallas_call | solution.py:96
  484.4 7.6 %collective-permute-start.25 = (bf16[96,3072]{1,0:T(8,128)(2,1)}, bf16[96,3072]{1,0:T(8,128)(2,1)}, u32[]{:S(2)}, u32[]{:S(2)}) collective-permute-start(bf16[96,3072]{1,0:T(8,128)(2,1)} %constant_dynamic-slice_fusion.7), channel_id=1, source_target_pairs={{0,4},{1,5},{2,6},{3,7},{4,0},{5,1},{6,2},{7,3},{8,12},{9,13},{10,... | collective-permute-start | bytes 1769480 | tf_op jit(solution)/shard_map/ppermute | solution.py:781
  498.3 16.9 %shard_map.275 = (bf16[384,3072]{1,0:T(8,128)(2,1)}, bf16[384,3072]{1,0:T(8,128)(2,1)S(1)}) custom-call(s32[60]{0:T(128)S(1)} %reshape.556.sp_ref, bf16[5,512,768]{2,1,0:T(8,128)(2,1)} %get-tuple-element.338.refs_1_.refs_0_, bf16[5,512,768]{2,1,0:T(8,128)(2,1)} %get-tuple-element.344.refs_0_.refs_11_.refs_1_, ...), custom_call_target="tpu_custom_call" | custom-call | flops 16999999488 | bytes 17000000 | tf_op jit(solution)/shard_map/pallas_call | solution.py:96
  525.8 19.2 %collective-permute-done.24 = bf16[192,3072]{1,0:T(8,128)(2,1)} collective-permute-done((bf16[192,3072]{1,0:T(8,128)(2,1)}, bf16[192,3072]{1,0:T(8,128)(2,1)}, u32[]{:S(2)}, u32[]{:S(2)}) %collective-permute-start.24) | collective-permute-done | bytes 1179680 | tf_op jit(solution)/shard_map/ppermute | solution.py:781
  594.4 9.4 %collective-permute-done.32 = bf16[96,3072]{1,0:T(8,128)(2,1)} collective-permute-done((bf16[96,3072]{1,0:T(8,128)(2,1)}, bf16[96,3072]{1,0:T(8,128)(2,1)}, u32[]{:S(2)}, u32[]{:S(2)}) %collective-permute-start.32) | collective-permute-done | bytes 589856 | tf_op jit(solution)/shard_map/ppermute | solution.py:781
  617.5 30.4 %collective-permute-done.30 = bf16[96,3072]{1,0:T(8,128)(2,1)} collective-permute-done((bf16[96,3072]{1,0:T(8,128)(2,1)}, bf16[96,3072]{1,0:T(8,128)(2,1)}, u32[]{:S(2)}, u32[]{:S(2)}) %collective-permute-start.30) | collective-permute-done | bytes 589856 | tf_op jit(solution)/shard_map/ppermute | solution.py:781
  650.0 8.6 %collective-permute-done.35 = bf16[96,3072]{1,0:T(8,128)(2,1)} collective-permute-done((bf16[96,3072]{1,0:T(8,128)(2,1)}, bf16[96,3072]{1,0:T(8,128)(2,1)}, u32[]{:S(2)}, u32[]{:S(2)}) %collective-permute-start.35) | collective-permute-done | bytes 589856 | tf_op jit(solution)/shard_map/ppermute | solution.py:781
  662.8 8.3 %collective-permute-done.33 = bf16[96,3072]{1,0:T(8,128)(2,1)S(1)} collective-permute-done((bf16[96,3072]{1,0:T(8,128)(2,1)S(1)}, bf16[96,3072]{1,0:T(8,128)(2,1)S(1)}, u32[]{:S(2)}, u32[]{:S(2)}) %collective-permute-start.33) | collective-permute-done | bytes 589856 | tf_op jit(solution)/shard_map/ppermute | solution.py:781
  682.4 16.8 %collective-permute-done.37 = bf16[192,3072]{1,0:T(8,128)(2,1)S(1)} collective-permute-done((bf16[192,3072]{1,0:T(8,128)(2,1)S(1)}, bf16[192,3072]{1,0:T(8,128)(2,1)S(1)}, u32[]{:S(2)}, u32[]{:S(2)}) %collective-permute-start.37) | collective-permute-done | bytes 1179680 | tf_op jit(solution)/shard_map/ppermute | solution.py:781
  (449 shorter events, 294.4 us)
Async XLA Ops:
  2.7 22.2 %collective-permute-start = (s32[2,2176]{1,0:T(2,128)}, s32[2,2176]{1,0:T(2,128)}, u32[]{:S(2)}, u32[]{:S(2)}) collective-permute-start(s32[2,2176]{1,0:T(2,128)} %pad_add_fusion), channel_id=1, source_target_pairs={{0,1},{1,0},{2,3},{3,2},{4,5},{5,4},{6,7},{7,6},{8,9},{9,8},{10,11... | collective-permute-start | bytes 52232 | tf_op jit(solution)/shard_map/ppermute | solution.py:849
  6.4 25.0 %collective-permute-start.1 = (bf16[2,512,768]{2,1,0:T(8,128)(2,1)}, bf16[2,512,768]{2,1,0:T(8,128)(2,1)}, u32[]{:S(2)}, u32[]{:S(2)}) collective-permute-start(bf16[2,512,768]{2,1,0:T(8,128)(2,1)} %select_bitcast_fusion.2), channel_id=1, source_target_pairs={{0,1},{1,0},{2,3},{3,2},{4,5},{5,4},{6,7},{7,6},{8,9},{9,8},{10,11... | collective-permute-start | bytes 4718600 | tf_op jit(solution)/shard_map/ppermute | solution.py:849
  73.9 18.6 %collective-permute-start.3 = (bf16[512,768]{1,0:T(8,128)(2,1)S(1)}, bf16[512,768]{1,0:T(8,128)(2,1)S(1)}, u32[]{:S(2)}, u32[]{:S(2)}) collective-permute-start(bf16[512,768]{1,0:T(8,128)(2,1)S(1)} %get-tuple-element.262), channel_id=1, source_target_pairs={{0,16},{1,17},{2,18},{3,19},{4,20},{5,21},{6,22},{7,23},{8,24},{9,... | collective-permute-start | bytes 2359304 | tf_op jit(solution)/shard_map/ppermute | solution.py:988
  124.5 29.4 %collective-permute-start.5 = (bf16[512,768]{1,0:T(8,128)(2,1)S(1)}, bf16[512,768]{1,0:T(8,128)(2,1)S(1)}, u32[]{:S(2)}, u32[]{:S(2)}) collective-permute-start(bf16[512,768]{1,0:T(8,128)(2,1)S(1)} %get-tuple-element.429), channel_id=1, source_target_pairs={{0,16},{1,17},{2,18},{3,19},{4,20},{5,21},{6,22},{7,23},{8,24},{9,... | collective-permute-start | bytes 2359304 | tf_op jit(solution)/shard_map/ppermute | solution.py:988
  166.1 37.8 %collective-permute-start.8 = (bf16[512,768]{1,0:T(8,128)(2,1)S(1)}, bf16[512,768]{1,0:T(8,128)(2,1)S(1)}, u32[]{:S(2)}, u32[]{:S(2)}) collective-permute-start(bf16[512,768]{1,0:T(8,128)(2,1)S(1)} %get-tuple-element.305), channel_id=1, source_target_pairs={{16,0},{17,1},{18,2},{19,3},{20,4},{21,5},{22,6},{23,7},{24,8},{25... | collective-permute-start | bytes 2359304 | tf_op jit(solution)/shard_map/ppermute | solution.py:995
  190.4 48.9 %collective-permute-start.10 = (bf16[512,768]{1,0:T(8,128)(2,1)S(1)}, bf16[512,768]{1,0:T(8,128)(2,1)S(1)}, u32[]{:S(2)}, u32[]{:S(2)}) collective-permute-start(bf16[512,768]{1,0:T(8,128)(2,1)S(1)} %get-tuple-element.431), channel_id=1, source_target_pairs={{0,16},{1,17},{2,18},{3,19},{4,20},{5,21},{6,22},{7,23},{8,24},{9,... | collective-permute-start | bytes 2359304 | tf_op jit(solution)/shard_map/ppermute | solution.py:988
  251.1 28.8 %collective-permute-start.14 = (bf16[512,768]{1,0:T(8,128)(2,1)S(1)}, bf16[512,768]{1,0:T(8,128)(2,1)S(1)}, u32[]{:S(2)}, u32[]{:S(2)}) collective-permute-start(bf16[512,768]{1,0:T(8,128)(2,1)S(1)} %get-tuple-element.428), channel_id=1, source_target_pairs={{16,0},{17,1},{18,2},{19,3},{20,4},{21,5},{22,6},{23,7},{24,8},{25... | collective-permute-start | bytes 2359304 | tf_op jit(solution)/shard_map/ppermute | solution.py:995
  275.3 36.2 %collective-permute-start.12 = (bf16[512,768]{1,0:T(8,128)(2,1)S(1)}, bf16[512,768]{1,0:T(8,128)(2,1)S(1)}, u32[]{:S(2)}, u32[]{:S(2)}) collective-permute-start(bf16[512,768]{1,0:T(8,128)(2,1)S(1)} %get-tuple-element.433), channel_id=1, source_target_pairs={{0,16},{1,17},{2,18},{3,19},{4,20},{5,21},{6,22},{7,23},{8,24},{9,... | collective-permute-start | bytes 2359304 | tf_op jit(solution)/shard_map/ppermute | solution.py:988
  323.4 21.3 %collective-permute-start.16 = (bf16[512,768]{1,0:T(8,128)(2,1)S(1)}, bf16[512,768]{1,0:T(8,128)(2,1)S(1)}, u32[]{:S(2)}, u32[]{:S(2)}) collective-permute-start(bf16[512,768]{1,0:T(8,128)(2,1)S(1)} %get-tuple-element.430), channel_id=1, source_target_pairs={{16,0},{17,1},{18,2},{19,3},{20,4},{21,5},{22,6},{23,7},{24,8},{25... | collective-permute-start | bytes 2359304 | tf_op jit(solution)/shard_map/ppermute | solution.py:995
  387.1 26.1 %collective-permute-start.18 = (bf16[512,768]{1,0:T(8,128)(2,1)S(1)}, bf16[512,768]{1,0:T(8,128)(2,1)S(1)}, u32[]{:S(2)}, u32[]{:S(2)}) collective-permute-start(bf16[512,768]{1,0:T(8,128)(2,1)S(1)} %get-tuple-element.432), channel_id=1, source_target_pairs={{16,0},{17,1},{18,2},{19,3},{20,4},{21,5},{22,6},{23,7},{24,8},{25... | collective-permute-start | bytes 2359304 | tf_op jit(solution)/shard_map/ppermute | solution.py:995
  448.0 26.1 %collective-permute-start.22 = (bf16[384,3072]{1,0:T(8,128)(2,1)}, bf16[384,3072]{1,0:T(8,128)(2,1)}, u32[]{:S(2)}, u32[]{:S(2)}) collective-permute-start(bf16[384,3072]{1,0:T(8,128)(2,1)} %get-tuple-element.406), channel_id=1, source_target_pairs={{0,1},{1,0},{2,3},{3,2},{4,5},{5,4},{6,7},{7,6},{8,9},{9,8},{10,11... | collective-permute-start | bytes 7077896 | tf_op jit(solution)/shard_map/ppermute | solution.py:784
  452.2 29.5 %collective-permute-start.21 = (bf16[192,3072]{1,0:T(8,128)(2,1)}, bf16[192,3072]{1,0:T(8,128)(2,1)}, u32[]{:S(2)}, u32[]{:S(2)}) collective-permute-start(bf16[192,3072]{1,0:T(8,128)(2,1)} %constant_dynamic-slice_fusion.9), channel_id=1, source_target_pairs={{0,2},{1,3},{2,0},{3,1},{4,6},{5,7},{6,4},{7,5},{8,10},{9,11},{10,... | collective-permute-start | bytes 3538952 | tf_op jit(solution)/shard_map/ppermute | solution.py:781
  474.1 17.9 %collective-permute-start.20 = (bf16[512,1536]{1,0:T(8,128)(2,1)}, bf16[512,1536]{1,0:T(8,128)(2,1)}, u32[]{:S(2)}, u32[]{:S(2)}) collective-permute-start(bf16[512,1536]{1,0:T(8,128)(2,1)} %get-tuple-element.414), channel_id=1, source_target_pairs={{0,1},{1,0},{2,3},{3,2},{4,5},{5,4},{6,7},{7,6},{8,9},{9,8},{10,11... | collective-permute-start | bytes 4718600 | tf_op jit(solution)/shard_map/ppermute | solution.py:849
  484.4 33.5 %collective-permute-start.25 = (bf16[96,3072]{1,0:T(8,128)(2,1)}, bf16[96,3072]{1,0:T(8,128)(2,1)}, u32[]{:S(2)}, u32[]{:S(2)}) collective-permute-start(bf16[96,3072]{1,0:T(8,128)(2,1)} %constant_dynamic-slice_fusion.7), channel_id=1, source_target_pairs={{0,4},{1,5},{2,6},{3,7},{4,0},{5,1},{6,2},{7,3},{8,12},{9,13},{10,... | collective-permute-start | bytes 1769480 | tf_op jit(solution)/shard_map/ppermute | solution.py:781
  515.2 33.0 %collective-permute-start.23 = (bf16[384,3072]{1,0:T(8,128)(2,1)}, bf16[384,3072]{1,0:T(8,128)(2,1)}, u32[]{:S(2)}, u32[]{:S(2)}) collective-permute-start(bf16[384,3072]{1,0:T(8,128)(2,1)} %get-tuple-element.424), channel_id=1, source_target_pairs={{0,1},{1,0},{2,3},{3,2},{4,5},{5,4},{6,7},{7,6},{8,9},{9,8},{10,11... | collective-permute-start | bytes 7077896 | tf_op jit(solution)/shard_map/ppermute | solution.py:784
  516.4 28.7 %collective-permute-start.24 = (bf16[192,3072]{1,0:T(8,128)(2,1)}, bf16[192,3072]{1,0:T(8,128)(2,1)}, u32[]{:S(2)}, u32[]{:S(2)}) collective-permute-start(bf16[192,3072]{1,0:T(8,128)(2,1)} %constant_dynamic-slice_fusion.8), channel_id=1, source_target_pairs={{0,2},{1,3},{2,0},{3,1},{4,6},{5,7},{6,4},{7,5},{8,10},{9,11},{10,... | collective-permute-start | bytes 3538952 | tf_op jit(solution)/shard_map/ppermute | solution.py:781
  519.9 58.8 %collective-permute-start.28 = (bf16[96,3072]{1,0:T(8,128)(2,1)}, bf16[96,3072]{1,0:T(8,128)(2,1)}, u32[]{:S(2)}, u32[]{:S(2)}) collective-permute-start(bf16[96,3072]{1,0:T(8,128)(2,1)} %dynamic-slice_add_fusion.5), channel_id=1, source_target_pairs={{0,8},{1,9},{2,10},{3,11},{4,12},{5,13},{6,14},{7,15},{8,0},{9,1},... | collective-permute-start | bytes 1769480 | tf_op jit(solution)/shard_map/ppermute | solution.py:781
  548.0 35.2 %collective-permute-start.27 = (bf16[96,3072]{1,0:T(8,128)(2,1)}, bf16[96,3072]{1,0:T(8,128)(2,1)}, u32[]{:S(2)}, u32[]{:S(2)}) collective-permute-start(bf16[96,3072]{1,0:T(8,128)(2,1)} %constant_dynamic-slice_fusion.2), channel_id=1, source_target_pairs={{0,4},{1,5},{2,6},{3,7},{4,0},{5,1},{6,2},{7,3},{8,12},{9,13},{10,... | collective-permute-start | bytes 1769480 | tf_op jit(solution)/shard_map/ppermute | solution.py:781
  581.4 24.5 %collective-permute-start.31 = (bf16[96,3072]{1,0:T(8,128)(2,1)}, bf16[96,3072]{1,0:T(8,128)(2,1)}, u32[]{:S(2)}, u32[]{:S(2)}) collective-permute-start(bf16[96,3072]{1,0:T(8,128)(2,1)} %add.286), channel_id=1, source_target_pairs={{0,4},{1,5},{2,6},{3,7},{4,0},{5,1},{6,2},{7,3},{8,12},{9,13},{10,... | collective-permute-start | bytes 1769480 | tf_op jit(solution)/shard_map/ppermute | solution.py:781
  586.2 17.6 %collective-permute-start.32 = (bf16[96,3072]{1,0:T(8,128)(2,1)}, bf16[96,3072]{1,0:T(8,128)(2,1)}, u32[]{:S(2)}, u32[]{:S(2)}) collective-permute-start(bf16[96,3072]{1,0:T(8,128)(2,1)} %constant_dynamic-slice_fusion), channel_id=1, source_target_pairs={{0,4},{1,3},{2,6},{3,1},{4,0},{5,7},{6,2},{7,5},{8,12},{9,11},{10,... | collective-permute-start | bytes 1769480 | tf_op jit(solution)/shard_map/ppermute | solution.py:781
  609.2 51.5 %collective-permute-start.34 = (bf16[192,3072]{1,0:T(8,128)(2,1)}, bf16[192,3072]{1,0:T(8,128)(2,1)}, u32[]{:S(2)}, u32[]{:S(2)}) collective-permute-start(bf16[192,3072]{1,0:T(8,128)(2,1)} %pad_maximum_fusion.8), channel_id=1, source_target_pairs={{0,2},{1,3},{2,0},{3,1},{4,6},{5,7},{6,4},{7,5},{8,10},{9,11},{10,... | collective-permute-start | bytes 3538952 | tf_op jit(solution)/shard_map/ppermute | solution.py:781
  610.9 37.1 %collective-permute-start.30 = (bf16[96,3072]{1,0:T(8,128)(2,1)}, bf16[96,3072]{1,0:T(8,128)(2,1)}, u32[]{:S(2)}, u32[]{:S(2)}) collective-permute-start(bf16[96,3072]{1,0:T(8,128)(2,1)} %dynamic-slice_add_fusion.4), channel_id=1, source_target_pairs={{0,8},{1,9},{2,10},{3,11},{4,12},{5,13},{6,14},{7,15},{8,0},{9,1},... | collective-permute-start | bytes 1769480 | tf_op jit(solution)/shard_map/ppermute | solution.py:781
  616.9 41.7 %collective-permute-start.35 = (bf16[96,3072]{1,0:T(8,128)(2,1)}, bf16[96,3072]{1,0:T(8,128)(2,1)}, u32[]{:S(2)}, u32[]{:S(2)}) collective-permute-start(bf16[96,3072]{1,0:T(8,128)(2,1)} %dynamic-slice_add_fusion.3), channel_id=1, source_target_pairs={{0,8},{1,9},{2,10},{3,11},{4,12},{5,13},{6,14},{7,15},{8,0},{9,1},... | collective-permute-start | bytes 1769480 | tf_op jit(solution)/shard_map/ppermute | solution.py:781
  617.0 32.4 %collective-permute-start.36 = (f32[88,128]{1,0:T(8,128)S(1)}, f32[88,128]{1,0:T(8,128)S(1)}, u32[]{:S(2)}, u32[]{:S(2)}) collective-permute-start(f32[88,128]{1,0:T(8,128)S(1)} %pad_bitcast_fusion), channel_id=1, source_target_pairs={{0,1},{1,0},{2,3},{3,2},{4,5},{5,4},{6,7},{7,6},{8,9},{9,8},{10,11... | collective-permute-start | bytes 135176 | tf_op jit(solution)/shard_map/ppermute | solution.py:820
  617.0 106.9 %collective-permute-start.26 = (bf16[2,512,768]{2,1,0:T(8,128)(2,1)}, bf16[2,512,768]{2,1,0:T(8,128)(2,1)S(1)}, u32[]{:S(2)}, u32[]{:S(2)}) collective-permute-start(bf16[2,512,768]{2,1,0:T(8,128)(2,1)} %broadcast_select_fusion.1), channel_id=1, source_target_pairs={{0,1},{1,0},{2,3},{3,2},{4,5},{5,4},{6,7},{7,6},{8,9},{9,8},{10,11... | collective-permute-start | bytes 4718600 | tf_op jit(solution)/shard_map/ppermute | solution.py:849
  649.4 21.7 %collective-permute-start.33 = (bf16[96,3072]{1,0:T(8,128)(2,1)S(1)}, bf16[96,3072]{1,0:T(8,128)(2,1)S(1)}, u32[]{:S(2)}, u32[]{:S(2)}) collective-permute-start(bf16[96,3072]{1,0:T(8,128)(2,1)S(1)} %add.291), channel_id=1, source_target_pairs={{0,4},{1,5},{2,6},{3,7},{4,0},{5,1},{6,2},{7,3},{8,12},{9,13},{10,... | collective-permute-start | bytes 1769480 | tf_op jit(solution)/shard_map/ppermute | solution.py:781
  649.5 23.5 %collective-permute-start.40 = (f32[88,128]{1,0:T(8,128)S(1)}, f32[88,128]{1,0:T(8,128)S(1)}, u32[]{:S(2)}, u32[]{:S(2)}) collective-permute-start(f32[88,128]{1,0:T(8,128)S(1)} %fusion.35), channel_id=1, source_target_pairs={{0,2},{1,3},{2,0},{3,1},{4,6},{5,7},{6,4},{7,5},{8,10},{9,11},{10,... | collective-permute-start | bytes 135176 | tf_op jit(solution)/shard_map/ppermute | solution.py:820
  660.1 19.4 %collective-permute-start.39 = (bf16[96,3072]{1,0:T(8,128)(2,1)S(1)}, bf16[96,3072]{1,0:T(8,128)(2,1)S(1)}, u32[]{:S(2)}, u32[]{:S(2)}) collective-permute-start(bf16[96,3072]{1,0:T(8,128)(2,1)S(1)} %add.293), channel_id=1, source_target_pairs={{0,4},{1,3},{2,6},{3,1},{4,0},{5,7},{6,2},{7,5},{8,12},{9,11},{10,... | collective-permute-start | bytes 1769480 | tf_op jit(solution)/shard_map/ppermute | solution.py:781
  662.7 19.7 %collective-permute-start.38 = (bf16[384,3072]{1,0:T(8,128)(2,1)S(1)}, bf16[384,3072]{1,0:T(8,128)(2,1)S(1)}, u32[]{:S(2)}, u32[]{:S(2)}) collective-permute-start(bf16[384,3072]{1,0:T(8,128)(2,1)S(1)} %pad_maximum_fusion.3.refs_0_), channel_id=1, source_target_pairs={{0,1},{1,0},{2,3},{3,2},{4,5},{5,4},{6,7},{7,6},{8,9},{9,8},{10,11... | collective-permute-start | bytes 7077896 | tf_op jit(solution)/shard_map/ppermute | solution.py:784
  671.3 28.0 %collective-permute-start.37 = (bf16[192,3072]{1,0:T(8,128)(2,1)S(1)}, bf16[192,3072]{1,0:T(8,128)(2,1)S(1)}, u32[]{:S(2)}, u32[]{:S(2)}) collective-permute-start(bf16[192,3072]{1,0:T(8,128)(2,1)S(1)} %pad_maximum_fusion.9), channel_id=1, source_target_pairs={{0,2},{1,3},{2,0},{3,1},{4,6},{5,7},{6,4},{7,5},{8,10},{9,11},{10,... | collective-permute-start | bytes 3538952 | tf_op jit(solution)/shard_map/ppermute | solution.py:781
  672.9 32.5 %collective-permute-start.41 = (f32[88,128]{1,0:T(8,128)S(1)}, f32[88,128]{1,0:T(8,128)S(1)}, u32[]{:S(2)}, u32[]{:S(2)}) collective-permute-start(f32[88,128]{1,0:T(8,128)S(1)} %fusion.42), channel_id=1, source_target_pairs={{0,4},{1,5},{2,6},{3,7},{4,0},{5,1},{6,2},{7,3},{8,12},{9,13},{10,... | collective-permute-start | bytes 135176 | tf_op jit(solution)/shard_map/ppermute | solution.py:820
  679.6 32.3 %collective-permute-start.44 = (bf16[192,3072]{1,0:T(8,128)(2,1)S(1)}, bf16[192,3072]{1,0:T(8,128)(2,1)S(1)}, u32[]{:S(2)}, u32[]{:S(2)}) collective-permute-start(bf16[192,3072]{1,0:T(8,128)(2,1)S(1)} %pad_maximum_fusion.10), channel_id=1, source_target_pairs={{0,2},{1,5},{2,0},{3,7},{4,6},{5,1},{6,4},{7,3},{8,10},{9,13},{10,... | collective-permute-start | bytes 3538952 | tf_op jit(solution)/shard_map/ppermute | solution.py:781
  (119 other events, 1000.8 us)

commit v8 on v6

--- a/solution.py
+++ b/solution.py
@@ -11,6 +11,8 @@
 GRID = 16
 SPAN = 32
 KEY_BLOCK = 256
+KEY_STEP = 128
+LEAST_KEYS = 256
 ROW_BLOCK = 256
 FF_BLOCK = 768
 PAIRS = 2
@@ -256,8 +258,9 @@
             lse = jnp.where(low, peaks[0], peaks[1]) + jnp.log(total)
             lse_ref[0, :, cols] = split_three(-lse)
 
-    for blocks in range(1, 2 * rows // KEY_BLOCK + 1):
-        pl.when(sp[1] == blocks)(functools.partial(variant, blocks * KEY_BLOCK))
+    for keys in range(KEY_STEP, 2 * rows + 1, KEY_STEP):
+        if keys >= LEAST_KEYS:
+            pl.when(sp[1] == keys)(functools.partial(variant, keys))
 
 
 def attend_call(sp, q_all, kv_own, kv_peer, side_all, hot_all, matrix, bufs):
@@ -480,11 +483,9 @@
     total = 2 * rows
     first = sp[2] == 0
 
-    def variant(blocks):
-        keys = blocks * KEY_BLOCK
+    def variant(keys):
         low = low_half((rows, PAIR))
         key_low = low_half((keys, PAIR))
-        block_low = low_half((KEY_BLOCK, PAIR))
         place = lax.broadcasted_iota(jnp.int32, (KEY_BLOCK, PAIR), 1)
         three = jnp.where(place % HALF < 3, 1.0, 0.0).astype(bf16)
         lone = [
@@ -512,14 +513,16 @@
             dks = []
             dvs = []
             gs = []
-            for b in range(blocks):
-                at = slice(b * KEY_BLOCK, (b + 1) * KEY_BLOCK)
+            for begin in range(0, keys, KEY_BLOCK):
+                size = min(KEY_BLOCK, keys - begin)
+                at = slice(begin, begin + size)
+                block_low = low_half((size, PAIR))
                 vb = v[at]
-                vc = (jnp.where(block_low, vb, three), jnp.where(block_low, three, vb))
+                vc = (jnp.where(block_low, vb, three[:size]), jnp.where(block_low, three[:size], vb))
                 part_v = []
                 part_k = []
                 for head in (0, 1):
-                    kb = jnp.concatenate([kc[head][at], lone[head]], axis=1)
+                    kb = jnp.concatenate([kc[head][at], lone[head][:size]], axis=1)
                     p = jnp.exp(dot_nt(kb, qe[head]))
                     dp = dot_nt(vc[head], dc[head])
                     ds = (p * dp).astype(bf16)
@@ -540,8 +543,9 @@
             keep_ref[:, kv] = jnp.where(first, grads[:rows], grads[rows:])
             send_ref[:, kv] = jnp.where(first, grads[rows:], grads[:rows])
 
-    for blocks in range(1, total // KEY_BLOCK + 1):
-        pl.when(sp[1] == blocks)(functools.partial(variant, blocks))
+    for keys in range(KEY_STEP, total + 1, KEY_STEP):
+        if keys >= LEAST_KEYS:
+            pl.when(sp[1] == keys)(functools.partial(variant, keys))
 
 
 def attend_back_call(
@@ -910,7 +914,7 @@
     given_lengths = jnp.sum(jnp.where(hits, lengths[None, :windows], 0), axis=1)
     infos = jnp.stack(
         [
-            infos, (given_lengths + KEY_BLOCK - 1) // KEY_BLOCK, jnp.full_like(infos, core),
+            infos, (given_lengths + KEY_STEP - 1) // KEY_STEP * KEY_STEP, jnp.full_like(infos, core),
             given_lengths, jnp.full_like(infos, section), given_ids,
         ],
         axis=1,

time: 722 us -> 782 us (1.083)
  Pallas kernels: 411 us -> 455 us
  starting transfers between devices: 54.6 us -> 80.4 us
  waiting for transfers between devices: 122 us -> 110 us
    pallas_call x38, Pallas kernels: 406 us -> 450 us  [call(): pl.pallas_call(run, grid_spec=pltpu.PrefetchScalarGridSpec(num_scalar_pre...]
    ppermute x18, starting transfers between devices: 11.6 us -> 30 us  [send(): return lax.ppermute(a, 'dp', pairs)]
    ppermute x18, waiting for transfers between devices: 89.3 us -> 81.2 us  [send(): return lax.ppermute(a, 'dp', pairs)]
  transfers between devices with their start and end apart: 49 -> 49, of which waited for: 14 -> 13; matrix products, arithmetic and copies ran while one was open for 11% -> 11% of each run, Pallas kernels for 38% -> 39%
where the time goes in v8:
time: 782 us; the launch traced here: 771 us
  Pallas kernels  455 us (58%)
  waiting for transfers between devices  110 us (14%)
  starting transfers between devices  80.4 us (10%)
  other arithmetic  60.5 us (8%)
  local copies, waits for them, and re-layouts  51.6 us (7%)
  between operations  10.6 us (1%)
    pallas_call x38, Pallas kernels, call(): pl.pallas_call(run, grid_spec=pltpu.PrefetchScalarGridSpec(num_scalar_pre...  450 us
    ppermute x18, waiting for transfers between devices, send(): return lax.ppermute(a, 'dp', pairs)  81.2 us
    ppermute x4, starting transfers between devices, on_device(): got['F', zero] = lax.ppermute(out, 'section', [(0, 1)])  32.9 us
    ppermute x18, starting transfers between devices, send(): return lax.ppermute(a, 'dp', pairs)  30 us
    unnamed x231, local copies, waits for them, and re-layouts  28.7 us
    add x12, other arithmetic, stages(): part = keep + order(got)  21.2 us
    ppermute x4, waiting for transfers between devices, on_device(): got['F', zero] = lax.ppermute(out, 'section', [(0, 1)])  17.2 us
  transfers between devices with their start and end apart: 49, of which 13 were waited for; matrix products, arithmetic and copies ran while one was open for 11% of the time, Pallas kernels for 39%

profile of v8, /device:TPU:0, one launch (start us, length us, event | category | flops | bytes accessed | tf_op | source)
XLA Modules:
  0.0 771.2 jit_solution(11161050371931967557)
XLA Ops:
  47.8 15.6 %shard_map.242 = (bf16[5,512,768]{2,1,0:T(8,128)(2,1)}, bf16[5,512,768]{2,1,0:T(8,128)(2,1)}, bf16[5,512,768]{2,1,0:T(8,128)(2,1)}, bf16[5,512,1536]{2,1,0:T(8,128)(2,1)}) custom-call(s32[60]{0:T(128)S(1)} %reshape.559.sp_ref, ...), custom_call_target="tpu_custom_call", output_to_operand_aliasing={{0}: (7, {}), {1}: (8, {}), {2}: (9, {}), {3}: (10, {})} | custom-call | flops 14000000000 | bytes 14000000 | tf_op jit(solution)/shard_map/pallas_call | solution.py:98
  63.5 11.3 %shard_map.243 = (bf16[5,512,768]{2,1,0:T(8,128)(2,1)}, bf16[5,512,768]{2,1,0:T(8,128)(2,1)}, bf16[5,512,3072]{2,1,0:T(8,128)(2,1)}, bf16[5,512,3072]{2,1,0:T(8,...) custom-call(s32[60]{0:T(128)S(1)} %reshape.559.sp_ref, ...), custom_call_target="tpu_custom_call", output_to_operand_aliasing={{0}: (9, {}), {1}: (10, {}), {2}: (11, {}), {3}: (12, {}), ... | custom-call | flops 10000000000 | bytes 10000000 | tf_op jit(solution)/shard_map/pallas_call | solution.py:98
  76.1 17.2 %collective-permute-done.3.refs_1_ = bf16[512,768]{1,0:T(8,128)(2,1)S(1)} collective-permute-done((bf16[512,768]{1,0:T(8,128)(2,1)S(1)}, bf16[512,768]{1,0:T(8,128)(2,1)S(1)}, u32[]{:S(2)}, u32[]{:S(2)}) %collective-permute-start.3) | collective-permute-done | bytes 786464 | tf_op jit(solution)/shard_map/ppermute | solution.py:988
  102.1 12.1 %shard_map.245 = (bf16[5,512,768]{2,1,0:T(8,128)(2,1)}, bf16[5,512,768]{2,1,0:T(8,128)(2,1)}, bf16[5,512,768]{2,1,0:T(8,128)(2,1)}, bf16[5,512,1536]{2,1,0:T(8,128)(2,1)}) custom-call(s32[60]{0:T(128)S(1)} %reshape.559.sp_ref, ...), custom_call_target="tpu_custom_call", output_to_operand_aliasing={{0}: (7, {}), {1}: (8, {}), {2}: (9, {}), {3}: (10, {})} | custom-call | flops 14000000000 | bytes 14000000 | tf_op jit(solution)/shard_map/pallas_call | solution.py:98
  114.2 11.0 %shard_map.246 = (bf16[5,512,768]{2,1,0:T(8,128)(2,1)}, bf16[5,512,768]{2,1,0:T(8,128)(2,1)}, bf16[5,512,3072]{2,1,0:T(8,128)(2,1)}, bf16[5,512,3072]{2,1,0:T(8,...) custom-call(s32[60]{0:T(128)S(1)} %reshape.559.sp_ref, ...), custom_call_target="tpu_custom_call", output_to_operand_aliasing={{0}: (9, {}), {1}: (10, {}), {2}: (11, {}), {3}: (12, {}), ... | custom-call | flops 10000000000 | bytes 10000000 | tf_op jit(solution)/shard_map/pallas_call | solution.py:98
  133.0 12.4 %shard_map.249 = (bf16[5,512,768]{2,1,0:T(8,128)(2,1)}, bf16[5,512,3072]{2,1,0:T(8,128)(2,1)}, bf16[5,512,768]{2,1,0:T(8,128)(2,1)}, f32[5,8,768]{2,1,0:T(8,128)...) custom-call(s32[60]{0:T(128)S(1)} %reshape.559.sp_ref, ...), custom_call_target="tpu_custom_call", output_to_operand_aliasing={{0}: (14, {}), {1}: (15, {}), {2}: (16, {}), {3}: (17, {}),... | custom-call | flops 10000000000 | bytes 10000000 | tf_op jit(solution)/shard_map/pallas_call | solution.py:98
  145.4 10.0 %shard_map.250 = (f32[5,64,768]{2,1,0:T(8,128)}, bf16[512,768]{1,0:T(8,128)(2,1)S(1)}, bf16[512,1536]{1,0:T(8,128)(2,1)S(1)}, bf16[512,1536]{1,0:T(8,128)(2,1)}) custom-call(s32[60]{0:T(128)S(1)} %reshape.559.sp_ref, bf16[5,512,768]{2,1,0:T(8,128)(2,1)} %get-tuple-element.267.refs_0_.refs_5_, ...), custom_call_target="tpu_custom_call", output_to_operand_aliasing={{0}: (11, {})} | custom-call | flops 20000000000 | bytes 20000000 | tf_op jit(solution)/shard_map/pallas_call | solution.py:98
  169.7 12.2 %shard_map.248 = (bf16[5,512,768]{2,1,0:T(8,128)(2,1)}, bf16[5,512,768]{2,1,0:T(8,128)(2,1)}, bf16[5,512,768]{2,1,0:T(8,128)(2,1)}, bf16[5,512,1536]{2,1,0:T(8,128)(2,1)}) custom-call(s32[60]{0:T(128)S(1)} %reshape.559.sp_ref, ...), custom_call_target="tpu_custom_call", output_to_operand_aliasing={{0}: (7, {}), {1}: (8, {}), {2}: (9, {}), {3}: (10, {})} | custom-call | flops 14000000000 | bytes 14000000 | tf_op jit(solution)/shard_map/pallas_call | solution.py:98
  181.9 11.0 %shard_map.252 = (bf16[5,512,768]{2,1,0:T(8,128)(2,1)}, bf16[5,512,768]{2,1,0:T(8,128)(2,1)}, bf16[5,512,3072]{2,1,0:T(8,128)(2,1)}, bf16[5,512,3072]{2,1,0:T(8,...) custom-call(s32[60]{0:T(128)S(1)} %reshape.559.sp_ref, ...), custom_call_target="tpu_custom_call", output_to_operand_aliasing={{0}: (9, {}), {1}: (10, {}), {2}: (11, {}), {3}: (12, {}), ... | custom-call | flops 10000000000 | bytes 10000000 | tf_op jit(solution)/shard_map/pallas_call | solution.py:98
  192.9 16.9 %collective-permute-start.10 = (bf16[512,768]{1,0:T(8,128)(2,1)S(1)}, bf16[512,768]{1,0:T(8,128)(2,1)S(1)}, u32[]{:S(2)}, u32[]{:S(2)}) collective-permute-start(bf16[512,768]{1,0:T(8,128)(2,1)S(1)} %get-tuple-element.434), channel_id=1, source_target_pairs={{0,16},{1,17},{2,18},{3,19},{4,20},{5,21},{6,22},{7,23},{8,24},{9,... | collective-permute-start | bytes 2359304 | tf_op jit(solution)/shard_map/ppermute | solution.py:988
  209.8 12.4 %shard_map.253 = (bf16[5,512,768]{2,1,0:T(8,128)(2,1)}, bf16[5,512,3072]{2,1,0:T(8,128)(2,1)}, bf16[5,512,768]{2,1,0:T(8,128)(2,1)}, f32[5,8,768]{2,1,0:T(8,128)...) custom-call(s32[60]{0:T(128)S(1)} %reshape.559.sp_ref, ...), custom_call_target="tpu_custom_call", output_to_operand_aliasing={{0}: (14, {}), {1}: (15, {}), {2}: (16, {}), {3}: (17, {}),... | custom-call | flops 10000000000 | bytes 10000000 | tf_op jit(solution)/shard_map/pallas_call | solution.py:98
  222.3 25.1 %shard_map.254 = (f32[5,64,768]{2,1,0:T(8,128)}, bf16[512,768]{1,0:T(8,128)(2,1)S(1)}, bf16[512,1536]{1,0:T(8,128)(2,1)S(1)}, bf16[512,1536]{1,0:T(8,128)(2,1)}) custom-call(s32[60]{0:T(128)S(1)} %reshape.559.sp_ref, bf16[5,512,768]{2,1,0:T(8,128)(2,1)} %get-tuple-element.282.refs_0_.refs_5_, ...), custom_call_target="tpu_custom_call", output_to_operand_aliasing={{0}: (11, {})} | custom-call | flops 20000000000 | bytes 20000000 | tf_op jit(solution)/shard_map/pallas_call | solution.py:98
  261.6 10.3 %shard_map.257 = (bf16[5,512,768]{2,1,0:T(8,128)(2,1)}, bf16[5,512,768]{2,1,0:T(8,128)(2,1)}, bf16[5,512,768]{2,1,0:T(8,128)(2,1)}, bf16[5,512,1536]{2,1,0:T(8,128)(2,1)}) custom-call(s32[60]{0:T(128)S(1)} %reshape.559.sp_ref, ...), custom_call_target="tpu_custom_call", output_to_operand_aliasing={{0}: (7, {}), {1}: (8, {}), {2}: (9, {}), {3}: (10, {})} | custom-call | flops 14000000000 | bytes 14000000 | tf_op jit(solution)/shard_map/pallas_call | solution.py:98
  271.9 11.0 %shard_map.258 = (bf16[5,512,768]{2,1,0:T(8,128)(2,1)}, bf16[5,512,768]{2,1,0:T(8,128)(2,1)}, bf16[5,512,3072]{2,1,0:T(8,128)(2,1)}, bf16[5,512,3072]{2,1,0:T(8,...) custom-call(s32[60]{0:T(128)S(1)} %reshape.559.sp_ref, ...), custom_call_target="tpu_custom_call", output_to_operand_aliasing={{0}: (9, {}), {1}: (10, {}), {2}: (11, {}), {3}: (12, {}), ... | custom-call | flops 10000000000 | bytes 10000000 | tf_op jit(solution)/shard_map/pallas_call | solution.py:98
  289.9 12.4 %shard_map.261 = (bf16[5,512,768]{2,1,0:T(8,128)(2,1)}, bf16[5,512,3072]{2,1,0:T(8,128)(2,1)}, bf16[5,512,768]{2,1,0:T(8,128)(2,1)}, f32[5,8,768]{2,1,0:T(8,128)...) custom-call(s32[60]{0:T(128)S(1)} %reshape.559.sp_ref, ...), custom_call_target="tpu_custom_call", output_to_operand_aliasing={{0}: (14, {}), {1}: (15, {}), {2}: (16, {}), {3}: (17, {}),... | custom-call | flops 10000000000 | bytes 10000000 | tf_op jit(solution)/shard_map/pallas_call | solution.py:98
  302.4 22.5 %shard_map.262 = (f32[5,64,768]{2,1,0:T(8,128)}, bf16[512,768]{1,0:T(8,128)(2,1)S(1)}, bf16[512,1536]{1,0:T(8,128)(2,1)S(1)}, bf16[512,1536]{1,0:T(8,128)(2,1)}) custom-call(s32[60]{0:T(128)S(1)} %reshape.559.sp_ref, bf16[5,512,768]{2,1,0:T(8,128)(2,1)} %get-tuple-element.333.refs_0_.refs_5_, ...), custom_call_target="tpu_custom_call", output_to_operand_aliasing={{0}: (11, {})} | custom-call | flops 20000000000 | bytes 20000000 | tf_op jit(solution)/shard_map/pallas_call | solution.py:98
  339.2 9.3 %shard_map.260 = (bf16[5,512,768]{2,1,0:T(8,128)(2,1)}, bf16[5,512,768]{2,1,0:T(8,128)(2,1)}, bf16[5,512,768]{2,1,0:T(8,128)(2,1)}, bf16[5,512,1536]{2,1,0:T(8,128)(2,1)}) custom-call(s32[60]{0:T(128)S(1)} %reshape.559.sp_ref, ...), custom_call_target="tpu_custom_call", output_to_operand_aliasing={{0}: (7, {}), {1}: (8, {}), {2}: (9, {}), {3}: (10, {})} | custom-call | flops 14000000000 | bytes 14000000 | tf_op jit(solution)/shard_map/pallas_call | solution.py:98
  348.5 11.0 %shard_map.264 = (bf16[5,512,768]{2,1,0:T(8,128)(2,1)}, bf16[5,512,768]{2,1,0:T(8,128)(2,1)}, bf16[5,512,3072]{2,1,0:T(8,128)(2,1)}, bf16[5,512,3072]{2,1,0:T(8,...) custom-call(s32[60]{0:T(128)S(1)} %reshape.559.sp_ref, ...), custom_call_target="tpu_custom_call", output_to_operand_aliasing={{0}: (9, {}), {1}: (10, {}), {2}: (11, {}), {3}: (12, {}), ... | custom-call | flops 10000000000 | bytes 10000000 | tf_op jit(solution)/shard_map/pallas_call | solution.py:98
  360.4 12.9 %shard_map.265 = (bf16[5,512,768]{2,1,0:T(8,128)(2,1)}, bf16[5,512,3072]{2,1,0:T(8,128)(2,1)}, bf16[5,512,768]{2,1,0:T(8,128)(2,1)}, f32[5,8,768]{2,1,0:T(8,128)...) custom-call(s32[60]{0:T(128)S(1)} %reshape.559.sp_ref, ...), custom_call_target="tpu_custom_call", output_to_operand_aliasing={{0}: (14, {}), {1}: (15, {}), {2}: (16, {}), {3}: (17, {}),... | custom-call | flops 10000000000 | bytes 10000000 | tf_op jit(solution)/shard_map/pallas_call | solution.py:98
  373.3 41.7 %shard_map.266 = (f32[5,64,768]{2,1,0:T(8,128)}, bf16[512,768]{1,0:T(8,128)(2,1)S(1)}, bf16[512,1536]{1,0:T(8,128)(2,1)S(1)}, bf16[512,1536]{1,0:T(8,128)(2,1)S(1)}) custom-call(s32[60]{0:T(128)S(1)} %reshape.559.sp_ref, bf16[5,512,768]{2,1,0:T(8,128)(2,1)} %get-tuple-element.342.refs_0_, ...), custom_call_target="tpu_custom_call", output_to_operand_aliasing={{0}: (11, {})} | custom-call | flops 20000000000 | bytes 20000000 | tf_op jit(solution)/shard_map/pallas_call | solution.py:98
  428.3 11.5 %shard_map.268 = (bf16[384,3072]{1,0:T(8,128)(2,1)S(1)}, bf16[384,3072]{1,0:T(8,128)(2,1)S(1)}) custom-call(s32[60]{0:T(128)S(1)} %reshape.559.sp_ref, bf16[5,512,768]{2,1,0:T(8,128)(2,1)} %get-tuple-element.392.refs_0_.refs_13_, bf16[5,512,3072]{2,1,0:T(8,128)(2,1)} %get-tuple-element.393.refs_1_), custom_call_target="tpu_custom_call" | custom-call | flops 14000000000 | bytes 14000000 | tf_op jit(solution)/shard_map/pallas_call | solution.py:98
  439.9 11.8 %shard_map.269 = (bf16[384,3072]{1,0:T(8,128)(2,1)S(1)}, bf16[384,3072]{1,0:T(8,128)(2,1)S(1)}) custom-call(s32[60]{0:T(128)S(1)} %reshape.559.sp_ref, bf16[5,512,768]{2,1,0:T(8,128)(2,1)} %get-tuple-element.406.refs_0_, bf16[5,512,3072]{2,1,0:T(8,128)(2,1)} %get-tuple-element.396.refs_1_.refs_14_), custom_call_target="tpu_custom_call" | custom-call | flops 14000000000 | bytes 14000000 | tf_op jit(solution)/shard_map/pallas_call | solution.py:98
  453.1 12.7 %shard_map.270 = (bf16[5,512,768]{2,1,0:T(8,128)(2,1)}, bf16[5,512,3072]{2,1,0:T(8,128)(2,1)}, bf16[5,512,768]{2,1,0:T(8,128)(2,1)}, f32[5,8,768]{2,1,0:T(8,128)...) custom-call(s32[60]{0:T(128)S(1)} %reshape.559.sp_ref, ...), custom_call_target="tpu_custom_call", output_to_operand_aliasing={{0}: (14, {}), {1}: (15, {}), {2}: (16, {}), {3}: (17, {}),... | custom-call | flops 10000000000 | bytes 10000000 | tf_op jit(solution)/shard_map/pallas_call | solution.py:98
  493.3 37.1 %shard_map.273 = (f32[5,64,768]{2,1,0:T(8,128)}, bf16[512,768]{1,0:T(8,128)(2,1)S(1)}, bf16[512,1536]{1,0:T(8,128)(2,1)S(1)}, bf16[512,1536]{1,0:T(8,128)(2,1)}) custom-call(s32[60]{0:T(128)S(1)} %reshape.559.sp_ref, bf16[5,512,768]{2,1,0:T(8,128)(2,1)} %get-tuple-element.342.refs_0_, ...), custom_call_target="tpu_custom_call", output_to_operand_aliasing={{0}: (11, {})} | custom-call | flops 20000000000 | bytes 20000000 | tf_op jit(solution)/shard_map/pallas_call | solution.py:98
  539.6 13.3 %collective-permute-start.25 = (bf16[96,3072]{1,0:T(8,128)(2,1)}, bf16[96,3072]{1,0:T(8,128)(2,1)}, u32[]{:S(2)}, u32[]{:S(2)}) collective-permute-start(bf16[96,3072]{1,0:T(8,128)(2,1)} %constant_dynamic-slice_fusion.10), channel_id=1, source_target_pairs={{0,4},{1,5},{2,6},{3,7},{4,0},{5,1},{6,2},{7,3},{8,12},{9,13},{10,... | collective-permute-start | bytes 1769480 | tf_op jit(solution)/shard_map/ppermute | solution.py:785
  559.1 17.0 %shard_map.275 = (bf16[384,3072]{1,0:T(8,128)(2,1)}, bf16[384,3072]{1,0:T(8,128)(2,1)S(1)}) custom-call(s32[60]{0:T(128)S(1)} %reshape.559.sp_ref, bf16[5,512,768]{2,1,0:T(8,128)(2,1)} %get-tuple-element.341.refs_1_.refs_0_, bf16[5,512,768]{2,1,0:T(8,128)(2,1)} %get-tuple-element.347.refs_0_.refs_11_.refs_1_, ...), custom_call_target="tpu_custom_call" | custom-call | flops 16999999488 | bytes 17000000 | tf_op jit(solution)/shard_map/pallas_call | solution.py:98
  628.6 11.4 %collective-permute-done.33 = bf16[96,3072]{1,0:T(8,128)(2,1)} collective-permute-done((bf16[96,3072]{1,0:T(8,128)(2,1)}, bf16[96,3072]{1,0:T(8,128)(2,1)}, u32[]{:S(2)}, u32[]{:S(2)}) %collective-permute-start.33) | collective-permute-done | bytes 589856 | tf_op jit(solution)/shard_map/ppermute | solution.py:785
  649.5 18.7 %collective-permute-done.37 = bf16[48,3072]{1,0:T(8,128)(2,1)S(1)} collective-permute-done((bf16[48,3072]{1,0:T(8,128)(2,1)S(1)}, bf16[48,3072]{1,0:T(8,128)(2,1)S(1)}, u32[]{:S(2)}, u32[]{:S(2)}) %collective-permute-start.37) | collective-permute-done | bytes 294944 | tf_op jit(solution)/shard_map/ppermute | solution.py:785
  669.6 11.2 %collective-permute-done.35 = bf16[48,3072]{1,0:T(8,128)(2,1)S(1)} collective-permute-done((bf16[48,3072]{1,0:T(8,128)(2,1)S(1)}, bf16[48,3072]{1,0:T(8,128)(2,1)S(1)}, u32[]{:S(2)}, u32[]{:S(2)}) %collective-permute-start.35) | collective-permute-done | bytes 294944 | tf_op jit(solution)/shard_map/ppermute | solution.py:785
  687.8 8.1 %collective-permute-done.40 = bf16[192,3072]{1,0:T(8,128)(2,1)S(1)} collective-permute-done((bf16[192,3072]{1,0:T(8,128)(2,1)S(1)}, bf16[192,3072]{1,0:T(8,128)(2,1)S(1)}, u32[]{:S(2)}, u32[]{:S(2)}) %collective-permute-start.40) | collective-permute-done | bytes 1179680 | tf_op jit(solution)/shard_map/ppermute | solution.py:785
  713.8 16.2 %collective-permute-done.43 = bf16[192,3072]{1,0:T(8,128)(2,1)} collective-permute-done((bf16[192,3072]{1,0:T(8,128)(2,1)}, bf16[192,3072]{1,0:T(8,128)(2,1)}, u32[]{:S(2)}, u32[]{:S(2)}) %collective-permute-start.43) | collective-permute-done | bytes 1179680 | tf_op jit(solution)/shard_map/ppermute | solution.py:785
  754.6 8.6 %shard_map.277 = (f32[768,2304]{1,0:T(8,128)}, f32[768,768]{1,0:T(8,128)}) custom-call(s32[60]{0:T(128)S(1)} %reshape.559.sp_ref, bf16[384,3072]{1,0:T(8,128)(2,1)} %pad_maximum_fusion.5.refs_0_, bf16[384,3072]{1,0:T(8,128)(2,1)} %collective-permute-done.47.refs_1_), custom_call_target="tpu_custom_call" | custom-call | flops 5000000000 | bytes 5000000 | tf_op jit(solution)/shard_map/pallas_call | solution.py:98
  (483 shorter events, 284.9 us)
Async XLA Ops:
  2.7 22.1 %collective-permute-start = (s32[2,2176]{1,0:T(2,128)}, s32[2,2176]{1,0:T(2,128)}, u32[]{:S(2)}, u32[]{:S(2)}) collective-permute-start(s32[2,2176]{1,0:T(2,128)} %pad_add_fusion), channel_id=1, source_target_pairs={{0,1},{1,0},{2,3},{3,2},{4,5},{5,4},{6,7},{7,6},{8,9},{9,8},{10,11... | collective-permute-start | bytes 52232 | tf_op jit(solution)/shard_map/ppermute | solution.py:849
  6.4 24.9 %collective-permute-start.1 = (bf16[2,512,768]{2,1,0:T(8,128)(2,1)}, bf16[2,512,768]{2,1,0:T(8,128)(2,1)}, u32[]{:S(2)}, u32[]{:S(2)}) collective-permute-start(bf16[2,512,768]{2,1,0:T(8,128)(2,1)} %select_bitcast_fusion.2), channel_id=1, source_target_pairs={{0,1},{1,0},{2,3},{3,2},{4,5},{5,4},{6,7},{7,6},{8,9},{9,8},{10,11... | collective-permute-start | bytes 4718600 | tf_op jit(solution)/shard_map/ppermute | solution.py:849
  74.8 18.6 %collective-permute-start.3 = (bf16[512,768]{1,0:T(8,128)(2,1)S(1)}, bf16[512,768]{1,0:T(8,128)(2,1)S(1)}, u32[]{:S(2)}, u32[]{:S(2)}) collective-permute-start(bf16[512,768]{1,0:T(8,128)(2,1)S(1)} %get-tuple-element.265), channel_id=1, source_target_pairs={{0,16},{1,17},{2,18},{3,19},{4,20},{5,21},{6,22},{7,23},{8,24},{9,... | collective-permute-start | bytes 2359304 | tf_op jit(solution)/shard_map/ppermute | solution.py:988
  125.2 31.1 %collective-permute-start.5 = (bf16[512,768]{1,0:T(8,128)(2,1)S(1)}, bf16[512,768]{1,0:T(8,128)(2,1)S(1)}, u32[]{:S(2)}, u32[]{:S(2)}) collective-permute-start(bf16[512,768]{1,0:T(8,128)(2,1)S(1)} %get-tuple-element.432), channel_id=1, source_target_pairs={{0,16},{1,17},{2,18},{3,19},{4,20},{5,21},{6,22},{7,23},{8,24},{9,... | collective-permute-start | bytes 2359304 | tf_op jit(solution)/shard_map/ppermute | solution.py:988
  168.4 41.4 %collective-permute-start.8 = (bf16[512,768]{1,0:T(8,128)(2,1)S(1)}, bf16[512,768]{1,0:T(8,128)(2,1)S(1)}, u32[]{:S(2)}, u32[]{:S(2)}) collective-permute-start(bf16[512,768]{1,0:T(8,128)(2,1)S(1)} %get-tuple-element.308), channel_id=1, source_target_pairs={{16,0},{17,1},{18,2},{19,3},{20,4},{21,5},{22,6},{23,7},{24,8},{25... | collective-permute-start | bytes 2359304 | tf_op jit(solution)/shard_map/ppermute | solution.py:995
  192.9 55.6 %collective-permute-start.10 = (bf16[512,768]{1,0:T(8,128)(2,1)S(1)}, bf16[512,768]{1,0:T(8,128)(2,1)S(1)}, u32[]{:S(2)}, u32[]{:S(2)}) collective-permute-start(bf16[512,768]{1,0:T(8,128)(2,1)S(1)} %get-tuple-element.434), channel_id=1, source_target_pairs={{0,16},{1,17},{2,18},{3,19},{4,20},{5,21},{6,22},{7,23},{8,24},{9,... | collective-permute-start | bytes 2359304 | tf_op jit(solution)/shard_map/ppermute | solution.py:988
  260.3 29.6 %collective-permute-start.14 = (bf16[512,768]{1,0:T(8,128)(2,1)S(1)}, bf16[512,768]{1,0:T(8,128)(2,1)S(1)}, u32[]{:S(2)}, u32[]{:S(2)}) collective-permute-start(bf16[512,768]{1,0:T(8,128)(2,1)S(1)} %get-tuple-element.431), channel_id=1, source_target_pairs={{16,0},{17,1},{18,2},{19,3},{20,4},{21,5},{22,6},{23,7},{24,8},{25... | collective-permute-start | bytes 2359304 | tf_op jit(solution)/shard_map/ppermute | solution.py:995
  282.9 43.1 %collective-permute-start.12 = (bf16[512,768]{1,0:T(8,128)(2,1)S(1)}, bf16[512,768]{1,0:T(8,128)(2,1)S(1)}, u32[]{:S(2)}, u32[]{:S(2)}) collective-permute-start(bf16[512,768]{1,0:T(8,128)(2,1)S(1)} %get-tuple-element.436), channel_id=1, source_target_pairs={{0,16},{1,17},{2,18},{3,19},{4,20},{5,21},{6,22},{7,23},{8,24},{9,... | collective-permute-start | bytes 2359304 | tf_op jit(solution)/shard_map/ppermute | solution.py:988
  337.9 22.5 %collective-permute-start.16 = (bf16[512,768]{1,0:T(8,128)(2,1)S(1)}, bf16[512,768]{1,0:T(8,128)(2,1)S(1)}, u32[]{:S(2)}, u32[]{:S(2)}) collective-permute-start(bf16[512,768]{1,0:T(8,128)(2,1)S(1)} %get-tuple-element.433), channel_id=1, source_target_pairs={{16,0},{17,1},{18,2},{19,3},{20,4},{21,5},{22,6},{23,7},{24,8},{25... | collective-permute-start | bytes 2359304 | tf_op jit(solution)/shard_map/ppermute | solution.py:995
  427.0 26.1 %collective-permute-start.18 = (bf16[512,768]{1,0:T(8,128)(2,1)S(1)}, bf16[512,768]{1,0:T(8,128)(2,1)S(1)}, u32[]{:S(2)}, u32[]{:S(2)}) collective-permute-start(bf16[512,768]{1,0:T(8,128)(2,1)S(1)} %get-tuple-element.435), channel_id=1, source_target_pairs={{16,0},{17,1},{18,2},{19,3},{20,4},{21,5},{22,6},{23,7},{24,8},{25... | collective-permute-start | bytes 2359304 | tf_op jit(solution)/shard_map/ppermute | solution.py:995
  487.9 43.8 %collective-permute-start.22 = (bf16[384,3072]{1,0:T(8,128)(2,1)}, bf16[384,3072]{1,0:T(8,128)(2,1)}, u32[]{:S(2)}, u32[]{:S(2)}) collective-permute-start(bf16[384,3072]{1,0:T(8,128)(2,1)} %get-tuple-element.409), channel_id=1, source_target_pairs={{0,1},{1,0},{2,3},{3,2},{4,5},{5,4},{6,7},{7,6},{8,9},{9,8},{10,11... | collective-permute-start | bytes 7077896 | tf_op jit(solution)/shard_map/ppermute | solution.py:788
  491.9 44.1 %collective-permute-start.21 = (bf16[192,3072]{1,0:T(8,128)(2,1)}, bf16[192,3072]{1,0:T(8,128)(2,1)}, u32[]{:S(2)}, u32[]{:S(2)}) collective-permute-start(bf16[192,3072]{1,0:T(8,128)(2,1)} %constant_dynamic-slice_fusion.12), channel_id=1, source_target_pairs={{0,2},{1,3},{2,0},{3,1},{4,6},{5,7},{6,4},{7,5},{8,10},{9,11},{10,... | collective-permute-start | bytes 3538952 | tf_op jit(solution)/shard_map/ppermute | solution.py:785
  531.6 21.3 %collective-permute-start.20 = (bf16[512,1536]{1,0:T(8,128)(2,1)}, bf16[512,1536]{1,0:T(8,128)(2,1)}, u32[]{:S(2)}, u32[]{:S(2)}) collective-permute-start(bf16[512,1536]{1,0:T(8,128)(2,1)} %get-tuple-element.417), channel_id=1, source_target_pairs={{0,1},{1,0},{2,3},{3,2},{4,5},{5,4},{6,7},{7,6},{8,9},{9,8},{10,11... | collective-permute-start | bytes 4718600 | tf_op jit(solution)/shard_map/ppermute | solution.py:849
  535.5 41.9 %collective-permute-start.24 = (bf16[192,3072]{1,0:T(8,128)(2,1)}, bf16[192,3072]{1,0:T(8,128)(2,1)}, u32[]{:S(2)}, u32[]{:S(2)}) collective-permute-start(bf16[192,3072]{1,0:T(8,128)(2,1)} %constant_dynamic-slice_fusion.11), channel_id=1, source_target_pairs={{0,2},{1,3},{2,0},{3,1},{4,6},{5,7},{6,4},{7,5},{8,10},{9,11},{10,... | collective-permute-start | bytes 3538952 | tf_op jit(solution)/shard_map/ppermute | solution.py:785
  539.6 36.6 %collective-permute-start.25 = (bf16[96,3072]{1,0:T(8,128)(2,1)}, bf16[96,3072]{1,0:T(8,128)(2,1)}, u32[]{:S(2)}, u32[]{:S(2)}) collective-permute-start(bf16[96,3072]{1,0:T(8,128)(2,1)} %constant_dynamic-slice_fusion.10), channel_id=1, source_target_pairs={{0,4},{1,5},{2,6},{3,7},{4,0},{5,1},{6,2},{7,3},{8,12},{9,13},{10,... | collective-permute-start | bytes 1769480 | tf_op jit(solution)/shard_map/ppermute | solution.py:785
  580.6 35.9 %collective-permute-start.27 = (bf16[96,3072]{1,0:T(8,128)(2,1)}, bf16[96,3072]{1,0:T(8,128)(2,1)}, u32[]{:S(2)}, u32[]{:S(2)}) collective-permute-start(bf16[96,3072]{1,0:T(8,128)(2,1)} %constant_dynamic-slice_fusion.5), channel_id=1, source_target_pairs={{0,4},{1,5},{2,6},{3,7},{4,0},{5,1},{6,2},{7,3},{8,12},{9,13},{10,... | collective-permute-start | bytes 1769480 | tf_op jit(solution)/shard_map/ppermute | solution.py:785
  581.4 32.7 %collective-permute-start.28 = (bf16[48,3072]{1,0:T(8,128)(2,1)}, bf16[48,3072]{1,0:T(8,128)(2,1)}, u32[]{:S(2)}, u32[]{:S(2)}) collective-permute-start(bf16[48,3072]{1,0:T(8,128)(2,1)} %constant_dynamic-slice_fusion.4), channel_id=1, source_target_pairs={{0,8},{1,9},{2,10},{3,11},{4,12},{5,13},{6,14},{7,15},{8,0},{9,1},... | collective-permute-start | bytes 884744 | tf_op jit(solution)/shard_map/ppermute | solution.py:785
  615.8 25.4 %collective-permute-start.32 = (bf16[48,3072]{1,0:T(8,128)(2,1)}, bf16[48,3072]{1,0:T(8,128)(2,1)}, u32[]{:S(2)}, u32[]{:S(2)}) collective-permute-start(bf16[48,3072]{1,0:T(8,128)(2,1)} %dynamic-slice_add_fusion.8), channel_id=1, source_target_pairs={{0,8},{1,9},{2,10},{3,11},{4,12},{5,13},{6,14},{7,15},{8,0},{9,1},... | collective-permute-start | bytes 884744 | tf_op jit(solution)/shard_map/ppermute | solution.py:785
  625.0 23.3 %collective-permute-start.30 = (f32[88,128]{1,0:T(8,128)S(1)}, f32[88,128]{1,0:T(8,128)S(1)}, u32[]{:S(2)}, u32[]{:S(2)}) collective-permute-start(f32[88,128]{1,0:T(8,128)S(1)} %pad_bitcast_fusion), channel_id=1, source_target_pairs={{0,1},{1,0},{2,3},{3,2},{4,5},{5,4},{6,7},{7,6},{8,9},{9,8},{10,11... | collective-permute-start | bytes 135176 | tf_op jit(solution)/shard_map/ppermute | solution.py:820
  626.1 19.2 %collective-permute-start.31 = (bf16[48,3072]{1,0:T(8,128)(2,1)S(1)}, bf16[48,3072]{1,0:T(8,128)(2,1)S(1)}, u32[]{:S(2)}, u32[]{:S(2)}) collective-permute-start(bf16[48,3072]{1,0:T(8,128)(2,1)S(1)} %constant_dynamic-slice_fusion.2), channel_id=1, source_target_pairs={{0,8},{1,9},{2,10},{3,11},{4,12},{5,13},{6,14},{7,15},{8,0},{9,1},... | collective-permute-start | bytes 884744 | tf_op jit(solution)/shard_map/ppermute | solution.py:785
  642.4 26.0 %collective-permute-start.36 = (bf16[96,3072]{1,0:T(8,128)(2,1)S(1)}, bf16[96,3072]{1,0:T(8,128)(2,1)S(1)}, u32[]{:S(2)}, u32[]{:S(2)}) collective-permute-start(bf16[96,3072]{1,0:T(8,128)(2,1)S(1)} %pad_maximum_fusion.11), channel_id=1, source_target_pairs={{0,4},{1,5},{2,6},{3,7},{4,0},{5,1},{6,2},{7,3},{8,12},{9,13},{10,... | collective-permute-start | bytes 1769480 | tf_op jit(solution)/shard_map/ppermute | solution.py:785
  645.3 22.9 %collective-permute-start.37 = (bf16[48,3072]{1,0:T(8,128)(2,1)S(1)}, bf16[48,3072]{1,0:T(8,128)(2,1)S(1)}, u32[]{:S(2)}, u32[]{:S(2)}) collective-permute-start(bf16[48,3072]{1,0:T(8,128)(2,1)S(1)} %constant_dynamic-slice_fusion), channel_id=1, source_target_pairs={{0,8},{1,9},{2,10},{3,11},{4,12},{5,13},{6,14},{7,15},{8,0},{9,1},... | collective-permute-start | bytes 884744 | tf_op jit(solution)/shard_map/ppermute | solution.py:785
  645.3 35.5 %collective-permute-start.35 = (bf16[48,3072]{1,0:T(8,128)(2,1)S(1)}, bf16[48,3072]{1,0:T(8,128)(2,1)S(1)}, u32[]{:S(2)}, u32[]{:S(2)}) collective-permute-start(bf16[48,3072]{1,0:T(8,128)(2,1)S(1)} %dynamic-slice_add_fusion.7), channel_id=1, source_target_pairs={{0,8},{1,9},{2,10},{3,11},{4,12},{5,13},{6,14},{7,15},{8,0},{9,1},... | collective-permute-start | bytes 884744 | tf_op jit(solution)/shard_map/ppermute | solution.py:785
  648.4 32.7 %collective-permute-start.34 = (f32[88,128]{1,0:T(8,128)S(1)}, f32[88,128]{1,0:T(8,128)S(1)}, u32[]{:S(2)}, u32[]{:S(2)}) collective-permute-start(f32[88,128]{1,0:T(8,128)S(1)} %fusion.36), channel_id=1, source_target_pairs={{0,2},{1,3},{2,0},{3,1},{4,6},{5,7},{6,4},{7,5},{8,10},{9,11},{10,... | collective-permute-start | bytes 135176 | tf_op jit(solution)/shard_map/ppermute | solution.py:820
  668.3 18.6 %collective-permute-start.41 = (bf16[48,3072]{1,0:T(8,128)(2,1)S(1)}, bf16[48,3072]{1,0:T(8,128)(2,1)S(1)}, u32[]{:S(2)}, u32[]{:S(2)}) collective-permute-start(bf16[48,3072]{1,0:T(8,128)(2,1)S(1)} %dynamic-slice_add_fusion.6), channel_id=1, source_target_pairs={{0,8},{1,9},{2,10},{3,11},{4,12},{5,13},{6,14},{7,15},{8,0},{9,1},... | collective-permute-start | bytes 884744 | tf_op jit(solution)/shard_map/ppermute | solution.py:785
  668.7 27.2 %collective-permute-start.40 = (bf16[192,3072]{1,0:T(8,128)(2,1)S(1)}, bf16[192,3072]{1,0:T(8,128)(2,1)S(1)}, u32[]{:S(2)}, u32[]{:S(2)}) collective-permute-start(bf16[192,3072]{1,0:T(8,128)(2,1)S(1)} %pad_maximum_fusion.8), channel_id=1, source_target_pairs={{0,2},{1,3},{2,0},{3,1},{4,6},{5,7},{6,4},{7,5},{8,10},{9,11},{10,... | collective-permute-start | bytes 3538952 | tf_op jit(solution)/shard_map/ppermute | solution.py:785
  680.9 18.4 %collective-permute-start.39 = (bf16[96,3072]{1,0:T(8,128)(2,1)S(1)}, bf16[96,3072]{1,0:T(8,128)(2,1)S(1)}, u32[]{:S(2)}, u32[]{:S(2)}) collective-permute-start(bf16[96,3072]{1,0:T(8,128)(2,1)S(1)} %pad_maximum_fusion.12), channel_id=1, source_target_pairs={{0,4},{1,5},{2,6},{3,7},{4,0},{5,1},{6,2},{7,3},{8,12},{9,13},{10,... | collective-permute-start | bytes 1769480 | tf_op jit(solution)/shard_map/ppermute | solution.py:785
  700.8 29.2 %collective-permute-start.43 = (bf16[192,3072]{1,0:T(8,128)(2,1)}, bf16[192,3072]{1,0:T(8,128)(2,1)}, u32[]{:S(2)}, u32[]{:S(2)}) collective-permute-start(bf16[192,3072]{1,0:T(8,128)(2,1)} %pad_maximum_fusion.9), channel_id=1, source_target_pairs={{0,2},{1,3},{2,0},{3,1},{4,6},{5,7},{6,4},{7,5},{8,10},{9,11},{10,... | collective-permute-start | bytes 3538952 | tf_op jit(solution)/shard_map/ppermute | solution.py:785
  701.7 41.7 %collective-permute-start.26 = (bf16[2,512,768]{2,1,0:T(8,128)(2,1)}, bf16[2,512,768]{2,1,0:T(8,128)(2,1)S(1)}, u32[]{:S(2)}, u32[]{:S(2)}) collective-permute-start(bf16[2,512,768]{2,1,0:T(8,128)(2,1)} %broadcast_select_fusion.1), channel_id=1, source_target_pairs={{0,1},{1,0},{2,3},{3,2},{4,5},{5,4},{6,7},{7,6},{8,9},{9,8},{10,11... | collective-permute-start | bytes 4718600 | tf_op jit(solution)/shard_map/ppermute | solution.py:849
  708.6 34.8 %collective-permute-start.42 = (f32[88,128]{1,0:T(8,128)S(1)}, f32[88,128]{1,0:T(8,128)S(1)}, u32[]{:S(2)}, u32[]{:S(2)}) collective-permute-start(f32[88,128]{1,0:T(8,128)S(1)} %add.313), channel_id=1, source_target_pairs={{0,8},{1,9},{2,10},{3,11},{4,12},{5,13},{6,14},{7,15},{8,0},{9,1},... | collective-permute-start | bytes 135176 | tf_op jit(solution)/shard_map/ppermute | solution.py:820
  712.8 33.3 %collective-permute-start.46 = (bf16[192,3072]{1,0:T(8,128)(2,1)S(1)}, bf16[192,3072]{1,0:T(8,128)(2,1)S(1)}, u32[]{:S(2)}, u32[]{:S(2)}) collective-permute-start(bf16[192,3072]{1,0:T(8,128)(2,1)S(1)} %pad_maximum_fusion.10), channel_id=1, source_target_pairs={{0,2},{1,5},{2,0},{3,7},{4,6},{5,1},{6,4},{7,3},{8,10},{9,13},{10,... | collective-permute-start | bytes 3538952 | tf_op jit(solution)/shard_map/ppermute | solution.py:785
  732.1 22.5 %collective-permute-start.48 = (bf16[384,3072]{1,0:T(8,128)(2,1)S(1)}, bf16[384,3072]{1,0:T(8,128)(2,1)}, u32[]{:S(2)}, u32[]{:S(2)}) collective-permute-start(bf16[384,3072]{1,0:T(8,128)(2,1)S(1)} %pad_maximum_fusion.4.refs_0_), channel_id=1, source_target_pairs={{0,1},{1,0},{2,3},{3,2},{4,5},{5,4},{6,7},{7,6},{8,9},{9,8},{10,11... | collective-permute-start | bytes 7077896 | tf_op jit(solution)/shard_map/ppermute | solution.py:788
  (131 other events, 1083.6 us)

commit v9 on v6

--- a/solution.py
+++ b/solution.py
@@ -1026,10 +1026,10 @@
     cell, dq, keep, send = attend_back_kernel(sp, st, grads)
     got = exchange(send)
     done = expand.advance(dq)
-    done = contract.advance(done)
     got = after(got, done)
     st, grads_in[SLOTS[-1][1]] = input_back(sp, dict(st, cell=cell), dq, keep, got)
-    halves = weight_call(sp, 0, windows, [(st["x"], st["dj"]), (st["a"], st["db1"])])
+    done = contract.advance(st["dj"])
+    halves = weight_call(sp, 0, windows, [(after(st["x"], done), st["dj"]), (st["a"], st["db1"])])
     given, attend = weight_sum(ring.mixed, *halves)
     done = contract.advance(given)
     done = expand.advance(done)

time: 722 us -> 740 us (1.025)
  starting transfers between devices: 54.6 us -> 101 us
  Pallas kernels: 411 us -> 381 us
    ppermute x18, starting transfers between devices: 11.6 us -> 57.3 us  [send(): return lax.ppermute(a, 'dp', pairs)]
    pallas_call x38, Pallas kernels: 406 us -> 376 us  [call(): pl.pallas_call(run, grid_spec=pltpu.PrefetchScalarGridSpec(num_scalar_pre...]
    ppermute x18, waiting for transfers between devices: 89.3 us -> 97 us  [send(): return lax.ppermute(a, 'dp', pairs)]
    unnamed x231 -> x221, local copies, waits for them, and re-layouts: 28.7 us -> 26.1 us
  transfers between devices with their start and end apart: 49 -> 49, of which waited for: 14 -> 15; matrix products, arithmetic and copies ran while one was open for 11% -> 11% of each run, Pallas kernels for 38% -> 35%
where the time goes in v9:
time: 740 us; the launch traced here: 733 us
  Pallas kernels  381 us (51%)
  waiting for transfers between devices  129 us (17%)
  starting transfers between devices  101 us (14%)
  other arithmetic  59.3 us (8%)
  local copies, waits for them, and re-layouts  50.1 us (7%)
  between operations  10.7 us (1%)
    pallas_call x38, Pallas kernels, call(): pl.pallas_call(run, grid_spec=pltpu.PrefetchScalarGridSpec(num_scalar_pre...  376 us
    ppermute x18, waiting for transfers between devices, send(): return lax.ppermute(a, 'dp', pairs)  97 us
    ppermute x18, starting transfers between devices, send(): return lax.ppermute(a, 'dp', pairs)  57.3 us
    unnamed x221, local copies, waits for them, and re-layouts  26.1 us
    ppermute x4, starting transfers between devices, on_device(): got['F', zero] = lax.ppermute(out, 'section', [(0, 1)])  22.4 us
    add x12, other arithmetic, stages(): part = keep + order(got)  19.8 us
    ppermute x4, waiting for transfers between devices, on_device(): got['F', zero] = lax.ppermute(out, 'section', [(0, 1)])  17.2 us
  transfers between devices with their start and end apart: 49, of which 15 were waited for; matrix products, arithmetic and copies ran while one was open for 11% of the time, Pallas kernels for 35%

profile of v9, /device:TPU:0, one launch (start us, length us, event | category | flops | bytes accessed | tf_op | source)
XLA Modules:
  0.0 733.3 jit_solution(2802510780501890891)
XLA Ops:
  47.9 12.6 %shard_map.242 = (bf16[5,512,768]{2,1,0:T(8,128)(2,1)}, bf16[5,512,768]{2,1,0:T(8,128)(2,1)}, bf16[5,512,768]{2,1,0:T(8,128)(2,1)}, bf16[5,512,1536]{2,1,0:T(8,128)(2,1)}) custom-call(s32[60]{0:T(128)S(1)} %reshape.556.sp_ref, ...), custom_call_target="tpu_custom_call", output_to_operand_aliasing={{0}: (7, {}), {1}: (8, {}), {2}: (9, {}), {3}: (10, {})} | custom-call | flops 14000000000 | bytes 14000000 | tf_op jit(solution)/shard_map/pallas_call | solution.py:96
  60.6 11.3 %shard_map.243 = (bf16[5,512,768]{2,1,0:T(8,128)(2,1)}, bf16[5,512,768]{2,1,0:T(8,128)(2,1)}, bf16[5,512,3072]{2,1,0:T(8,128)(2,1)}, bf16[5,512,3072]{2,1,0:T(8,...) custom-call(s32[60]{0:T(128)S(1)} %reshape.556.sp_ref, ...), custom_call_target="tpu_custom_call", output_to_operand_aliasing={{0}: (9, {}), {1}: (10, {}), {2}: (11, {}), {3}: (12, {}), ... | custom-call | flops 10000000000 | bytes 10000000 | tf_op jit(solution)/shard_map/pallas_call | solution.py:96
  73.2 17.2 %collective-permute-done.3.refs_1_ = bf16[512,768]{1,0:T(8,128)(2,1)S(1)} collective-permute-done((bf16[512,768]{1,0:T(8,128)(2,1)S(1)}, bf16[512,768]{1,0:T(8,128)(2,1)S(1)}, u32[]{:S(2)}, u32[]{:S(2)}) %collective-permute-start.3) | collective-permute-done | bytes 786464 | tf_op jit(solution)/shard_map/ppermute | solution.py:984
  99.6 11.8 %shard_map.245 = (bf16[5,512,768]{2,1,0:T(8,128)(2,1)}, bf16[5,512,768]{2,1,0:T(8,128)(2,1)}, bf16[5,512,768]{2,1,0:T(8,128)(2,1)}, bf16[5,512,1536]{2,1,0:T(8,128)(2,1)}) custom-call(s32[60]{0:T(128)S(1)} %reshape.556.sp_ref, ...), custom_call_target="tpu_custom_call", output_to_operand_aliasing={{0}: (7, {}), {1}: (8, {}), {2}: (9, {}), {3}: (10, {})} | custom-call | flops 14000000000 | bytes 14000000 | tf_op jit(solution)/shard_map/pallas_call | solution.py:96
  111.4 11.0 %shard_map.246 = (bf16[5,512,768]{2,1,0:T(8,128)(2,1)}, bf16[5,512,768]{2,1,0:T(8,128)(2,1)}, bf16[5,512,3072]{2,1,0:T(8,128)(2,1)}, bf16[5,512,3072]{2,1,0:T(8,...) custom-call(s32[60]{0:T(128)S(1)} %reshape.556.sp_ref, ...), custom_call_target="tpu_custom_call", output_to_operand_aliasing={{0}: (9, {}), {1}: (10, {}), {2}: (11, {}), {3}: (12, {}), ... | custom-call | flops 10000000000 | bytes 10000000 | tf_op jit(solution)/shard_map/pallas_call | solution.py:96
  126.9 12.4 %shard_map.249 = (bf16[5,512,768]{2,1,0:T(8,128)(2,1)}, bf16[5,512,3072]{2,1,0:T(8,128)(2,1)}, bf16[5,512,768]{2,1,0:T(8,128)(2,1)}, f32[5,8,768]{2,1,0:T(8,128)...) custom-call(s32[60]{0:T(128)S(1)} %reshape.556.sp_ref, ...), custom_call_target="tpu_custom_call", output_to_operand_aliasing={{0}: (14, {}), {1}: (15, {}), {2}: (16, {}), {3}: (17, {}),... | custom-call | flops 10000000000 | bytes 10000000 | tf_op jit(solution)/shard_map/pallas_call | solution.py:96
  139.3 9.5 %shard_map.250 = (f32[5,64,768]{2,1,0:T(8,128)}, bf16[512,768]{1,0:T(8,128)(2,1)S(1)}, bf16[512,1536]{1,0:T(8,128)(2,1)S(1)}, bf16[512,1536]{1,0:T(8,128)(2,1)}) custom-call(s32[60]{0:T(128)S(1)} %reshape.556.sp_ref, bf16[5,512,768]{2,1,0:T(8,128)(2,1)} %get-tuple-element.268.refs_0_.refs_5_, ...), custom_call_target="tpu_custom_call", output_to_operand_aliasing={{0}: (11, {})} | custom-call | flops 20000000000 | bytes 20000000 | tf_op jit(solution)/shard_map/pallas_call | solution.py:96
  163.2 9.8 %shard_map.248 = (bf16[5,512,768]{2,1,0:T(8,128)(2,1)}, bf16[5,512,768]{2,1,0:T(8,128)(2,1)}, bf16[5,512,768]{2,1,0:T(8,128)(2,1)}, bf16[5,512,1536]{2,1,0:T(8,128)(2,1)}) custom-call(s32[60]{0:T(128)S(1)} %reshape.556.sp_ref, ...), custom_call_target="tpu_custom_call", output_to_operand_aliasing={{0}: (7, {}), {1}: (8, {}), {2}: (9, {}), {3}: (10, {})} | custom-call | flops 14000000000 | bytes 14000000 | tf_op jit(solution)/shard_map/pallas_call | solution.py:96
  173.1 11.0 %shard_map.252 = (bf16[5,512,768]{2,1,0:T(8,128)(2,1)}, bf16[5,512,768]{2,1,0:T(8,128)(2,1)}, bf16[5,512,3072]{2,1,0:T(8,128)(2,1)}, bf16[5,512,3072]{2,1,0:T(8,...) custom-call(s32[60]{0:T(128)S(1)} %reshape.556.sp_ref, ...), custom_call_target="tpu_custom_call", output_to_operand_aliasing={{0}: (9, {}), {1}: (10, {}), {2}: (11, {}), {3}: (12, {}), ... | custom-call | flops 10000000000 | bytes 10000000 | tf_op jit(solution)/shard_map/pallas_call | solution.py:96
  184.1 12.0 %collective-permute-start.10 = (bf16[512,768]{1,0:T(8,128)(2,1)S(1)}, bf16[512,768]{1,0:T(8,128)(2,1)S(1)}, u32[]{:S(2)}, u32[]{:S(2)}) collective-permute-start(bf16[512,768]{1,0:T(8,128)(2,1)S(1)} %get-tuple-element.436), channel_id=1, source_target_pairs={{0,16},{1,17},{2,18},{3,19},{4,20},{5,21},{6,22},{7,23},{8,24},{9,... | collective-permute-start | bytes 2359304 | tf_op jit(solution)/shard_map/ppermute | solution.py:984
  196.1 12.4 %shard_map.253 = (bf16[5,512,768]{2,1,0:T(8,128)(2,1)}, bf16[5,512,3072]{2,1,0:T(8,128)(2,1)}, bf16[5,512,768]{2,1,0:T(8,128)(2,1)}, f32[5,8,768]{2,1,0:T(8,128)...) custom-call(s32[60]{0:T(128)S(1)} %reshape.556.sp_ref, ...), custom_call_target="tpu_custom_call", output_to_operand_aliasing={{0}: (14, {}), {1}: (15, {}), {2}: (16, {}), {3}: (17, {}),... | custom-call | flops 10000000000 | bytes 10000000 | tf_op jit(solution)/shard_map/pallas_call | solution.py:96
  208.6 18.1 %shard_map.254 = (f32[5,64,768]{2,1,0:T(8,128)}, bf16[512,768]{1,0:T(8,128)(2,1)S(1)}, bf16[512,1536]{1,0:T(8,128)(2,1)S(1)}, bf16[512,1536]{1,0:T(8,128)(2,1)}) custom-call(s32[60]{0:T(128)S(1)} %reshape.556.sp_ref, bf16[5,512,768]{2,1,0:T(8,128)(2,1)} %get-tuple-element.283.refs_0_.refs_5_, ...), custom_call_target="tpu_custom_call", output_to_operand_aliasing={{0}: (11, {})} | custom-call | flops 20000000000 | bytes 20000000 | tf_op jit(solution)/shard_map/pallas_call | solution.py:96
  241.0 9.6 %shard_map.257 = (bf16[5,512,768]{2,1,0:T(8,128)(2,1)}, bf16[5,512,768]{2,1,0:T(8,128)(2,1)}, bf16[5,512,768]{2,1,0:T(8,128)(2,1)}, bf16[5,512,1536]{2,1,0:T(8,128)(2,1)}) custom-call(s32[60]{0:T(128)S(1)} %reshape.556.sp_ref, ...), custom_call_target="tpu_custom_call", output_to_operand_aliasing={{0}: (7, {}), {1}: (8, {}), {2}: (9, {}), {3}: (10, {})} | custom-call | flops 14000000000 | bytes 14000000 | tf_op jit(solution)/shard_map/pallas_call | solution.py:96
  250.6 11.1 %shard_map.258 = (bf16[5,512,768]{2,1,0:T(8,128)(2,1)}, bf16[5,512,768]{2,1,0:T(8,128)(2,1)}, bf16[5,512,3072]{2,1,0:T(8,128)(2,1)}, bf16[5,512,3072]{2,1,0:T(8,...) custom-call(s32[60]{0:T(128)S(1)} %reshape.556.sp_ref, ...), custom_call_target="tpu_custom_call", output_to_operand_aliasing={{0}: (9, {}), {1}: (10, {}), {2}: (11, {}), {3}: (12, {}), ... | custom-call | flops 10000000000 | bytes 10000000 | tf_op jit(solution)/shard_map/pallas_call | solution.py:96
  266.3 12.4 %shard_map.261 = (bf16[5,512,768]{2,1,0:T(8,128)(2,1)}, bf16[5,512,3072]{2,1,0:T(8,128)(2,1)}, bf16[5,512,768]{2,1,0:T(8,128)(2,1)}, f32[5,8,768]{2,1,0:T(8,128)...) custom-call(s32[60]{0:T(128)S(1)} %reshape.556.sp_ref, ...), custom_call_target="tpu_custom_call", output_to_operand_aliasing={{0}: (14, {}), {1}: (15, {}), {2}: (16, {}), {3}: (17, {}),... | custom-call | flops 10000000000 | bytes 10000000 | tf_op jit(solution)/shard_map/pallas_call | solution.py:96
  278.8 17.9 %shard_map.262 = (f32[5,64,768]{2,1,0:T(8,128)}, bf16[512,768]{1,0:T(8,128)(2,1)S(1)}, bf16[512,1536]{1,0:T(8,128)(2,1)S(1)}, bf16[512,1536]{1,0:T(8,128)(2,1)}) custom-call(s32[60]{0:T(128)S(1)} %reshape.556.sp_ref, bf16[5,512,768]{2,1,0:T(8,128)(2,1)} %get-tuple-element.334.refs_0_.refs_5_, ...), custom_call_target="tpu_custom_call", output_to_operand_aliasing={{0}: (11, {})} | custom-call | flops 20000000000 | bytes 20000000 | tf_op jit(solution)/shard_map/pallas_call | solution.py:96
  316.4 11.0 %shard_map.264 = (bf16[5,512,768]{2,1,0:T(8,128)(2,1)}, bf16[5,512,768]{2,1,0:T(8,128)(2,1)}, bf16[5,512,3072]{2,1,0:T(8,128)(2,1)}, bf16[5,512,3072]{2,1,0:T(8,...) custom-call(s32[60]{0:T(128)S(1)} %reshape.556.sp_ref, ...), custom_call_target="tpu_custom_call", output_to_operand_aliasing={{0}: (9, {}), {1}: (10, {}), {2}: (11, {}), {3}: (12, {}), ... | custom-call | flops 10000000000 | bytes 10000000 | tf_op jit(solution)/shard_map/pallas_call | solution.py:96
  331.2 12.4 %shard_map.265 = (bf16[5,512,768]{2,1,0:T(8,128)(2,1)}, bf16[5,512,3072]{2,1,0:T(8,128)(2,1)}, bf16[5,512,768]{2,1,0:T(8,128)(2,1)}, f32[5,8,768]{2,1,0:T(8,128)...) custom-call(s32[60]{0:T(128)S(1)} %reshape.556.sp_ref, ...), custom_call_target="tpu_custom_call", output_to_operand_aliasing={{0}: (14, {}), {1}: (15, {}), {2}: (16, {}), {3}: (17, {}),... | custom-call | flops 10000000000 | bytes 10000000 | tf_op jit(solution)/shard_map/pallas_call | solution.py:96
  343.6 13.5 %shard_map.266 = (f32[5,64,768]{2,1,0:T(8,128)}, bf16[512,768]{1,0:T(8,128)(2,1)S(1)}, bf16[512,1536]{1,0:T(8,128)(2,1)S(1)}, bf16[512,1536]{1,0:T(8,128)(2,1)S(1)}) custom-call(s32[60]{0:T(128)S(1)} %reshape.556.sp_ref, bf16[5,512,768]{2,1,0:T(8,128)(2,1)} %get-tuple-element.343.refs_0_, ...), custom_call_target="tpu_custom_call", output_to_operand_aliasing={{0}: (11, {})} | custom-call | flops 20000000000 | bytes 20000000 | tf_op jit(solution)/shard_map/pallas_call | solution.py:96
  370.4 11.6 %shard_map.268 = (bf16[384,3072]{1,0:T(8,128)(2,1)S(1)}, bf16[384,3072]{1,0:T(8,128)(2,1)S(1)}) custom-call(s32[60]{0:T(128)S(1)} %reshape.556.sp_ref, bf16[5,512,768]{2,1,0:T(8,128)(2,1)} %get-tuple-element.393.refs_0_.refs_13_, bf16[5,512,3072]{2,1,0:T(8,128)(2,1)} %get-tuple-element.394.refs_1_), custom_call_target="tpu_custom_call" | custom-call | flops 14000000000 | bytes 14000000 | tf_op jit(solution)/shard_map/pallas_call | solution.py:96
  384.7 11.5 %shard_map.269 = (bf16[384,3072]{1,0:T(8,128)(2,1)S(1)}, bf16[384,3072]{1,0:T(8,128)(2,1)S(1)}) custom-call(s32[60]{0:T(128)S(1)} %reshape.556.sp_ref, bf16[5,512,768]{2,1,0:T(8,128)(2,1)} %get-tuple-element.406.refs_0_, bf16[5,512,3072]{2,1,0:T(8,128)(2,1)} %get-tuple-element.397.refs_1_.refs_14_), custom_call_target="tpu_custom_call" | custom-call | flops 14000000000 | bytes 14000000 | tf_op jit(solution)/shard_map/pallas_call | solution.py:96
  396.3 13.5 %shard_map.270 = (bf16[5,512,768]{2,1,0:T(8,128)(2,1)}, bf16[5,512,3072]{2,1,0:T(8,128)(2,1)}, bf16[5,512,768]{2,1,0:T(8,128)(2,1)}, f32[5,8,768]{2,1,0:T(8,128)...) custom-call(s32[60]{0:T(128)S(1)} %reshape.556.sp_ref, ...), custom_call_target="tpu_custom_call", output_to_operand_aliasing={{0}: (14, {}), {1}: (15, {}), {2}: (16, {}), {3}: (17, {}),... | custom-call | flops 10000000000 | bytes 10000000 | tf_op jit(solution)/shard_map/pallas_call | solution.py:96
  429.9 13.3 %shard_map.273 = (f32[5,64,768]{2,1,0:T(8,128)}, bf16[512,768]{1,0:T(8,128)(2,1)S(1)}, bf16[512,1536]{1,0:T(8,128)(2,1)S(1)}, bf16[512,1536]{1,0:T(8,128)(2,1)}) custom-call(s32[60]{0:T(128)S(1)} %reshape.556.sp_ref, bf16[5,512,768]{2,1,0:T(8,128)(2,1)} %get-tuple-element.343.refs_0_, ...), custom_call_target="tpu_custom_call", output_to_operand_aliasing={{0}: (11, {})} | custom-call | flops 20000000000 | bytes 20000000 | tf_op jit(solution)/shard_map/pallas_call | solution.py:96
  446.9 40.9 %collective-permute-start.20 = (bf16[192,3072]{1,0:T(8,128)(2,1)}, bf16[192,3072]{1,0:T(8,128)(2,1)}, u32[]{:S(2)}, u32[]{:S(2)}) collective-permute-start(bf16[192,3072]{1,0:T(8,128)(2,1)} %constant_dynamic-slice_fusion.12), channel_id=1, source_target_pairs={{0,2},{1,3},{2,0},{3,1},{4,6},{5,7},{6,4},{7,5},{8,10},{9,11},{10,... | collective-permute-start | bytes 3538952 | tf_op jit(solution)/shard_map/ppermute | solution.py:781
  499.5 15.4 %collective-permute-done.20 = bf16[192,3072]{1,0:T(8,128)(2,1)} collective-permute-done((bf16[192,3072]{1,0:T(8,128)(2,1)}, bf16[192,3072]{1,0:T(8,128)(2,1)}, u32[]{:S(2)}, u32[]{:S(2)}) %collective-permute-start.20) | collective-permute-done | bytes 1179680 | tf_op jit(solution)/shard_map/ppermute | solution.py:781
  517.4 16.9 %shard_map.275 = (bf16[384,3072]{1,0:T(8,128)(2,1)}, bf16[384,3072]{1,0:T(8,128)(2,1)S(1)}) custom-call(s32[60]{0:T(128)S(1)} %reshape.556.sp_ref, bf16[5,512,768]{2,1,0:T(8,128)(2,1)} %get-tuple-element.427.refs_1_.refs_0_, bf16[5,512,768]{2,1,0:T(8,128)(2,1)} %get-tuple-element.369.refs_0_.refs_11_.refs_1_, ...), custom_call_target="tpu_custom_call" | custom-call | flops 16999999488 | bytes 17000000 | tf_op jit(solution)/shard_map/pallas_call | solution.py:96
  591.0 9.5 %collective-permute-done.33 = bf16[96,3072]{1,0:T(8,128)(2,1)} collective-permute-done((bf16[96,3072]{1,0:T(8,128)(2,1)}, bf16[96,3072]{1,0:T(8,128)(2,1)}, u32[]{:S(2)}, u32[]{:S(2)}) %collective-permute-start.33) | collective-permute-done | bytes 589856 | tf_op jit(solution)/shard_map/ppermute | solution.py:781
  609.1 19.4 %collective-permute-done.37 = bf16[48,3072]{1,0:T(8,128)(2,1)S(1)} collective-permute-done((bf16[48,3072]{1,0:T(8,128)(2,1)S(1)}, bf16[48,3072]{1,0:T(8,128)(2,1)S(1)}, u32[]{:S(2)}, u32[]{:S(2)}) %collective-permute-start.37) | collective-permute-done | bytes 294944 | tf_op jit(solution)/shard_map/ppermute | solution.py:781
  629.1 12.1 %collective-permute-done.35 = bf16[48,3072]{1,0:T(8,128)(2,1)S(1)} collective-permute-done((bf16[48,3072]{1,0:T(8,128)(2,1)S(1)}, bf16[48,3072]{1,0:T(8,128)(2,1)S(1)}, u32[]{:S(2)}, u32[]{:S(2)}) %collective-permute-start.35) | collective-permute-done | bytes 294944 | tf_op jit(solution)/shard_map/ppermute | solution.py:781
  674.9 16.6 %collective-permute-done.43 = bf16[192,3072]{1,0:T(8,128)(2,1)} collective-permute-done((bf16[192,3072]{1,0:T(8,128)(2,1)}, bf16[192,3072]{1,0:T(8,128)(2,1)}, u32[]{:S(2)}, u32[]{:S(2)}) %collective-permute-start.43) | collective-permute-done | bytes 1179680 | tf_op jit(solution)/shard_map/ppermute | solution.py:781
  697.4 7.8 %shard_map.276 = f32[768,3072]{1,0:T(8,128)} custom-call(s32[60]{0:T(128)S(1)} %reshape.556.sp_ref, bf16[384,3072]{1,0:T(8,128)(2,1)S(1)} %copy-done.12, bf16[384,3072]{1,0:T(8,128)(2,1)} %collective-permute-done.44.refs_1_), custom_call_target="tpu_custom_call" | custom-call | flops 5000000000 | bytes 5000000 | tf_op jit(solution)/shard_map/pallas_call | solution.py:96
  716.5 8.6 %shard_map.277 = (f32[768,2304]{1,0:T(8,128)}, f32[768,768]{1,0:T(8,128)}) custom-call(s32[60]{0:T(128)S(1)} %reshape.556.sp_ref, bf16[384,3072]{1,0:T(8,128)(2,1)} %pad_maximum_fusion.5.refs_0_, bf16[384,3072]{1,0:T(8,128)(2,1)} %collective-permute-done.47.refs_1_), custom_call_target="tpu_custom_call" | custom-call | flops 5000000000 | bytes 5000000 | tf_op jit(solution)/shard_map/pallas_call | solution.py:96
  (473 shorter events, 288.1 us)
Async XLA Ops:
  2.7 22.1 %collective-permute-start = (s32[2,2176]{1,0:T(2,128)}, s32[2,2176]{1,0:T(2,128)}, u32[]{:S(2)}, u32[]{:S(2)}) collective-permute-start(s32[2,2176]{1,0:T(2,128)} %pad_add_fusion), channel_id=1, source_target_pairs={{0,1},{1,0},{2,3},{3,2},{4,5},{5,4},{6,7},{7,6},{8,9},{9,8},{10,11... | collective-permute-start | bytes 52232 | tf_op jit(solution)/shard_map/ppermute | solution.py:845
  6.4 24.9 %collective-permute-start.1 = (bf16[2,512,768]{2,1,0:T(8,128)(2,1)}, bf16[2,512,768]{2,1,0:T(8,128)(2,1)}, u32[]{:S(2)}, u32[]{:S(2)}) collective-permute-start(bf16[2,512,768]{2,1,0:T(8,128)(2,1)} %select_bitcast_fusion.2), channel_id=1, source_target_pairs={{0,1},{1,0},{2,3},{3,2},{4,5},{5,4},{6,7},{7,6},{8,9},{9,8},{10,11... | collective-permute-start | bytes 4718600 | tf_op jit(solution)/shard_map/ppermute | solution.py:845
  71.8 18.6 %collective-permute-start.3 = (bf16[512,768]{1,0:T(8,128)(2,1)S(1)}, bf16[512,768]{1,0:T(8,128)(2,1)S(1)}, u32[]{:S(2)}, u32[]{:S(2)}) collective-permute-start(bf16[512,768]{1,0:T(8,128)(2,1)S(1)} %get-tuple-element.266), channel_id=1, source_target_pairs={{0,16},{1,17},{2,18},{3,19},{4,20},{5,21},{6,22},{7,23},{8,24},{9,... | collective-permute-start | bytes 2359304 | tf_op jit(solution)/shard_map/ppermute | solution.py:984
  122.4 27.3 %collective-permute-start.5 = (bf16[512,768]{1,0:T(8,128)(2,1)S(1)}, bf16[512,768]{1,0:T(8,128)(2,1)S(1)}, u32[]{:S(2)}, u32[]{:S(2)}) collective-permute-start(bf16[512,768]{1,0:T(8,128)(2,1)S(1)} %get-tuple-element.434), channel_id=1, source_target_pairs={{0,16},{1,17},{2,18},{3,19},{4,20},{5,21},{6,22},{7,23},{8,24},{9,... | collective-permute-start | bytes 2359304 | tf_op jit(solution)/shard_map/ppermute | solution.py:984
  161.9 34.1 %collective-permute-start.8 = (bf16[512,768]{1,0:T(8,128)(2,1)S(1)}, bf16[512,768]{1,0:T(8,128)(2,1)S(1)}, u32[]{:S(2)}, u32[]{:S(2)}) collective-permute-start(bf16[512,768]{1,0:T(8,128)(2,1)S(1)} %get-tuple-element.309), channel_id=1, source_target_pairs={{16,0},{17,1},{18,2},{19,3},{20,4},{21,5},{22,6},{23,7},{24,8},{25... | collective-permute-start | bytes 2359304 | tf_op jit(solution)/shard_map/ppermute | solution.py:991
  184.1 43.8 %collective-permute-start.10 = (bf16[512,768]{1,0:T(8,128)(2,1)S(1)}, bf16[512,768]{1,0:T(8,128)(2,1)S(1)}, u32[]{:S(2)}, u32[]{:S(2)}) collective-permute-start(bf16[512,768]{1,0:T(8,128)(2,1)S(1)} %get-tuple-element.436), channel_id=1, source_target_pairs={{0,16},{1,17},{2,18},{3,19},{4,20},{5,21},{6,22},{7,23},{8,24},{9,... | collective-permute-start | bytes 2359304 | tf_op jit(solution)/shard_map/ppermute | solution.py:984
  239.7 26.6 %collective-permute-start.14 = (bf16[512,768]{1,0:T(8,128)(2,1)S(1)}, bf16[512,768]{1,0:T(8,128)(2,1)S(1)}, u32[]{:S(2)}, u32[]{:S(2)}) collective-permute-start(bf16[512,768]{1,0:T(8,128)(2,1)S(1)} %get-tuple-element.433), channel_id=1, source_target_pairs={{16,0},{17,1},{18,2},{19,3},{20,4},{21,5},{22,6},{23,7},{24,8},{25... | collective-permute-start | bytes 2359304 | tf_op jit(solution)/shard_map/ppermute | solution.py:991
  261.7 36.2 %collective-permute-start.12 = (bf16[512,768]{1,0:T(8,128)(2,1)S(1)}, bf16[512,768]{1,0:T(8,128)(2,1)S(1)}, u32[]{:S(2)}, u32[]{:S(2)}) collective-permute-start(bf16[512,768]{1,0:T(8,128)(2,1)S(1)} %get-tuple-element.438), channel_id=1, source_target_pairs={{0,16},{1,17},{2,18},{3,19},{4,20},{5,21},{6,22},{7,23},{8,24},{9,... | collective-permute-start | bytes 2359304 | tf_op jit(solution)/shard_map/ppermute | solution.py:984
  309.8 21.3 %collective-permute-start.16 = (bf16[512,768]{1,0:T(8,128)(2,1)S(1)}, bf16[512,768]{1,0:T(8,128)(2,1)S(1)}, u32[]{:S(2)}, u32[]{:S(2)}) collective-permute-start(bf16[512,768]{1,0:T(8,128)(2,1)S(1)} %get-tuple-element.435), channel_id=1, source_target_pairs={{16,0},{17,1},{18,2},{19,3},{20,4},{21,5},{22,6},{23,7},{24,8},{25... | collective-permute-start | bytes 2359304 | tf_op jit(solution)/shard_map/ppermute | solution.py:991
  369.1 27.2 %collective-permute-start.18 = (bf16[512,768]{1,0:T(8,128)(2,1)S(1)}, bf16[512,768]{1,0:T(8,128)(2,1)S(1)}, u32[]{:S(2)}, u32[]{:S(2)}) collective-permute-start(bf16[512,768]{1,0:T(8,128)(2,1)S(1)} %get-tuple-element.437), channel_id=1, source_target_pairs={{16,0},{17,1},{18,2},{19,3},{20,4},{21,5},{22,6},{23,7},{24,8},{25... | collective-permute-start | bytes 2359304 | tf_op jit(solution)/shard_map/ppermute | solution.py:991
  427.3 60.6 %collective-permute-start.22 = (bf16[384,3072]{1,0:T(8,128)(2,1)}, bf16[384,3072]{1,0:T(8,128)(2,1)}, u32[]{:S(2)}, u32[]{:S(2)}) collective-permute-start(bf16[384,3072]{1,0:T(8,128)(2,1)} %get-tuple-element.409), channel_id=1, source_target_pairs={{0,1},{1,0},{2,3},{3,2},{4,5},{5,4},{6,7},{7,6},{8,9},{9,8},{10,11... | collective-permute-start | bytes 7077896 | tf_op jit(solution)/shard_map/ppermute | solution.py:784
  444.4 47.3 %collective-permute-start.21 = (bf16[512,1536]{1,0:T(8,128)(2,1)}, bf16[512,1536]{1,0:T(8,128)(2,1)}, u32[]{:S(2)}, u32[]{:S(2)}) collective-permute-start(bf16[512,1536]{1,0:T(8,128)(2,1)} %get-tuple-element.418), channel_id=1, source_target_pairs={{0,1},{1,0},{2,3},{3,2},{4,5},{5,4},{6,7},{7,6},{8,9},{9,8},{10,11... | collective-permute-start | bytes 4718600 | tf_op jit(solution)/shard_map/ppermute | solution.py:845
  446.9 68.0 %collective-permute-start.20 = (bf16[192,3072]{1,0:T(8,128)(2,1)}, bf16[192,3072]{1,0:T(8,128)(2,1)}, u32[]{:S(2)}, u32[]{:S(2)}) collective-permute-start(bf16[192,3072]{1,0:T(8,128)(2,1)} %constant_dynamic-slice_fusion.12), channel_id=1, source_target_pairs={{0,2},{1,3},{2,0},{3,1},{4,6},{5,7},{6,4},{7,5},{8,10},{9,11},{10,... | collective-permute-start | bytes 3538952 | tf_op jit(solution)/shard_map/ppermute | solution.py:781
  491.7 48.2 %collective-permute-start.24 = (bf16[192,3072]{1,0:T(8,128)(2,1)}, bf16[192,3072]{1,0:T(8,128)(2,1)}, u32[]{:S(2)}, u32[]{:S(2)}) collective-permute-start(bf16[192,3072]{1,0:T(8,128)(2,1)} %constant_dynamic-slice_fusion.11), channel_id=1, source_target_pairs={{0,2},{1,3},{2,0},{3,1},{4,6},{5,7},{6,4},{7,5},{8,10},{9,11},{10,... | collective-permute-start | bytes 3538952 | tf_op jit(solution)/shard_map/ppermute | solution.py:781
  517.4 16.9 %collective-permute-start.25 = (bf16[96,3072]{1,0:T(8,128)(2,1)}, bf16[96,3072]{1,0:T(8,128)(2,1)}, u32[]{:S(2)}, u32[]{:S(2)}) collective-permute-start(bf16[96,3072]{1,0:T(8,128)(2,1)} %constant_dynamic-slice_fusion.10), channel_id=1, source_target_pairs={{0,4},{1,5},{2,6},{3,7},{4,0},{5,1},{6,2},{7,3},{8,12},{9,13},{10,... | collective-permute-start | bytes 1769480 | tf_op jit(solution)/shard_map/ppermute | solution.py:781
  542.9 35.9 %collective-permute-start.27 = (bf16[96,3072]{1,0:T(8,128)(2,1)}, bf16[96,3072]{1,0:T(8,128)(2,1)}, u32[]{:S(2)}, u32[]{:S(2)}) collective-permute-start(bf16[96,3072]{1,0:T(8,128)(2,1)} %constant_dynamic-slice_fusion.5), channel_id=1, source_target_pairs={{0,4},{1,5},{2,6},{3,7},{4,0},{5,1},{6,2},{7,3},{8,12},{9,13},{10,... | collective-permute-start | bytes 1769480 | tf_op jit(solution)/shard_map/ppermute | solution.py:781
  543.6 30.5 %collective-permute-start.28 = (bf16[48,3072]{1,0:T(8,128)(2,1)}, bf16[48,3072]{1,0:T(8,128)(2,1)}, u32[]{:S(2)}, u32[]{:S(2)}) collective-permute-start(bf16[48,3072]{1,0:T(8,128)(2,1)} %constant_dynamic-slice_fusion.4), channel_id=1, source_target_pairs={{0,8},{1,9},{2,10},{3,11},{4,12},{5,13},{6,14},{7,15},{8,0},{9,1},... | collective-permute-start | bytes 884744 | tf_op jit(solution)/shard_map/ppermute | solution.py:781
  575.8 25.9 %collective-permute-start.32 = (bf16[48,3072]{1,0:T(8,128)(2,1)}, bf16[48,3072]{1,0:T(8,128)(2,1)}, u32[]{:S(2)}, u32[]{:S(2)}) collective-permute-start(bf16[48,3072]{1,0:T(8,128)(2,1)} %dynamic-slice_add_fusion.8), channel_id=1, source_target_pairs={{0,8},{1,9},{2,10},{3,11},{4,12},{5,13},{6,14},{7,15},{8,0},{9,1},... | collective-permute-start | bytes 884744 | tf_op jit(solution)/shard_map/ppermute | solution.py:781
  587.3 20.8 %collective-permute-start.30 = (f32[88,128]{1,0:T(8,128)S(1)}, f32[88,128]{1,0:T(8,128)S(1)}, u32[]{:S(2)}, u32[]{:S(2)}) collective-permute-start(f32[88,128]{1,0:T(8,128)S(1)} %pad_bitcast_fusion), channel_id=1, source_target_pairs={{0,1},{1,0},{2,3},{3,2},{4,5},{5,4},{6,7},{7,6},{8,9},{9,8},{10,11... | collective-permute-start | bytes 135176 | tf_op jit(solution)/shard_map/ppermute | solution.py:816
  602.9 25.8 %collective-permute-start.36 = (bf16[96,3072]{1,0:T(8,128)(2,1)S(1)}, bf16[96,3072]{1,0:T(8,128)(2,1)S(1)}, u32[]{:S(2)}, u32[]{:S(2)}) collective-permute-start(bf16[96,3072]{1,0:T(8,128)(2,1)S(1)} %pad_maximum_fusion.11), channel_id=1, source_target_pairs={{0,4},{1,5},{2,6},{3,7},{4,0},{5,1},{6,2},{7,3},{8,12},{9,13},{10,... | collective-permute-start | bytes 1769480 | tf_op jit(solution)/shard_map/ppermute | solution.py:781
  605.0 23.5 %collective-permute-start.37 = (bf16[48,3072]{1,0:T(8,128)(2,1)S(1)}, bf16[48,3072]{1,0:T(8,128)(2,1)S(1)}, u32[]{:S(2)}, u32[]{:S(2)}) collective-permute-start(bf16[48,3072]{1,0:T(8,128)(2,1)S(1)} %constant_dynamic-slice_fusion), channel_id=1, source_target_pairs={{0,8},{1,9},{2,10},{3,11},{4,12},{5,13},{6,14},{7,15},{8,0},{9,1},... | collective-permute-start | bytes 884744 | tf_op jit(solution)/shard_map/ppermute | solution.py:781
  607.7 33.5 %collective-permute-start.35 = (bf16[48,3072]{1,0:T(8,128)(2,1)S(1)}, bf16[48,3072]{1,0:T(8,128)(2,1)S(1)}, u32[]{:S(2)}, u32[]{:S(2)}) collective-permute-start(bf16[48,3072]{1,0:T(8,128)(2,1)S(1)} %dynamic-slice_add_fusion.7), channel_id=1, source_target_pairs={{0,8},{1,9},{2,10},{3,11},{4,12},{5,13},{6,14},{7,15},{8,0},{9,1},... | collective-permute-start | bytes 884744 | tf_op jit(solution)/shard_map/ppermute | solution.py:781
  608.1 34.5 %collective-permute-start.34 = (f32[88,128]{1,0:T(8,128)S(1)}, f32[88,128]{1,0:T(8,128)S(1)}, u32[]{:S(2)}, u32[]{:S(2)}) collective-permute-start(f32[88,128]{1,0:T(8,128)S(1)} %fusion.35), channel_id=1, source_target_pairs={{0,2},{1,3},{2,0},{3,1},{4,6},{5,7},{6,4},{7,5},{8,10},{9,11},{10,... | collective-permute-start | bytes 135176 | tf_op jit(solution)/shard_map/ppermute | solution.py:816
  628.6 18.8 %collective-permute-start.41 = (bf16[48,3072]{1,0:T(8,128)(2,1)S(1)}, bf16[48,3072]{1,0:T(8,128)(2,1)S(1)}, u32[]{:S(2)}, u32[]{:S(2)}) collective-permute-start(bf16[48,3072]{1,0:T(8,128)(2,1)S(1)} %dynamic-slice_add_fusion.6), channel_id=1, source_target_pairs={{0,8},{1,9},{2,10},{3,11},{4,12},{5,13},{6,14},{7,15},{8,0},{9,1},... | collective-permute-start | bytes 884744 | tf_op jit(solution)/shard_map/ppermute | solution.py:781
  629.0 26.9 %collective-permute-start.40 = (bf16[192,3072]{1,0:T(8,128)(2,1)S(1)}, bf16[192,3072]{1,0:T(8,128)(2,1)S(1)}, u32[]{:S(2)}, u32[]{:S(2)}) collective-permute-start(bf16[192,3072]{1,0:T(8,128)(2,1)S(1)} %pad_maximum_fusion.8), channel_id=1, source_target_pairs={{0,2},{1,3},{2,0},{3,1},{4,6},{5,7},{6,4},{7,5},{8,10},{9,11},{10,... | collective-permute-start | bytes 3538952 | tf_op jit(solution)/shard_map/ppermute | solution.py:781
  641.2 19.7 %collective-permute-start.39 = (bf16[96,3072]{1,0:T(8,128)(2,1)S(1)}, bf16[96,3072]{1,0:T(8,128)(2,1)S(1)}, u32[]{:S(2)}, u32[]{:S(2)}) collective-permute-start(bf16[96,3072]{1,0:T(8,128)(2,1)S(1)} %pad_maximum_fusion.12), channel_id=1, source_target_pairs={{0,4},{1,5},{2,6},{3,7},{4,0},{5,1},{6,2},{7,3},{8,12},{9,13},{10,... | collective-permute-start | bytes 1769480 | tf_op jit(solution)/shard_map/ppermute | solution.py:781
  656.6 18.3 %collective-permute-start.44 = (bf16[384,3072]{1,0:T(8,128)(2,1)S(1)}, bf16[384,3072]{1,0:T(8,128)(2,1)}, u32[]{:S(2)}, u32[]{:S(2)}) collective-permute-start(bf16[384,3072]{1,0:T(8,128)(2,1)S(1)} %pad_maximum_fusion.3.refs_0_), channel_id=1, source_target_pairs={{0,1},{1,0},{2,3},{3,2},{4,5},{5,4},{6,7},{7,6},{8,9},{9,8},{10,11... | collective-permute-start | bytes 7077896 | tf_op jit(solution)/shard_map/ppermute | solution.py:784
  662.3 29.2 %collective-permute-start.43 = (bf16[192,3072]{1,0:T(8,128)(2,1)}, bf16[192,3072]{1,0:T(8,128)(2,1)}, u32[]{:S(2)}, u32[]{:S(2)}) collective-permute-start(bf16[192,3072]{1,0:T(8,128)(2,1)} %pad_maximum_fusion.9), channel_id=1, source_target_pairs={{0,2},{1,3},{2,0},{3,1},{4,6},{5,7},{6,4},{7,5},{8,10},{9,11},{10,... | collective-permute-start | bytes 3538952 | tf_op jit(solution)/shard_map/ppermute | solution.py:781
  663.0 42.3 %collective-permute-start.26 = (bf16[2,512,768]{2,1,0:T(8,128)(2,1)}, bf16[2,512,768]{2,1,0:T(8,128)(2,1)S(1)}, u32[]{:S(2)}, u32[]{:S(2)}) collective-permute-start(bf16[2,512,768]{2,1,0:T(8,128)(2,1)} %broadcast_select_fusion.1), channel_id=1, source_target_pairs={{0,1},{1,0},{2,3},{3,2},{4,5},{5,4},{6,7},{7,6},{8,9},{9,8},{10,11... | collective-permute-start | bytes 4718600 | tf_op jit(solution)/shard_map/ppermute | solution.py:845
  670.8 34.5 %collective-permute-start.42 = (f32[88,128]{1,0:T(8,128)S(1)}, f32[88,128]{1,0:T(8,128)S(1)}, u32[]{:S(2)}, u32[]{:S(2)}) collective-permute-start(f32[88,128]{1,0:T(8,128)S(1)} %add.313), channel_id=1, source_target_pairs={{0,8},{1,9},{2,10},{3,11},{4,12},{5,13},{6,14},{7,15},{8,0},{9,1},... | collective-permute-start | bytes 135176 | tf_op jit(solution)/shard_map/ppermute | solution.py:816
  674.8 33.1 %collective-permute-start.46 = (bf16[192,3072]{1,0:T(8,128)(2,1)S(1)}, bf16[192,3072]{1,0:T(8,128)(2,1)S(1)}, u32[]{:S(2)}, u32[]{:S(2)}) collective-permute-start(bf16[192,3072]{1,0:T(8,128)(2,1)S(1)} %pad_maximum_fusion.10), channel_id=1, source_target_pairs={{0,2},{1,5},{2,0},{3,7},{4,6},{5,1},{6,4},{7,3},{8,10},{9,13},{10,... | collective-permute-start | bytes 3538952 | tf_op jit(solution)/shard_map/ppermute | solution.py:781
  693.6 22.8 %collective-permute-start.48 = (bf16[384,3072]{1,0:T(8,128)(2,1)S(1)}, bf16[384,3072]{1,0:T(8,128)(2,1)}, u32[]{:S(2)}, u32[]{:S(2)}) collective-permute-start(bf16[384,3072]{1,0:T(8,128)(2,1)S(1)} %pad_maximum_fusion.4.refs_0_), channel_id=1, source_target_pairs={{0,1},{1,0},{2,3},{3,2},{4,5},{5,4},{6,7},{7,6},{8,9},{9,8},{10,11... | collective-permute-start | bytes 7077896 | tf_op jit(solution)/shard_map/ppermute | solution.py:784
  (126 other events, 958.1 us)
